TPU v7x, 32 devices: a whole 2x2x4 slice. The times are simulated.
32 devices in a mesh: group: 2 (over x), dp: 4 (over y, core), mp: 4 (over z).
Axes of the slice: x: 2, y: 2, z: 4, core: 2. Of those that a mesh axis runs over, the one named last changes fastest.
Arguments:
- query_passage_words: int32 [2, 12, 128], P('group'), may hold values from 0 to 16383, as said below
- difficult_distractors: int32 [12, 7], P('dp'), may hold values from 0 to 11
- vocabulary_vectors: bfloat16 [4096, 16384], P('dp'), may hold values from -6 to 6
- layer_weight_matrix: bfloat16 [4096, 4096], P('dp', 'mp'), may hold values from -0.09375 to 0.09375
- lowering_factor_matrix: bfloat16 [16, 4096], replicated, may hold values from -0.09375 to 0.09375
- raising_factor_matrix: bfloat16 [16, 4096], P(None, 'mp'), may hold values from -1.5 to 1.5
- logit_sharpness: float32 [1], replicated, may hold values from 10 to 500
Outputs:
- embeddings: bfloat16 [2, 12, 4096], P('group', 'dp', 'mp')
- losses: float32 [2, 12], P('group', 'dp')
- adapter_up_gradient: float32 [16, 4096], P(None, 'mp')
Inputs may be any that keep to these rules, and one draw needn't show every extreme that they name: `query_passage_words`: id 0 is padding and fills only the end of a text; every text has at least 16 real tokens, and the first text of each side has 128. A query shares about half of its token slots with its paired passage.
All inputs are finite; a program needn't handle non-finite values.
Results may differ from a plain program's by a relative error of at most 0.018.
Values may be sent and summed in bfloat16 or wider, within the bound.
No kernel may reach another device: no remote copies, remote signals or barrier semaphores. Data moves between devices by JAX's collectives and lax.ppermute only.
A program may use at most 192 MiB of HBM per device.

v0:
```python
import functools

import jax
import jax.numpy as jnp
from jax import lax
from jax.experimental import pallas as pl
from jax.experimental.pallas import tpu as pltpu
from jax.sharding import PartitionSpec as P


def general_body(
    query_passage_words,
    difficult_distractors,
    vocabulary_vectors,
    layer_weight_matrix,
    lowering_factor_matrix,
    raising_factor_matrix,
    logit_sharpness,
):
    group_index = lax.axis_index("group")
    shard_index = lax.axis_index("dp")
    part_index = lax.axis_index("mp")
    shard_count = lax.axis_size("dp")
    side_ids = query_passage_words[0]
    text_count = side_ids.shape[0]
    length = side_ids.shape[1]
    per_shard = text_count // shard_count
    own_ids = lax.dynamic_slice_in_dim(side_ids, shard_index * per_shard, per_shard, 0)
    columns = jnp.take(vocabulary_vectors, side_ids.reshape(-1), axis=1)
    inputs = lax.all_to_all(columns, "dp", split_axis=1, concat_axis=0, tiled=True)
    tokens = inputs.shape[1]
    feature_width = raising_factor_matrix.shape[1]
    wide_inputs = inputs.astype(jnp.float32)
    inverse = lax.rsqrt(jnp.mean(wide_inputs * wide_inputs, axis=0) + 1e-05)
    normed_state = (wide_inputs * inverse[None, :]).astype(jnp.bfloat16)
    linear_map = lax.dot_general(
        lax.all_gather(layer_weight_matrix, "dp", axis=0, tiled=True),
        normed_state,
        (((0,), (0,)), ((), ())),
        preferred_element_type=jnp.float32,
    )
    reduced_sum = jnp.dot(
        lowering_factor_matrix, normed_state, preferred_element_type=jnp.float32
    ).astype(jnp.bfloat16)
    linear_map = linear_map + lax.dot_general(
        raising_factor_matrix,
        reduced_sum,
        (((0,), (0,)), ((), ())),
        preferred_element_type=jnp.float32,
    )
    own_inputs = lax.dynamic_slice_in_dim(
        inputs, part_index * feature_width, feature_width, 0
    ).astype(jnp.float32)
    hidden_state = own_inputs + jax.nn.silu(linear_map)
    mask = (own_ids != 0).astype(jnp.float32)
    counts = jnp.sum(mask, axis=1)
    summed = jnp.einsum("dnl,nl->nd", hidden_state.reshape(feature_width, per_shard, length), mask)
    pooled = (summed / counts[:, None]).astype(jnp.bfloat16)
    gathered = lax.all_gather(pooled, ("group", "dp"), axis=0, tiled=True)
    part_scores = lax.dot_general(
        pooled, gathered, (((1,), (1,)), ((), ())), preferred_element_type=jnp.float32
    )
    gathered_wide = gathered.astype(jnp.float32)
    part_norms = jnp.sum(gathered_wide * gathered_wide, axis=1)
    dots, norms = lax.psum((part_scores, part_norms), "mp")
    rnorm_all = lax.rsqrt(norms + 1e-06)
    all_count = gathered.shape[0]
    half_count = all_count // 2
    own_rows = (
        group_index * half_count + shard_index * per_shard + jnp.arange(per_shard, dtype=jnp.int32)
    )
    rnorm_own = jnp.take(rnorm_all, own_rows)
    cosine = dots * rnorm_own[:, None] * rnorm_all[None, :]
    multiplier_factor = logit_sharpness[0]
    scores = multiplier_factor * cosine
    column_ids = jnp.arange(all_count, dtype=jnp.int32)
    keep = column_ids[None, :] != own_rows[:, None]
    pair = (own_rows + half_count) % all_count
    weight = (group_index == 0).astype(jnp.float32)
    neg_cols = half_count + difficult_distractors
    top = jnp.max(jnp.where(keep, scores, -jnp.inf), axis=1)
    safe_scores = jnp.where(keep, scores, top[:, None])
    expd = jnp.where(keep, jnp.exp(safe_scores - top[:, None]), 0.0)
    neg_exp = (
        jnp.exp(jnp.minimum(jnp.take_along_axis(scores, neg_cols, axis=1) - top[:, None], 0.0))
        * weight
    )
    total = jnp.sum(expd, axis=1) + jnp.sum(neg_exp, axis=1)
    pair_score = jnp.take_along_axis(scores, pair[:, None], axis=1)[:, 0]
    losses = top + jnp.log(total) - pair_score
    onehot = (column_ids[None, None, :] == neg_cols[:, :, None]).astype(jnp.float32)
    probs = (expd + jnp.einsum("rk,rkc->rc", neg_exp, onehot)) / total[:, None]
    target = (column_ids[None, :] == pair[:, None]).astype(jnp.float32)
    grad_scores = (probs - target) / all_count
    coeff = (grad_scores * rnorm_own[:, None] * rnorm_all[None, :]).astype(jnp.bfloat16)
    along = jnp.dot(coeff, gathered, preferred_element_type=jnp.float32)
    pooled_wide = pooled.astype(jnp.float32)
    radial = jnp.sum(grad_scores * cosine, axis=1) * rnorm_own * rnorm_own
    embedding_gradient = multiplier_factor * (along - radial[:, None] * pooled_wide)
    token_grad = jnp.einsum("nd,nl->dnl", embedding_gradient / counts[:, None], mask).reshape(
        feature_width, tokens
    )
    sigma = jax.nn.sigmoid(linear_map)
    local = (token_grad * sigma * (1.0 + linear_map * (1.0 - sigma))).astype(jnp.bfloat16)
    up_portion = lax.dot_general(
        reduced_sum, local, (((1,), (1,)), ((), ())), preferred_element_type=jnp.float32
    )
    adapter_up_gradient = lax.psum(up_portion, ("group", "dp"))
    embeddings = (pooled_wide * rnorm_own[:, None]).astype(jnp.bfloat16)[None]
    return (embeddings, losses[None], adapter_up_gradient)


BLOCK_BITS, GROUP_BITS, CHUNK_BITS, LANE_BITS, ROW_BITS = 11, 9, 8, 7, 4
IDS_PER_BLOCK = 1 << BLOCK_BITS
IDS_PER_GROUP = 1 << GROUP_BITS
CHUNK = 1 << CHUNK_BITS
ROWS = 1 << ROW_BITS
LANES = 1 << LANE_BITS
FEATURE_ROWS = 128
TAKEN = 640
FIRST = 1024
NT = (((1,), (1,)), ((), ()))
VMEM_BYTES = 60 * 1024 * 1024


def mm(a, b, dims=(((1,), (0,)), ((), ()))):
    return lax.dot_general(a, b, dims, preferred_element_type=jnp.float32)


def split(x):
    high = x.astype(jnp.bfloat16)
    return high, (x - high.astype(jnp.float32)).astype(jnp.bfloat16)


def iota(shape, dim):
    return lax.broadcasted_iota(jnp.int32, shape, dim)


def quarter_of(dp_index, cores=2):
    return (dp_index % cores) * 2 + dp_index // cores


def split_quarter(i, j, cores=2):
    shard = lax.axis_index("dp")
    core, side_y = lax.rem(shard, cores), lax.div(shard, cores)
    return (core ^ i) * 2 + (side_y ^ j)


def take_lanes(x, lanes):
    numbers = lax.GatherDimensionNumbers(
        offset_dims=(),
        collapsed_slice_dims=(1,),
        start_index_map=(1,),
        operand_batching_dims=(0,),
        start_indices_batching_dims=(0,),
    )
    mode = lax.GatherScatterMode.PROMISE_IN_BOUNDS
    return lax.gather(x, lanes[..., None], numbers, slice_sizes=(1, 1), mode=mode)


def project_kernel(
    ids_ref,
    hard_ref,
    vocab_ref,
    weight_ref,
    lower_ref,
    out00,
    out01,
    out10,
    out11,
    member_ref,
    held,
    weight,
    lower,
    turned,
    picked_turned,
    parts,
    token_ref,
    small,
    ranks,
    squares,
    residual,
    counted,
    bounds,
    held_sems,
    weight_sem,
    lower_sem,
    bounds_sem,
    out_sems,
    base,
):
    texts, length = ids_ref.shape
    features, vocab = vocab_ref.shape
    blocks = vocab // IDS_PER_BLOCK
    groups = vocab // IDS_PER_GROUP
    span = member_ref.shape[0]
    chunks = span // CHUNK
    per_shard, negatives = hard_ref.shape
    width = out00.shape[1]
    outs = (out00, out01, out10, out11)
    shard = lax.axis_index("dp")

    def vocab_copy(b):
        columns = pl.ds(pl.multiple_of(b * IDS_PER_BLOCK, LANES), IDS_PER_BLOCK)
        return pltpu.make_async_copy(vocab_ref.at[:, columns], held.at[b], held_sems.at[b])

    weight_copy = pltpu.make_async_copy(weight_ref, weight, weight_sem)
    lower_copy = pltpu.make_async_copy(
        lower_ref.at[:, pl.ds(pl.multiple_of(shard * features, LANES), features)], lower, lower_sem
    )
    vocab_copy(0).start()
    lower_copy.start()
    weight_copy.start()
    for b in range(1, blocks):
        vocab_copy(b).start()

    ids = ids_ref[...]
    valid = ids != 0
    group_of = jnp.where(valid, lax.shift_right_logical(ids, GROUP_BITS), groups)
    group_rows = counted.shape[0]
    group_id = iota((group_rows, length), 0)
    below = jnp.zeros((group_rows, length), jnp.float32)
    for text in range(texts):
        below += jnp.where(group_of[text : text + 1] < group_id, 1.0, 0.0)
    before = jnp.broadcast_to(jnp.sum(below, axis=1, keepdims=True), (group_rows, length))
    counted[...] = before.astype(jnp.int32)
    bounds_copy = pltpu.make_async_copy(counted, bounds, bounds_sem)
    bounds_copy.start()
    earlier = jnp.where(iota((length, length), 0) < iota((length, length), 1), 1.0, 0.0).astype(
        jnp.bfloat16
    )
    for text in range(texts):
        here = jnp.where(group_of[text : text + 1] == group_id, 1.0, 0.0)
        inside = mm(here.astype(jnp.bfloat16), earlier)
        ranks[pl.ds(text, 1), :] = jnp.sum(here * (inside + before), axis=0, keepdims=True)
        before += jnp.broadcast_to(jnp.sum(here, axis=1, keepdims=True), (group_rows, length))
    text_of = iota((texts, length), 0)
    carried = jnp.where(valid, lax.shift_left(ids, ROW_BITS) + text_of, 0).astype(jnp.float32)
    rank = ranks[...]

    def place(p, carry):
        position = (iota((LANES, length), 0) + (p * LANES + base)).astype(jnp.float32)
        total = jnp.zeros((LANES, length), jnp.float32)
        for text in range(texts):
            total += jnp.where(rank[text : text + 1] == position, carried[text : text + 1], 0.0)
        found = jnp.broadcast_to(jnp.sum(total, axis=1, keepdims=True), (LANES, LANES))
        start = pl.multiple_of(p * LANES, LANES)
        row = found.T[0:1].astype(jnp.int32)
        token = lax.shift_right_logical(row, ROW_BITS)
        token_ref[pl.ds(p, 1), :] = jnp.where(token == 0, -vocab, token)
        found = found.astype(jnp.int32)
        real = (found >= ROWS) & ((found & (ROWS - 1)) == iota((LANES, LANES), 1))
        member_ref[pl.ds(start, LANES), :] = jnp.where(real, 1.0, 0.0).astype(jnp.bfloat16)
        turned[:, pl.ds(start, LANES)] = jnp.zeros((TAKEN, LANES), jnp.bfloat16)
        picked_turned[:, pl.ds(start, LANES)] = jnp.zeros((features - TAKEN, LANES), jnp.bfloat16)
        return carry

    lax.fori_loop(0, span // LANES, place, 0)
    residual[...] = jnp.zeros_like(residual)
    squares[...] = jnp.zeros_like(squares)
    small[...] = jnp.zeros_like(small)
    small[0:per_shard, chunks : chunks + negatives] = hard_ref[...].astype(jnp.float32)
    lower_copy.wait()
    weight_copy.wait()
    bounds_copy.wait()

    def send(start, size):
        rows = pl.ds(start, size)
        for q in range(4):
            pltpu.make_async_copy(parts.at[q, rows], outs[q].at[rows], out_sems.at[q]).start()

    def project(k, carry):
        start = pl.multiple_of(k * CHUNK, CHUNK)
        across = pl.ds(start, CHUNK)
        upright = jnp.concatenate([turned[:, across], picked_turned[:, across]], axis=0)
        x = upright.T
        for q in range(4):
            at = pl.multiple_of(split_quarter(q // 2, q % 2) * width, LANES)
            product = mm(x, weight[:, pl.ds(at, width)])
            parts[q, pl.ds(start, CHUNK), :] = product.astype(jnp.bfloat16)
        send(start, CHUNK)
        reduced = mm(lower[...], upright).astype(jnp.bfloat16)
        for q in range(4):
            parts[q, pl.ds(pl.multiple_of(span + k * ROWS, ROWS), ROWS), :] = reduced
        wide = upright.astype(jnp.float32)
        squares[pl.ds(k, 1), :] = jnp.sum(wide * wide, axis=0, keepdims=True)
        member = member_ref[pl.ds(start, CHUNK), :].astype(jnp.float32).T.astype(jnp.bfloat16)
        residual[...] += mm(member[0:ROWS], x)
        return carry

    def zero(k, carry):
        start = pl.multiple_of(k * CHUNK, CHUNK)
        for q in range(4):
            parts[q, pl.ds(start, CHUNK), :] = jnp.zeros((CHUNK, width), jnp.bfloat16)
            parts[q, pl.ds(pl.multiple_of(span + k * ROWS, ROWS), ROWS), :] = jnp.zeros(
                (ROWS, width), jnp.bfloat16
            )
        send(start, CHUNK)
        return carry

    def within(place):
        return jnp.clip(place - base, 0, span)

    def take(b, done):
        vocab_copy(b).wait()
        for part in range(IDS_PER_BLOCK // IDS_PER_GROUP):
            group = b * (IDS_PER_BLOCK // IDS_PER_GROUP) + part
            first, last = within(bounds[group, 0]), within(bounds[group + 1, 0])
            begin = lax.shift_right_logical(first, LANE_BITS)
            end = lax.shift_right_logical(last + LANES - 1, LANE_BITS)

            def window(p, carry):
                at = pl.ds(pl.multiple_of(p * LANES, LANES), LANES)
                token = token_ref[pl.ds(p, 1), :] - group * IDS_PER_GROUP
                token = jnp.broadcast_to(token, (IDS_PER_GROUP, LANES))
                short = token.astype(jnp.int16)
                picked = jnp.where(
                    short == iota((IDS_PER_GROUP, LANES), 0).astype(jnp.int16), 1.0, 0.0
                ).astype(jnp.bfloat16)
                columns = pl.ds(part * IDS_PER_GROUP, IDS_PER_GROUP)
                found = mm(held[b, TAKEN:features, columns], picked)
                lane = (token[0:FEATURE_ROWS] & (LANES - 1)).astype(jnp.int16)
                tile = lax.shift_right_arithmetic(token[0:FEATURE_ROWS], LANE_BITS)
                tile = tile.astype(jnp.int16)
                for f in range(TAKEN // FEATURE_ROWS):
                    rows = pl.ds(f * FEATURE_ROWS, FEATURE_ROWS)
                    total = turned[rows, at]
                    for j in range(IDS_PER_GROUP // LANES):
                        columns = pl.ds(part * IDS_PER_GROUP + j * LANES, LANES)
                        total = jnp.where(tile == j, take_lanes(held[b, rows, columns], lane), total)
                    turned[rows, at] = total
                picked_turned[:, at] += found.astype(jnp.bfloat16)
                return carry

            lax.fori_loop(begin, jnp.where(last > first, end, begin), window, 0)
        full = lax.shift_right_logical(last, CHUNK_BITS)
        lax.fori_loop(done, full, project, 0)
        return full

    done = lax.fori_loop(0, blocks, take, 0)
    used = lax.shift_right_logical(within(bounds[groups, 0]) + CHUNK - 1, CHUNK_BITS)
    lax.fori_loop(done, used, project, 0)
    lax.fori_loop(used, chunks, zero, 0)

    hard = small[...].T[0:ROWS]
    lane = iota((ROWS, width), 1)
    misc = jnp.concatenate([squares[...], jnp.zeros((ROWS - squares.shape[0], width), jnp.float32)])
    for i in range(per_shard):
        misc += jnp.where(lane == shard * per_shard + i, hard[:, i : i + 1], 0.0)
    mine = lax.axis_index("mp") == shard
    for q in range(4):
        start = pl.multiple_of(split_quarter(q // 2, q % 2) * width, LANES)
        part = jnp.where(mine, residual[:, pl.ds(start, width)], 0.0)
        parts[q, pl.ds(span + chunks * ROWS, ROWS), :] = misc.astype(jnp.bfloat16)
        parts[q, pl.ds(span + (chunks + 1) * ROWS, ROWS), :] = part.astype(jnp.bfloat16)
    send(span, (chunks + 2) * ROWS)
    for q in range(4):
        pltpu.make_async_copy(parts.at[q], outs[q], out_sems.at[q]).wait()


def pool_kernel(
    ids_ref,
    own_ref,
    core_ref,
    far_ref,
    member_ref,
    own_rest,
    core_rest,
    far_rest,
    member_rest,
    raise_ref,
    pooled_ref,
    slope_ref,
    reduced_ref,
    misc_ref,
    raised,
    total,
    model_width,
):
    texts, length = ids_ref.shape
    width = own_ref.shape[1]
    quarter = quarter_of(lax.axis_index("dp"))
    raised[...] = jnp.zeros_like(raised)
    raised[0:ROWS, :] = raise_ref[:, pl.ds(pl.multiple_of(quarter * width, LANES), width)]
    total[...] = jnp.zeros_like(total)

    def add(refs, member_ref, base):
        span = member_ref.shape[0]
        chunks = span // CHUNK

        def summed(start, size):
            return sum(ref[pl.ds(start, size), :].astype(jnp.float32) for ref in refs)

        misc = summed(span + chunks * ROWS, ROWS)
        if base == 0:
            misc_ref[...] = misc
        inverse = lax.rsqrt(misc / model_width + 1e-05)
        for k in range(chunks):
            at = base + k * CHUNK
            scale = inverse[k : k + 1]
            reduced = (summed(span + k * ROWS, ROWS) * scale).astype(jnp.bfloat16)
            reduced_ref[:, at : at + CHUNK] = reduced
            stacked = jnp.concatenate(
                [reduced.astype(jnp.float32), jnp.broadcast_to(scale, (LANES - ROWS, CHUNK))]
            )
            turned = stacked.T
            low = turned.astype(jnp.bfloat16)
            linear = summed(k * CHUNK, CHUNK) * turned[:, ROWS : ROWS + 1] + mm(low, raised[...])
            sigma = 1.0 / (1.0 + jnp.exp(-linear))
            slope_ref[pl.ds(at, CHUNK), :] = sigma * (1.0 + linear * (1.0 - sigma))
            member = member_ref[pl.ds(k * CHUNK, CHUNK), :].astype(jnp.float32).T
            member = member[0:ROWS].astype(jnp.bfloat16)
            high, rest = split(linear * sigma)
            total[...] += mm(member, high) + mm(member, rest)
        total[...] += summed(span + (chunks + 1) * ROWS, ROWS)

    add((own_ref, core_ref, far_ref), member_ref, 0)
    real = (ids_ref[...] != 0).astype(jnp.float32)

    @pl.when(jnp.sum(real) > member_ref.shape[0])
    def _():
        add((own_rest, core_rest, far_rest), member_rest, member_ref.shape[0])

    counts = jnp.sum(real, axis=1, keepdims=True)
    pooled = total[0:texts] / counts
    pooled = jnp.concatenate([pooled, jnp.zeros((ROWS - texts, width), jnp.float32)])
    pooled_ref[...] = pooled.astype(jnp.bfloat16)


def both_sides(near, far):
    queries = lax.axis_index("group") == 0
    return jnp.concatenate([jnp.where(queries, near, far), jnp.where(queries, far, near)], axis=0)


def dots_kernel(near_ref, far_ref, packed_ref):
    near = near_ref[...]
    block = both_sides(near, far_ref[...])
    dots = mm(block, block, NT)
    rows = 2 * ROWS
    packed_ref[...] = jnp.zeros_like(packed_ref)
    packed_ref[0:rows, 0:rows] = dots
    for part in range(near.shape[1] // LANES):
        start = rows + part * ROWS
        packed_ref[start : start + ROWS, :] = near[:, part * LANES : (part + 1) * LANES].astype(
            jnp.float32
        )


def score_kernel(
    ids_ref,
    near_ref,
    far_ref,
    packed0,
    packed1,
    packed2,
    packed3,
    dots0,
    dots1,
    dots2,
    dots3,
    misc_ref,
    slope_ref,
    reduced_ref,
    member_ref,
    member_rest,
    sharp_ref,
    embed_ref,
    loss_ref,
    up_ref,
    negatives,
):
    texts, length = ids_ref.shape
    chunks = member_ref.shape[0] // CHUNK
    rows = 2 * ROWS
    width = near_ref.shape[1]
    per_shard = loss_ref.shape[1]
    group, shard = lax.axis_index("group"), lax.axis_index("dp")
    dots = ((dots0[...] + dots1[...]) + (dots2[...] + dots3[...]))[:, 0:rows]
    down, across = iota((rows, rows), 0), iota((rows, rows), 1)
    same = down == across
    real = (lax.rem(down, ROWS) < texts) & (lax.rem(across, ROWS) < texts)
    diagonal = jnp.where(same, dots, 0.0)
    rnorm_row = lax.rsqrt(jnp.sum(diagonal, axis=0, keepdims=True) + 1e-06)
    rnorm_col = lax.rsqrt(jnp.sum(diagonal, axis=1, keepdims=True) + 1e-06)
    sharpness = sharp_ref[0]
    cosine = dots * rnorm_col * rnorm_row
    scores = sharpness * cosine
    keep = real & ~same
    top = jnp.max(jnp.where(keep, scores, -jnp.inf), axis=0, keepdims=True)
    top = jnp.where(lax.rem(across[0:1], ROWS) < texts, top, 0.0)
    powers = jnp.exp(jnp.where(real, jnp.minimum(scores - top, 0.0), 0.0))
    hard = misc_ref[chunks : chunks + negatives, 0:rows].astype(jnp.int32) + ROWS
    times = jnp.zeros((rows, rows), jnp.float32)
    for k in range(negatives):
        times += jnp.where(hard[k : k + 1] == down, 1.0, 0.0)
    times = jnp.where(across < texts, times, 0.0)
    weights = (jnp.where(keep, 1.0, 0.0) + jnp.where(real, times, 0.0)) * powers
    total = jnp.sum(weights, axis=0, keepdims=True)
    total = jnp.where(lax.rem(across[0:1], ROWS) < texts, total, 1.0)
    pair = (down == lax.rem(across + ROWS, rows)) & real
    pair_score = jnp.sum(jnp.where(pair, scores, 0.0), axis=0, keepdims=True)
    losses = top + jnp.log(total) - pair_score
    grad_scores = (weights / total - jnp.where(pair, 1.0, 0.0)) / (2 * texts)
    coeff = (grad_scores * rnorm_col * rnorm_row).astype(jnp.bfloat16)
    radial = jnp.sum(grad_scores * cosine, axis=0, keepdims=True) * rnorm_row * rnorm_row

    first = shard * per_shard
    loss_col = jnp.sum(jnp.where(same, losses, 0.0), axis=1, keepdims=True)
    at = (iota((rows, LANES), 0) == group * ROWS + first + iota((rows, LANES), 1)) & (
        iota((rows, LANES), 1) < per_shard
    )
    loss_ref[...] = jnp.sum(jnp.where(at, loss_col, 0.0), axis=0, keepdims=True)[:, 0:per_shard]

    mine = both_sides(near_ref[...], far_ref[...])
    along = mm(coeff.astype(jnp.float32).T.astype(jnp.bfloat16), mine)
    radial_col = jnp.sum(jnp.where(same, radial, 0.0), axis=1, keepdims=True)
    grad = sharpness * (along - radial_col * mine.astype(jnp.float32))
    grad = jnp.where(group == 0, grad[0:ROWS], grad[ROWS:rows])
    real_tokens = (ids_ref[...] != 0).astype(jnp.float32)
    counts = jnp.sum(real_tokens, axis=1, keepdims=True)
    grad = grad[0:texts] / counts
    grad = jnp.concatenate([grad, jnp.zeros((LANES - texts, width), jnp.float32)])
    high, rest = split(grad)

    def update(member_ref, base):
        total = jnp.zeros((ROWS, width), jnp.float32)
        for k in range(member_ref.shape[0] // CHUNK):
            at = base + k * CHUNK
            member = member_ref[pl.ds(k * CHUNK, CHUNK), :]
            token_grad = mm(member, high) + mm(member, rest)
            local = (token_grad * slope_ref[pl.ds(at, CHUNK), :]).astype(jnp.bfloat16)
            total += mm(reduced_ref[:, at : at + CHUNK], local)
        return total

    first_part = update(member_ref, 0)
    up_ref[...] = first_part

    @pl.when(jnp.sum(real_tokens) > member_ref.shape[0])
    def _():
        up_ref[...] = first_part + update(member_rest, member_ref.shape[0])

    rnorm_own = jnp.where(group == 0, rnorm_col[0:ROWS], rnorm_col[ROWS:rows])
    chosen = iota((ROWS, ROWS), 1) == iota((ROWS, ROWS), 0) + first
    chosen = jnp.where(chosen & (iota((ROWS, ROWS), 0) < per_shard), 1.0, 0.0).astype(jnp.bfloat16)
    for o, packed in enumerate((packed0, packed1, packed2, packed3)):
        halves = [
            packed[rows + part * ROWS : rows + (part + 1) * ROWS, :]
            for part in range(width // LANES)
        ]
        block = jnp.concatenate(halves, axis=1) * rnorm_own
        picked = mm(chosen, block.astype(jnp.bfloat16)).astype(jnp.bfloat16)
        at = pl.multiple_of(quarter_of(shard ^ o) * width, LANES)
        embed_ref[0, :, pl.ds(at, width)] = picked[0:per_shard]


def any_spec():
    return pl.BlockSpec(memory_space=pl.ANY)


def vmem_spec():
    return pl.BlockSpec(memory_space=pltpu.VMEM)


def smem_spec():
    return pl.BlockSpec(memory_space=pltpu.SMEM)


def exchange(x, axis, size):
    steps = [[(i, i ^ o) for i in range(size)] for o in range(1, size)]
    return [x] + [lax.ppermute(x, axis, step) for step in steps]


def split_body(
    query_passage_words,
    difficult_distractors,
    vocabulary_vectors,
    layer_weight_matrix,
    lowering_factor_matrix,
    raising_factor_matrix,
    logit_sharpness,
):
    shards, parts = lax.axis_size("dp"), lax.axis_size("mp")
    ids = query_passage_words[0]
    texts, length = ids.shape
    tokens = texts * length
    features, vocab = vocabulary_vectors.shape
    blocks = vocab // IDS_PER_BLOCK
    group_rows = 8 * pl.cdiv(vocab // IDS_PER_GROUP + 1, 8)
    per_shard, negatives = difficult_distractors.shape
    rank = lowering_factor_matrix.shape[0]
    part_width = layer_weight_matrix.shape[1]
    width = part_width // shards
    params = pltpu.CompilerParams(vmem_limit_bytes=VMEM_BYTES)
    other_core = [(d, d ^ 1) for d in range(shards)]
    other_y = [(d, d ^ 2) for d in range(shards)]

    def project(base, span):
        rows = span + (span // CHUNK + 2) * ROWS
        own0, own1, away0, away1, member = pl.pallas_call(
            functools.partial(project_kernel, base=base),
            out_shape=[jax.ShapeDtypeStruct((rows, width), jnp.bfloat16)] * 4
            + [jax.ShapeDtypeStruct((span, LANES), jnp.bfloat16)],
            in_specs=[vmem_spec()] * 2 + [any_spec()] * 3,
            out_specs=[any_spec()] * 4 + [vmem_spec()],
            scratch_shapes=[
                pltpu.VMEM((blocks, features, IDS_PER_BLOCK), jnp.bfloat16),
                pltpu.VMEM((features, part_width), jnp.bfloat16),
                pltpu.VMEM((rank, features), jnp.bfloat16),
                pltpu.VMEM((TAKEN, span), jnp.bfloat16),
                pltpu.VMEM((features - TAKEN, span), jnp.bfloat16),
                pltpu.VMEM((4, rows, width), jnp.bfloat16),
                pltpu.VMEM((8 * pl.cdiv(span // LANES, 8), LANES), jnp.int32),
                pltpu.VMEM((LANES, LANES), jnp.float32),
                pltpu.VMEM((texts, length), jnp.float32),
                pltpu.VMEM((8, width), jnp.float32),
                pltpu.VMEM((ROWS, features), jnp.float32),
                pltpu.VMEM((group_rows, length), jnp.int32),
                pltpu.SMEM((group_rows, length), jnp.int32),
                pltpu.SemaphoreType.DMA((blocks,)),
                pltpu.SemaphoreType.DMA,
                pltpu.SemaphoreType.DMA,
                pltpu.SemaphoreType.DMA,
                pltpu.SemaphoreType.DMA((4,)),
            ],
            compiler_params=params,
            name="project",
        )(
            ids,
            difficult_distractors,
            vocabulary_vectors,
            layer_weight_matrix,
            lowering_factor_matrix,
        )
        core1 = lax.ppermute(away1, "dp", other_core)
        core0 = lax.ppermute(away0, "dp", other_core)
        chip1 = (own1.astype(jnp.float32) + core1.astype(jnp.float32)).astype(jnp.bfloat16)
        far = lax.ppermute(chip1, "dp", other_y)
        return own0, core0, far, member

    first = project(0, FIRST)
    many = jnp.sum((ids != 0).astype(jnp.int32)) > FIRST
    left = tokens - FIRST
    shapes = jax.eval_shape(lambda: project(FIRST, left))
    rest = lax.cond(
        many,
        lambda: project(FIRST, left),
        lambda: tuple(jnp.zeros(x.shape, x.dtype) for x in shapes),
    )
    pooled, slope, reduced, misc = pl.pallas_call(
        functools.partial(pool_kernel, model_width=float(features * shards)),
        out_shape=[
            jax.ShapeDtypeStruct((ROWS, width), jnp.bfloat16),
            jax.ShapeDtypeStruct((tokens, width), jnp.float32),
            jax.ShapeDtypeStruct((ROWS, tokens), jnp.bfloat16),
            jax.ShapeDtypeStruct((ROWS, width), jnp.float32),
        ],
        in_specs=[vmem_spec()] * 10,
        out_specs=[vmem_spec()] * 4,
        scratch_shapes=[
            pltpu.VMEM((LANES, width), jnp.bfloat16),
            pltpu.VMEM((ROWS, width), jnp.float32),
        ],
        compiler_params=params,
        name="pool",
    )(ids, *first, *rest, raising_factor_matrix)
    member, member_rest = first[3], rest[3]
    far_side = lax.ppermute(pooled, "group", [(0, 1), (1, 0)])
    rows = 2 * ROWS
    packed = pl.pallas_call(
        dots_kernel,
        out_shape=jax.ShapeDtypeStruct((rows + width // LANES * ROWS, LANES), jnp.float32),
        in_specs=[vmem_spec()] * 2,
        out_specs=vmem_spec(),
        compiler_params=params,
        name="dots",
    )(pooled, far_side)
    packed = exchange(packed, "dp", shards)
    dots = [x[0:rows] for x in packed]
    dots = exchange((dots[0] + dots[1]) + (dots[2] + dots[3]), "mp", parts)
    embeddings, losses, update = pl.pallas_call(
        functools.partial(score_kernel, negatives=negatives),
        out_shape=[
            jax.ShapeDtypeStruct((1, per_shard, part_width), jnp.bfloat16),
            jax.ShapeDtypeStruct((1, per_shard), jnp.float32),
            jax.ShapeDtypeStruct((ROWS, width), jnp.float32),
        ],
        in_specs=[vmem_spec()] * 16 + [smem_spec()],
        out_specs=[vmem_spec()] * 3,
        compiler_params=params,
        name="score",
    )(
        ids,
        pooled,
        far_side,
        *packed,
        *dots,
        misc,
        slope,
        reduced,
        member,
        member_rest,
        logit_sharpness,
    )
    update = update + lax.ppermute(update, "group", [(0, 1), (1, 0)])
    updates = exchange(update, "dp", shards)
    shard = lax.axis_index("dp")
    columns = [lax.select_n(shard ^ quarter_of(q), *updates) for q in range(shards)]
    return (embeddings, losses, jnp.concatenate(columns, axis=1))


def body(words, hard, vocabulary, weight, lowering, raising, sharpness):
    shards, parts = lax.axis_size("dp"), lax.axis_size("mp")
    texts, length = words.shape[1:]
    features, vocab = vocabulary.shape
    negatives = hard.shape[1]
    square = shards == 4 and features == weight.shape[1] and parts == shards
    small = texts <= ROWS - 2 and length == LANES and FIRST < texts * length <= 2048
    even = (texts * length) % CHUNK == 0 and vocab % IDS_PER_BLOCK == 0
    fits = features * vocab <= 2**24 and features % (4 * LANES) == 0
    spare = FIRST // CHUNK + negatives <= ROWS and lowering.shape[0] == ROWS
    fast = square and small and even and fits and spare and lax.axis_size("group") == 2
    chosen = split_body if fast else general_body
    return chosen(words, hard, vocabulary, weight, lowering, raising, sharpness)


def solution(mesh):
    in_specs = (
        P("group", None, None),
        P("dp", None),
        P("dp", None),
        P("dp", "mp"),
        P(),
        P(None, "mp"),
        P(),
    )
    out_specs = (P("group", "dp", "mp"), P("group", "dp"), P(None, "mp"))
    return jax.shard_map(body, mesh=mesh, in_specs=in_specs, out_specs=out_specs, check_vma=False)
```

profile of v0, /device:TPU:0, one launch (start us, length us, event | category | flops | bytes accessed | tf_op | source)
XLA Modules:
  0.0 90.1 jit_solution(11985069907680101564)
XLA Ops:
  1.3 29.8 %project.3 = (bf16[1120,256]{1,0:T(8,128)(2,1)}, bf16[1120,256]{1,0:T(8,128)(2,1)}, bf16[1120,256]{1,0:T(8,128)(2,1)}, bf16[1120,256]{1,0:T(8,128)(2,1)}, bf16[1024,128]{1,0:T(8,128)(2,1)}) custom-call(s32[12,128]{1,0:T(8,128)S(1)} %bitcast.5, s32[3,7]{1,0:T(4,128)} %hard_ref.1, bf16[1024,16384]{1,0:T(8,128)(2,1)} %vocab_ref.1, ...), custom_call_target="tpu_custom_call" | custom-call | tf_op jit(solution)/shard_map/project/pallas_call | solution.py:599
  31.8 1.8 %collective-permute-done.4 = bf16[1120,256]{1,0:T(8,128)(2,1)S(1)} collective-permute-done((bf16[1120,256]{1,0:T(8,128)(2,1)}, bf16[1120,256]{1,0:T(8,128)(2,1)S(1)}, u32[]{:S(2)}, u32[]{:S(2)}) %collective-permute-start.4) | collective-permute-done | bytes 573472 | tf_op jit(solution)/shard_map/ppermute | solution.py:634
  33.5 1.2 %add_convert_fusion.1 = bf16[1120,256]{1,0:T(8,128)(2,1)S(1)} fusion(bf16[1120,256]{1,0:T(8,128)(2,1)S(1)} %collective-permute-done.4, bf16[1120,256]{1,0:T(8,128)(2,1)} %get-tuple-element.41), kind=kLoop, calls=%fused_computation.1 | loop fusion | flops 1146880 | bytes 1720320 | tf_op jit(solution)/shard_map/convert_element_type | solution.py:636
  34.7 3.0 %collective-permute-start.5 = (bf16[1120,256]{1,0:T(8,128)(2,1)S(1)}, bf16[1120,256]{1,0:T(8,128)(2,1)}, u32[]{:S(2)}, u32[]{:S(2)}) collective-permute-start(bf16[1120,256]{1,0:T(8,128)(2,1)S(1)} %add_convert_fusion.1), channel_id=1, source_target_pairs={{0,8},{4,12},{8,0},{12,4},{1,9},{5,13},{9,1},{13,5},{2,10},{6,14},... | collective-permute-start | bytes 1720328 | tf_op jit(solution)/shard_map/ppermute | solution.py:637
  39.0 1.5 %conditional.1 = (bf16[576,256]{1,0:T(8,128)(2,1)S(1)}, bf16[576,256]{1,0:T(8,128)(2,1)}, bf16[576,256]{1,0:T(8,128)(2,1)}, bf16[512,128]{1,0:T(8,128)(2,1)S(1)}) conditional(s32[]{:T(128)} %convert_element_type.28, () %tuple.16, (s32[12,128]{1,0:T(8,128)S(1)}, s32[3,7]{1,0:T(4,128)S(1)}, bf16[1024,16384]{1,0:T(8,128)(2,1)}, ...), branch_computations={%region_1.0_spmd, %region_2.0_spmd} | conditional | flops 589824 | bytes 4423832 | solution.py:644
  39.1 0.8 broadcast.4.clone
  40.6 10.5 %collective-permute-done.5.far_ref = bf16[1120,256]{1,0:T(8,128)(2,1)} collective-permute-done((bf16[1120,256]{1,0:T(8,128)(2,1)S(1)}, bf16[1120,256]{1,0:T(8,128)(2,1)}, u32[]{:S(2)}, u32[]{:S(2)}) %collective-permute-start.5) | collective-permute-done | bytes 573472 | tf_op jit(solution)/shard_map/ppermute | solution.py:637
  51.1 3.9 %pool.1 = (bf16[16,256]{1,0:T(8,128)(2,1)}, f32[1536,256]{1,0:T(8,128)}, bf16[16,1536]{1,0:T(8,128)(2,1)}, f32[16,256]{1,0:T(8,128)}) custom-call(s32[12,128]{1,0:T(8,128)S(1)} %bitcast.7, bf16[1120,256]{1,0:T(8,128)(2,1)} %get-tuple-element.39.own_ref, bf16[1120,256]{1,0:T(8,128)(2,1)} %collective-permute-done.3.core_ref, ...), custom_call_target="tpu_custom_call" | custom-call | tf_op jit(solution)/shard_map/pool/pallas_call | solution.py:649
  55.0 1.7 %collective-permute-start.6 = (bf16[16,256]{1,0:T(8,128)(2,1)}, bf16[16,256]{1,0:T(8,128)(2,1)S(1)}, u32[]{:S(2)}, u32[]{:S(2)}) collective-permute-start(bf16[16,256]{1,0:T(8,128)(2,1)} %get-tuple-element.48.near_ref), channel_id=1, source_target_pairs={{0,16},{16,0},{1,17},{17,1},{2,18},{18,2},{3,19},{19,3},{4,20},{20... | collective-permute-start | bytes 24584 | tf_op jit(solution)/shard_map/ppermute | solution.py:667
  56.6 2.2 %collective-permute-done.6.far_ref = bf16[16,256]{1,0:T(8,128)(2,1)S(1)} collective-permute-done((bf16[16,256]{1,0:T(8,128)(2,1)}, bf16[16,256]{1,0:T(8,128)(2,1)S(1)}, u32[]{:S(2)}, u32[]{:S(2)}) %collective-permute-start.6) | collective-permute-done | bytes 8224 | tf_op jit(solution)/shard_map/ppermute | solution.py:667
  59.4 1.4 %dots.1.packed0 = f32[64,128]{1,0:T(8,128)} custom-call(bf16[16,256]{1,0:T(8,128)(2,1)} %get-tuple-element.48.near_ref, bf16[16,256]{1,0:T(8,128)(2,1)} %copy-done.6), custom_call_target="tpu_custom_call" | custom-call | tf_op jit(solution)/shard_map/dots/pallas_call | solution.py:669
  60.9 1.7 %collective-permute-start.8 = (f32[64,128]{1,0:T(8,128)}, f32[64,128]{1,0:T(8,128)S(1)}, u32[]{:S(2)}, u32[]{:S(2)}) collective-permute-start(f32[64,128]{1,0:T(8,128)} %dots.1.packed0), channel_id=1, source_target_pairs={{0,8},{4,12},{8,0},{12,4},{1,9},{5,13},{9,1},{13,5},{2,10},{6,14},... | collective-permute-start | bytes 98312 | tf_op jit(solution)/shard_map/ppermute | solution.py:570
  62.8 2.2 %collective-permute-done.8.packed2 = f32[64,128]{1,0:T(8,128)S(1)} collective-permute-done((f32[64,128]{1,0:T(8,128)}, f32[64,128]{1,0:T(8,128)S(1)}, u32[]{:S(2)}, u32[]{:S(2)}) %collective-permute-start.8) | collective-permute-done | bytes 32800 | tf_op jit(solution)/shard_map/ppermute | solution.py:570
  65.0 1.2 %collective-permute-done.9.packed3 = f32[64,128]{1,0:T(8,128)S(1)} collective-permute-done((f32[64,128]{1,0:T(8,128)}, f32[64,128]{1,0:T(8,128)S(1)}, u32[]{:S(2)}, u32[]{:S(2)}) %collective-permute-start.9) | collective-permute-done | bytes 32800 | tf_op jit(solution)/shard_map/ppermute | solution.py:570
  66.9 1.6 %collective-permute-start.10 = (f32[32,128]{1,0:T(8,128)S(1)}, f32[32,128]{1,0:T(8,128)S(1)}, u32[]{:S(2)}, u32[]{:S(2)}) collective-permute-start(f32[32,128]{1,0:T(8,128)S(1)} %fusion.dots0), channel_id=1, source_target_pairs={{0,1},{1,0},{2,3},{3,2},{4,5},{5,4},{6,7},{7,6},{8,9},{9,8},{10,11... | collective-permute-start | bytes 49160 | tf_op jit(solution)/shard_map/ppermute | solution.py:570
  68.5 2.6 %collective-permute-start.11 = (f32[32,128]{1,0:T(8,128)S(1)}, f32[32,128]{1,0:T(8,128)S(1)}, u32[]{:S(2)}, u32[]{:S(2)}) collective-permute-start(f32[32,128]{1,0:T(8,128)S(1)} %fusion.dots0), channel_id=1, source_target_pairs={{0,2},{1,3},{2,0},{3,1},{4,6},{5,7},{6,4},{7,5},{8,10},{9,11},{10,... | collective-permute-start | bytes 49160 | tf_op jit(solution)/shard_map/ppermute | solution.py:570
  72.0 1.2 %collective-permute-done.11.dots2 = f32[32,128]{1,0:T(8,128)S(1)} collective-permute-done((f32[32,128]{1,0:T(8,128)S(1)}, f32[32,128]{1,0:T(8,128)S(1)}, u32[]{:S(2)}, u32[]{:S(2)}) %collective-permute-start.11) | collective-permute-done | bytes 16416 | tf_op jit(solution)/shard_map/ppermute | solution.py:570
  73.2 3.4 %collective-permute-done.12.dots3 = f32[32,128]{1,0:T(8,128)S(1)} collective-permute-done((f32[32,128]{1,0:T(8,128)S(1)}, f32[32,128]{1,0:T(8,128)S(1)}, u32[]{:S(2)}, u32[]{:S(2)}) %collective-permute-start.12) | collective-permute-done | bytes 16416 | tf_op jit(solution)/shard_map/ppermute | solution.py:570
  77.2 3.5 %score.1 = (bf16[1,3,1024]{2,1,0:T(4,128)(2,1)}, f32[1,3]{1,0:T(1,128)}, f32[16,256]{1,0:T(8,128)}) custom-call(s32[12,128]{1,0:T(8,128)S(1)} %bitcast.8, bf16[16,256]{1,0:T(8,128)(2,1)} %get-tuple-element.48.near_ref, bf16[16,256]{1,0:T(8,128)(2,1)} %copy-done.6, f32[64,128]{1,0:T(8,128)} %dots.1.packed0, f32[64,128]{1,0:T(8,128)} %copy-done.2, ...), custom_call_target="tpu_custom_call" | custom-call | tf_op jit(solution)/shard_map/score/pallas_call | solution.py:680
  80.7 1.5 %collective-permute-start.13 = (f32[16,256]{1,0:T(8,128)}, f32[16,256]{1,0:T(8,128)S(1)}, u32[]{:S(2)}, u32[]{:S(2)}) collective-permute-start(f32[16,256]{1,0:T(8,128)} %get-tuple-element.54), channel_id=1, source_target_pairs={{0,16},{16,0},{1,17},{17,1},{2,18},{18,2},{3,19},{19,3},{4,20},{20... | collective-permute-start | bytes 49160 | tf_op jit(solution)/shard_map/ppermute | solution.py:704
  82.2 2.5 %collective-permute-done.13 = f32[16,256]{1,0:T(8,128)S(1)} collective-permute-done((f32[16,256]{1,0:T(8,128)}, f32[16,256]{1,0:T(8,128)S(1)}, u32[]{:S(2)}, u32[]{:S(2)}) %collective-permute-start.13) | collective-permute-done | bytes 16416 | tf_op jit(solution)/shard_map/ppermute | solution.py:704
  85.4 0.8 collective-permute-start.15
  86.3 1.0 %collective-permute-start.16 = (f32[16,256]{1,0:T(8,128)S(1)}, f32[16,256]{1,0:T(8,128)S(1)}, u32[]{:S(2)}, u32[]{:S(2)}) collective-permute-start(f32[16,256]{1,0:T(8,128)S(1)} %add.22), channel_id=1, source_target_pairs={{0,12},{4,8},{8,4},{12,0},{1,13},{5,9},{9,5},{13,1},{2,14},{6,10},... | collective-permute-start | bytes 49160 | tf_op jit(solution)/shard_map/ppermute | solution.py:570
  87.3 1.9 %collective-permute-done.15 = f32[16,256]{1,0:T(8,128)S(1)} collective-permute-done((f32[16,256]{1,0:T(8,128)S(1)}, f32[16,256]{1,0:T(8,128)S(1)}, u32[]{:S(2)}, u32[]{:S(2)}) %collective-permute-start.15) | collective-permute-done | bytes 16416 | tf_op jit(solution)/shard_map/ppermute | solution.py:570
  (44 shorter events, 6.7 us)
Async XLA Ops:
  1.3 37.7 %copy-start = (bf16[1024,1024]{1,0:T(8,128)(2,1)S(1)}, bf16[1024,1024]{1,0:T(8,128)(2,1)}, u32[]{:S(2)}) copy-start(bf16[1024,1024]{1,0:T(8,128)(2,1)} %weight_ref.1) | copy-start | bytes 6291460
  31.1 6.6 %copy-start.7 = (s32[1,12,128]{2,0,1:T(1,128)S(1)}, s32[1,12,128]{2,0,1:T(1,128)}, u32[]{:S(2)}) copy-start(s32[1,12,128]{2,0,1:T(1,128)} %param.9) | copy-start | bytes 18436
  31.1 7.9 %copy-start.1 = (bf16[16,4096]{1,0:T(8,128)(2,1)S(1)}, bf16[16,4096]{1,0:T(8,128)(2,1)}, u32[]{:S(2)}) copy-start(bf16[16,4096]{1,0:T(8,128)(2,1)} %lower_ref.1) | copy-start | bytes 393220
  31.1 7.9 %copy-start.11 = (s32[3,7]{1,0:T(4,128)S(1)}, s32[3,7]{1,0:T(4,128)}, u32[]{:S(2)}) copy-start(s32[3,7]{1,0:T(4,128)} %hard_ref.1) | copy-start | bytes 256
  31.1 2.4 %collective-permute-start.4 = (bf16[1120,256]{1,0:T(8,128)(2,1)}, bf16[1120,256]{1,0:T(8,128)(2,1)S(1)}, u32[]{:S(2)}, u32[]{:S(2)}) collective-permute-start(bf16[1120,256]{1,0:T(8,128)(2,1)} %get-tuple-element.42), channel_id=1, source_target_pairs={{0,4},{4,0},{8,12},{12,8},{1,5},{5,1},{9,13},{13,9},{2,6},{6,2},{1... | collective-permute-start | bytes 1720328 | tf_op jit(solution)/shard_map/ppermute | solution.py:634
  31.7 8.9 %collective-permute-start.3 = (bf16[1120,256]{1,0:T(8,128)(2,1)}, bf16[1120,256]{1,0:T(8,128)(2,1)}, u32[]{:S(2)}, u32[]{:S(2)}) collective-permute-start(bf16[1120,256]{1,0:T(8,128)(2,1)} %get-tuple-element.40), channel_id=1, source_target_pairs={{0,4},{4,0},{8,12},{12,8},{1,5},{5,1},{9,13},{13,9},{2,6},{6,2},{1... | collective-permute-start | bytes 1720328 | tf_op jit(solution)/shard_map/ppermute | solution.py:635
  34.7 16.3 %collective-permute-start.5 = (bf16[1120,256]{1,0:T(8,128)(2,1)S(1)}, bf16[1120,256]{1,0:T(8,128)(2,1)}, u32[]{:S(2)}, u32[]{:S(2)}) collective-permute-start(bf16[1120,256]{1,0:T(8,128)(2,1)S(1)} %add_convert_fusion.1), channel_id=1, source_target_pairs={{0,8},{4,12},{8,0},{12,4},{1,9},{5,13},{9,1},{13,5},{2,10},{6,14},... | collective-permute-start | bytes 1720328 | tf_op jit(solution)/shard_map/ppermute | solution.py:637
  55.0 3.9 %collective-permute-start.6 = (bf16[16,256]{1,0:T(8,128)(2,1)}, bf16[16,256]{1,0:T(8,128)(2,1)S(1)}, u32[]{:S(2)}, u32[]{:S(2)}) collective-permute-start(bf16[16,256]{1,0:T(8,128)(2,1)} %get-tuple-element.48.near_ref), channel_id=1, source_target_pairs={{0,16},{16,0},{1,17},{17,1},{2,18},{18,2},{3,19},{19,3},{4,20},{20... | collective-permute-start | bytes 24584 | tf_op jit(solution)/shard_map/ppermute | solution.py:667
  60.9 1.9 %collective-permute-start.7 = (f32[64,128]{1,0:T(8,128)}, f32[64,128]{1,0:T(8,128)S(1)}, u32[]{:S(2)}, u32[]{:S(2)}) collective-permute-start(f32[64,128]{1,0:T(8,128)} %dots.1.packed0), channel_id=1, source_target_pairs={{0,4},{4,0},{8,12},{12,8},{1,5},{5,1},{9,13},{13,9},{2,6},{6,2},{1... | collective-permute-start | bytes 98312 | tf_op jit(solution)/shard_map/ppermute | solution.py:570
  60.9 4.1 %collective-permute-start.8 = (f32[64,128]{1,0:T(8,128)}, f32[64,128]{1,0:T(8,128)S(1)}, u32[]{:S(2)}, u32[]{:S(2)}) collective-permute-start(f32[64,128]{1,0:T(8,128)} %dots.1.packed0), channel_id=1, source_target_pairs={{0,8},{4,12},{8,0},{12,4},{1,9},{5,13},{9,1},{13,5},{2,10},{6,14},... | collective-permute-start | bytes 98312 | tf_op jit(solution)/shard_map/ppermute | solution.py:570
  62.6 3.6 %collective-permute-start.9 = (f32[64,128]{1,0:T(8,128)}, f32[64,128]{1,0:T(8,128)S(1)}, u32[]{:S(2)}, u32[]{:S(2)}) collective-permute-start(f32[64,128]{1,0:T(8,128)} %dots.1.packed0), channel_id=1, source_target_pairs={{0,12},{4,8},{8,4},{12,0},{1,13},{5,9},{9,5},{13,1},{2,14},{6,10},... | collective-permute-start | bytes 98312 | tf_op jit(solution)/shard_map/ppermute | solution.py:570
  62.8 13.9 %copy-start.2 = (f32[64,128]{1,0:T(8,128)}, f32[64,128]{1,0:T(8,128)S(1)}, u32[]{:S(2)}) copy-start(f32[64,128]{1,0:T(8,128)S(1)} %collective-permute-done.7.packed1) | copy-start | bytes 98308
  65.0 11.7 %copy-start.3 = (f32[64,128]{1,0:T(8,128)}, f32[64,128]{1,0:T(8,128)S(1)}, u32[]{:S(2)}) copy-start(f32[64,128]{1,0:T(8,128)S(1)} %collective-permute-done.8.packed2) | copy-start | bytes 98308
  66.2 10.5 %copy-start.4 = (f32[64,128]{1,0:T(8,128)}, f32[64,128]{1,0:T(8,128)S(1)}, u32[]{:S(2)}) copy-start(f32[64,128]{1,0:T(8,128)S(1)} %collective-permute-done.9.packed3) | copy-start | bytes 98308
  66.9 9.8 %copy-start.5 = (f32[32,128]{1,0:T(8,128)}, f32[32,128]{1,0:T(8,128)S(1)}, u32[]{:S(2)}) copy-start(f32[32,128]{1,0:T(8,128)S(1)} %fusion.dots0) | copy-start | bytes 49156
  66.9 5.1 %collective-permute-start.10 = (f32[32,128]{1,0:T(8,128)S(1)}, f32[32,128]{1,0:T(8,128)S(1)}, u32[]{:S(2)}, u32[]{:S(2)}) collective-permute-start(f32[32,128]{1,0:T(8,128)S(1)} %fusion.dots0), channel_id=1, source_target_pairs={{0,1},{1,0},{2,3},{3,2},{4,5},{5,4},{6,7},{7,6},{8,9},{9,8},{10,11... | collective-permute-start | bytes 49160 | tf_op jit(solution)/shard_map/ppermute | solution.py:570
  68.5 4.7 %collective-permute-start.11 = (f32[32,128]{1,0:T(8,128)S(1)}, f32[32,128]{1,0:T(8,128)S(1)}, u32[]{:S(2)}, u32[]{:S(2)}) collective-permute-start(f32[32,128]{1,0:T(8,128)S(1)} %fusion.dots0), channel_id=1, source_target_pairs={{0,2},{1,3},{2,0},{3,1},{4,6},{5,7},{6,4},{7,5},{8,10},{9,11},{10,... | collective-permute-start | bytes 49160 | tf_op jit(solution)/shard_map/ppermute | solution.py:570
  71.1 5.5 %collective-permute-start.12 = (f32[32,128]{1,0:T(8,128)S(1)}, f32[32,128]{1,0:T(8,128)S(1)}, u32[]{:S(2)}, u32[]{:S(2)}) collective-permute-start(f32[32,128]{1,0:T(8,128)S(1)} %fusion.dots0), channel_id=1, source_target_pairs={{0,3},{1,2},{2,1},{3,0},{4,7},{5,6},{6,5},{7,4},{8,11},{9,10},{10,... | collective-permute-start | bytes 49160 | tf_op jit(solution)/shard_map/ppermute | solution.py:570
  72.0 4.7 %copy-start.8 = (f32[32,128]{1,0:T(8,128)}, f32[32,128]{1,0:T(8,128)S(1)}, u32[]{:S(2)}) copy-start(f32[32,128]{1,0:T(8,128)S(1)} %collective-permute-done.10.dots1) | copy-start | bytes 49156
  73.2 3.4 %copy-start.9 = (f32[32,128]{1,0:T(8,128)}, f32[32,128]{1,0:T(8,128)S(1)}, u32[]{:S(2)}) copy-start(f32[32,128]{1,0:T(8,128)S(1)} %collective-permute-done.11.dots2) | copy-start | bytes 49156
  80.7 3.9 %collective-permute-start.13 = (f32[16,256]{1,0:T(8,128)}, f32[16,256]{1,0:T(8,128)S(1)}, u32[]{:S(2)}, u32[]{:S(2)}) collective-permute-start(f32[16,256]{1,0:T(8,128)} %get-tuple-element.54), channel_id=1, source_target_pairs={{0,16},{16,0},{1,17},{17,1},{2,18},{18,2},{3,19},{19,3},{4,20},{20... | collective-permute-start | bytes 49160 | tf_op jit(solution)/shard_map/ppermute | solution.py:704
  85.4 1.9 %collective-permute-start.14 = (f32[16,256]{1,0:T(8,128)S(1)}, f32[16,256]{1,0:T(8,128)S(1)}, u32[]{:S(2)}, u32[]{:S(2)}) collective-permute-start(f32[16,256]{1,0:T(8,128)S(1)} %add.22), channel_id=1, source_target_pairs={{0,4},{4,0},{8,12},{12,8},{1,5},{5,1},{9,13},{13,9},{2,6},{6,2},{1... | collective-permute-start | bytes 49160 | tf_op jit(solution)/shard_map/ppermute | solution.py:570
  85.4 3.7 %collective-permute-start.15 = (f32[16,256]{1,0:T(8,128)S(1)}, f32[16,256]{1,0:T(8,128)S(1)}, u32[]{:S(2)}, u32[]{:S(2)}) collective-permute-start(f32[16,256]{1,0:T(8,128)S(1)} %add.22), channel_id=1, source_target_pairs={{0,8},{4,12},{8,0},{12,4},{1,9},{5,13},{9,1},{13,5},{2,10},{6,14},... | collective-permute-start | bytes 49160 | tf_op jit(solution)/shard_map/ppermute | solution.py:570
  86.3 3.2 %collective-permute-start.16 = (f32[16,256]{1,0:T(8,128)S(1)}, f32[16,256]{1,0:T(8,128)S(1)}, u32[]{:S(2)}, u32[]{:S(2)}) collective-permute-start(f32[16,256]{1,0:T(8,128)S(1)} %add.22), channel_id=1, source_target_pairs={{0,12},{4,8},{8,4},{12,0},{1,13},{5,9},{9,5},{13,1},{2,14},{6,10},... | collective-permute-start | bytes 49160 | tf_op jit(solution)/shard_map/ppermute | solution.py:570
  (2 other events, 1.2 us)
where the time goes:
time: 90.6 us; the launch traced here: 90.1 us
  Pallas kernels  38.6 us (43%)
  waiting for transfers between devices  27.1 us (30%)
  starting transfers between devices  14.9 us (16%)
  other arithmetic  3.94 us (4%)
  local copies, waits for them, and re-layouts  3.41 us (4%)
  between operations  2.08 us (2%)
    pallas_call x1, Pallas kernels, project(): pl.pallas_call(functools.partial(project_kernel, base=base), out_shape=[j...  29.8 us
    ppermute x1, waiting for transfers between devices, project(): far = lax.ppermute(chip1, 'dp', other_y)  10.5 us
    ppermute x9, waiting for transfers between devices, exchange(): return [x] + [lax.ppermute(x, axis, step) for step in steps]  10.2 us
    ppermute x9, starting transfers between devices, exchange(): return [x] + [lax.ppermute(x, axis, step) for step in steps]  8.19 us
    pallas_call x1, Pallas kernels, split_body(): pl.pallas_call(functools.partial(pool_kernel, model_width=float(features...  3.88 us
    pallas_call x1, Pallas kernels, split_body(): pl.pallas_call(functools.partial(score_kernel, negatives=negatives), out_...  3.51 us
    ppermute x1, starting transfers between devices, project(): far = lax.ppermute(chip1, 'dp', other_y)  2.96 us
    ppermute x1, waiting for transfers between devices, split_body(): update = update + lax.ppermute(update, 'group', [(0, 1), (1, 0)])  2.46 us
  transfers between devices with their start and end apart: 14, of which 10 were waited for; matrix products, arithmetic and copies ran while one was open for 4% of the time, Pallas kernels for 0%

commit v1 on v0

--- a/solution.py
+++ b/solution.py
@@ -110,15 +110,15 @@
     return (embeddings, losses[None], adapter_up_gradient)
 
 
-BLOCK_BITS, GROUP_BITS, CHUNK_BITS, LANE_BITS, ROW_BITS = 11, 9, 8, 7, 4
+BLOCK_BITS, GROUP_BITS, LANE_BITS, ROW_BITS = 10, 8, 7, 4
 IDS_PER_BLOCK = 1 << BLOCK_BITS
 IDS_PER_GROUP = 1 << GROUP_BITS
-CHUNK = 1 << CHUNK_BITS
+CHUNK = 384
+STRIPE = 256
 ROWS = 1 << ROW_BITS
 LANES = 1 << LANE_BITS
 FEATURE_ROWS = 128
-TAKEN = 640
-FIRST = 1024
+FIRST = 1152
 NT = (((1,), (1,)), ((), ()))
 VMEM_BYTES = 60 * 1024 * 1024
 
@@ -173,12 +173,11 @@
     weight,
     lower,
     turned,
-    picked_turned,
     parts,
     token_ref,
     small,
     ranks,
-    squares,
+    statistics,
     residual,
     counted,
     bounds,
@@ -195,6 +194,7 @@
     groups = vocab // IDS_PER_GROUP
     span = member_ref.shape[0]
     chunks = span // CHUNK
+    stripes = pl.cdiv(span, STRIPE)
     per_shard, negatives = hard_ref.shape
     width = out00.shape[1]
     outs = (out00, out01, out10, out11)
@@ -251,15 +251,14 @@
         found = found.astype(jnp.int32)
         real = (found >= ROWS) & ((found & (ROWS - 1)) == iota((LANES, LANES), 1))
         member_ref[pl.ds(start, LANES), :] = jnp.where(real, 1.0, 0.0).astype(jnp.bfloat16)
-        turned[:, pl.ds(start, LANES)] = jnp.zeros((TAKEN, LANES), jnp.bfloat16)
-        picked_turned[:, pl.ds(start, LANES)] = jnp.zeros((features - TAKEN, LANES), jnp.bfloat16)
+        turned[:, pl.ds(start, LANES)] = jnp.zeros((features, LANES), jnp.bfloat16)
         return carry
 
     lax.fori_loop(0, span // LANES, place, 0)
     residual[...] = jnp.zeros_like(residual)
-    squares[...] = jnp.zeros_like(squares)
+    statistics[...] = jnp.zeros_like(statistics)
     small[...] = jnp.zeros_like(small)
-    small[0:per_shard, chunks : chunks + negatives] = hard_ref[...].astype(jnp.float32)
+    small[0:per_shard, stripes : stripes + negatives] = hard_ref[...].astype(jnp.float32)
     lower_copy.wait()
     weight_copy.wait()
     bounds_copy.wait()
@@ -270,31 +269,26 @@
             pltpu.make_async_copy(parts.at[q, rows], outs[q].at[rows], out_sems.at[q]).start()
 
     def project(k, carry):
-        start = pl.multiple_of(k * CHUNK, CHUNK)
+        start = pl.multiple_of(k * CHUNK, LANES)
         across = pl.ds(start, CHUNK)
-        upright = jnp.concatenate([turned[:, across], picked_turned[:, across]], axis=0)
+        upright = turned[:, across]
         x = upright.T
         for q in range(4):
             at = pl.multiple_of(split_quarter(q // 2, q % 2) * width, LANES)
             product = mm(x, weight[:, pl.ds(at, width)])
-            parts[q, pl.ds(start, CHUNK), :] = product.astype(jnp.bfloat16)
+            parts[q, across, :] = product.astype(jnp.bfloat16)
         send(start, CHUNK)
-        reduced = mm(lower[...], upright).astype(jnp.bfloat16)
-        for q in range(4):
-            parts[q, pl.ds(pl.multiple_of(span + k * ROWS, ROWS), ROWS), :] = reduced
         wide = upright.astype(jnp.float32)
-        squares[pl.ds(k, 1), :] = jnp.sum(wide * wide, axis=0, keepdims=True)
-        member = member_ref[pl.ds(start, CHUNK), :].astype(jnp.float32).T.astype(jnp.bfloat16)
+        statistics[0:ROWS, across] = mm(lower[...], upright)
+        statistics[ROWS : ROWS + 1, across] = jnp.sum(wide * wide, axis=0, keepdims=True)
+        member = member_ref[across, :].astype(jnp.float32).T.astype(jnp.bfloat16)
         residual[...] += mm(member[0:ROWS], x)
         return carry
 
     def zero(k, carry):
-        start = pl.multiple_of(k * CHUNK, CHUNK)
+        start = pl.multiple_of(k * CHUNK, LANES)
         for q in range(4):
             parts[q, pl.ds(start, CHUNK), :] = jnp.zeros((CHUNK, width), jnp.bfloat16)
-            parts[q, pl.ds(pl.multiple_of(span + k * ROWS, ROWS), ROWS), :] = jnp.zeros(
-                (ROWS, width), jnp.bfloat16
-            )
         send(start, CHUNK)
         return carry
 
@@ -312,48 +306,49 @@
             def window(p, carry):
                 at = pl.ds(pl.multiple_of(p * LANES, LANES), LANES)
                 token = token_ref[pl.ds(p, 1), :] - group * IDS_PER_GROUP
-                token = jnp.broadcast_to(token, (IDS_PER_GROUP, LANES))
-                short = token.astype(jnp.int16)
-                picked = jnp.where(
-                    short == iota((IDS_PER_GROUP, LANES), 0).astype(jnp.int16), 1.0, 0.0
-                ).astype(jnp.bfloat16)
-                columns = pl.ds(part * IDS_PER_GROUP, IDS_PER_GROUP)
-                found = mm(held[b, TAKEN:features, columns], picked)
-                lane = (token[0:FEATURE_ROWS] & (LANES - 1)).astype(jnp.int16)
-                tile = lax.shift_right_arithmetic(token[0:FEATURE_ROWS], LANE_BITS)
-                tile = tile.astype(jnp.int16)
-                for f in range(TAKEN // FEATURE_ROWS):
+                token = jnp.broadcast_to(token, (FEATURE_ROWS, LANES))
+                lane = token & (LANES - 1)
+                tile = lax.shift_right_arithmetic(token, LANE_BITS)
+                for f in range(features // FEATURE_ROWS):
                     rows = pl.ds(f * FEATURE_ROWS, FEATURE_ROWS)
-                    total = turned[rows, at]
+                    total = turned[rows, at].astype(jnp.float32)
                     for j in range(IDS_PER_GROUP // LANES):
                         columns = pl.ds(part * IDS_PER_GROUP + j * LANES, LANES)
-                        total = jnp.where(tile == j, take_lanes(held[b, rows, columns], lane), total)
-                    turned[rows, at] = total
-                picked_turned[:, at] += found.astype(jnp.bfloat16)
+                        found = take_lanes(held[b, rows, columns].astype(jnp.float32), lane)
+                        total = jnp.where(tile == j, found, total)
+                    turned[rows, at] = total.astype(jnp.bfloat16)
                 return carry
 
             lax.fori_loop(begin, jnp.where(last > first, end, begin), window, 0)
-        full = lax.shift_right_logical(last, CHUNK_BITS)
+        full = lax.div(last, CHUNK)
         lax.fori_loop(done, full, project, 0)
         return full
 
     done = lax.fori_loop(0, blocks, take, 0)
-    used = lax.shift_right_logical(within(bounds[groups, 0]) + CHUNK - 1, CHUNK_BITS)
+    used = lax.div(within(bounds[groups, 0]) + CHUNK - 1, CHUNK)
     lax.fori_loop(done, used, project, 0)
     lax.fori_loop(used, chunks, zero, 0)
 
     hard = small[...].T[0:ROWS]
     lane = iota((ROWS, width), 1)
-    misc = jnp.concatenate([squares[...], jnp.zeros((ROWS - squares.shape[0], width), jnp.float32)])
+    misc = jnp.zeros((ROWS, width), jnp.float32)
+    for stripe in range(stripes):
+        across = pl.ds(stripe * STRIPE, STRIPE)
+        for q in range(4):
+            parts[q, pl.ds(span + stripe * ROWS, ROWS), :] = statistics[0:ROWS, across].astype(
+                jnp.bfloat16
+            )
+        squares = jnp.broadcast_to(statistics[ROWS : ROWS + 1, across], (ROWS, STRIPE))
+        misc = jnp.where(iota((ROWS, width), 0) == stripe, squares, misc)
     for i in range(per_shard):
         misc += jnp.where(lane == shard * per_shard + i, hard[:, i : i + 1], 0.0)
     mine = lax.axis_index("mp") == shard
     for q in range(4):
         start = pl.multiple_of(split_quarter(q // 2, q % 2) * width, LANES)
         part = jnp.where(mine, residual[:, pl.ds(start, width)], 0.0)
-        parts[q, pl.ds(span + chunks * ROWS, ROWS), :] = misc.astype(jnp.bfloat16)
-        parts[q, pl.ds(span + (chunks + 1) * ROWS, ROWS), :] = part.astype(jnp.bfloat16)
-    send(span, (chunks + 2) * ROWS)
+        parts[q, pl.ds(span + stripes * ROWS, ROWS), :] = misc.astype(jnp.bfloat16)
+        parts[q, pl.ds(span + (stripes + 1) * ROWS, ROWS), :] = part.astype(jnp.bfloat16)
+    send(span, (stripes + 2) * ROWS)
     for q in range(4):
         pltpu.make_async_copy(parts.at[q], outs[q], out_sems.at[q]).wait()
 
@@ -386,33 +381,34 @@
 
     def add(refs, member_ref, base):
         span = member_ref.shape[0]
-        chunks = span // CHUNK
+        stripes = pl.cdiv(span, STRIPE)
 
         def summed(start, size):
             return sum(ref[pl.ds(start, size), :].astype(jnp.float32) for ref in refs)
 
-        misc = summed(span + chunks * ROWS, ROWS)
+        misc = summed(span + stripes * ROWS, ROWS)
         if base == 0:
             misc_ref[...] = misc
         inverse = lax.rsqrt(misc / model_width + 1e-05)
-        for k in range(chunks):
-            at = base + k * CHUNK
+        for k in range(stripes):
+            at = base + k * STRIPE
+            size = min(STRIPE, span - k * STRIPE)
             scale = inverse[k : k + 1]
             reduced = (summed(span + k * ROWS, ROWS) * scale).astype(jnp.bfloat16)
-            reduced_ref[:, at : at + CHUNK] = reduced
+            reduced_ref[:, at : at + size] = reduced[:, 0:size]
             stacked = jnp.concatenate(
-                [reduced.astype(jnp.float32), jnp.broadcast_to(scale, (LANES - ROWS, CHUNK))]
+                [reduced.astype(jnp.float32), jnp.broadcast_to(scale, (LANES - ROWS, STRIPE))]
             )
-            turned = stacked.T
+            turned = stacked[:, 0:size].T
             low = turned.astype(jnp.bfloat16)
-            linear = summed(k * CHUNK, CHUNK) * turned[:, ROWS : ROWS + 1] + mm(low, raised[...])
+            linear = summed(k * STRIPE, size) * turned[:, ROWS : ROWS + 1] + mm(low, raised[...])
             sigma = 1.0 / (1.0 + jnp.exp(-linear))
-            slope_ref[pl.ds(at, CHUNK), :] = sigma * (1.0 + linear * (1.0 - sigma))
-            member = member_ref[pl.ds(k * CHUNK, CHUNK), :].astype(jnp.float32).T
+            slope_ref[pl.ds(at, size), :] = sigma * (1.0 + linear * (1.0 - sigma))
+            member = member_ref[pl.ds(k * STRIPE, size), :].astype(jnp.float32).T
             member = member[0:ROWS].astype(jnp.bfloat16)
             high, rest = split(linear * sigma)
             total[...] += mm(member, high) + mm(member, rest)
-        total[...] += summed(span + (chunks + 1) * ROWS, ROWS)
+        total[...] += summed(span + (stripes + 1) * ROWS, ROWS)
 
     add((own_ref, core_ref, far_ref), member_ref, 0)
     real = (ids_ref[...] != 0).astype(jnp.float32)
@@ -470,7 +466,7 @@
     negatives,
 ):
     texts, length = ids_ref.shape
-    chunks = member_ref.shape[0] // CHUNK
+    stripes = pl.cdiv(member_ref.shape[0], STRIPE)
     rows = 2 * ROWS
     width = near_ref.shape[1]
     per_shard = loss_ref.shape[1]
@@ -489,7 +485,7 @@
     top = jnp.max(jnp.where(keep, scores, -jnp.inf), axis=0, keepdims=True)
     top = jnp.where(lax.rem(across[0:1], ROWS) < texts, top, 0.0)
     powers = jnp.exp(jnp.where(real, jnp.minimum(scores - top, 0.0), 0.0))
-    hard = misc_ref[chunks : chunks + negatives, 0:rows].astype(jnp.int32) + ROWS
+    hard = misc_ref[stripes : stripes + negatives, 0:rows].astype(jnp.int32) + ROWS
     times = jnp.zeros((rows, rows), jnp.float32)
     for k in range(negatives):
         times += jnp.where(hard[k : k + 1] == down, 1.0, 0.0)
@@ -595,7 +591,8 @@
     other_y = [(d, d ^ 2) for d in range(shards)]
 
     def project(base, span):
-        rows = span + (span // CHUNK + 2) * ROWS
+        stripes = pl.cdiv(span, STRIPE)
+        rows = span + (stripes + 2) * ROWS
         own0, own1, away0, away1, member = pl.pallas_call(
             functools.partial(project_kernel, base=base),
             out_shape=[jax.ShapeDtypeStruct((rows, width), jnp.bfloat16)] * 4
@@ -606,13 +603,12 @@
                 pltpu.VMEM((blocks, features, IDS_PER_BLOCK), jnp.bfloat16),
                 pltpu.VMEM((features, part_width), jnp.bfloat16),
                 pltpu.VMEM((rank, features), jnp.bfloat16),
-                pltpu.VMEM((TAKEN, span), jnp.bfloat16),
-                pltpu.VMEM((features - TAKEN, span), jnp.bfloat16),
+                pltpu.VMEM((features, span), jnp.bfloat16),
                 pltpu.VMEM((4, rows, width), jnp.bfloat16),
                 pltpu.VMEM((8 * pl.cdiv(span // LANES, 8), LANES), jnp.int32),
                 pltpu.VMEM((LANES, LANES), jnp.float32),
                 pltpu.VMEM((texts, length), jnp.float32),
-                pltpu.VMEM((8, width), jnp.float32),
+                pltpu.VMEM((ROWS + 8, stripes * STRIPE), jnp.float32),
                 pltpu.VMEM((ROWS, features), jnp.float32),
                 pltpu.VMEM((group_rows, length), jnp.int32),
                 pltpu.SMEM((group_rows, length), jnp.int32),
@@ -713,11 +709,11 @@
     texts, length = words.shape[1:]
     features, vocab = vocabulary.shape
     negatives = hard.shape[1]
-    square = shards == 4 and features == weight.shape[1] and parts == shards
+    square = shards == 4 and features == weight.shape[1] == 4 * STRIPE and parts == shards
     small = texts <= ROWS - 2 and length == LANES and FIRST < texts * length <= 2048
-    even = (texts * length) % CHUNK == 0 and vocab % IDS_PER_BLOCK == 0
+    even = (texts * length - FIRST) % CHUNK == 0 and vocab % IDS_PER_BLOCK == 0
     fits = features * vocab <= 2**24 and features % (4 * LANES) == 0
-    spare = FIRST // CHUNK + negatives <= ROWS and lowering.shape[0] == ROWS
+    spare = pl.cdiv(FIRST, STRIPE) + negatives <= ROWS and lowering.shape[0] == ROWS
     fast = square and small and even and fits and spare and lax.axis_size("group") == 2
     chosen = split_body if fast else general_body
     return chosen(words, hard, vocabulary, weight, lowering, raising, sharpness)

time: 90.6 us -> 97.2 us (1.073)
  Pallas kernels: 38.6 us -> 42.4 us
  waiting for transfers between devices: 27.1 us -> 29.9 us
    pallas_call x1, Pallas kernels: 29.8 us -> 33.6 us  [project(): pl.pallas_call(functools.partial(project_kernel, base=base), out_shape=[j...]
    ppermute x1, waiting for transfers between devices: 10.5 us -> 12.3 us  [project(): far = lax.ppermute(chip1, 'dp', other_y)]
where the time goes in v1:
time: 97.2 us; the launch traced here: 96.6 us
  Pallas kernels  42.4 us (44%)
  waiting for transfers between devices  29.9 us (31%)
  starting transfers between devices  14 us (14%)
  other arithmetic  4.86 us (5%)
  local copies, waits for them, and re-layouts  3.36 us (3%)
  between operations  2.08 us (2%)
    pallas_call x1, Pallas kernels, project(): pl.pallas_call(functools.partial(project_kernel, base=base), out_shape=[j...  33.6 us
    ppermute x1, waiting for transfers between devices, project(): far = lax.ppermute(chip1, 'dp', other_y)  12.3 us
    ppermute x9, waiting for transfers between devices, exchange(): return [x] + [lax.ppermute(x, axis, step) for step in steps]  10.2 us
    ppermute x9, starting transfers between devices, exchange(): return [x] + [lax.ppermute(x, axis, step) for step in steps]  8.2 us
    pallas_call x1, Pallas kernels, split_body(): pl.pallas_call(functools.partial(pool_kernel, model_width=float(features...  4.02 us
    pallas_call x1, Pallas kernels, split_body(): pl.pallas_call(functools.partial(score_kernel, negatives=negatives), out_...  3.36 us
    ppermute x1, waiting for transfers between devices, split_body(): update = update + lax.ppermute(update, 'group', [(0, 1), (1, 0)])  2.9 us
    ppermute x1, starting transfers between devices, project(): far = lax.ppermute(chip1, 'dp', other_y)  2.9 us
  transfers between devices with their start and end apart: 14, of which 10 were waited for; matrix products, arithmetic and copies ran while one was open for 4% of the time, Pallas kernels for 0%

profile of v1, /device:TPU:0, one launch (start us, length us, event | category | flops | bytes accessed | tf_op | source)
XLA Modules:
  0.0 96.6 jit_solution(10195141905699374691)
XLA Ops:
  1.3 33.6 %project.3 = (bf16[1264,256]{1,0:T(8,128)(2,1)}, bf16[1264,256]{1,0:T(8,128)(2,1)}, bf16[1264,256]{1,0:T(8,128)(2,1)}, bf16[1264,256]{1,0:T(8,128)(2,1)}, bf16[1152,128]{1,0:T(8,128)(2,1)}) custom-call(s32[12,128]{1,0:T(8,128)S(1)} %bitcast.5, s32[3,7]{1,0:T(4,128)} %hard_ref.1, bf16[1024,16384]{1,0:T(8,128)(2,1)} %vocab_ref.1, ...), custom_call_target="tpu_custom_call" | custom-call | tf_op jit(solution)/shard_map/project/pallas_call | solution.py:596
  35.5 1.8 %collective-permute-done.4 = bf16[1264,256]{1,0:T(8,128)(2,1)S(1)} collective-permute-done((bf16[1264,256]{1,0:T(8,128)(2,1)}, bf16[1264,256]{1,0:T(8,128)(2,1)S(1)}, u32[]{:S(2)}, u32[]{:S(2)}) %collective-permute-start.4) | collective-permute-done | bytes 647200 | tf_op jit(solution)/shard_map/ppermute | solution.py:630
  37.4 2.1 %add_convert_fusion.1 = bf16[1264,256]{1,0:T(8,128)(2,1)} fusion(bf16[1264,256]{1,0:T(8,128)(2,1)S(1)} %collective-permute-done.4, bf16[1264,256]{1,0:T(8,128)(2,1)} %get-tuple-element.41), kind=kLoop, calls=%fused_computation.1 | loop fusion | flops 1294336 | bytes 1941504 | tf_op jit(solution)/shard_map/convert_element_type | solution.py:632
  39.5 2.9 %collective-permute-start.5 = (bf16[1264,256]{1,0:T(8,128)(2,1)}, bf16[1264,256]{1,0:T(8,128)(2,1)}, u32[]{:S(2)}, u32[]{:S(2)}) collective-permute-start(bf16[1264,256]{1,0:T(8,128)(2,1)} %add_convert_fusion.1), channel_id=1, source_target_pairs={{0,8},{4,12},{8,0},{12,4},{1,9},{5,13},{9,1},{13,5},{2,10},{6,14},... | collective-permute-start | bytes 1941512 | tf_op jit(solution)/shard_map/ppermute | solution.py:633
  43.7 1.5 %conditional.1 = (bf16[448,256]{1,0:T(8,128)(2,1)S(1)}, bf16[448,256]{1,0:T(8,128)(2,1)}, bf16[448,256]{1,0:T(8,128)(2,1)}, bf16[384,128]{1,0:T(8,128)(2,1)S(1)}) conditional(s32[]{:T(128)} %convert_element_type.28, () %tuple.16, (s32[12,128]{1,0:T(8,128)S(1)}, s32[3,7]{1,0:T(4,128)S(1)}, bf16[1024,16384]{1,0:T(8,128)(2,1)}, ...), branch_computations={%region_1.0_spmd, %region_2.0_spmd} | conditional | flops 458752 | bytes 3440792 | solution.py:640
  45.2 12.3 %collective-permute-done.5.far_ref = bf16[1264,256]{1,0:T(8,128)(2,1)} collective-permute-done((bf16[1264,256]{1,0:T(8,128)(2,1)}, bf16[1264,256]{1,0:T(8,128)(2,1)}, u32[]{:S(2)}, u32[]{:S(2)}) %collective-permute-start.5) | collective-permute-done | bytes 647200 | tf_op jit(solution)/shard_map/ppermute | solution.py:633
  57.6 4.0 %pool.1 = (bf16[16,256]{1,0:T(8,128)(2,1)}, f32[1536,256]{1,0:T(8,128)}, bf16[16,1536]{1,0:T(8,128)(2,1)}, f32[16,256]{1,0:T(8,128)}) custom-call(s32[12,128]{1,0:T(8,128)S(1)} %bitcast.7, bf16[1264,256]{1,0:T(8,128)(2,1)} %get-tuple-element.39.own_ref, bf16[1264,256]{1,0:T(8,128)(2,1)} %copy-done.1, bf16[1264,256]{1,0:T(8,128)(2,1)} %collective-permute-done.5.far_ref, ...), custom_call_target="tpu_custom_call" | custom-call | tf_op jit(solution)/shard_map/pool/pallas_call | solution.py:645
  61.6 1.3 %collective-permute-start.6 = (bf16[16,256]{1,0:T(8,128)(2,1)}, bf16[16,256]{1,0:T(8,128)(2,1)S(1)}, u32[]{:S(2)}, u32[]{:S(2)}) collective-permute-start(bf16[16,256]{1,0:T(8,128)(2,1)} %get-tuple-element.48.near_ref), channel_id=1, source_target_pairs={{0,16},{16,0},{1,17},{17,1},{2,18},{18,2},{3,19},{19,3},{4,20},{20... | collective-permute-start | bytes 24584 | tf_op jit(solution)/shard_map/ppermute | solution.py:663
  62.9 2.6 %collective-permute-done.6.far_ref = bf16[16,256]{1,0:T(8,128)(2,1)S(1)} collective-permute-done((bf16[16,256]{1,0:T(8,128)(2,1)}, bf16[16,256]{1,0:T(8,128)(2,1)S(1)}, u32[]{:S(2)}, u32[]{:S(2)}) %collective-permute-start.6) | collective-permute-done | bytes 8224 | tf_op jit(solution)/shard_map/ppermute | solution.py:663
  66.1 1.5 %dots.1.packed0 = f32[64,128]{1,0:T(8,128)} custom-call(bf16[16,256]{1,0:T(8,128)(2,1)} %get-tuple-element.48.near_ref, bf16[16,256]{1,0:T(8,128)(2,1)} %copy-done.7), custom_call_target="tpu_custom_call" | custom-call | tf_op jit(solution)/shard_map/dots/pallas_call | solution.py:665
  67.5 1.7 %collective-permute-start.8 = (f32[64,128]{1,0:T(8,128)}, f32[64,128]{1,0:T(8,128)S(1)}, u32[]{:S(2)}, u32[]{:S(2)}) collective-permute-start(f32[64,128]{1,0:T(8,128)} %dots.1.packed0), channel_id=1, source_target_pairs={{0,8},{4,12},{8,0},{12,4},{1,9},{5,13},{9,1},{13,5},{2,10},{6,14},... | collective-permute-start | bytes 98312 | tf_op jit(solution)/shard_map/ppermute | solution.py:566
  69.4 2.2 %collective-permute-done.8.packed2 = f32[64,128]{1,0:T(8,128)S(1)} collective-permute-done((f32[64,128]{1,0:T(8,128)}, f32[64,128]{1,0:T(8,128)S(1)}, u32[]{:S(2)}, u32[]{:S(2)}) %collective-permute-start.8) | collective-permute-done | bytes 32800 | tf_op jit(solution)/shard_map/ppermute | solution.py:566
  71.6 1.2 %collective-permute-done.9.packed3 = f32[64,128]{1,0:T(8,128)S(1)} collective-permute-done((f32[64,128]{1,0:T(8,128)}, f32[64,128]{1,0:T(8,128)S(1)}, u32[]{:S(2)}, u32[]{:S(2)}) %collective-permute-start.9) | collective-permute-done | bytes 32800 | tf_op jit(solution)/shard_map/ppermute | solution.py:566
  72.8 0.7 fusion.dots0
  73.5 1.6 %collective-permute-start.10 = (f32[32,128]{1,0:T(8,128)S(1)}, f32[32,128]{1,0:T(8,128)S(1)}, u32[]{:S(2)}, u32[]{:S(2)}) collective-permute-start(f32[32,128]{1,0:T(8,128)S(1)} %fusion.dots0), channel_id=1, source_target_pairs={{0,1},{1,0},{2,3},{3,2},{4,5},{5,4},{6,7},{7,6},{8,9},{9,8},{10,11... | collective-permute-start | bytes 49160 | tf_op jit(solution)/shard_map/ppermute | solution.py:566
  75.2 2.6 %collective-permute-start.11 = (f32[32,128]{1,0:T(8,128)S(1)}, f32[32,128]{1,0:T(8,128)S(1)}, u32[]{:S(2)}, u32[]{:S(2)}) collective-permute-start(f32[32,128]{1,0:T(8,128)S(1)} %fusion.dots0), channel_id=1, source_target_pairs={{0,2},{1,3},{2,0},{3,1},{4,6},{5,7},{6,4},{7,5},{8,10},{9,11},{10,... | collective-permute-start | bytes 49160 | tf_op jit(solution)/shard_map/ppermute | solution.py:566
  78.7 1.2 %collective-permute-done.11.dots2 = f32[32,128]{1,0:T(8,128)S(1)} collective-permute-done((f32[32,128]{1,0:T(8,128)S(1)}, f32[32,128]{1,0:T(8,128)S(1)}, u32[]{:S(2)}, u32[]{:S(2)}) %collective-permute-start.11) | collective-permute-done | bytes 16416 | tf_op jit(solution)/shard_map/ppermute | solution.py:566
  79.9 3.4 %collective-permute-done.12.dots3 = f32[32,128]{1,0:T(8,128)S(1)} collective-permute-done((f32[32,128]{1,0:T(8,128)S(1)}, f32[32,128]{1,0:T(8,128)S(1)}, u32[]{:S(2)}, u32[]{:S(2)}) %collective-permute-start.12) | collective-permute-done | bytes 16416 | tf_op jit(solution)/shard_map/ppermute | solution.py:566
  83.9 3.4 %score.1 = (bf16[1,3,1024]{2,1,0:T(4,128)(2,1)}, f32[1,3]{1,0:T(1,128)}, f32[16,256]{1,0:T(8,128)}) custom-call(s32[12,128]{1,0:T(8,128)S(1)} %bitcast.8, bf16[16,256]{1,0:T(8,128)(2,1)} %get-tuple-element.48.near_ref, bf16[16,256]{1,0:T(8,128)(2,1)} %copy-done.7, f32[64,128]{1,0:T(8,128)} %dots.1.packed0, f32[64,128]{1,0:T(8,128)} %copy-done.3, ...), custom_call_target="tpu_custom_call" | custom-call | tf_op jit(solution)/shard_map/score/pallas_call | solution.py:676
  87.3 1.0 %collective-permute-start.13 = (f32[16,256]{1,0:T(8,128)}, f32[16,256]{1,0:T(8,128)S(1)}, u32[]{:S(2)}, u32[]{:S(2)}) collective-permute-start(f32[16,256]{1,0:T(8,128)} %get-tuple-element.54), channel_id=1, source_target_pairs={{0,16},{16,0},{1,17},{17,1},{2,18},{18,2},{3,19},{19,3},{4,20},{20... | collective-permute-start | bytes 49160 | tf_op jit(solution)/shard_map/ppermute | solution.py:700
  88.3 2.9 %collective-permute-done.13 = f32[16,256]{1,0:T(8,128)S(1)} collective-permute-done((f32[16,256]{1,0:T(8,128)}, f32[16,256]{1,0:T(8,128)S(1)}, u32[]{:S(2)}, u32[]{:S(2)}) %collective-permute-start.13) | collective-permute-done | bytes 16416 | tf_op jit(solution)/shard_map/ppermute | solution.py:700
  91.9 0.9 collective-permute-start.15
  92.8 1.0 %collective-permute-start.16 = (f32[16,256]{1,0:T(8,128)S(1)}, f32[16,256]{1,0:T(8,128)S(1)}, u32[]{:S(2)}, u32[]{:S(2)}) collective-permute-start(f32[16,256]{1,0:T(8,128)S(1)} %add.22), channel_id=1, source_target_pairs={{0,12},{4,8},{8,4},{12,0},{1,13},{5,9},{9,5},{13,1},{2,14},{6,10},... | collective-permute-start | bytes 49160 | tf_op jit(solution)/shard_map/ppermute | solution.py:566
  93.8 1.9 %collective-permute-done.15 = f32[16,256]{1,0:T(8,128)S(1)} collective-permute-done((f32[16,256]{1,0:T(8,128)S(1)}, f32[16,256]{1,0:T(8,128)S(1)}, u32[]{:S(2)}, u32[]{:S(2)}) %collective-permute-start.15) | collective-permute-done | bytes 16416 | tf_op jit(solution)/shard_map/ppermute | solution.py:566
  (46 shorter events, 6.6 us)
Async XLA Ops:
  1.3 42.4 %copy-start = (bf16[1024,1024]{1,0:T(8,128)(2,1)S(1)}, bf16[1024,1024]{1,0:T(8,128)(2,1)}, u32[]{:S(2)}) copy-start(bf16[1024,1024]{1,0:T(8,128)(2,1)} %weight_ref.1) | copy-start | bytes 6291460
  34.9 7.5 %copy-start.8 = (s32[1,12,128]{2,0,1:T(1,128)S(1)}, s32[1,12,128]{2,0,1:T(1,128)}, u32[]{:S(2)}) copy-start(s32[1,12,128]{2,0,1:T(1,128)} %param.9) | copy-start | bytes 18436
  34.9 8.8 %copy-start.2 = (bf16[16,4096]{1,0:T(8,128)(2,1)S(1)}, bf16[16,4096]{1,0:T(8,128)(2,1)}, u32[]{:S(2)}) copy-start(bf16[16,4096]{1,0:T(8,128)(2,1)} %lower_ref.1) | copy-start | bytes 393220
  34.9 8.8 %copy-start.12 = (s32[3,7]{1,0:T(4,128)S(1)}, s32[3,7]{1,0:T(4,128)}, u32[]{:S(2)}) copy-start(s32[3,7]{1,0:T(4,128)} %hard_ref.1) | copy-start | bytes 256
  35.0 2.4 %collective-permute-start.4 = (bf16[1264,256]{1,0:T(8,128)(2,1)}, bf16[1264,256]{1,0:T(8,128)(2,1)S(1)}, u32[]{:S(2)}, u32[]{:S(2)}) collective-permute-start(bf16[1264,256]{1,0:T(8,128)(2,1)} %get-tuple-element.42), channel_id=1, source_target_pairs={{0,4},{4,0},{8,12},{12,8},{1,5},{5,1},{9,13},{13,9},{2,6},{6,2},{1... | collective-permute-start | bytes 1941512 | tf_op jit(solution)/shard_map/ppermute | solution.py:630
  35.5 9.8 %collective-permute-start.3 = (bf16[1264,256]{1,0:T(8,128)(2,1)}, bf16[1264,256]{1,0:T(8,128)(2,1)S(1)}, u32[]{:S(2)}, u32[]{:S(2)}) collective-permute-start(bf16[1264,256]{1,0:T(8,128)(2,1)} %get-tuple-element.40), channel_id=1, source_target_pairs={{0,4},{4,0},{8,12},{12,8},{1,5},{5,1},{9,13},{13,9},{2,6},{6,2},{1... | collective-permute-start | bytes 1941512 | tf_op jit(solution)/shard_map/ppermute | solution.py:631
  39.5 18.1 %collective-permute-start.5 = (bf16[1264,256]{1,0:T(8,128)(2,1)}, bf16[1264,256]{1,0:T(8,128)(2,1)}, u32[]{:S(2)}, u32[]{:S(2)}) collective-permute-start(bf16[1264,256]{1,0:T(8,128)(2,1)} %add_convert_fusion.1), channel_id=1, source_target_pairs={{0,8},{4,12},{8,0},{12,4},{1,9},{5,13},{9,1},{13,5},{2,10},{6,14},... | collective-permute-start | bytes 1941512 | tf_op jit(solution)/shard_map/ppermute | solution.py:633
  45.2 12.3 %copy-start.1 = (bf16[1264,256]{1,0:T(8,128)(2,1)}, bf16[1264,256]{1,0:T(8,128)(2,1)S(1)}, u32[]{:S(2)}) copy-start(bf16[1264,256]{1,0:T(8,128)(2,1)S(1)} %collective-permute-done.3.core_ref) | copy-start | bytes 1941508
  61.6 3.9 %collective-permute-start.6 = (bf16[16,256]{1,0:T(8,128)(2,1)}, bf16[16,256]{1,0:T(8,128)(2,1)S(1)}, u32[]{:S(2)}, u32[]{:S(2)}) collective-permute-start(bf16[16,256]{1,0:T(8,128)(2,1)} %get-tuple-element.48.near_ref), channel_id=1, source_target_pairs={{0,16},{16,0},{1,17},{17,1},{2,18},{18,2},{3,19},{19,3},{4,20},{20... | collective-permute-start | bytes 24584 | tf_op jit(solution)/shard_map/ppermute | solution.py:663
  67.5 1.9 %collective-permute-start.7 = (f32[64,128]{1,0:T(8,128)}, f32[64,128]{1,0:T(8,128)S(1)}, u32[]{:S(2)}, u32[]{:S(2)}) collective-permute-start(f32[64,128]{1,0:T(8,128)} %dots.1.packed0), channel_id=1, source_target_pairs={{0,4},{4,0},{8,12},{12,8},{1,5},{5,1},{9,13},{13,9},{2,6},{6,2},{1... | collective-permute-start | bytes 98312 | tf_op jit(solution)/shard_map/ppermute | solution.py:566
  67.5 4.1 %collective-permute-start.8 = (f32[64,128]{1,0:T(8,128)}, f32[64,128]{1,0:T(8,128)S(1)}, u32[]{:S(2)}, u32[]{:S(2)}) collective-permute-start(f32[64,128]{1,0:T(8,128)} %dots.1.packed0), channel_id=1, source_target_pairs={{0,8},{4,12},{8,0},{12,4},{1,9},{5,13},{9,1},{13,5},{2,10},{6,14},... | collective-permute-start | bytes 98312 | tf_op jit(solution)/shard_map/ppermute | solution.py:566
  69.3 3.6 %collective-permute-start.9 = (f32[64,128]{1,0:T(8,128)}, f32[64,128]{1,0:T(8,128)S(1)}, u32[]{:S(2)}, u32[]{:S(2)}) collective-permute-start(f32[64,128]{1,0:T(8,128)} %dots.1.packed0), channel_id=1, source_target_pairs={{0,12},{4,8},{8,4},{12,0},{1,13},{5,9},{9,5},{13,1},{2,14},{6,10},... | collective-permute-start | bytes 98312 | tf_op jit(solution)/shard_map/ppermute | solution.py:566
  69.4 13.9 %copy-start.3 = (f32[64,128]{1,0:T(8,128)}, f32[64,128]{1,0:T(8,128)S(1)}, u32[]{:S(2)}) copy-start(f32[64,128]{1,0:T(8,128)S(1)} %collective-permute-done.7.packed1) | copy-start | bytes 98308
  71.6 11.7 %copy-start.4 = (f32[64,128]{1,0:T(8,128)}, f32[64,128]{1,0:T(8,128)S(1)}, u32[]{:S(2)}) copy-start(f32[64,128]{1,0:T(8,128)S(1)} %collective-permute-done.8.packed2) | copy-start | bytes 98308
  72.8 10.5 %copy-start.5 = (f32[64,128]{1,0:T(8,128)}, f32[64,128]{1,0:T(8,128)S(1)}, u32[]{:S(2)}) copy-start(f32[64,128]{1,0:T(8,128)S(1)} %collective-permute-done.9.packed3) | copy-start | bytes 98308
  73.5 9.8 %copy-start.6 = (f32[32,128]{1,0:T(8,128)}, f32[32,128]{1,0:T(8,128)S(1)}, u32[]{:S(2)}) copy-start(f32[32,128]{1,0:T(8,128)S(1)} %fusion.dots0) | copy-start | bytes 49156
  73.5 5.1 %collective-permute-start.10 = (f32[32,128]{1,0:T(8,128)S(1)}, f32[32,128]{1,0:T(8,128)S(1)}, u32[]{:S(2)}, u32[]{:S(2)}) collective-permute-start(f32[32,128]{1,0:T(8,128)S(1)} %fusion.dots0), channel_id=1, source_target_pairs={{0,1},{1,0},{2,3},{3,2},{4,5},{5,4},{6,7},{7,6},{8,9},{9,8},{10,11... | collective-permute-start | bytes 49160 | tf_op jit(solution)/shard_map/ppermute | solution.py:566
  75.2 4.7 %collective-permute-start.11 = (f32[32,128]{1,0:T(8,128)S(1)}, f32[32,128]{1,0:T(8,128)S(1)}, u32[]{:S(2)}, u32[]{:S(2)}) collective-permute-start(f32[32,128]{1,0:T(8,128)S(1)} %fusion.dots0), channel_id=1, source_target_pairs={{0,2},{1,3},{2,0},{3,1},{4,6},{5,7},{6,4},{7,5},{8,10},{9,11},{10,... | collective-permute-start | bytes 49160 | tf_op jit(solution)/shard_map/ppermute | solution.py:566
  77.8 5.5 %collective-permute-start.12 = (f32[32,128]{1,0:T(8,128)S(1)}, f32[32,128]{1,0:T(8,128)S(1)}, u32[]{:S(2)}, u32[]{:S(2)}) collective-permute-start(f32[32,128]{1,0:T(8,128)S(1)} %fusion.dots0), channel_id=1, source_target_pairs={{0,3},{1,2},{2,1},{3,0},{4,7},{5,6},{6,5},{7,4},{8,11},{9,10},{10,... | collective-permute-start | bytes 49160 | tf_op jit(solution)/shard_map/ppermute | solution.py:566
  78.7 4.7 %copy-start.9 = (f32[32,128]{1,0:T(8,128)}, f32[32,128]{1,0:T(8,128)S(1)}, u32[]{:S(2)}) copy-start(f32[32,128]{1,0:T(8,128)S(1)} %collective-permute-done.10.dots1) | copy-start | bytes 49156
  87.3 3.9 %collective-permute-start.13 = (f32[16,256]{1,0:T(8,128)}, f32[16,256]{1,0:T(8,128)S(1)}, u32[]{:S(2)}, u32[]{:S(2)}) collective-permute-start(f32[16,256]{1,0:T(8,128)} %get-tuple-element.54), channel_id=1, source_target_pairs={{0,16},{16,0},{1,17},{17,1},{2,18},{18,2},{3,19},{19,3},{4,20},{20... | collective-permute-start | bytes 49160 | tf_op jit(solution)/shard_map/ppermute | solution.py:700
  91.9 1.9 %collective-permute-start.14 = (f32[16,256]{1,0:T(8,128)S(1)}, f32[16,256]{1,0:T(8,128)S(1)}, u32[]{:S(2)}, u32[]{:S(2)}) collective-permute-start(f32[16,256]{1,0:T(8,128)S(1)} %add.22), channel_id=1, source_target_pairs={{0,4},{4,0},{8,12},{12,8},{1,5},{5,1},{9,13},{13,9},{2,6},{6,2},{1... | collective-permute-start | bytes 49160 | tf_op jit(solution)/shard_map/ppermute | solution.py:566
  91.9 3.7 %collective-permute-start.15 = (f32[16,256]{1,0:T(8,128)S(1)}, f32[16,256]{1,0:T(8,128)S(1)}, u32[]{:S(2)}, u32[]{:S(2)}) collective-permute-start(f32[16,256]{1,0:T(8,128)S(1)} %add.22), channel_id=1, source_target_pairs={{0,8},{4,12},{8,0},{12,4},{1,9},{5,13},{9,1},{13,5},{2,10},{6,14},... | collective-permute-start | bytes 49160 | tf_op jit(solution)/shard_map/ppermute | solution.py:566
  92.8 3.2 %collective-permute-start.16 = (f32[16,256]{1,0:T(8,128)S(1)}, f32[16,256]{1,0:T(8,128)S(1)}, u32[]{:S(2)}, u32[]{:S(2)}) collective-permute-start(f32[16,256]{1,0:T(8,128)S(1)} %add.22), channel_id=1, source_target_pairs={{0,12},{4,8},{8,4},{12,0},{1,13},{5,9},{9,5},{13,1},{2,14},{6,10},... | collective-permute-start | bytes 49160 | tf_op jit(solution)/shard_map/ppermute | solution.py:566
  (3 other events, 4.6 us)

commit v2 on v1

--- a/solution.py
+++ b/solution.py
@@ -158,34 +158,24 @@
     return lax.gather(x, lanes[..., None], numbers, slice_sizes=(1, 1), mode=mode)
 
 
-def project_kernel(
+def gather_kernel(
     ids_ref,
     hard_ref,
     vocab_ref,
-    weight_ref,
     lower_ref,
-    out00,
-    out01,
-    out10,
-    out11,
+    turned,
     member_ref,
+    extra_ref,
     held,
-    weight,
     lower,
-    turned,
-    parts,
     token_ref,
     small,
     ranks,
-    statistics,
-    residual,
     counted,
     bounds,
     held_sems,
-    weight_sem,
     lower_sem,
     bounds_sem,
-    out_sems,
     base,
 ):
     texts, length = ids_ref.shape
@@ -193,24 +183,19 @@
     blocks = vocab // IDS_PER_BLOCK
     groups = vocab // IDS_PER_GROUP
     span = member_ref.shape[0]
-    chunks = span // CHUNK
     stripes = pl.cdiv(span, STRIPE)
     per_shard, negatives = hard_ref.shape
-    width = out00.shape[1]
-    outs = (out00, out01, out10, out11)
     shard = lax.axis_index("dp")
 
     def vocab_copy(b):
         columns = pl.ds(pl.multiple_of(b * IDS_PER_BLOCK, LANES), IDS_PER_BLOCK)
         return pltpu.make_async_copy(vocab_ref.at[:, columns], held.at[b], held_sems.at[b])
 
-    weight_copy = pltpu.make_async_copy(weight_ref, weight, weight_sem)
     lower_copy = pltpu.make_async_copy(
         lower_ref.at[:, pl.ds(pl.multiple_of(shard * features, LANES), features)], lower, lower_sem
     )
     vocab_copy(0).start()
     lower_copy.start()
-    weight_copy.start()
     for b in range(1, blocks):
         vocab_copy(b).start()
 
@@ -255,47 +240,15 @@
         return carry
 
     lax.fori_loop(0, span // LANES, place, 0)
-    residual[...] = jnp.zeros_like(residual)
-    statistics[...] = jnp.zeros_like(statistics)
     small[...] = jnp.zeros_like(small)
     small[0:per_shard, stripes : stripes + negatives] = hard_ref[...].astype(jnp.float32)
     lower_copy.wait()
-    weight_copy.wait()
     bounds_copy.wait()
-
-    def send(start, size):
-        rows = pl.ds(start, size)
-        for q in range(4):
-            pltpu.make_async_copy(parts.at[q, rows], outs[q].at[rows], out_sems.at[q]).start()
-
-    def project(k, carry):
-        start = pl.multiple_of(k * CHUNK, LANES)
-        across = pl.ds(start, CHUNK)
-        upright = turned[:, across]
-        x = upright.T
-        for q in range(4):
-            at = pl.multiple_of(split_quarter(q // 2, q % 2) * width, LANES)
-            product = mm(x, weight[:, pl.ds(at, width)])
-            parts[q, across, :] = product.astype(jnp.bfloat16)
-        send(start, CHUNK)
-        wide = upright.astype(jnp.float32)
-        statistics[0:ROWS, across] = mm(lower[...], upright)
-        statistics[ROWS : ROWS + 1, across] = jnp.sum(wide * wide, axis=0, keepdims=True)
-        member = member_ref[across, :].astype(jnp.float32).T.astype(jnp.bfloat16)
-        residual[...] += mm(member[0:ROWS], x)
-        return carry
-
-    def zero(k, carry):
-        start = pl.multiple_of(k * CHUNK, LANES)
-        for q in range(4):
-            parts[q, pl.ds(start, CHUNK), :] = jnp.zeros((CHUNK, width), jnp.bfloat16)
-        send(start, CHUNK)
-        return carry
 
     def within(place):
         return jnp.clip(place - base, 0, span)
 
-    def take(b, done):
+    def take(b, carry):
         vocab_copy(b).wait()
         for part in range(IDS_PER_BLOCK // IDS_PER_GROUP):
             group = b * (IDS_PER_BLOCK // IDS_PER_GROUP) + part
@@ -307,50 +260,49 @@
                 at = pl.ds(pl.multiple_of(p * LANES, LANES), LANES)
                 token = token_ref[pl.ds(p, 1), :] - group * IDS_PER_GROUP
                 token = jnp.broadcast_to(token, (FEATURE_ROWS, LANES))
-                lane = token & (LANES - 1)
-                tile = lax.shift_right_arithmetic(token, LANE_BITS)
+                lane = (token & (LANES - 1)).astype(jnp.int16)
+                tile = lax.shift_right_arithmetic(token, LANE_BITS).astype(jnp.int16)
                 for f in range(features // FEATURE_ROWS):
                     rows = pl.ds(f * FEATURE_ROWS, FEATURE_ROWS)
-                    total = turned[rows, at].astype(jnp.float32)
+                    total = turned[rows, at]
                     for j in range(IDS_PER_GROUP // LANES):
                         columns = pl.ds(part * IDS_PER_GROUP + j * LANES, LANES)
-                        found = take_lanes(held[b, rows, columns].astype(jnp.float32), lane)
+                        found = take_lanes(held[b, rows, columns], lane)
                         total = jnp.where(tile == j, found, total)
-                    turned[rows, at] = total.astype(jnp.bfloat16)
+                    turned[rows, at] = total
                 return carry
 
             lax.fori_loop(begin, jnp.where(last > first, end, begin), window, 0)
-        full = lax.div(last, CHUNK)
-        lax.fori_loop(done, full, project, 0)
-        return full
-
-    done = lax.fori_loop(0, blocks, take, 0)
-    used = lax.div(within(bounds[groups, 0]) + CHUNK - 1, CHUNK)
-    lax.fori_loop(done, used, project, 0)
-    lax.fori_loop(used, chunks, zero, 0)
-
+        return carry
+
+    lax.fori_loop(0, blocks, take, 0)
+
+    misc = jnp.zeros((ROWS, STRIPE), jnp.float32)
+    residual = jnp.zeros((features, LANES), jnp.float32)
+    for stripe in range(stripes):
+        size = min(STRIPE, span - stripe * STRIPE)
+        across = pl.ds(stripe * STRIPE, size)
+        upright = turned[:, across]
+        wide = upright.astype(jnp.float32)
+        square = jnp.sum(wide * wide, axis=0, keepdims=True)
+        reduced = mm(lower[...], upright)
+        if size < STRIPE:
+            none = jnp.zeros((ROWS, STRIPE - size), jnp.float32)
+            reduced = jnp.concatenate([reduced, none], axis=1)
+            square = jnp.concatenate([square, none[0:1]], axis=1)
+        extra_ref[stripe * ROWS : (stripe + 1) * ROWS, :] = reduced.astype(jnp.bfloat16)
+        misc = jnp.where(iota((ROWS, STRIPE), 0) == stripe, square, misc)
+        residual += mm(upright, member_ref[across, :])
     hard = small[...].T[0:ROWS]
-    lane = iota((ROWS, width), 1)
-    misc = jnp.zeros((ROWS, width), jnp.float32)
-    for stripe in range(stripes):
-        across = pl.ds(stripe * STRIPE, STRIPE)
-        for q in range(4):
-            parts[q, pl.ds(span + stripe * ROWS, ROWS), :] = statistics[0:ROWS, across].astype(
-                jnp.bfloat16
-            )
-        squares = jnp.broadcast_to(statistics[ROWS : ROWS + 1, across], (ROWS, STRIPE))
-        misc = jnp.where(iota((ROWS, width), 0) == stripe, squares, misc)
     for i in range(per_shard):
-        misc += jnp.where(lane == shard * per_shard + i, hard[:, i : i + 1], 0.0)
-    mine = lax.axis_index("mp") == shard
-    for q in range(4):
-        start = pl.multiple_of(split_quarter(q // 2, q % 2) * width, LANES)
-        part = jnp.where(mine, residual[:, pl.ds(start, width)], 0.0)
-        parts[q, pl.ds(span + stripes * ROWS, ROWS), :] = misc.astype(jnp.bfloat16)
-        parts[q, pl.ds(span + (stripes + 1) * ROWS, ROWS), :] = part.astype(jnp.bfloat16)
-    send(span, (stripes + 2) * ROWS)
-    for q in range(4):
-        pltpu.make_async_copy(parts.at[q], outs[q], out_sems.at[q]).wait()
+        misc += jnp.where(iota((ROWS, STRIPE), 1) == shard * per_shard + i, hard[:, i : i + 1], 0.0)
+    extra_ref[stripes * ROWS : (stripes + 1) * ROWS, :] = misc.astype(jnp.bfloat16)
+    residual = jnp.where(lax.axis_index("mp") == shard, residual.T[0:ROWS], 0.0)
+    for q in range(features // STRIPE):
+        start = (stripes + 1 + q) * ROWS
+        extra_ref[start : start + ROWS, :] = residual[:, q * STRIPE : (q + 1) * STRIPE].astype(
+            jnp.bfloat16
+        )
 
 
 def pool_kernel(
@@ -358,10 +310,12 @@
     own_ref,
     core_ref,
     far_ref,
+    extra_ref,
     member_ref,
     own_rest,
     core_rest,
     far_rest,
+    extra_rest,
     member_rest,
     raise_ref,
     pooled_ref,
@@ -379,14 +333,14 @@
     raised[0:ROWS, :] = raise_ref[:, pl.ds(pl.multiple_of(quarter * width, LANES), width)]
     total[...] = jnp.zeros_like(total)
 
-    def add(refs, member_ref, base):
+    def add(refs, extra_ref, member_ref, base):
         span = member_ref.shape[0]
         stripes = pl.cdiv(span, STRIPE)
 
         def summed(start, size):
             return sum(ref[pl.ds(start, size), :].astype(jnp.float32) for ref in refs)
 
-        misc = summed(span + stripes * ROWS, ROWS)
+        misc = extra_ref[stripes * ROWS : (stripes + 1) * ROWS, :]
         if base == 0:
             misc_ref[...] = misc
         inverse = lax.rsqrt(misc / model_width + 1e-05)
@@ -394,7 +348,7 @@
             at = base + k * STRIPE
             size = min(STRIPE, span - k * STRIPE)
             scale = inverse[k : k + 1]
-            reduced = (summed(span + k * ROWS, ROWS) * scale).astype(jnp.bfloat16)
+            reduced = (extra_ref[k * ROWS : (k + 1) * ROWS, :] * scale).astype(jnp.bfloat16)
             reduced_ref[:, at : at + size] = reduced[:, 0:size]
             stacked = jnp.concatenate(
                 [reduced.astype(jnp.float32), jnp.broadcast_to(scale, (LANES - ROWS, STRIPE))]
@@ -408,14 +362,15 @@
             member = member[0:ROWS].astype(jnp.bfloat16)
             high, rest = split(linear * sigma)
             total[...] += mm(member, high) + mm(member, rest)
-        total[...] += summed(span + (stripes + 1) * ROWS, ROWS)
-
-    add((own_ref, core_ref, far_ref), member_ref, 0)
+        start = pl.multiple_of((stripes + 1 + quarter) * ROWS, ROWS)
+        total[...] += extra_ref[pl.ds(start, ROWS), :]
+
+    add((own_ref, core_ref, far_ref), extra_ref, member_ref, 0)
     real = (ids_ref[...] != 0).astype(jnp.float32)
 
     @pl.when(jnp.sum(real) > member_ref.shape[0])
     def _():
-        add((own_rest, core_rest, far_rest), member_rest, member_ref.shape[0])
+        add((own_rest, core_rest, far_rest), extra_rest, member_rest, member_ref.shape[0])
 
     counts = jnp.sum(real, axis=1, keepdims=True)
     pooled = total[0:texts] / counts
@@ -590,48 +545,52 @@
     other_core = [(d, d ^ 1) for d in range(shards)]
     other_y = [(d, d ^ 2) for d in range(shards)]
 
+    def columns(i, j):
+        start = split_quarter(i, j) * width
+        return lax.dynamic_slice(layer_weight_matrix, (0, start), (features, width))
+
     def project(base, span):
         stripes = pl.cdiv(span, STRIPE)
-        rows = span + (stripes + 2) * ROWS
-        own0, own1, away0, away1, member = pl.pallas_call(
-            functools.partial(project_kernel, base=base),
-            out_shape=[jax.ShapeDtypeStruct((rows, width), jnp.bfloat16)] * 4
-            + [jax.ShapeDtypeStruct((span, LANES), jnp.bfloat16)],
-            in_specs=[vmem_spec()] * 2 + [any_spec()] * 3,
-            out_specs=[any_spec()] * 4 + [vmem_spec()],
+        extra_rows = (stripes + 1 + shards) * ROWS
+        turned, member, extra = pl.pallas_call(
+            functools.partial(gather_kernel, base=base),
+            out_shape=[
+                jax.ShapeDtypeStruct((features, span), jnp.bfloat16),
+                jax.ShapeDtypeStruct((span, LANES), jnp.bfloat16),
+                jax.ShapeDtypeStruct((extra_rows, STRIPE), jnp.bfloat16),
+            ],
+            in_specs=[vmem_spec()] * 2 + [any_spec()] * 2,
+            out_specs=[vmem_spec()] * 3,
             scratch_shapes=[
                 pltpu.VMEM((blocks, features, IDS_PER_BLOCK), jnp.bfloat16),
-                pltpu.VMEM((features, part_width), jnp.bfloat16),
                 pltpu.VMEM((rank, features), jnp.bfloat16),
-                pltpu.VMEM((features, span), jnp.bfloat16),
-                pltpu.VMEM((4, rows, width), jnp.bfloat16),
                 pltpu.VMEM((8 * pl.cdiv(span // LANES, 8), LANES), jnp.int32),
                 pltpu.VMEM((LANES, LANES), jnp.float32),
                 pltpu.VMEM((texts, length), jnp.float32),
-                pltpu.VMEM((ROWS + 8, stripes * STRIPE), jnp.float32),
-                pltpu.VMEM((ROWS, features), jnp.float32),
                 pltpu.VMEM((group_rows, length), jnp.int32),
                 pltpu.SMEM((group_rows, length), jnp.int32),
                 pltpu.SemaphoreType.DMA((blocks,)),
                 pltpu.SemaphoreType.DMA,
                 pltpu.SemaphoreType.DMA,
-                pltpu.SemaphoreType.DMA,
-                pltpu.SemaphoreType.DMA((4,)),
             ],
             compiler_params=params,
-            name="project",
-        )(
-            ids,
-            difficult_distractors,
-            vocabulary_vectors,
-            layer_weight_matrix,
-            lowering_factor_matrix,
-        )
-        core1 = lax.ppermute(away1, "dp", other_core)
-        core0 = lax.ppermute(away0, "dp", other_core)
-        chip1 = (own1.astype(jnp.float32) + core1.astype(jnp.float32)).astype(jnp.bfloat16)
-        far = lax.ppermute(chip1, "dp", other_y)
-        return own0, core0, far, member
+            name="gather",
+        )(ids, difficult_distractors, vocabulary_vectors, lowering_factor_matrix)
+
+        def product(i, j):
+            return mm(turned, columns(i, j), (((0,), (0,)), ((), ())))
+
+        def narrow(x):
+            return x.astype(jnp.bfloat16)
+
+        chip = extra.astype(jnp.float32)
+        chip += lax.ppermute(extra, "dp", other_core).astype(jnp.float32)
+        extra = chip + lax.ppermute(narrow(chip), "dp", other_y).astype(jnp.float32)
+        core1 = lax.ppermute(narrow(product(1, 1)), "dp", other_core)
+        far = lax.ppermute(narrow(product(0, 1) + core1.astype(jnp.float32)), "dp", other_y)
+        core0 = lax.ppermute(narrow(product(1, 0)), "dp", other_core)
+        own0 = narrow(product(0, 0))
+        return own0, core0, far, extra, member
 
     first = project(0, FIRST)
     many = jnp.sum((ids != 0).astype(jnp.int32)) > FIRST
@@ -650,7 +609,7 @@
             jax.ShapeDtypeStruct((ROWS, tokens), jnp.bfloat16),
             jax.ShapeDtypeStruct((ROWS, width), jnp.float32),
         ],
-        in_specs=[vmem_spec()] * 10,
+        in_specs=[vmem_spec()] * 12,
         out_specs=[vmem_spec()] * 4,
         scratch_shapes=[
             pltpu.VMEM((LANES, width), jnp.bfloat16),
@@ -659,7 +618,7 @@
         compiler_params=params,
         name="pool",
     )(ids, *first, *rest, raising_factor_matrix)
-    member, member_rest = first[3], rest[3]
+    member, member_rest = first[4], rest[4]
     far_side = lax.ppermute(pooled, "group", [(0, 1), (1, 0)])
     rows = 2 * ROWS
     packed = pl.pallas_call(

time: 97.2 us -> 102 us (1.049)
  matrix products: 0 us -> 11.9 us
  Pallas kernels: 42.4 us -> 37.4 us
  other arithmetic: 4.86 us -> 3.46 us
  waiting for transfers between devices: 29.9 us -> 28.6 us
    dot_general x0 -> x4, matrix products: none -> 11.9 us  [mm(): return lax.dot_general(a, b, dims, preferred_element_type=jnp.float32)]
    pallas_call x1, Pallas kernels: 33.6 us -> 28.6 us  [project(): pl.pallas_call(functools.partial(gather_kernel, base=base), out_shape=[ja...]
    convert_element_type x1, other arithmetic: 2.12 us -> 0.02 us  [narrow(): return x.astype(jnp.bfloat16)]
    ppermute x3 -> x5, waiting for transfers between devices: 14.2 us -> 12.9 us  [the longest x1 12.9 us: project(): extra = chip + lax.ppermute(narrow(chip), 'dp', other_y).astype(jnp.float32)]
    unnamed x27 -> x33, local copies, waits for them, and re-layouts: 1.89 us -> 2.89 us
    ppermute x3 -> x5, starting transfers between devices: 3.48 us -> 3.75 us  [the longest x1 2.63 us: project(): lax.ppermute(narrow(product(0, 1) + core1.astype(jnp.float32)), 'dp', oth...]
  transfers between devices with their start and end apart: 14 -> 16, of which waited for: 10 -> 9; matrix products, arithmetic and copies ran while one was open for 4% -> 11% of each run, Pallas kernels for 0% -> 0%
where the time goes in v2:
time: 102 us
  Pallas kernels  37.4 us (37%)
  waiting for transfers between devices  28.6 us (28%)
  starting transfers between devices  14.2 us (14%)
  matrix products  11.9 us (12%)
  local copies, waits for them, and re-layouts  4.31 us (4%)
  other arithmetic  3.46 us (3%)
  between operations  2.11 us (2%)
    pallas_call x1, Pallas kernels, project(): pl.pallas_call(functools.partial(gather_kernel, base=base), out_shape=[ja...  28.6 us
    ppermute x1, waiting for transfers between devices, project(): extra = chip + lax.ppermute(narrow(chip), 'dp', other_y).astype(jnp.float32)  12.9 us
    dot_general x4, matrix products, mm(): return lax.dot_general(a, b, dims, preferred_element_type=jnp.float32)  11.9 us
    ppermute x9, waiting for transfers between devices, exchange(): return [x] + [lax.ppermute(x, axis, step) for step in steps]  10.2 us
    ppermute x9, starting transfers between devices, exchange(): return [x] + [lax.ppermute(x, axis, step) for step in steps]  8.14 us
    pallas_call x1, Pallas kernels, split_body(): pl.pallas_call(functools.partial(pool_kernel, model_width=float(features...  3.98 us
    pallas_call x1, Pallas kernels, split_body(): pl.pallas_call(functools.partial(score_kernel, negatives=negatives), out_...  3.36 us
    unnamed x33, local copies, waits for them, and re-layouts  2.89 us
  transfers between devices with their start and end apart: 16, of which 9 were waited for; matrix products, arithmetic and copies ran while one was open for 11% of the time, Pallas kernels for 0%

profile of v2, /device:TPU:0, one launch (start us, length us, event | category | flops | bytes accessed | tf_op | source)
XLA Modules:
  0.0 102.1 jit_solution(6228319419212726941)
XLA Ops:
  1.3 28.6 %gather.3 = (bf16[1024,1152]{1,0:T(8,128)(2,1)}, bf16[1152,128]{1,0:T(8,128)(2,1)}, bf16[160,256]{1,0:T(8,128)(2,1)}) custom-call(s32[12,128]{1,0:T(8,128)S(1)} %bitcast.13, s32[3,7]{1,0:T(4,128)} %hard_ref.1, bf16[1024,16384]{1,0:T(8,128)(2,1)} %vocab_ref.1, bf16[16,4096]{1,0:T(8,128)(2,1)} %lower_ref.1), custom_call_target="tpu_custom_call" | custom-call | tf_op jit(solution)/shard_map/gather/pallas_call | solution.py:555
  30.0 3.5 %convolution_convert_fusion.3 = bf16[1152,256]{1,0:T(8,128)(2,1)} fusion(bf16[1024,1152]{1,0:T(8,128)(2,1)} %get-tuple-element.36, bf16[1024,1024]{1,0:T(8,128)(2,1)} %param.12, s32[]{:T(128)S(6)} %select_n.135), kind=kOutput, calls=%fused_computation.16 | convolution fusion | flops 604274688 | bytes 3473412 | tf_op jit(solution)/shard_map/dot_general | solution.py:127
  34.0 2.7 %convolution_convert_fusion.4 = bf16[1152,256]{1,0:T(8,128)(2,1)} fusion(bf16[1024,1152]{1,0:T(8,128)(2,1)S(1)} %copy-done.15, bf16[1024,1024]{1,0:T(8,128)(2,1)} %param.12, s32[]{:T(128)S(6)} %select_n.133), kind=kOutput, calls=%fused_computation.17 | convolution fusion | flops 604274688 | bytes 3473412 | tf_op jit(solution)/shard_map/dot_general | solution.py:127
  38.1 1.5 %conditional.1 = (bf16[384,256]{1,0:T(8,128)(2,1)S(1)}, bf16[384,256]{1,0:T(8,128)(2,1)}, bf16[384,256]{1,0:T(8,128)(2,1)}, f32[112,256]{1,0:T(8,128)S(1)}, bf16[384,128]{1,0:T(8,128)(2,1)S(1)}) conditional(s32[]{:T(128)} %convert_element_type.70, () %tuple.16, (s32[12,128]{1,0:T(8,128)S(1)}, s32[3,7]{1,0:T(4,128)S(1)}, ...), branch_computations={%region_1.0_spmd, %region_2.0_spmd} | conditional | flops 806154240 | bytes 18121424 | solution.py:599
  40.1 2.9 %add_convert_fusion.1 = bf16[1152,256]{1,0:T(8,128)(2,1)S(1)} fusion(bf16[1152,256]{1,0:T(8,128)(2,1)} %collective-permute-done.6, bf16[1024,1152]{1,0:T(8,128)(2,1)} %get-tuple-element.36, bf16[1024,1024]{1,0:T(8,128)(2,1)} %param.12, s32[]{:T(128)S(6)} %select_n.134), kind=kOutput, calls=%fused_computation.19 | convolution fusion | flops 604864512 | bytes 4063236 | tf_op jit(solution)/shard_map/dot_general | solution.py:127
  43.0 2.6 %collective-permute-start.7 = (bf16[1152,256]{1,0:T(8,128)(2,1)S(1)}, bf16[1152,256]{1,0:T(8,128)(2,1)S(1)}, u32[]{:S(2)}, u32[]{:S(2)}) collective-permute-start(bf16[1152,256]{1,0:T(8,128)(2,1)S(1)} %add_convert_fusion.1), channel_id=1, source_target_pairs={{0,8},{4,12},{8,0},{12,4},{1,9},{5,13},{9,1},{13,5},{2,10},{6,14},... | collective-permute-start | bytes 1769480 | tf_op jit(solution)/shard_map/ppermute | solution.py:590
  45.8 2.7 %convolution_convert_fusion.5.own_ref = bf16[1152,256]{1,0:T(8,128)(2,1)} fusion(bf16[1024,1152]{1,0:T(8,128)(2,1)S(1)} %copy-done.16, bf16[1024,1024]{1,0:T(8,128)(2,1)} %param.12, s32[]{:T(128)S(6)} %select_n.132), kind=kOutput, calls=%fused_computation.18 | convolution fusion | flops 604274688 | bytes 3473412 | tf_op jit(solution)/shard_map/dot_general | solution.py:127
  48.5 12.9 %collective-permute-done.9 = bf16[160,256]{1,0:T(8,128)(2,1)S(1)} collective-permute-done((bf16[160,256]{1,0:T(8,128)(2,1)S(1)}, bf16[160,256]{1,0:T(8,128)(2,1)S(1)}, u32[]{:S(2)}, u32[]{:S(2)}) %collective-permute-start.9) | collective-permute-done | bytes 81952 | tf_op jit(solution)/shard_map/ppermute | solution.py:588
  63.1 4.0 %pool.1 = (bf16[16,256]{1,0:T(8,128)(2,1)}, f32[1536,256]{1,0:T(8,128)}, bf16[16,1536]{1,0:T(8,128)(2,1)}, f32[16,256]{1,0:T(8,128)}) custom-call(s32[12,128]{1,0:T(8,128)S(1)} %bitcast.15, bf16[1152,256]{1,0:T(8,128)(2,1)} %convolution_convert_fusion.5.own_ref, bf16[1152,256]{1,0:T(8,128)(2,1)} %copy-done, bf16[1152,256]{1,0:T(8,128)(2,1)} %copy-done.1, ...), custom_call_target="tpu_custom_call" | custom-call | tf_op jit(solution)/shard_map/pool/pallas_call | solution.py:604
  67.1 1.3 %collective-permute-start.10 = (bf16[16,256]{1,0:T(8,128)(2,1)}, bf16[16,256]{1,0:T(8,128)(2,1)S(1)}, u32[]{:S(2)}, u32[]{:S(2)}) collective-permute-start(bf16[16,256]{1,0:T(8,128)(2,1)} %get-tuple-element.44.near_ref), channel_id=1, source_target_pairs={{0,16},{16,0},{1,17},{17,1},{2,18},{18,2},{3,19},{19,3},{4,20},{20... | collective-permute-start | bytes 24584 | tf_op jit(solution)/shard_map/ppermute | solution.py:622
  68.4 2.6 %collective-permute-done.10.far_ref = bf16[16,256]{1,0:T(8,128)(2,1)S(1)} collective-permute-done((bf16[16,256]{1,0:T(8,128)(2,1)}, bf16[16,256]{1,0:T(8,128)(2,1)S(1)}, u32[]{:S(2)}, u32[]{:S(2)}) %collective-permute-start.10) | collective-permute-done | bytes 8224 | tf_op jit(solution)/shard_map/ppermute | solution.py:622
  71.5 1.4 %dots.1.packed0 = f32[64,128]{1,0:T(8,128)} custom-call(bf16[16,256]{1,0:T(8,128)(2,1)} %get-tuple-element.44.near_ref, bf16[16,256]{1,0:T(8,128)(2,1)} %copy-done.9), custom_call_target="tpu_custom_call" | custom-call | tf_op jit(solution)/shard_map/dots/pallas_call | solution.py:624
  73.0 1.7 %collective-permute-start.12 = (f32[64,128]{1,0:T(8,128)}, f32[64,128]{1,0:T(8,128)S(1)}, u32[]{:S(2)}, u32[]{:S(2)}) collective-permute-start(f32[64,128]{1,0:T(8,128)} %dots.1.packed0), channel_id=1, source_target_pairs={{0,8},{4,12},{8,0},{12,4},{1,9},{5,13},{9,1},{13,5},{2,10},{6,14},... | collective-permute-start | bytes 98312 | tf_op jit(solution)/shard_map/ppermute | solution.py:521
  74.9 2.2 %collective-permute-done.12.packed2 = f32[64,128]{1,0:T(8,128)S(1)} collective-permute-done((f32[64,128]{1,0:T(8,128)}, f32[64,128]{1,0:T(8,128)S(1)}, u32[]{:S(2)}, u32[]{:S(2)}) %collective-permute-start.12) | collective-permute-done | bytes 32800 | tf_op jit(solution)/shard_map/ppermute | solution.py:521
  77.1 1.2 %collective-permute-done.13.packed3 = f32[64,128]{1,0:T(8,128)S(1)} collective-permute-done((f32[64,128]{1,0:T(8,128)}, f32[64,128]{1,0:T(8,128)S(1)}, u32[]{:S(2)}, u32[]{:S(2)}) %collective-permute-start.13) | collective-permute-done | bytes 32800 | tf_op jit(solution)/shard_map/ppermute | solution.py:521
  79.0 1.6 %collective-permute-start.14 = (f32[32,128]{1,0:T(8,128)S(1)}, f32[32,128]{1,0:T(8,128)S(1)}, u32[]{:S(2)}, u32[]{:S(2)}) collective-permute-start(f32[32,128]{1,0:T(8,128)S(1)} %fusion.20.dots0), channel_id=1, source_target_pairs={{0,1},{1,0},{2,3},{3,2},{4,5},{5,4},{6,7},{7,6},{8,9},{9,8},{10,11... | collective-permute-start | bytes 49160 | tf_op jit(solution)/shard_map/ppermute | solution.py:521
  80.6 2.6 %collective-permute-start.15 = (f32[32,128]{1,0:T(8,128)S(1)}, f32[32,128]{1,0:T(8,128)S(1)}, u32[]{:S(2)}, u32[]{:S(2)}) collective-permute-start(f32[32,128]{1,0:T(8,128)S(1)} %fusion.20.dots0), channel_id=1, source_target_pairs={{0,2},{1,3},{2,0},{3,1},{4,6},{5,7},{6,4},{7,5},{8,10},{9,11},{10,... | collective-permute-start | bytes 49160 | tf_op jit(solution)/shard_map/ppermute | solution.py:521
  84.1 1.2 %collective-permute-done.15.dots2 = f32[32,128]{1,0:T(8,128)S(1)} collective-permute-done((f32[32,128]{1,0:T(8,128)S(1)}, f32[32,128]{1,0:T(8,128)S(1)}, u32[]{:S(2)}, u32[]{:S(2)}) %collective-permute-start.15) | collective-permute-done | bytes 16416 | tf_op jit(solution)/shard_map/ppermute | solution.py:521
  85.3 3.4 %collective-permute-done.16.dots3 = f32[32,128]{1,0:T(8,128)S(1)} collective-permute-done((f32[32,128]{1,0:T(8,128)S(1)}, f32[32,128]{1,0:T(8,128)S(1)}, u32[]{:S(2)}, u32[]{:S(2)}) %collective-permute-start.16) | collective-permute-done | bytes 16416 | tf_op jit(solution)/shard_map/ppermute | solution.py:521
  89.3 3.4 %score.1 = (bf16[1,3,1024]{2,1,0:T(4,128)(2,1)}, f32[1,3]{1,0:T(1,128)}, f32[16,256]{1,0:T(8,128)}) custom-call(s32[12,128]{1,0:T(8,128)S(1)} %bitcast.16, bf16[16,256]{1,0:T(8,128)(2,1)} %get-tuple-element.44.near_ref, bf16[16,256]{1,0:T(8,128)(2,1)} %copy-done.9, f32[64,128]{1,0:T(8,128)} %dots.1.packed0, f32[64,128]{1,0:T(8,128)} %copy-done.5, ...), custom_call_target="tpu_custom_call" | custom-call | tf_op jit(solution)/shard_map/score/pallas_call | solution.py:635
  92.7 1.1 %collective-permute-start.17 = (f32[16,256]{1,0:T(8,128)}, f32[16,256]{1,0:T(8,128)S(1)}, u32[]{:S(2)}, u32[]{:S(2)}) collective-permute-start(f32[16,256]{1,0:T(8,128)} %get-tuple-element.50), channel_id=1, source_target_pairs={{0,16},{16,0},{1,17},{17,1},{2,18},{18,2},{3,19},{19,3},{4,20},{20... | collective-permute-start | bytes 49160 | tf_op jit(solution)/shard_map/ppermute | solution.py:659
  93.8 2.9 %collective-permute-done.17 = f32[16,256]{1,0:T(8,128)S(1)} collective-permute-done((f32[16,256]{1,0:T(8,128)}, f32[16,256]{1,0:T(8,128)S(1)}, u32[]{:S(2)}, u32[]{:S(2)}) %collective-permute-start.17) | collective-permute-done | bytes 16416 | tf_op jit(solution)/shard_map/ppermute | solution.py:659
  98.2 1.0 collective-permute-start.20
  99.2 1.9 %collective-permute-done.19 = f32[16,256]{1,0:T(8,128)S(1)} collective-permute-done((f32[16,256]{1,0:T(8,128)S(1)}, f32[16,256]{1,0:T(8,128)S(1)}, u32[]{:S(2)}, u32[]{:S(2)}) %collective-permute-start.19) | collective-permute-done | bytes 16416 | tf_op jit(solution)/shard_map/ppermute | solution.py:521
  (62 shorter events, 10.5 us)
Async XLA Ops:
  33.5 6.6 %collective-permute-start.6 = (bf16[1152,256]{1,0:T(8,128)(2,1)}, bf16[1152,256]{1,0:T(8,128)(2,1)}, u32[]{:S(2)}, u32[]{:S(2)}) collective-permute-start(bf16[1152,256]{1,0:T(8,128)(2,1)} %convolution_convert_fusion.3), channel_id=1, source_target_pairs={{0,4},{4,0},{8,12},{12,8},{1,5},{5,1},{9,13},{13,9},{2,6},{6,2},{1... | collective-permute-start | bytes 1769480 | tf_op jit(solution)/shard_map/ppermute | solution.py:589
  34.0 4.1 %copy-start.2 = (bf16[16,4096]{1,0:T(8,128)(2,1)S(1)}, bf16[16,4096]{1,0:T(8,128)(2,1)}, u32[]{:S(2)}) copy-start(bf16[16,4096]{1,0:T(8,128)(2,1)} %lower_ref.1) | copy-start | bytes 393220
  34.0 4.1 %copy-start.14 = (s32[3,7]{1,0:T(4,128)S(1)}, s32[3,7]{1,0:T(4,128)}, u32[]{:S(2)}) copy-start(s32[3,7]{1,0:T(4,128)} %hard_ref.1) | copy-start | bytes 256
  36.8 25.3 %collective-permute-start.5 = (bf16[1152,256]{1,0:T(8,128)(2,1)}, bf16[1152,256]{1,0:T(8,128)(2,1)S(1)}, u32[]{:S(2)}, u32[]{:S(2)}) collective-permute-start(bf16[1152,256]{1,0:T(8,128)(2,1)} %convolution_convert_fusion.4), channel_id=1, source_target_pairs={{0,4},{4,0},{8,12},{12,8},{1,5},{5,1},{9,13},{13,9},{2,6},{6,2},{1... | collective-permute-start | bytes 1769480 | tf_op jit(solution)/shard_map/ppermute | solution.py:591
  39.6 6.1 %collective-permute-start.8 = (bf16[160,256]{1,0:T(8,128)(2,1)S(1)}, bf16[160,256]{1,0:T(8,128)(2,1)S(1)}, u32[]{:S(2)}, u32[]{:S(2)}) collective-permute-start(bf16[160,256]{1,0:T(8,128)(2,1)S(1)} %copy-done.3), channel_id=1, source_target_pairs={{0,4},{4,0},{8,12},{12,8},{1,5},{5,1},{9,13},{13,9},{2,6},{6,2},{1... | collective-permute-start | bytes 245768 | tf_op jit(solution)/shard_map/ppermute | solution.py:587
  40.1 5.7 %copy-start.16 = (bf16[1024,1152]{1,0:T(8,128)(2,1)S(1)}, bf16[1024,1152]{1,0:T(8,128)(2,1)}, u32[]{:S(2)}) copy-start(bf16[1024,1152]{1,0:T(8,128)(2,1)} %get-tuple-element.36) | copy-start | bytes 7077892
  43.0 19.0 %collective-permute-start.7 = (bf16[1152,256]{1,0:T(8,128)(2,1)S(1)}, bf16[1152,256]{1,0:T(8,128)(2,1)S(1)}, u32[]{:S(2)}, u32[]{:S(2)}) collective-permute-start(bf16[1152,256]{1,0:T(8,128)(2,1)S(1)} %add_convert_fusion.1), channel_id=1, source_target_pairs={{0,8},{4,12},{8,0},{12,4},{1,9},{5,13},{9,1},{13,5},{2,10},{6,14},... | collective-permute-start | bytes 1769480 | tf_op jit(solution)/shard_map/ppermute | solution.py:590
  45.7 15.7 %collective-permute-start.9 = (bf16[160,256]{1,0:T(8,128)(2,1)S(1)}, bf16[160,256]{1,0:T(8,128)(2,1)S(1)}, u32[]{:S(2)}, u32[]{:S(2)}) collective-permute-start(bf16[160,256]{1,0:T(8,128)(2,1)S(1)} %fusion.19), channel_id=1, source_target_pairs={{0,8},{4,12},{8,0},{12,4},{1,9},{5,13},{9,1},{13,5},{2,10},{6,14},... | collective-permute-start | bytes 245768 | tf_op jit(solution)/shard_map/ppermute | solution.py:588
  67.1 3.9 %collective-permute-start.10 = (bf16[16,256]{1,0:T(8,128)(2,1)}, bf16[16,256]{1,0:T(8,128)(2,1)S(1)}, u32[]{:S(2)}, u32[]{:S(2)}) collective-permute-start(bf16[16,256]{1,0:T(8,128)(2,1)} %get-tuple-element.44.near_ref), channel_id=1, source_target_pairs={{0,16},{16,0},{1,17},{17,1},{2,18},{18,2},{3,19},{19,3},{4,20},{20... | collective-permute-start | bytes 24584 | tf_op jit(solution)/shard_map/ppermute | solution.py:622
  73.0 1.9 %collective-permute-start.11 = (f32[64,128]{1,0:T(8,128)}, f32[64,128]{1,0:T(8,128)S(1)}, u32[]{:S(2)}, u32[]{:S(2)}) collective-permute-start(f32[64,128]{1,0:T(8,128)} %dots.1.packed0), channel_id=1, source_target_pairs={{0,4},{4,0},{8,12},{12,8},{1,5},{5,1},{9,13},{13,9},{2,6},{6,2},{1... | collective-permute-start | bytes 98312 | tf_op jit(solution)/shard_map/ppermute | solution.py:521
  73.0 4.1 %collective-permute-start.12 = (f32[64,128]{1,0:T(8,128)}, f32[64,128]{1,0:T(8,128)S(1)}, u32[]{:S(2)}, u32[]{:S(2)}) collective-permute-start(f32[64,128]{1,0:T(8,128)} %dots.1.packed0), channel_id=1, source_target_pairs={{0,8},{4,12},{8,0},{12,4},{1,9},{5,13},{9,1},{13,5},{2,10},{6,14},... | collective-permute-start | bytes 98312 | tf_op jit(solution)/shard_map/ppermute | solution.py:521
  74.7 3.6 %collective-permute-start.13 = (f32[64,128]{1,0:T(8,128)}, f32[64,128]{1,0:T(8,128)S(1)}, u32[]{:S(2)}, u32[]{:S(2)}) collective-permute-start(f32[64,128]{1,0:T(8,128)} %dots.1.packed0), channel_id=1, source_target_pairs={{0,12},{4,8},{8,4},{12,0},{1,13},{5,9},{9,5},{13,1},{2,14},{6,10},... | collective-permute-start | bytes 98312 | tf_op jit(solution)/shard_map/ppermute | solution.py:521
  74.9 13.8 %copy-start.5 = (f32[64,128]{1,0:T(8,128)}, f32[64,128]{1,0:T(8,128)S(1)}, u32[]{:S(2)}) copy-start(f32[64,128]{1,0:T(8,128)S(1)} %collective-permute-done.11.packed1) | copy-start | bytes 98308
  77.1 11.6 %copy-start.6 = (f32[64,128]{1,0:T(8,128)}, f32[64,128]{1,0:T(8,128)S(1)}, u32[]{:S(2)}) copy-start(f32[64,128]{1,0:T(8,128)S(1)} %collective-permute-done.12.packed2) | copy-start | bytes 98308
  78.3 10.5 %copy-start.7 = (f32[64,128]{1,0:T(8,128)}, f32[64,128]{1,0:T(8,128)S(1)}, u32[]{:S(2)}) copy-start(f32[64,128]{1,0:T(8,128)S(1)} %collective-permute-done.13.packed3) | copy-start | bytes 98308
  79.0 9.7 %copy-start.8 = (f32[32,128]{1,0:T(8,128)}, f32[32,128]{1,0:T(8,128)S(1)}, u32[]{:S(2)}) copy-start(f32[32,128]{1,0:T(8,128)S(1)} %fusion.20.dots0) | copy-start | bytes 49156
  79.0 5.0 %collective-permute-start.14 = (f32[32,128]{1,0:T(8,128)S(1)}, f32[32,128]{1,0:T(8,128)S(1)}, u32[]{:S(2)}, u32[]{:S(2)}) collective-permute-start(f32[32,128]{1,0:T(8,128)S(1)} %fusion.20.dots0), channel_id=1, source_target_pairs={{0,1},{1,0},{2,3},{3,2},{4,5},{5,4},{6,7},{7,6},{8,9},{9,8},{10,11... | collective-permute-start | bytes 49160 | tf_op jit(solution)/shard_map/ppermute | solution.py:521
  80.6 4.7 %collective-permute-start.15 = (f32[32,128]{1,0:T(8,128)S(1)}, f32[32,128]{1,0:T(8,128)S(1)}, u32[]{:S(2)}, u32[]{:S(2)}) collective-permute-start(f32[32,128]{1,0:T(8,128)S(1)} %fusion.20.dots0), channel_id=1, source_target_pairs={{0,2},{1,3},{2,0},{3,1},{4,6},{5,7},{6,4},{7,5},{8,10},{9,11},{10,... | collective-permute-start | bytes 49160 | tf_op jit(solution)/shard_map/ppermute | solution.py:521
  83.2 5.5 %collective-permute-start.16 = (f32[32,128]{1,0:T(8,128)S(1)}, f32[32,128]{1,0:T(8,128)S(1)}, u32[]{:S(2)}, u32[]{:S(2)}) collective-permute-start(f32[32,128]{1,0:T(8,128)S(1)} %fusion.20.dots0), channel_id=1, source_target_pairs={{0,3},{1,2},{2,1},{3,0},{4,7},{5,6},{6,5},{7,4},{8,11},{9,10},{10,... | collective-permute-start | bytes 49160 | tf_op jit(solution)/shard_map/ppermute | solution.py:521
  84.1 4.7 %copy-start.11 = (f32[32,128]{1,0:T(8,128)}, f32[32,128]{1,0:T(8,128)S(1)}, u32[]{:S(2)}) copy-start(f32[32,128]{1,0:T(8,128)S(1)} %collective-permute-done.14.dots1) | copy-start | bytes 49156
  92.7 3.9 %collective-permute-start.17 = (f32[16,256]{1,0:T(8,128)}, f32[16,256]{1,0:T(8,128)S(1)}, u32[]{:S(2)}, u32[]{:S(2)}) collective-permute-start(f32[16,256]{1,0:T(8,128)} %get-tuple-element.50), channel_id=1, source_target_pairs={{0,16},{16,0},{1,17},{17,1},{2,18},{18,2},{3,19},{19,3},{4,20},{20... | collective-permute-start | bytes 49160 | tf_op jit(solution)/shard_map/ppermute | solution.py:659
  97.4 1.9 %collective-permute-start.18 = (f32[16,256]{1,0:T(8,128)S(1)}, f32[16,256]{1,0:T(8,128)S(1)}, u32[]{:S(2)}, u32[]{:S(2)}) collective-permute-start(f32[16,256]{1,0:T(8,128)S(1)} %add.92), channel_id=1, source_target_pairs={{0,4},{4,0},{8,12},{12,8},{1,5},{5,1},{9,13},{13,9},{2,6},{6,2},{1... | collective-permute-start | bytes 49160 | tf_op jit(solution)/shard_map/ppermute | solution.py:521
  97.4 3.7 %collective-permute-start.19 = (f32[16,256]{1,0:T(8,128)S(1)}, f32[16,256]{1,0:T(8,128)S(1)}, u32[]{:S(2)}, u32[]{:S(2)}) collective-permute-start(f32[16,256]{1,0:T(8,128)S(1)} %add.92), channel_id=1, source_target_pairs={{0,8},{4,12},{8,0},{12,4},{1,9},{5,13},{9,1},{13,5},{2,10},{6,14},... | collective-permute-start | bytes 49160 | tf_op jit(solution)/shard_map/ppermute | solution.py:521
  98.2 3.2 %collective-permute-start.20 = (f32[16,256]{1,0:T(8,128)S(1)}, f32[16,256]{1,0:T(8,128)S(1)}, u32[]{:S(2)}, u32[]{:S(2)}) collective-permute-start(f32[16,256]{1,0:T(8,128)S(1)} %add.92), channel_id=1, source_target_pairs={{0,12},{4,8},{8,4},{12,0},{1,13},{5,9},{9,5},{13,1},{2,14},{6,10},... | collective-permute-start | bytes 49160 | tf_op jit(solution)/shard_map/ppermute | solution.py:521
  (8 other events, 14.8 us)

commit v3 on v2

--- a/solution.py
+++ b/solution.py
@@ -110,7 +110,7 @@
     return (embeddings, losses[None], adapter_up_gradient)
 
 
-BLOCK_BITS, GROUP_BITS, LANE_BITS, ROW_BITS = 10, 8, 7, 4
+BLOCK_BITS, GROUP_BITS, LANE_BITS, ROW_BITS = 10, 9, 7, 4
 IDS_PER_BLOCK = 1 << BLOCK_BITS
 IDS_PER_GROUP = 1 << GROUP_BITS
 CHUNK = 384
@@ -262,13 +262,16 @@
                 token = jnp.broadcast_to(token, (FEATURE_ROWS, LANES))
                 lane = (token & (LANES - 1)).astype(jnp.int16)
                 tile = lax.shift_right_arithmetic(token, LANE_BITS).astype(jnp.int16)
-                for f in range(features // FEATURE_ROWS):
-                    rows = pl.ds(f * FEATURE_ROWS, FEATURE_ROWS)
-                    total = turned[rows, at]
+                pieces = [pl.ds(f, FEATURE_ROWS) for f in range(0, features, FEATURE_ROWS)]
+                fresh = []
+                for rows in pieces:
+                    total = jnp.zeros((FEATURE_ROWS, LANES), jnp.bfloat16)
                     for j in range(IDS_PER_GROUP // LANES):
                         columns = pl.ds(part * IDS_PER_GROUP + j * LANES, LANES)
-                        found = take_lanes(held[b, rows, columns], lane)
-                        total = jnp.where(tile == j, found, total)
+                        total = jnp.where(tile == j, take_lanes(held[b, rows, columns], lane), total)
+                    fresh.append(total)
+                fresh = [turned[rows, at] + total for rows, total in zip(pieces, fresh)]
+                for rows, total in zip(pieces, fresh):
                     turned[rows, at] = total
                 return carry
 
@@ -577,7 +580,7 @@
             name="gather",
         )(ids, difficult_distractors, vocabulary_vectors, lowering_factor_matrix)
 
-        def product(i, j):
+        def product(turned, i, j):
             return mm(turned, columns(i, j), (((0,), (0,)), ((), ())))
 
         def narrow(x):
@@ -586,14 +589,17 @@
         chip = extra.astype(jnp.float32)
         chip += lax.ppermute(extra, "dp", other_core).astype(jnp.float32)
         extra = chip + lax.ppermute(narrow(chip), "dp", other_y).astype(jnp.float32)
-        core1 = lax.ppermute(narrow(product(1, 1)), "dp", other_core)
-        far = lax.ppermute(narrow(product(0, 1) + core1.astype(jnp.float32)), "dp", other_y)
-        core0 = lax.ppermute(narrow(product(1, 0)), "dp", other_core)
-        own0 = narrow(product(0, 0))
+        core1 = lax.ppermute(narrow(product(turned, 1, 1)), "dp", other_core)
+        chip1 = narrow(product(turned, 0, 1) + core1.astype(jnp.float32))
+        far = lax.ppermute(chip1, "dp", other_y)
+        turned, _ = lax.optimization_barrier((turned, chip1))
+        core0 = lax.ppermute(narrow(product(turned, 1, 0)), "dp", other_core)
+        own0 = narrow(product(turned, 0, 0))
         return own0, core0, far, extra, member
 
     first = project(0, FIRST)
-    many = jnp.sum((ids != 0).astype(jnp.int32)) > FIRST
+    later, _ = lax.optimization_barrier((ids, first[0]))
+    many = jnp.sum((later != 0).astype(jnp.int32)) > FIRST
     left = tokens - FIRST
     shapes = jax.eval_shape(lambda: project(FIRST, left))
     rest = lax.cond(

time: 102 us -> 94.5 us (0.926)
  waiting for transfers between devices: 28.6 us -> 25.5 us
  matrix products: 11.9 us -> 9.18 us
  Pallas kernels: 37.4 us -> 36 us
    ppermute x1, waiting for transfers between devices: 12.9 us -> 0.01 us  [project(): extra = chip + lax.ppermute(narrow(chip), 'dp', other_y).astype(jnp.float32)]
    ppermute x3, waiting for transfers between devices: 0.01 us -> 8.29 us  [the longest x1 8.28 us: project(): far = lax.ppermute(chip1, 'dp', other_y)]
    ppermute x1, starting transfers between devices: 0.09 us -> 2.96 us  [project(): extra = chip + lax.ppermute(narrow(chip), 'dp', other_y).astype(jnp.float32)]
    dot_general x4, matrix products: 11.9 us -> 9.18 us  [mm(): return lax.dot_general(a, b, dims, preferred_element_type=jnp.float32)]
    ppermute x3, starting transfers between devices: 3.14 us -> 0.69 us  [the longest x1 0.51 us: project(): core1 = lax.ppermute(narrow(product(turned, 1, 1)), 'dp', other_core)]
    ppermute x1, waiting for transfers between devices: 0.01 us -> 1.66 us  [project(): chip += lax.ppermute(extra, 'dp', other_core).astype(jnp.float32)]
    pallas_call x1, Pallas kernels: 28.6 us -> 27.2 us  [project(): pl.pallas_call(functools.partial(gather_kernel, base=base), out_shape=[ja...]
    unnamed x33 -> x31, local copies, waits for them, and re-layouts: 2.89 us -> 2.69 us
  transfers between devices with their start and end apart: 16 -> 16, of which waited for: 9 -> 9; matrix products, arithmetic and copies ran while one was open for 11% -> 10% of each run, Pallas kernels for 0% -> 0%
where the time goes in v3:
time: 94.5 us; the launch traced here: 94.2 us
  Pallas kernels  36 us (38%)
  waiting for transfers between devices  25.5 us (27%)
  starting transfers between devices  13.7 us (14%)
  matrix products  9.18 us (10%)
  local copies, waits for them, and re-layouts  4.13 us (4%)
  other arithmetic  3.48 us (4%)
  between operations  2.1 us (2%)
    pallas_call x1, Pallas kernels, project(): pl.pallas_call(functools.partial(gather_kernel, base=base), out_shape=[ja...  27.2 us
    ppermute x9, waiting for transfers between devices, exchange(): return [x] + [lax.ppermute(x, axis, step) for step in steps]  9.37 us
    dot_general x4, matrix products, mm(): return lax.dot_general(a, b, dims, preferred_element_type=jnp.float32)  9.18 us
    ppermute x9, starting transfers between devices, exchange(): return [x] + [lax.ppermute(x, axis, step) for step in steps]  8.39 us
    ppermute x1, waiting for transfers between devices, project(): far = lax.ppermute(chip1, 'dp', other_y)  8.28 us
    pallas_call x1, Pallas kernels, split_body(): pl.pallas_call(functools.partial(pool_kernel, model_width=float(features...  3.99 us
    pallas_call x1, Pallas kernels, split_body(): pl.pallas_call(functools.partial(score_kernel, negatives=negatives), out_...  3.37 us
    ppermute x1, waiting for transfers between devices, split_body(): update = update + lax.ppermute(update, 'group', [(0, 1), (1, 0)])  3.15 us
  transfers between devices with their start and end apart: 16, of which 9 were waited for; matrix products, arithmetic and copies ran while one was open for 10% of the time, Pallas kernels for 0%

profile of v3, /device:TPU:0, one launch (start us, length us, event | category | flops | bytes accessed | tf_op | source)
XLA Modules:
  0.0 94.2 jit_solution(2411934764207680183)
XLA Ops:
  1.3 27.2 %gather.3 = (bf16[1024,1152]{1,0:T(8,128)(2,1)}, bf16[1152,128]{1,0:T(8,128)(2,1)}, bf16[160,256]{1,0:T(8,128)(2,1)}) custom-call(s32[12,128]{1,0:T(8,128)S(1)} %bitcast.11, s32[3,7]{1,0:T(4,128)} %hard_ref.1, bf16[1024,16384]{1,0:T(8,128)(2,1)} %vocab_ref.1, bf16[16,4096]{1,0:T(8,128)(2,1)} %lower_ref.1), custom_call_target="tpu_custom_call" | custom-call | tf_op jit(solution)/shard_map/gather/pallas_call | solution.py:558
  28.5 2.5 %convolution_convert_fusion.5 = bf16[1152,256]{1,0:T(8,128)(2,1)S(1)} fusion(bf16[1024,1152]{1,0:T(8,128)(2,1)} %get-tuple-element.40, bf16[1024,1024]{1,0:T(8,128)(2,1)S(1)} %copy-done.15, s32[]{:T(128)S(6)} %select_n.133), kind=kOutput, calls=%fused_computation.18 | convolution fusion | flops 604274688 | bytes 3473412 | tf_op jit(solution)/shard_map/dot_general | solution.py:127
  31.7 1.7 %collective-permute-done.8 = bf16[160,256]{1,0:T(8,128)(2,1)S(1)} collective-permute-done((bf16[160,256]{1,0:T(8,128)(2,1)S(1)}, bf16[160,256]{1,0:T(8,128)(2,1)S(1)}, u32[]{:S(2)}, u32[]{:S(2)}) %collective-permute-start.8) | collective-permute-done | bytes 81952 | tf_op jit(solution)/shard_map/ppermute | solution.py:590
  33.4 3.0 %collective-permute-start.9 = (bf16[160,256]{1,0:T(8,128)(2,1)S(1)}, bf16[160,256]{1,0:T(8,128)(2,1)S(1)}, u32[]{:S(2)}, u32[]{:S(2)}) collective-permute-start(bf16[160,256]{1,0:T(8,128)(2,1)S(1)} %fusion.19), channel_id=1, source_target_pairs={{0,8},{4,12},{8,0},{12,4},{1,9},{5,13},{9,1},{13,5},{2,10},{6,14},... | collective-permute-start | bytes 245768 | tf_op jit(solution)/shard_map/ppermute | solution.py:591
  36.3 3.3 %add_convert_fusion.1 = bf16[1152,256]{1,0:T(8,128)(2,1)} fusion(bf16[1152,256]{1,0:T(8,128)(2,1)S(1)} %collective-permute-done.5, bf16[1024,1152]{1,0:T(8,128)(2,1)} %get-tuple-element.40, bf16[1024,1024]{1,0:T(8,128)(2,1)S(1)} %copy-done.15, s32[]{:T(128)S(6)} %select_n.132), kind=kOutput, calls=%fused_computation.19 | convolution fusion | flops 604864512 | bytes 4063236 | tf_op jit(solution)/shard_map/dot_general | solution.py:127
  39.8 1.6 %convolution_convert_fusion.3 = bf16[1152,256]{1,0:T(8,128)(2,1)} fusion(bf16[1024,1152]{1,0:T(8,128)(2,1)S(1)} %copy-done.14, bf16[1024,1024]{1,0:T(8,128)(2,1)S(1)} %copy-done.15, s32[]{:T(128)S(6)} %select_n.135), kind=kOutput, calls=%fused_computation.16 | convolution fusion | flops 604274688 | bytes 3473412 | tf_op jit(solution)/shard_map/dot_general | solution.py:127
  42.2 1.7 %convolution_convert_fusion.4.own_ref = bf16[1152,256]{1,0:T(8,128)(2,1)} fusion(bf16[1024,1152]{1,0:T(8,128)(2,1)S(1)} %copy-done.14, bf16[1024,1024]{1,0:T(8,128)(2,1)S(1)} %copy-done.15, s32[]{:T(128)S(6)} %select_n.134), kind=kOutput, calls=%fused_computation.17 | convolution fusion | flops 604274688 | bytes 3473412 | tf_op jit(solution)/shard_map/dot_general | solution.py:127
  45.2 1.5 %conditional.1 = (bf16[384,256]{1,0:T(8,128)(2,1)S(1)}, bf16[384,256]{1,0:T(8,128)(2,1)}, bf16[384,256]{1,0:T(8,128)(2,1)}, f32[112,256]{1,0:T(8,128)S(1)}, bf16[384,128]{1,0:T(8,128)(2,1)S(1)}) conditional(s32[]{:T(128)} %convert_element_type.70, () %tuple.21, (s32[12,128]{1,0:T(8,128)S(1)}, s32[3,7]{1,0:T(4,128)S(1)}, ...), branch_computations={%region_1.0_spmd, %region_2.0_spmd} | conditional | flops 806154240 | bytes 29655804 | solution.py:605
  46.7 8.3 %collective-permute-done.7.far_ref = bf16[1152,256]{1,0:T(8,128)(2,1)S(1)} collective-permute-done((bf16[1152,256]{1,0:T(8,128)(2,1)}, bf16[1152,256]{1,0:T(8,128)(2,1)S(1)}, u32[]{:S(2)}, u32[]{:S(2)}) %collective-permute-start.7) | collective-permute-done | bytes 589856 | tf_op jit(solution)/shard_map/ppermute | solution.py:594
  55.0 0.8 copy-done
  55.8 4.0 %pool.1 = (bf16[16,256]{1,0:T(8,128)(2,1)}, f32[1536,256]{1,0:T(8,128)}, bf16[16,1536]{1,0:T(8,128)(2,1)}, f32[16,256]{1,0:T(8,128)}) custom-call(s32[12,128]{1,0:T(8,128)S(1)} %bitcast.14, bf16[1152,256]{1,0:T(8,128)(2,1)} %convolution_convert_fusion.4.own_ref, bf16[1152,256]{1,0:T(8,128)(2,1)} %copy-done.1, bf16[1152,256]{1,0:T(8,128)(2,1)} %copy-done, ...), custom_call_target="tpu_custom_call" | custom-call | tf_op jit(solution)/shard_map/pool/pallas_call | solution.py:610
  60.6 3.1 %collective-permute-done.10.far_ref = bf16[16,256]{1,0:T(8,128)(2,1)S(1)} collective-permute-done((bf16[16,256]{1,0:T(8,128)(2,1)}, bf16[16,256]{1,0:T(8,128)(2,1)S(1)}, u32[]{:S(2)}, u32[]{:S(2)}) %collective-permute-start.10) | collective-permute-done | bytes 8224 | tf_op jit(solution)/shard_map/ppermute | solution.py:628
  64.2 1.5 %dots.1.packed0 = f32[64,128]{1,0:T(8,128)} custom-call(bf16[16,256]{1,0:T(8,128)(2,1)} %get-tuple-element.49.near_ref, bf16[16,256]{1,0:T(8,128)(2,1)} %copy-done.9), custom_call_target="tpu_custom_call" | custom-call | tf_op jit(solution)/shard_map/dots/pallas_call | solution.py:630
  66.1 1.4 %collective-permute-start.13 = (f32[64,128]{1,0:T(8,128)}, f32[64,128]{1,0:T(8,128)S(1)}, u32[]{:S(2)}, u32[]{:S(2)}) collective-permute-start(f32[64,128]{1,0:T(8,128)} %dots.1.packed0), channel_id=1, source_target_pairs={{0,12},{4,8},{8,4},{12,0},{1,13},{5,9},{9,5},{13,1},{2,14},{6,10},... | collective-permute-start | bytes 98312 | tf_op jit(solution)/shard_map/ppermute | solution.py:524
  67.5 2.5 %collective-permute-done.12.packed2 = f32[64,128]{1,0:T(8,128)S(1)} collective-permute-done((f32[64,128]{1,0:T(8,128)}, f32[64,128]{1,0:T(8,128)S(1)}, u32[]{:S(2)}, u32[]{:S(2)}) %collective-permute-start.12) | collective-permute-done | bytes 32800 | tf_op jit(solution)/shard_map/ppermute | solution.py:524
  70.8 1.8 %collective-permute-start.14 = (f32[32,128]{1,0:T(8,128)S(1)}, f32[32,128]{1,0:T(8,128)S(1)}, u32[]{:S(2)}, u32[]{:S(2)}) collective-permute-start(f32[32,128]{1,0:T(8,128)S(1)} %fusion.20.dots0), channel_id=1, source_target_pairs={{0,1},{1,0},{2,3},{3,2},{4,5},{5,4},{6,7},{7,6},{8,9},{9,8},{10,11... | collective-permute-start | bytes 49160 | tf_op jit(solution)/shard_map/ppermute | solution.py:524
  72.6 2.6 %collective-permute-start.15 = (f32[32,128]{1,0:T(8,128)S(1)}, f32[32,128]{1,0:T(8,128)S(1)}, u32[]{:S(2)}, u32[]{:S(2)}) collective-permute-start(f32[32,128]{1,0:T(8,128)S(1)} %fusion.20.dots0), channel_id=1, source_target_pairs={{0,2},{1,3},{2,0},{3,1},{4,6},{5,7},{6,4},{7,5},{8,10},{9,11},{10,... | collective-permute-start | bytes 49160 | tf_op jit(solution)/shard_map/ppermute | solution.py:524
  75.9 1.4 %collective-permute-done.15.dots2 = f32[32,128]{1,0:T(8,128)S(1)} collective-permute-done((f32[32,128]{1,0:T(8,128)S(1)}, f32[32,128]{1,0:T(8,128)S(1)}, u32[]{:S(2)}, u32[]{:S(2)}) %collective-permute-start.15) | collective-permute-done | bytes 16416 | tf_op jit(solution)/shard_map/ppermute | solution.py:524
  77.2 3.5 %collective-permute-done.16.dots3 = f32[32,128]{1,0:T(8,128)S(1)} collective-permute-done((f32[32,128]{1,0:T(8,128)S(1)}, f32[32,128]{1,0:T(8,128)S(1)}, u32[]{:S(2)}, u32[]{:S(2)}) %collective-permute-start.16) | collective-permute-done | bytes 16416 | tf_op jit(solution)/shard_map/ppermute | solution.py:524
  81.3 3.4 %score.1 = (bf16[1,3,1024]{2,1,0:T(4,128)(2,1)}, f32[1,3]{1,0:T(1,128)}, f32[16,256]{1,0:T(8,128)}) custom-call(s32[12,128]{1,0:T(8,128)S(1)} %bitcast.15, bf16[16,256]{1,0:T(8,128)(2,1)} %get-tuple-element.49.near_ref, bf16[16,256]{1,0:T(8,128)(2,1)} %copy-done.9, f32[64,128]{1,0:T(8,128)} %dots.1.packed0, f32[64,128]{1,0:T(8,128)} %copy-done.5, ...), custom_call_target="tpu_custom_call" | custom-call | tf_op jit(solution)/shard_map/score/pallas_call | solution.py:641
  85.4 3.1 %collective-permute-done.17 = f32[16,256]{1,0:T(8,128)S(1)} collective-permute-done((f32[16,256]{1,0:T(8,128)}, f32[16,256]{1,0:T(8,128)S(1)}, u32[]{:S(2)}, u32[]{:S(2)}) %collective-permute-start.17) | collective-permute-done | bytes 16416 | tf_op jit(solution)/shard_map/ppermute | solution.py:665
  89.3 1.0 %collective-permute-start.19 = (f32[16,256]{1,0:T(8,128)S(1)}, f32[16,256]{1,0:T(8,128)S(1)}, u32[]{:S(2)}, u32[]{:S(2)}) collective-permute-start(f32[16,256]{1,0:T(8,128)S(1)} %add.92), channel_id=1, source_target_pairs={{0,8},{4,12},{8,0},{12,4},{1,9},{5,13},{9,1},{13,5},{2,10},{6,14},... | collective-permute-start | bytes 49160 | tf_op jit(solution)/shard_map/ppermute | solution.py:524
  90.3 1.1 %collective-permute-start.18 = (f32[16,256]{1,0:T(8,128)S(1)}, f32[16,256]{1,0:T(8,128)S(1)}, u32[]{:S(2)}, u32[]{:S(2)}) collective-permute-start(f32[16,256]{1,0:T(8,128)S(1)} %add.92), channel_id=1, source_target_pairs={{0,4},{4,0},{8,12},{12,8},{1,5},{5,1},{9,13},{13,9},{2,6},{6,2},{1... | collective-permute-start | bytes 49160 | tf_op jit(solution)/shard_map/ppermute | solution.py:524
  91.5 1.6 %collective-permute-done.19 = f32[16,256]{1,0:T(8,128)S(1)} collective-permute-done((f32[16,256]{1,0:T(8,128)S(1)}, f32[16,256]{1,0:T(8,128)S(1)}, u32[]{:S(2)}, u32[]{:S(2)}) %collective-permute-start.19) | collective-permute-done | bytes 16416 | tf_op jit(solution)/shard_map/ppermute | solution.py:524
  (60 shorter events, 10.1 us)
Async XLA Ops:
  1.3 27.2 %copy-start.15 = (bf16[1024,1024]{1,0:T(8,128)(2,1)S(1)}, bf16[1024,1024]{1,0:T(8,128)(2,1)}, u32[]{:S(2)}) copy-start(bf16[1024,1024]{1,0:T(8,128)(2,1)} %param.12) | copy-start | bytes 6291460
  31.1 5.3 %collective-permute-start.5 = (bf16[1152,256]{1,0:T(8,128)(2,1)S(1)}, bf16[1152,256]{1,0:T(8,128)(2,1)S(1)}, u32[]{:S(2)}, u32[]{:S(2)}) collective-permute-start(bf16[1152,256]{1,0:T(8,128)(2,1)S(1)} %convolution_convert_fusion.5), channel_id=1, source_target_pairs={{0,4},{4,0},{8,12},{12,8},{1,5},{5,1},{9,13},{13,9},{2,6},{6,2},{1... | collective-permute-start | bytes 1769480 | tf_op jit(solution)/shard_map/ppermute | solution.py:592
  31.6 1.7 %collective-permute-start.8 = (bf16[160,256]{1,0:T(8,128)(2,1)S(1)}, bf16[160,256]{1,0:T(8,128)(2,1)S(1)}, u32[]{:S(2)}, u32[]{:S(2)}) collective-permute-start(bf16[160,256]{1,0:T(8,128)(2,1)S(1)} %copy-done.3), channel_id=1, source_target_pairs={{0,4},{4,0},{8,12},{12,8},{1,5},{5,1},{9,13},{13,9},{2,6},{6,2},{1... | collective-permute-start | bytes 245768 | tf_op jit(solution)/shard_map/ppermute | solution.py:590
  33.4 6.5 %copy-start.14 = (bf16[1024,1152]{1,0:T(8,128)(2,1)S(1)}, bf16[1024,1152]{1,0:T(8,128)(2,1)}, u32[]{:S(2)}) copy-start(bf16[1024,1152]{1,0:T(8,128)(2,1)} %get-tuple-element.40) | copy-start | bytes 7077892
  33.4 8.1 %collective-permute-start.9 = (bf16[160,256]{1,0:T(8,128)(2,1)S(1)}, bf16[160,256]{1,0:T(8,128)(2,1)S(1)}, u32[]{:S(2)}, u32[]{:S(2)}) collective-permute-start(bf16[160,256]{1,0:T(8,128)(2,1)S(1)} %fusion.19), channel_id=1, source_target_pairs={{0,8},{4,12},{8,0},{12,4},{1,9},{5,13},{9,1},{13,5},{2,10},{6,14},... | collective-permute-start | bytes 245768 | tf_op jit(solution)/shard_map/ppermute | solution.py:591
  39.7 15.3 %collective-permute-start.7 = (bf16[1152,256]{1,0:T(8,128)(2,1)}, bf16[1152,256]{1,0:T(8,128)(2,1)S(1)}, u32[]{:S(2)}, u32[]{:S(2)}) collective-permute-start(bf16[1152,256]{1,0:T(8,128)(2,1)} %add_convert_fusion.1), channel_id=1, source_target_pairs={{0,8},{4,12},{8,0},{12,4},{1,9},{5,13},{9,1},{13,5},{2,10},{6,14},... | collective-permute-start | bytes 1769480 | tf_op jit(solution)/shard_map/ppermute | solution.py:594
  41.5 5.2 %collective-permute-start.6 = (bf16[1152,256]{1,0:T(8,128)(2,1)}, bf16[1152,256]{1,0:T(8,128)(2,1)S(1)}, u32[]{:S(2)}, u32[]{:S(2)}) collective-permute-start(bf16[1152,256]{1,0:T(8,128)(2,1)} %convolution_convert_fusion.3), channel_id=1, source_target_pairs={{0,4},{4,0},{8,12},{12,8},{1,5},{5,1},{9,13},{13,9},{2,6},{6,2},{1... | collective-permute-start | bytes 1769480 | tf_op jit(solution)/shard_map/ppermute | solution.py:596
  46.7 8.3 %copy-start.1 = (bf16[1152,256]{1,0:T(8,128)(2,1)}, bf16[1152,256]{1,0:T(8,128)(2,1)S(1)}, u32[]{:S(2)}) copy-start(bf16[1152,256]{1,0:T(8,128)(2,1)S(1)} %collective-permute-done.6.core_ref) | copy-start | bytes 1769476
  59.8 3.9 %collective-permute-start.10 = (bf16[16,256]{1,0:T(8,128)(2,1)}, bf16[16,256]{1,0:T(8,128)(2,1)S(1)}, u32[]{:S(2)}, u32[]{:S(2)}) collective-permute-start(bf16[16,256]{1,0:T(8,128)(2,1)} %get-tuple-element.49.near_ref), channel_id=1, source_target_pairs={{0,16},{16,0},{1,17},{17,1},{2,18},{18,2},{3,19},{19,3},{4,20},{20... | collective-permute-start | bytes 24584 | tf_op jit(solution)/shard_map/ppermute | solution.py:628
  65.7 1.9 %collective-permute-start.11 = (f32[64,128]{1,0:T(8,128)}, f32[64,128]{1,0:T(8,128)S(1)}, u32[]{:S(2)}, u32[]{:S(2)}) collective-permute-start(f32[64,128]{1,0:T(8,128)} %dots.1.packed0), channel_id=1, source_target_pairs={{0,4},{4,0},{8,12},{12,8},{1,5},{5,1},{9,13},{13,9},{2,6},{6,2},{1... | collective-permute-start | bytes 98312 | tf_op jit(solution)/shard_map/ppermute | solution.py:524
  65.7 4.4 %collective-permute-start.12 = (f32[64,128]{1,0:T(8,128)}, f32[64,128]{1,0:T(8,128)S(1)}, u32[]{:S(2)}, u32[]{:S(2)}) collective-permute-start(f32[64,128]{1,0:T(8,128)} %dots.1.packed0), channel_id=1, source_target_pairs={{0,8},{4,12},{8,0},{12,4},{1,9},{5,13},{9,1},{13,5},{2,10},{6,14},... | collective-permute-start | bytes 98312 | tf_op jit(solution)/shard_map/ppermute | solution.py:524
  66.1 3.9 %collective-permute-start.13 = (f32[64,128]{1,0:T(8,128)}, f32[64,128]{1,0:T(8,128)S(1)}, u32[]{:S(2)}, u32[]{:S(2)}) collective-permute-start(f32[64,128]{1,0:T(8,128)} %dots.1.packed0), channel_id=1, source_target_pairs={{0,12},{4,8},{8,4},{12,0},{1,13},{5,9},{9,5},{13,1},{2,14},{6,10},... | collective-permute-start | bytes 98312 | tf_op jit(solution)/shard_map/ppermute | solution.py:524
  67.5 13.2 %copy-start.5 = (f32[64,128]{1,0:T(8,128)}, f32[64,128]{1,0:T(8,128)S(1)}, u32[]{:S(2)}) copy-start(f32[64,128]{1,0:T(8,128)S(1)} %collective-permute-done.11.packed1) | copy-start | bytes 98308
  70.0 10.7 %copy-start.6 = (f32[64,128]{1,0:T(8,128)}, f32[64,128]{1,0:T(8,128)S(1)}, u32[]{:S(2)}) copy-start(f32[64,128]{1,0:T(8,128)S(1)} %collective-permute-done.12.packed2) | copy-start | bytes 98308
  70.0 10.7 %copy-start.7 = (f32[64,128]{1,0:T(8,128)}, f32[64,128]{1,0:T(8,128)S(1)}, u32[]{:S(2)}) copy-start(f32[64,128]{1,0:T(8,128)S(1)} %collective-permute-done.13.packed3) | copy-start | bytes 98308
  70.8 9.9 %copy-start.8 = (f32[32,128]{1,0:T(8,128)}, f32[32,128]{1,0:T(8,128)S(1)}, u32[]{:S(2)}) copy-start(f32[32,128]{1,0:T(8,128)S(1)} %fusion.20.dots0) | copy-start | bytes 49156
  70.8 5.0 %collective-permute-start.14 = (f32[32,128]{1,0:T(8,128)S(1)}, f32[32,128]{1,0:T(8,128)S(1)}, u32[]{:S(2)}, u32[]{:S(2)}) collective-permute-start(f32[32,128]{1,0:T(8,128)S(1)} %fusion.20.dots0), channel_id=1, source_target_pairs={{0,1},{1,0},{2,3},{3,2},{4,5},{5,4},{6,7},{7,6},{8,9},{9,8},{10,11... | collective-permute-start | bytes 49160 | tf_op jit(solution)/shard_map/ppermute | solution.py:524
  72.6 4.7 %collective-permute-start.15 = (f32[32,128]{1,0:T(8,128)S(1)}, f32[32,128]{1,0:T(8,128)S(1)}, u32[]{:S(2)}, u32[]{:S(2)}) collective-permute-start(f32[32,128]{1,0:T(8,128)S(1)} %fusion.20.dots0), channel_id=1, source_target_pairs={{0,2},{1,3},{2,0},{3,1},{4,6},{5,7},{6,4},{7,5},{8,10},{9,11},{10,... | collective-permute-start | bytes 49160 | tf_op jit(solution)/shard_map/ppermute | solution.py:524
  75.1 5.5 %collective-permute-start.16 = (f32[32,128]{1,0:T(8,128)S(1)}, f32[32,128]{1,0:T(8,128)S(1)}, u32[]{:S(2)}, u32[]{:S(2)}) collective-permute-start(f32[32,128]{1,0:T(8,128)S(1)} %fusion.20.dots0), channel_id=1, source_target_pairs={{0,3},{1,2},{2,1},{3,0},{4,7},{5,6},{6,5},{7,4},{8,11},{9,10},{10,... | collective-permute-start | bytes 49160 | tf_op jit(solution)/shard_map/ppermute | solution.py:524
  75.8 4.9 %copy-start.10 = (f32[32,128]{1,0:T(8,128)}, f32[32,128]{1,0:T(8,128)S(1)}, u32[]{:S(2)}) copy-start(f32[32,128]{1,0:T(8,128)S(1)} %collective-permute-done.14.dots1) | copy-start | bytes 49156
  84.6 3.9 %collective-permute-start.17 = (f32[16,256]{1,0:T(8,128)}, f32[16,256]{1,0:T(8,128)S(1)}, u32[]{:S(2)}, u32[]{:S(2)}) collective-permute-start(f32[16,256]{1,0:T(8,128)} %get-tuple-element.55), channel_id=1, source_target_pairs={{0,16},{16,0},{1,17},{17,1},{2,18},{18,2},{3,19},{19,3},{4,20},{20... | collective-permute-start | bytes 49160 | tf_op jit(solution)/shard_map/ppermute | solution.py:665
  89.3 3.7 %collective-permute-start.19 = (f32[16,256]{1,0:T(8,128)S(1)}, f32[16,256]{1,0:T(8,128)S(1)}, u32[]{:S(2)}, u32[]{:S(2)}) collective-permute-start(f32[16,256]{1,0:T(8,128)S(1)} %add.92), channel_id=1, source_target_pairs={{0,8},{4,12},{8,0},{12,4},{1,9},{5,13},{9,1},{13,5},{2,10},{6,14},... | collective-permute-start | bytes 49160 | tf_op jit(solution)/shard_map/ppermute | solution.py:524
  90.3 3.2 %collective-permute-start.20 = (f32[16,256]{1,0:T(8,128)S(1)}, f32[16,256]{1,0:T(8,128)S(1)}, u32[]{:S(2)}, u32[]{:S(2)}) collective-permute-start(f32[16,256]{1,0:T(8,128)S(1)} %add.92), channel_id=1, source_target_pairs={{0,12},{4,8},{8,4},{12,0},{1,13},{5,9},{9,5},{13,1},{2,14},{6,10},... | collective-permute-start | bytes 49160 | tf_op jit(solution)/shard_map/ppermute | solution.py:524
  90.3 3.2 %collective-permute-start.18 = (f32[16,256]{1,0:T(8,128)S(1)}, f32[16,256]{1,0:T(8,128)S(1)}, u32[]{:S(2)}, u32[]{:S(2)}) collective-permute-start(f32[16,256]{1,0:T(8,128)S(1)} %add.92), channel_id=1, source_target_pairs={{0,4},{4,0},{8,12},{12,8},{1,5},{5,1},{9,13},{13,9},{2,6},{6,2},{1... | collective-permute-start | bytes 49160 | tf_op jit(solution)/shard_map/ppermute | solution.py:524
  (7 other events, 14.5 us)

commit v4 on v3

--- a/solution.py
+++ b/solution.py
@@ -160,21 +160,15 @@
 
 def gather_kernel(
     ids_ref,
-    hard_ref,
     vocab_ref,
-    lower_ref,
     turned,
     member_ref,
-    extra_ref,
     held,
-    lower,
     token_ref,
-    small,
     ranks,
     counted,
     bounds,
     held_sems,
-    lower_sem,
     bounds_sem,
     base,
 ):
@@ -183,19 +177,12 @@
     blocks = vocab // IDS_PER_BLOCK
     groups = vocab // IDS_PER_GROUP
     span = member_ref.shape[0]
-    stripes = pl.cdiv(span, STRIPE)
-    per_shard, negatives = hard_ref.shape
-    shard = lax.axis_index("dp")
 
     def vocab_copy(b):
         columns = pl.ds(pl.multiple_of(b * IDS_PER_BLOCK, LANES), IDS_PER_BLOCK)
         return pltpu.make_async_copy(vocab_ref.at[:, columns], held.at[b], held_sems.at[b])
 
-    lower_copy = pltpu.make_async_copy(
-        lower_ref.at[:, pl.ds(pl.multiple_of(shard * features, LANES), features)], lower, lower_sem
-    )
     vocab_copy(0).start()
-    lower_copy.start()
     for b in range(1, blocks):
         vocab_copy(b).start()
 
@@ -240,9 +227,6 @@
         return carry
 
     lax.fori_loop(0, span // LANES, place, 0)
-    small[...] = jnp.zeros_like(small)
-    small[0:per_shard, stripes : stripes + negatives] = hard_ref[...].astype(jnp.float32)
-    lower_copy.wait()
     bounds_copy.wait()
 
     def within(place):
@@ -280,6 +264,16 @@
 
     lax.fori_loop(0, blocks, take, 0)
 
+
+def statistics_kernel(turned, member_ref, hard_ref, lower_ref, extra_ref, small):
+    features, span = turned.shape
+    stripes = pl.cdiv(span, STRIPE)
+    per_shard, negatives = hard_ref.shape
+    shard = lax.axis_index("dp")
+    small[...] = jnp.zeros_like(small)
+    small[0:per_shard, stripes : stripes + negatives] = hard_ref[...].astype(jnp.float32)
+    lower = lower_ref[:, pl.ds(pl.multiple_of(shard * features, LANES), features)]
+
     misc = jnp.zeros((ROWS, STRIPE), jnp.float32)
     residual = jnp.zeros((features, LANES), jnp.float32)
     for stripe in range(stripes):
@@ -288,7 +282,7 @@
         upright = turned[:, across]
         wide = upright.astype(jnp.float32)
         square = jnp.sum(wide * wide, axis=0, keepdims=True)
-        reduced = mm(lower[...], upright)
+        reduced = mm(lower, upright)
         if size < STRIPE:
             none = jnp.zeros((ROWS, STRIPE - size), jnp.float32)
             reduced = jnp.concatenate([reduced, none], axis=1)
@@ -541,7 +535,6 @@
     blocks = vocab // IDS_PER_BLOCK
     group_rows = 8 * pl.cdiv(vocab // IDS_PER_GROUP + 1, 8)
     per_shard, negatives = difficult_distractors.shape
-    rank = lowering_factor_matrix.shape[0]
     part_width = layer_weight_matrix.shape[1]
     width = part_width // shards
     params = pltpu.CompilerParams(vmem_limit_bytes=VMEM_BYTES)
@@ -555,30 +548,26 @@
     def project(base, span):
         stripes = pl.cdiv(span, STRIPE)
         extra_rows = (stripes + 1 + shards) * ROWS
-        turned, member, extra = pl.pallas_call(
+        turned, member = pl.pallas_call(
             functools.partial(gather_kernel, base=base),
             out_shape=[
                 jax.ShapeDtypeStruct((features, span), jnp.bfloat16),
                 jax.ShapeDtypeStruct((span, LANES), jnp.bfloat16),
-                jax.ShapeDtypeStruct((extra_rows, STRIPE), jnp.bfloat16),
             ],
-            in_specs=[vmem_spec()] * 2 + [any_spec()] * 2,
-            out_specs=[vmem_spec()] * 3,
+            in_specs=[vmem_spec(), any_spec()],
+            out_specs=[vmem_spec()] * 2,
             scratch_shapes=[
                 pltpu.VMEM((blocks, features, IDS_PER_BLOCK), jnp.bfloat16),
-                pltpu.VMEM((rank, features), jnp.bfloat16),
                 pltpu.VMEM((8 * pl.cdiv(span // LANES, 8), LANES), jnp.int32),
-                pltpu.VMEM((LANES, LANES), jnp.float32),
                 pltpu.VMEM((texts, length), jnp.float32),
                 pltpu.VMEM((group_rows, length), jnp.int32),
                 pltpu.SMEM((group_rows, length), jnp.int32),
                 pltpu.SemaphoreType.DMA((blocks,)),
                 pltpu.SemaphoreType.DMA,
-                pltpu.SemaphoreType.DMA,
             ],
             compiler_params=params,
             name="gather",
-        )(ids, difficult_distractors, vocabulary_vectors, lowering_factor_matrix)
+        )(ids, vocabulary_vectors)
 
         def product(turned, i, j):
             return mm(turned, columns(i, j), (((0,), (0,)), ((), ())))
@@ -586,25 +575,39 @@
         def narrow(x):
             return x.astype(jnp.bfloat16)
 
-        chip = extra.astype(jnp.float32)
-        chip += lax.ppermute(extra, "dp", other_core).astype(jnp.float32)
-        extra = chip + lax.ppermute(narrow(chip), "dp", other_y).astype(jnp.float32)
         core1 = lax.ppermute(narrow(product(turned, 1, 1)), "dp", other_core)
         chip1 = narrow(product(turned, 0, 1) + core1.astype(jnp.float32))
         far = lax.ppermute(chip1, "dp", other_y)
         turned, _ = lax.optimization_barrier((turned, chip1))
+        extra = pl.pallas_call(
+            statistics_kernel,
+            out_shape=jax.ShapeDtypeStruct((extra_rows, STRIPE), jnp.bfloat16),
+            in_specs=[vmem_spec()] * 4,
+            out_specs=vmem_spec(),
+            scratch_shapes=[pltpu.VMEM((LANES, LANES), jnp.float32)],
+            compiler_params=params,
+            cost_estimate=pl.CostEstimate(
+                flops=2 * features * span * (ROWS + LANES),
+                bytes_accessed=2 * features * span,
+                transcendentals=0,
+            ),
+            name="statistics",
+        )(turned, member, difficult_distractors, lowering_factor_matrix)
+        chip = extra.astype(jnp.float32)
+        chip += lax.ppermute(extra, "dp", other_core).astype(jnp.float32)
+        extra = chip + lax.ppermute(narrow(chip), "dp", other_y).astype(jnp.float32)
         core0 = lax.ppermute(narrow(product(turned, 1, 0)), "dp", other_core)
         own0 = narrow(product(turned, 0, 0))
-        return own0, core0, far, extra, member
-
-    first = project(0, FIRST)
-    later, _ = lax.optimization_barrier((ids, first[0]))
+        return (own0, core0, far, extra, member), chip
+
+    first, early = project(0, FIRST)
+    later, _ = lax.optimization_barrier((ids, early))
     many = jnp.sum((later != 0).astype(jnp.int32)) > FIRST
     left = tokens - FIRST
-    shapes = jax.eval_shape(lambda: project(FIRST, left))
+    shapes = jax.eval_shape(lambda: project(FIRST, left)[0])
     rest = lax.cond(
         many,
-        lambda: project(FIRST, left),
+        lambda: project(FIRST, left)[0],
         lambda: tuple(jnp.zeros(x.shape, x.dtype) for x in shapes),
     )
     pooled, slope, reduced, misc = pl.pallas_call(

time: 94.5 us -> 89.1 us (0.943)
  Pallas kernels: 36 us -> 29.8 us
  waiting for transfers between devices: 25.5 us -> 21.9 us
  matrix products: 9.18 us -> 10.8 us
  starting transfers between devices: 13.7 us -> 15.2 us
  local copies, waits for them, and re-layouts: 4.13 us -> 5.18 us
    pallas_call x1, Pallas kernels: 27.2 us -> 17.5 us  [project(): pl.pallas_call(functools.partial(gather_kernel, base=base), out_shape=[ja...]
    ppermute x1, waiting for transfers between devices: 8.28 us -> 0.01 us  [project(): far = lax.ppermute(chip1, 'dp', other_y)]
    ppermute x1, waiting for transfers between devices: 0.01 us -> 7.07 us  [project(): extra = chip + lax.ppermute(narrow(chip), 'dp', other_y).astype(jnp.float32)]
    pallas_call x0 -> x1, Pallas kernels: none -> 3.44 us  [project(): pl.pallas_call(statistics_kernel, out_shape=jax.ShapeDtypeStruct((extra_r...]
    ppermute x1, starting transfers between devices: 2.96 us -> 0.27 us  [project(): extra = chip + lax.ppermute(narrow(chip), 'dp', other_y).astype(jnp.float32)]
    ppermute x1, starting transfers between devices: 0.18 us -> 2.52 us  [project(): far = lax.ppermute(chip1, 'dp', other_y)]
    ppermute x1, waiting for transfers between devices: 1.66 us -> 0.01 us  [project(): chip += lax.ppermute(extra, 'dp', other_core).astype(jnp.float32)]
    dot_general x4, matrix products: 9.18 us -> 10.8 us  [mm(): return lax.dot_general(a, b, dims, preferred_element_type=jnp.float32)]
  transfers between devices with their start and end apart: 16 -> 16, of which waited for: 9 -> 9; matrix products, arithmetic and copies ran while one was open for 10% -> 8% of each run, Pallas kernels for 0% -> 4%
where the time goes in v4:
time: 89.1 us; the launch traced here: 88.5 us
  Pallas kernels  29.8 us (33%)
  waiting for transfers between devices  21.9 us (25%)
  starting transfers between devices  15.2 us (17%)
  matrix products  10.8 us (12%)
  local copies, waits for them, and re-layouts  5.18 us (6%)
  other arithmetic  3.45 us (4%)
  between operations  2.12 us (2%)
    pallas_call x1, Pallas kernels, project(): pl.pallas_call(functools.partial(gather_kernel, base=base), out_shape=[ja...  17.5 us
    dot_general x4, matrix products, mm(): return lax.dot_general(a, b, dims, preferred_element_type=jnp.float32)  10.8 us
    ppermute x9, waiting for transfers between devices, exchange(): return [x] + [lax.ppermute(x, axis, step) for step in steps]  10.2 us
    ppermute x9, starting transfers between devices, exchange(): return [x] + [lax.ppermute(x, axis, step) for step in steps]  8.2 us
    ppermute x1, waiting for transfers between devices, project(): extra = chip + lax.ppermute(narrow(chip), 'dp', other_y).astype(jnp.float32)  7.07 us
    pallas_call x1, Pallas kernels, split_body(): pl.pallas_call(functools.partial(pool_kernel, model_width=float(features...  3.99 us
    unnamed x35, local copies, waits for them, and re-layouts  3.73 us
    pallas_call x1, Pallas kernels, project(): pl.pallas_call(statistics_kernel, out_shape=jax.ShapeDtypeStruct((extra_r...  3.44 us
  transfers between devices with their start and end apart: 16, of which 9 were waited for; matrix products, arithmetic and copies ran while one was open for 8% of the time, Pallas kernels for 4%

profile of v4, /device:TPU:0, one launch (start us, length us, event | category | flops | bytes accessed | tf_op | source)
XLA Modules:
  0.0 88.5 jit_solution(15438801485199598112)
XLA Ops:
  1.3 17.5 %gather.3 = (bf16[1024,1152]{1,0:T(8,128)(2,1)}, bf16[1152,128]{1,0:T(8,128)(2,1)}) custom-call(s32[12,128]{1,0:T(8,128)S(1)} %bitcast.11, bf16[1024,16384]{1,0:T(8,128)(2,1)} %vocab_ref.1), custom_call_target="tpu_custom_call" | custom-call | tf_op jit(solution)/shard_map/gather/pallas_call | solution.py:551
  18.9 3.4 %convolution_convert_fusion.5 = bf16[1152,256]{1,0:T(8,128)(2,1)} fusion(bf16[1024,1152]{1,0:T(8,128)(2,1)} %get-tuple-element.38.turned, bf16[1024,1024]{1,0:T(8,128)(2,1)} %param.12, s32[]{:T(128)S(6)} %select_n.133), kind=kOutput, calls=%fused_computation.18 | convolution fusion | flops 604274688 | bytes 3473412 | tf_op jit(solution)/shard_map/dot_general | solution.py:127
  24.1 1.5 %conditional.1 = (bf16[384,256]{1,0:T(8,128)(2,1)S(1)}, bf16[384,256]{1,0:T(8,128)(2,1)}, bf16[384,256]{1,0:T(8,128)(2,1)}, f32[112,256]{1,0:T(8,128)S(1)}, bf16[384,128]{1,0:T(8,128)(2,1)S(1)}) conditional(s32[]{:T(128)} %convert_element_type.70, () %tuple.21, (s32[12,128]{1,0:T(8,128)S(1)}, bf16[1024,16384]{1,0:T(8,128)(2,1)}, ...), branch_computations={%region_1.0_spmd, %region_2.0_spmd} | conditional | flops 919400448 | bytes 14976144 | solution.py:608
  25.8 2.9 %add_convert_fusion.1 = bf16[1152,256]{1,0:T(8,128)(2,1)} fusion(bf16[1152,256]{1,0:T(8,128)(2,1)} %collective-permute-done.5, bf16[1024,1152]{1,0:T(8,128)(2,1)S(1)} %copy-done, bf16[1024,1024]{1,0:T(8,128)(2,1)} %param.12, s32[]{:T(128)S(6)} %select_n.132), kind=kOutput, calls=%fused_computation.19 | convolution fusion | flops 604864512 | bytes 4063236 | tf_op jit(solution)/shard_map/dot_general | solution.py:127
  28.7 2.5 %collective-permute-start.7 = (bf16[1152,256]{1,0:T(8,128)(2,1)}, bf16[1152,256]{1,0:T(8,128)(2,1)S(1)}, u32[]{:S(2)}, u32[]{:S(2)}) collective-permute-start(bf16[1152,256]{1,0:T(8,128)(2,1)} %add_convert_fusion.1), channel_id=1, source_target_pairs={{0,8},{4,12},{8,0},{12,4},{1,9},{5,13},{9,1},{13,5},{2,10},{6,14},... | collective-permute-start | bytes 1769480 | tf_op jit(solution)/shard_map/ppermute | solution.py:580
  31.2 3.4 %statistics.3 = bf16[160,256]{1,0:T(8,128)(2,1)} custom-call(bf16[1024,1152]{1,0:T(8,128)(2,1)} %get-tuple-element.38.turned, bf16[1152,128]{1,0:T(8,128)(2,1)} %get-tuple-element.39.member_ref, s32[3,7]{1,0:T(4,128)S(1)} %copy-done.21, bf16[16,4096]{1,0:T(8,128)(2,1)S(1)} %copy-done.8), custom_call_target="tpu_custom_call" | custom-call | flops 339738624 | bytes 2359296 | tf_op jit(solution)/shard_map/statistics/pallas_call | solution.py:582
  34.9 1.9 %convolution_convert_fusion.3 = bf16[1152,256]{1,0:T(8,128)(2,1)S(1)} fusion(bf16[1024,1152]{1,0:T(8,128)(2,1)S(1)} %copy-done.1, bf16[1024,1024]{1,0:T(8,128)(2,1)} %param.12, s32[]{:T(128)S(6)} %select_n.135), kind=kOutput, calls=%fused_computation.16 | convolution fusion | flops 604274688 | bytes 3473412 | tf_op jit(solution)/shard_map/dot_general | solution.py:127
  37.4 2.7 %convolution_convert_fusion.4.own_ref = bf16[1152,256]{1,0:T(8,128)(2,1)} fusion(bf16[1024,1152]{1,0:T(8,128)(2,1)S(1)} %copy-done.1, bf16[1024,1024]{1,0:T(8,128)(2,1)} %param.12, s32[]{:T(128)S(6)} %select_n.134), kind=kOutput, calls=%fused_computation.17 | convolution fusion | flops 604274688 | bytes 3473412 | tf_op jit(solution)/shard_map/dot_general | solution.py:127
  40.1 7.1 %collective-permute-done.9 = bf16[160,256]{1,0:T(8,128)(2,1)S(1)} collective-permute-done((bf16[160,256]{1,0:T(8,128)(2,1)S(1)}, bf16[160,256]{1,0:T(8,128)(2,1)S(1)}, u32[]{:S(2)}, u32[]{:S(2)}) %collective-permute-start.9) | collective-permute-done | bytes 81952 | tf_op jit(solution)/shard_map/ppermute | solution.py:598
  49.5 4.0 %pool.1 = (bf16[16,256]{1,0:T(8,128)(2,1)}, f32[1536,256]{1,0:T(8,128)}, bf16[16,1536]{1,0:T(8,128)(2,1)}, f32[16,256]{1,0:T(8,128)}) custom-call(s32[12,128]{1,0:T(8,128)S(1)} %bitcast.14, bf16[1152,256]{1,0:T(8,128)(2,1)} %convolution_convert_fusion.4.own_ref, bf16[1152,256]{1,0:T(8,128)(2,1)} %copy-done.7, bf16[1152,256]{1,0:T(8,128)(2,1)} %copy-done.6, ...), custom_call_target="tpu_custom_call" | custom-call | tf_op jit(solution)/shard_map/pool/pallas_call | solution.py:613
  53.5 1.7 %collective-permute-start.10 = (bf16[16,256]{1,0:T(8,128)(2,1)}, bf16[16,256]{1,0:T(8,128)(2,1)S(1)}, u32[]{:S(2)}, u32[]{:S(2)}) collective-permute-start(bf16[16,256]{1,0:T(8,128)(2,1)} %get-tuple-element.46.near_ref), channel_id=1, source_target_pairs={{0,16},{16,0},{1,17},{17,1},{2,18},{18,2},{3,19},{19,3},{4,20},{20... | collective-permute-start | bytes 24584 | tf_op jit(solution)/shard_map/ppermute | solution.py:631
  55.2 2.1 %collective-permute-done.10.far_ref = bf16[16,256]{1,0:T(8,128)(2,1)S(1)} collective-permute-done((bf16[16,256]{1,0:T(8,128)(2,1)}, bf16[16,256]{1,0:T(8,128)(2,1)S(1)}, u32[]{:S(2)}, u32[]{:S(2)}) %collective-permute-start.10) | collective-permute-done | bytes 8224 | tf_op jit(solution)/shard_map/ppermute | solution.py:631
  57.9 1.4 %dots.1.packed0 = f32[64,128]{1,0:T(8,128)} custom-call(bf16[16,256]{1,0:T(8,128)(2,1)} %get-tuple-element.46.near_ref, bf16[16,256]{1,0:T(8,128)(2,1)} %copy-done.17), custom_call_target="tpu_custom_call" | custom-call | tf_op jit(solution)/shard_map/dots/pallas_call | solution.py:633
  59.4 1.7 %collective-permute-start.12 = (f32[64,128]{1,0:T(8,128)}, f32[64,128]{1,0:T(8,128)S(1)}, u32[]{:S(2)}, u32[]{:S(2)}) collective-permute-start(f32[64,128]{1,0:T(8,128)} %dots.1.packed0), channel_id=1, source_target_pairs={{0,8},{4,12},{8,0},{12,4},{1,9},{5,13},{9,1},{13,5},{2,10},{6,14},... | collective-permute-start | bytes 98312 | tf_op jit(solution)/shard_map/ppermute | solution.py:518
  61.3 2.2 %collective-permute-done.12.packed2 = f32[64,128]{1,0:T(8,128)S(1)} collective-permute-done((f32[64,128]{1,0:T(8,128)}, f32[64,128]{1,0:T(8,128)S(1)}, u32[]{:S(2)}, u32[]{:S(2)}) %collective-permute-start.12) | collective-permute-done | bytes 32800 | tf_op jit(solution)/shard_map/ppermute | solution.py:518
  63.5 1.2 %collective-permute-done.13.packed3 = f32[64,128]{1,0:T(8,128)S(1)} collective-permute-done((f32[64,128]{1,0:T(8,128)}, f32[64,128]{1,0:T(8,128)S(1)}, u32[]{:S(2)}, u32[]{:S(2)}) %collective-permute-start.13) | collective-permute-done | bytes 32800 | tf_op jit(solution)/shard_map/ppermute | solution.py:518
  65.4 1.6 %collective-permute-start.14 = (f32[32,128]{1,0:T(8,128)S(1)}, f32[32,128]{1,0:T(8,128)S(1)}, u32[]{:S(2)}, u32[]{:S(2)}) collective-permute-start(f32[32,128]{1,0:T(8,128)S(1)} %fusion.19.dots0), channel_id=1, source_target_pairs={{0,1},{1,0},{2,3},{3,2},{4,5},{5,4},{6,7},{7,6},{8,9},{9,8},{10,11... | collective-permute-start | bytes 49160 | tf_op jit(solution)/shard_map/ppermute | solution.py:518
  67.1 2.6 %collective-permute-start.15 = (f32[32,128]{1,0:T(8,128)S(1)}, f32[32,128]{1,0:T(8,128)S(1)}, u32[]{:S(2)}, u32[]{:S(2)}) collective-permute-start(f32[32,128]{1,0:T(8,128)S(1)} %fusion.19.dots0), channel_id=1, source_target_pairs={{0,2},{1,3},{2,0},{3,1},{4,6},{5,7},{6,4},{7,5},{8,10},{9,11},{10,... | collective-permute-start | bytes 49160 | tf_op jit(solution)/shard_map/ppermute | solution.py:518
  70.5 1.2 %collective-permute-done.15.dots2 = f32[32,128]{1,0:T(8,128)S(1)} collective-permute-done((f32[32,128]{1,0:T(8,128)S(1)}, f32[32,128]{1,0:T(8,128)S(1)}, u32[]{:S(2)}, u32[]{:S(2)}) %collective-permute-start.15) | collective-permute-done | bytes 16416 | tf_op jit(solution)/shard_map/ppermute | solution.py:518
  71.8 3.4 %collective-permute-done.16.dots3 = f32[32,128]{1,0:T(8,128)S(1)} collective-permute-done((f32[32,128]{1,0:T(8,128)S(1)}, f32[32,128]{1,0:T(8,128)S(1)}, u32[]{:S(2)}, u32[]{:S(2)}) %collective-permute-start.16) | collective-permute-done | bytes 16416 | tf_op jit(solution)/shard_map/ppermute | solution.py:518
  75.8 3.4 %score.1 = (bf16[1,3,1024]{2,1,0:T(4,128)(2,1)}, f32[1,3]{1,0:T(1,128)}, f32[16,256]{1,0:T(8,128)}) custom-call(s32[12,128]{1,0:T(8,128)S(1)} %bitcast.15, bf16[16,256]{1,0:T(8,128)(2,1)} %get-tuple-element.46.near_ref, bf16[16,256]{1,0:T(8,128)(2,1)} %copy-done.17, f32[64,128]{1,0:T(8,128)} %dots.1.packed0, f32[64,128]{1,0:T(8,128)} %copy-done.13, ...), custom_call_target="tpu_custom_call" | custom-call | tf_op jit(solution)/shard_map/score/pallas_call | solution.py:644
  79.2 1.5 %collective-permute-start.17 = (f32[16,256]{1,0:T(8,128)}, f32[16,256]{1,0:T(8,128)S(1)}, u32[]{:S(2)}, u32[]{:S(2)}) collective-permute-start(f32[16,256]{1,0:T(8,128)} %get-tuple-element.52), channel_id=1, source_target_pairs={{0,16},{16,0},{1,17},{17,1},{2,18},{18,2},{3,19},{19,3},{4,20},{20... | collective-permute-start | bytes 49160 | tf_op jit(solution)/shard_map/ppermute | solution.py:668
  80.6 2.5 %collective-permute-done.17 = f32[16,256]{1,0:T(8,128)S(1)} collective-permute-done((f32[16,256]{1,0:T(8,128)}, f32[16,256]{1,0:T(8,128)S(1)}, u32[]{:S(2)}, u32[]{:S(2)}) %collective-permute-start.17) | collective-permute-done | bytes 16416 | tf_op jit(solution)/shard_map/ppermute | solution.py:668
  85.7 1.9 %collective-permute-done.19 = f32[16,256]{1,0:T(8,128)S(1)} collective-permute-done((f32[16,256]{1,0:T(8,128)S(1)}, f32[16,256]{1,0:T(8,128)S(1)}, u32[]{:S(2)}, u32[]{:S(2)}) %collective-permute-start.19) | collective-permute-done | bytes 16416 | tf_op jit(solution)/shard_map/ppermute | solution.py:518
  (65 shorter events, 12.5 us)
Async XLA Ops:
  1.3 22.7 %copy-start.11 = (s32[1,12,128]{2,1,0:T(8,128)}, s32[1,12,128]{2,1,0:T(8,128)S(1)}, u32[]{:S(2)}) copy-start(s32[1,12,128]{2,1,0:T(8,128)S(1)} %copy.12) | copy-start | bytes 18436
  22.3 3.3 %collective-permute-start.5 = (bf16[1152,256]{1,0:T(8,128)(2,1)}, bf16[1152,256]{1,0:T(8,128)(2,1)}, u32[]{:S(2)}, u32[]{:S(2)}) collective-permute-start(bf16[1152,256]{1,0:T(8,128)(2,1)} %convolution_convert_fusion.5), channel_id=1, source_target_pairs={{0,4},{4,0},{8,12},{12,8},{1,5},{5,1},{9,13},{13,9},{2,6},{6,2},{1... | collective-permute-start | bytes 1769480 | tf_op jit(solution)/shard_map/ppermute | solution.py:578
  25.6 5.6 %copy-start.8 = (bf16[16,4096]{1,0:T(8,128)(2,1)S(1)}, bf16[16,4096]{1,0:T(8,128)(2,1)}, u32[]{:S(2)}) copy-start(bf16[16,4096]{1,0:T(8,128)(2,1)} %lower_ref.1) | copy-start | bytes 393220
  28.7 6.2 %copy-start.1 = (bf16[1024,1152]{1,0:T(8,128)(2,1)S(1)}, bf16[1024,1152]{1,0:T(8,128)(2,1)}, u32[]{:S(2)}) copy-start(bf16[1024,1152]{1,0:T(8,128)(2,1)} %get-tuple-element.38.turned) | copy-start | bytes 7077892
  28.7 19.2 %collective-permute-start.7 = (bf16[1152,256]{1,0:T(8,128)(2,1)}, bf16[1152,256]{1,0:T(8,128)(2,1)S(1)}, u32[]{:S(2)}, u32[]{:S(2)}) collective-permute-start(bf16[1152,256]{1,0:T(8,128)(2,1)} %add_convert_fusion.1), channel_id=1, source_target_pairs={{0,8},{4,12},{8,0},{12,4},{1,9},{5,13},{9,1},{13,5},{2,10},{6,14},... | collective-permute-start | bytes 1769480 | tf_op jit(solution)/shard_map/ppermute | solution.py:580
  34.6 2.5 %collective-permute-start.8 = (bf16[160,256]{1,0:T(8,128)(2,1)}, bf16[160,256]{1,0:T(8,128)(2,1)S(1)}, u32[]{:S(2)}, u32[]{:S(2)}) collective-permute-start(bf16[160,256]{1,0:T(8,128)(2,1)} %statistics.3), channel_id=1, source_target_pairs={{0,4},{4,0},{8,12},{12,8},{1,5},{5,1},{9,13},{13,9},{2,6},{6,2},{1... | collective-permute-start | bytes 245768 | tf_op jit(solution)/shard_map/ppermute | solution.py:597
  36.7 11.1 %collective-permute-start.6 = (bf16[1152,256]{1,0:T(8,128)(2,1)S(1)}, bf16[1152,256]{1,0:T(8,128)(2,1)S(1)}, u32[]{:S(2)}, u32[]{:S(2)}) collective-permute-start(bf16[1152,256]{1,0:T(8,128)(2,1)S(1)} %convolution_convert_fusion.3), channel_id=1, source_target_pairs={{0,4},{4,0},{8,12},{12,8},{1,5},{5,1},{9,13},{13,9},{2,6},{6,2},{1... | collective-permute-start | bytes 1769480 | tf_op jit(solution)/shard_map/ppermute | solution.py:599
  37.1 12.4 %copy-start.12 = (s32[1,12,128]{2,1,0:T(8,128)S(1)}, s32[1,12,128]{2,1,0:T(8,128)}, u32[]{:S(2)}) copy-start(s32[1,12,128]{2,1,0:T(8,128)} %copy-done.11) | copy-start | bytes 18436
  37.1 10.0 %collective-permute-start.9 = (bf16[160,256]{1,0:T(8,128)(2,1)S(1)}, bf16[160,256]{1,0:T(8,128)(2,1)S(1)}, u32[]{:S(2)}, u32[]{:S(2)}) collective-permute-start(bf16[160,256]{1,0:T(8,128)(2,1)S(1)} %fusion.24), channel_id=1, source_target_pairs={{0,8},{4,12},{8,0},{12,4},{1,9},{5,13},{9,1},{13,5},{2,10},{6,14},... | collective-permute-start | bytes 245768 | tf_op jit(solution)/shard_map/ppermute | solution.py:598
  53.5 3.9 %collective-permute-start.10 = (bf16[16,256]{1,0:T(8,128)(2,1)}, bf16[16,256]{1,0:T(8,128)(2,1)S(1)}, u32[]{:S(2)}, u32[]{:S(2)}) collective-permute-start(bf16[16,256]{1,0:T(8,128)(2,1)} %get-tuple-element.46.near_ref), channel_id=1, source_target_pairs={{0,16},{16,0},{1,17},{17,1},{2,18},{18,2},{3,19},{19,3},{4,20},{20... | collective-permute-start | bytes 24584 | tf_op jit(solution)/shard_map/ppermute | solution.py:631
  59.4 1.9 %collective-permute-start.11 = (f32[64,128]{1,0:T(8,128)}, f32[64,128]{1,0:T(8,128)S(1)}, u32[]{:S(2)}, u32[]{:S(2)}) collective-permute-start(f32[64,128]{1,0:T(8,128)} %dots.1.packed0), channel_id=1, source_target_pairs={{0,4},{4,0},{8,12},{12,8},{1,5},{5,1},{9,13},{13,9},{2,6},{6,2},{1... | collective-permute-start | bytes 98312 | tf_op jit(solution)/shard_map/ppermute | solution.py:518
  59.4 4.1 %collective-permute-start.12 = (f32[64,128]{1,0:T(8,128)}, f32[64,128]{1,0:T(8,128)S(1)}, u32[]{:S(2)}, u32[]{:S(2)}) collective-permute-start(f32[64,128]{1,0:T(8,128)} %dots.1.packed0), channel_id=1, source_target_pairs={{0,8},{4,12},{8,0},{12,4},{1,9},{5,13},{9,1},{13,5},{2,10},{6,14},... | collective-permute-start | bytes 98312 | tf_op jit(solution)/shard_map/ppermute | solution.py:518
  61.1 3.6 %collective-permute-start.13 = (f32[64,128]{1,0:T(8,128)}, f32[64,128]{1,0:T(8,128)S(1)}, u32[]{:S(2)}, u32[]{:S(2)}) collective-permute-start(f32[64,128]{1,0:T(8,128)} %dots.1.packed0), channel_id=1, source_target_pairs={{0,12},{4,8},{8,4},{12,0},{1,13},{5,9},{9,5},{13,1},{2,14},{6,10},... | collective-permute-start | bytes 98312 | tf_op jit(solution)/shard_map/ppermute | solution.py:518
  61.3 13.9 %copy-start.13 = (f32[64,128]{1,0:T(8,128)}, f32[64,128]{1,0:T(8,128)S(1)}, u32[]{:S(2)}) copy-start(f32[64,128]{1,0:T(8,128)S(1)} %collective-permute-done.11.packed1) | copy-start | bytes 98308
  63.5 11.7 %copy-start.14 = (f32[64,128]{1,0:T(8,128)}, f32[64,128]{1,0:T(8,128)S(1)}, u32[]{:S(2)}) copy-start(f32[64,128]{1,0:T(8,128)S(1)} %collective-permute-done.12.packed2) | copy-start | bytes 98308
  64.7 10.5 %copy-start.15 = (f32[64,128]{1,0:T(8,128)}, f32[64,128]{1,0:T(8,128)S(1)}, u32[]{:S(2)}) copy-start(f32[64,128]{1,0:T(8,128)S(1)} %collective-permute-done.13.packed3) | copy-start | bytes 98308
  65.4 9.8 %copy-start.16 = (f32[32,128]{1,0:T(8,128)}, f32[32,128]{1,0:T(8,128)S(1)}, u32[]{:S(2)}) copy-start(f32[32,128]{1,0:T(8,128)S(1)} %fusion.19.dots0) | copy-start | bytes 49156
  65.4 5.1 %collective-permute-start.14 = (f32[32,128]{1,0:T(8,128)S(1)}, f32[32,128]{1,0:T(8,128)S(1)}, u32[]{:S(2)}, u32[]{:S(2)}) collective-permute-start(f32[32,128]{1,0:T(8,128)S(1)} %fusion.19.dots0), channel_id=1, source_target_pairs={{0,1},{1,0},{2,3},{3,2},{4,5},{5,4},{6,7},{7,6},{8,9},{9,8},{10,11... | collective-permute-start | bytes 49160 | tf_op jit(solution)/shard_map/ppermute | solution.py:518
  67.1 4.7 %collective-permute-start.15 = (f32[32,128]{1,0:T(8,128)S(1)}, f32[32,128]{1,0:T(8,128)S(1)}, u32[]{:S(2)}, u32[]{:S(2)}) collective-permute-start(f32[32,128]{1,0:T(8,128)S(1)} %fusion.19.dots0), channel_id=1, source_target_pairs={{0,2},{1,3},{2,0},{3,1},{4,6},{5,7},{6,4},{7,5},{8,10},{9,11},{10,... | collective-permute-start | bytes 49160 | tf_op jit(solution)/shard_map/ppermute | solution.py:518
  69.6 5.5 %collective-permute-start.16 = (f32[32,128]{1,0:T(8,128)S(1)}, f32[32,128]{1,0:T(8,128)S(1)}, u32[]{:S(2)}, u32[]{:S(2)}) collective-permute-start(f32[32,128]{1,0:T(8,128)S(1)} %fusion.19.dots0), channel_id=1, source_target_pairs={{0,3},{1,2},{2,1},{3,0},{4,7},{5,6},{6,5},{7,4},{8,11},{9,10},{10,... | collective-permute-start | bytes 49160 | tf_op jit(solution)/shard_map/ppermute | solution.py:518
  79.2 3.9 %collective-permute-start.17 = (f32[16,256]{1,0:T(8,128)}, f32[16,256]{1,0:T(8,128)S(1)}, u32[]{:S(2)}, u32[]{:S(2)}) collective-permute-start(f32[16,256]{1,0:T(8,128)} %get-tuple-element.52), channel_id=1, source_target_pairs={{0,16},{16,0},{1,17},{17,1},{2,18},{18,2},{3,19},{19,3},{4,20},{20... | collective-permute-start | bytes 49160 | tf_op jit(solution)/shard_map/ppermute | solution.py:668
  83.8 1.9 %collective-permute-start.18 = (f32[16,256]{1,0:T(8,128)S(1)}, f32[16,256]{1,0:T(8,128)S(1)}, u32[]{:S(2)}, u32[]{:S(2)}) collective-permute-start(f32[16,256]{1,0:T(8,128)S(1)} %add.92), channel_id=1, source_target_pairs={{0,4},{4,0},{8,12},{12,8},{1,5},{5,1},{9,13},{13,9},{2,6},{6,2},{1... | collective-permute-start | bytes 49160 | tf_op jit(solution)/shard_map/ppermute | solution.py:518
  83.8 3.7 %collective-permute-start.19 = (f32[16,256]{1,0:T(8,128)S(1)}, f32[16,256]{1,0:T(8,128)S(1)}, u32[]{:S(2)}, u32[]{:S(2)}) collective-permute-start(f32[16,256]{1,0:T(8,128)S(1)} %add.92), channel_id=1, source_target_pairs={{0,8},{4,12},{8,0},{12,4},{1,9},{5,13},{9,1},{13,5},{2,10},{6,14},... | collective-permute-start | bytes 49160 | tf_op jit(solution)/shard_map/ppermute | solution.py:518
  84.7 3.2 %collective-permute-start.20 = (f32[16,256]{1,0:T(8,128)S(1)}, f32[16,256]{1,0:T(8,128)S(1)}, u32[]{:S(2)}, u32[]{:S(2)}) collective-permute-start(f32[16,256]{1,0:T(8,128)S(1)} %add.92), channel_id=1, source_target_pairs={{0,12},{4,8},{8,4},{12,0},{1,13},{5,9},{9,5},{13,1},{2,14},{6,10},... | collective-permute-start | bytes 49160 | tf_op jit(solution)/shard_map/ppermute | solution.py:518
  (9 other events, 20.8 us)

commit v5 on v4

--- a/solution.py
+++ b/solution.py
@@ -265,11 +265,14 @@
     lax.fori_loop(0, blocks, take, 0)
 
 
-def statistics_kernel(turned, member_ref, hard_ref, lower_ref, extra_ref, small):
+def statistics_kernel(
+    ids_ref, turned, member_ref, hard_ref, lower_ref, extra_ref, count_ref, small
+):
     features, span = turned.shape
     stripes = pl.cdiv(span, STRIPE)
     per_shard, negatives = hard_ref.shape
     shard = lax.axis_index("dp")
+    count_ref[0] = jnp.sum((ids_ref[...] != 0).astype(jnp.float32)).astype(jnp.int32)
     small[...] = jnp.zeros_like(small)
     small[0:per_shard, stripes : stripes + negatives] = hard_ref[...].astype(jnp.float32)
     lower = lower_ref[:, pl.ds(pl.multiple_of(shard * features, LANES), features)]
@@ -307,20 +310,22 @@
     own_ref,
     core_ref,
     far_ref,
-    extra_ref,
+    chip_ref,
+    far_chip_ref,
     member_ref,
     own_rest,
     core_rest,
     far_rest,
-    extra_rest,
+    chip_rest,
+    far_chip_rest,
     member_rest,
     raise_ref,
     pooled_ref,
-    slope_ref,
-    reduced_ref,
+    slopes_ref,
     misc_ref,
     raised,
     total,
+    slopes,
     model_width,
 ):
     texts, length = ids_ref.shape
@@ -329,50 +334,55 @@
     raised[...] = jnp.zeros_like(raised)
     raised[0:ROWS, :] = raise_ref[:, pl.ds(pl.multiple_of(quarter * width, LANES), width)]
     total[...] = jnp.zeros_like(total)
-
-    def add(refs, extra_ref, member_ref, base):
+    slopes[...] = jnp.zeros_like(slopes)
+
+    def add(refs, extras, member_ref, base):
         span = member_ref.shape[0]
         stripes = pl.cdiv(span, STRIPE)
 
-        def summed(start, size):
+        def summed(refs, start, size):
             return sum(ref[pl.ds(start, size), :].astype(jnp.float32) for ref in refs)
 
-        misc = extra_ref[stripes * ROWS : (stripes + 1) * ROWS, :]
+        misc = summed(extras, stripes * ROWS, ROWS)
         if base == 0:
             misc_ref[...] = misc
         inverse = lax.rsqrt(misc / model_width + 1e-05)
         for k in range(stripes):
-            at = base + k * STRIPE
             size = min(STRIPE, span - k * STRIPE)
             scale = inverse[k : k + 1]
-            reduced = (extra_ref[k * ROWS : (k + 1) * ROWS, :] * scale).astype(jnp.bfloat16)
-            reduced_ref[:, at : at + size] = reduced[:, 0:size]
-            stacked = jnp.concatenate(
-                [reduced.astype(jnp.float32), jnp.broadcast_to(scale, (LANES - ROWS, STRIPE))]
-            )
+            reduced = (summed(extras, k * ROWS, ROWS) * scale).astype(jnp.bfloat16)
+            reduced = reduced.astype(jnp.float32)
+            stacked = jnp.concatenate([reduced, jnp.broadcast_to(scale, (LANES - ROWS, STRIPE))])
             turned = stacked[:, 0:size].T
             low = turned.astype(jnp.bfloat16)
-            linear = summed(k * STRIPE, size) * turned[:, ROWS : ROWS + 1] + mm(low, raised[...])
+            linear = summed(refs, k * STRIPE, size)
+            linear = linear * turned[:, ROWS : ROWS + 1] + mm(low, raised[...])
             sigma = 1.0 / (1.0 + jnp.exp(-linear))
-            slope_ref[pl.ds(at, size), :] = sigma * (1.0 + linear * (1.0 - sigma))
+            slope = (sigma * (1.0 + linear * (1.0 - sigma))).astype(jnp.bfloat16)
             member = member_ref[pl.ds(k * STRIPE, size), :].astype(jnp.float32).T
-            member = member[0:ROWS].astype(jnp.bfloat16)
             high, rest = split(linear * sigma)
-            total[...] += mm(member, high) + mm(member, rest)
+            chosen = member[0:ROWS].astype(jnp.bfloat16)
+            total[...] += mm(chosen, high) + mm(chosen, rest)
+            spread = [reduced[:, 0:size] * member[text : text + 1] for text in range(texts)]
+            slopes[...] += mm(jnp.concatenate(spread).astype(jnp.bfloat16), slope)
         start = pl.multiple_of((stripes + 1 + quarter) * ROWS, ROWS)
-        total[...] += extra_ref[pl.ds(start, ROWS), :]
-
-    add((own_ref, core_ref, far_ref), extra_ref, member_ref, 0)
+        total[...] += summed(extras, start, ROWS)
+
+    add((own_ref, core_ref, far_ref), (chip_ref, far_chip_ref), member_ref, 0)
     real = (ids_ref[...] != 0).astype(jnp.float32)
 
     @pl.when(jnp.sum(real) > member_ref.shape[0])
     def _():
-        add((own_rest, core_rest, far_rest), extra_rest, member_rest, member_ref.shape[0])
+        extras = (chip_rest, far_chip_rest)
+        add((own_rest, core_rest, far_rest), extras, member_rest, member_ref.shape[0])
 
     counts = jnp.sum(real, axis=1, keepdims=True)
     pooled = total[0:texts] / counts
     pooled = jnp.concatenate([pooled, jnp.zeros((ROWS - texts, width), jnp.float32)])
     pooled_ref[...] = pooled.astype(jnp.bfloat16)
+    for text in range(texts):
+        rows = pl.ds(text * ROWS, ROWS)
+        slopes_ref[rows, :] = (slopes[rows, :] / counts[text : text + 1]).astype(jnp.bfloat16)
 
 
 def both_sides(near, far):
@@ -380,47 +390,40 @@
     return jnp.concatenate([jnp.where(queries, near, far), jnp.where(queries, far, near)], axis=0)
 
 
-def dots_kernel(near_ref, far_ref, packed_ref):
-    near = near_ref[...]
-    block = both_sides(near, far_ref[...])
-    dots = mm(block, block, NT)
+def dots_kernel(near_ref, far_ref, slopes_ref, packed_ref, slopes_out):
+    block = both_sides(near_ref[...], far_ref[...])
     rows = 2 * ROWS
     packed_ref[...] = jnp.zeros_like(packed_ref)
-    packed_ref[0:rows, 0:rows] = dots
-    for part in range(near.shape[1] // LANES):
-        start = rows + part * ROWS
-        packed_ref[start : start + ROWS, :] = near[:, part * LANES : (part + 1) * LANES].astype(
-            jnp.float32
-        )
+    packed_ref[0:rows, 0:rows] = mm(block, block, NT)
+    for part in range(block.shape[1] // LANES):
+        piece = block[:, part * LANES : (part + 1) * LANES]
+        packed_ref[rows + part * rows : rows + (part + 1) * rows, :] = piece.astype(jnp.float32)
+    slopes_out[...] = slopes_ref[...]
 
 
 def score_kernel(
-    ids_ref,
-    near_ref,
-    far_ref,
     packed0,
     packed1,
     packed2,
     packed3,
+    slopes0,
+    slopes1,
+    slopes2,
+    slopes3,
     dots0,
     dots1,
     dots2,
     dots3,
     misc_ref,
-    slope_ref,
-    reduced_ref,
-    member_ref,
-    member_rest,
     sharp_ref,
     embed_ref,
     loss_ref,
     up_ref,
+    texts,
+    stripes,
     negatives,
 ):
-    texts, length = ids_ref.shape
-    stripes = pl.cdiv(member_ref.shape[0], STRIPE)
     rows = 2 * ROWS
-    width = near_ref.shape[1]
     per_shard = loss_ref.shape[1]
     group, shard = lax.axis_index("group"), lax.axis_index("dp")
     dots = ((dots0[...] + dots1[...]) + (dots2[...] + dots3[...]))[:, 0:rows]
@@ -459,45 +462,34 @@
     )
     loss_ref[...] = jnp.sum(jnp.where(at, loss_col, 0.0), axis=0, keepdims=True)[:, 0:per_shard]
 
-    mine = both_sides(near_ref[...], far_ref[...])
-    along = mm(coeff.astype(jnp.float32).T.astype(jnp.bfloat16), mine)
+    along_rows = coeff.astype(jnp.float32).T.astype(jnp.bfloat16)
     radial_col = jnp.sum(jnp.where(same, radial, 0.0), axis=1, keepdims=True)
-    grad = sharpness * (along - radial_col * mine.astype(jnp.float32))
-    grad = jnp.where(group == 0, grad[0:ROWS], grad[ROWS:rows])
-    real_tokens = (ids_ref[...] != 0).astype(jnp.float32)
-    counts = jnp.sum(real_tokens, axis=1, keepdims=True)
-    grad = grad[0:texts] / counts
-    grad = jnp.concatenate([grad, jnp.zeros((LANES - texts, width), jnp.float32)])
-    high, rest = split(grad)
-
-    def update(member_ref, base):
-        total = jnp.zeros((ROWS, width), jnp.float32)
-        for k in range(member_ref.shape[0] // CHUNK):
-            at = base + k * CHUNK
-            member = member_ref[pl.ds(k * CHUNK, CHUNK), :]
-            token_grad = mm(member, high) + mm(member, rest)
-            local = (token_grad * slope_ref[pl.ds(at, CHUNK), :]).astype(jnp.bfloat16)
-            total += mm(reduced_ref[:, at : at + CHUNK], local)
-        return total
-
-    first_part = update(member_ref, 0)
-    up_ref[...] = first_part
-
-    @pl.when(jnp.sum(real_tokens) > member_ref.shape[0])
-    def _():
-        up_ref[...] = first_part + update(member_rest, member_ref.shape[0])
-
     rnorm_own = jnp.where(group == 0, rnorm_col[0:ROWS], rnorm_col[ROWS:rows])
     chosen = iota((ROWS, ROWS), 1) == iota((ROWS, ROWS), 0) + first
     chosen = jnp.where(chosen & (iota((ROWS, ROWS), 0) < per_shard), 1.0, 0.0).astype(jnp.bfloat16)
-    for o, packed in enumerate((packed0, packed1, packed2, packed3)):
-        halves = [
-            packed[rows + part * ROWS : rows + (part + 1) * ROWS, :]
-            for part in range(width // LANES)
-        ]
-        block = jnp.concatenate(halves, axis=1) * rnorm_own
-        picked = mm(chosen, block.astype(jnp.bfloat16)).astype(jnp.bfloat16)
+    blocks = ((packed0, slopes0), (packed1, slopes1), (packed2, slopes2), (packed3, slopes3))
+    for o, (packed, slopes) in enumerate(blocks):
+        parts = packed.shape[0] // rows - 1
+        width = parts * LANES
+        halves = [packed[rows * (part + 1) : rows * (part + 2), :] for part in range(parts)]
+        block = jnp.concatenate(halves, axis=1)
+        along = mm(along_rows, block.astype(jnp.bfloat16))
+        grad = sharpness * (along - radial_col * block)
+        near, far = slopes[0 : slopes.shape[0] // 2], slopes[slopes.shape[0] // 2 :]
+        queries = group == 0
+        grad_near = jnp.where(queries, grad[0:ROWS], grad[ROWS:rows])
+        grad_far = jnp.where(queries, grad[ROWS:rows], grad[0:ROWS])
+        update = []
+        for side, side_grad in ((near, grad_near), (far, grad_far)):
+            total = jnp.zeros((ROWS, width), jnp.float32)
+            for text in range(texts):
+                slope = side[text * ROWS : (text + 1) * ROWS].astype(jnp.float32)
+                total += side_grad[text : text + 1] * slope
+            update.append(total)
         at = pl.multiple_of(quarter_of(shard ^ o) * width, LANES)
+        up_ref[:, pl.ds(at, width)] = update[0] + update[1]
+        own = jnp.where(queries, block[0:ROWS], block[ROWS:rows]) * rnorm_own
+        picked = mm(chosen, own.astype(jnp.bfloat16)).astype(jnp.bfloat16)
         embed_ref[0, :, pl.ds(at, width)] = picked[0:per_shard]
 
 
@@ -579,11 +571,14 @@
         chip1 = narrow(product(turned, 0, 1) + core1.astype(jnp.float32))
         far = lax.ppermute(chip1, "dp", other_y)
         turned, _ = lax.optimization_barrier((turned, chip1))
-        extra = pl.pallas_call(
+        extra, count = pl.pallas_call(
             statistics_kernel,
-            out_shape=jax.ShapeDtypeStruct((extra_rows, STRIPE), jnp.bfloat16),
-            in_specs=[vmem_spec()] * 4,
-            out_specs=vmem_spec(),
+            out_shape=[
+                jax.ShapeDtypeStruct((extra_rows, STRIPE), jnp.bfloat16),
+                jax.ShapeDtypeStruct((1,), jnp.int32),
+            ],
+            in_specs=[vmem_spec()] * 5,
+            out_specs=[vmem_spec(), smem_spec()],
             scratch_shapes=[pltpu.VMEM((LANES, LANES), jnp.float32)],
             compiler_params=params,
             cost_estimate=pl.CostEstimate(
@@ -592,17 +587,16 @@
                 transcendentals=0,
             ),
             name="statistics",
-        )(turned, member, difficult_distractors, lowering_factor_matrix)
+        )(ids, turned, member, difficult_distractors, lowering_factor_matrix)
         chip = extra.astype(jnp.float32)
-        chip += lax.ppermute(extra, "dp", other_core).astype(jnp.float32)
-        extra = chip + lax.ppermute(narrow(chip), "dp", other_y).astype(jnp.float32)
+        chip = narrow(chip + lax.ppermute(extra, "dp", other_core).astype(jnp.float32))
+        far_chip = lax.ppermute(chip, "dp", other_y)
         core0 = lax.ppermute(narrow(product(turned, 1, 0)), "dp", other_core)
         own0 = narrow(product(turned, 0, 0))
-        return (own0, core0, far, extra, member), chip
-
-    first, early = project(0, FIRST)
-    later, _ = lax.optimization_barrier((ids, early))
-    many = jnp.sum((later != 0).astype(jnp.int32)) > FIRST
+        return (own0, core0, far, chip, far_chip, member), count
+
+    first, count = project(0, FIRST)
+    many = count[0] > FIRST
     left = tokens - FIRST
     shapes = jax.eval_shape(lambda: project(FIRST, left)[0])
     rest = lax.cond(
@@ -610,66 +604,57 @@
         lambda: project(FIRST, left)[0],
         lambda: tuple(jnp.zeros(x.shape, x.dtype) for x in shapes),
     )
-    pooled, slope, reduced, misc = pl.pallas_call(
+    pooled, slopes, misc = pl.pallas_call(
         functools.partial(pool_kernel, model_width=float(features * shards)),
         out_shape=[
             jax.ShapeDtypeStruct((ROWS, width), jnp.bfloat16),
-            jax.ShapeDtypeStruct((tokens, width), jnp.float32),
-            jax.ShapeDtypeStruct((ROWS, tokens), jnp.bfloat16),
+            jax.ShapeDtypeStruct((texts * ROWS, width), jnp.bfloat16),
             jax.ShapeDtypeStruct((ROWS, width), jnp.float32),
         ],
-        in_specs=[vmem_spec()] * 12,
-        out_specs=[vmem_spec()] * 4,
+        in_specs=[vmem_spec()] * 14,
+        out_specs=[vmem_spec()] * 3,
         scratch_shapes=[
             pltpu.VMEM((LANES, width), jnp.bfloat16),
             pltpu.VMEM((ROWS, width), jnp.float32),
+            pltpu.VMEM((texts * ROWS, width), jnp.float32),
         ],
         compiler_params=params,
         name="pool",
     )(ids, *first, *rest, raising_factor_matrix)
-    member, member_rest = first[4], rest[4]
-    far_side = lax.ppermute(pooled, "group", [(0, 1), (1, 0)])
+    other_side = [(0, 1), (1, 0)]
+    far_side = lax.ppermute(pooled, "group", other_side)
     rows = 2 * ROWS
-    packed = pl.pallas_call(
+    packed, slopes = pl.pallas_call(
         dots_kernel,
-        out_shape=jax.ShapeDtypeStruct((rows + width // LANES * ROWS, LANES), jnp.float32),
-        in_specs=[vmem_spec()] * 2,
-        out_specs=vmem_spec(),
+        out_shape=[
+            jax.ShapeDtypeStruct((rows + width // LANES * rows, LANES), jnp.float32),
+            jax.ShapeDtypeStruct(slopes.shape, slopes.dtype),
+        ],
+        in_specs=[vmem_spec()] * 3,
+        out_specs=[vmem_spec()] * 2,
         compiler_params=params,
         name="dots",
-    )(pooled, far_side)
+    )(pooled, far_side, slopes)
     packed = exchange(packed, "dp", shards)
     dots = [x[0:rows] for x in packed]
     dots = exchange((dots[0] + dots[1]) + (dots[2] + dots[3]), "mp", parts)
+    slopes = jnp.concatenate([slopes, lax.ppermute(slopes, "group", other_side)])
+    slopes = exchange(slopes, "dp", shards)
     embeddings, losses, update = pl.pallas_call(
-        functools.partial(score_kernel, negatives=negatives),
+        functools.partial(
+            score_kernel, texts=texts, stripes=pl.cdiv(FIRST, STRIPE), negatives=negatives
+        ),
         out_shape=[
             jax.ShapeDtypeStruct((1, per_shard, part_width), jnp.bfloat16),
             jax.ShapeDtypeStruct((1, per_shard), jnp.float32),
-            jax.ShapeDtypeStruct((ROWS, width), jnp.float32),
+            jax.ShapeDtypeStruct((ROWS, part_width), jnp.float32),
         ],
-        in_specs=[vmem_spec()] * 16 + [smem_spec()],
+        in_specs=[vmem_spec()] * 13 + [smem_spec()],
         out_specs=[vmem_spec()] * 3,
         compiler_params=params,
         name="score",
-    )(
-        ids,
-        pooled,
-        far_side,
-        *packed,
-        *dots,
-        misc,
-        slope,
-        reduced,
-        member,
-        member_rest,
-        logit_sharpness,
-    )
-    update = update + lax.ppermute(update, "group", [(0, 1), (1, 0)])
-    updates = exchange(update, "dp", shards)
-    shard = lax.axis_index("dp")
-    columns = [lax.select_n(shard ^ quarter_of(q), *updates) for q in range(shards)]
-    return (embeddings, losses, jnp.concatenate(columns, axis=1))
+    )(*packed, *slopes, *dots, misc, logit_sharpness)
+    return (embeddings, losses, update)
 
 
 def body(words, hard, vocabulary, weight, lowering, raising, sharpness):

time: 89.1 us -> 90.1 us (1.011)
  other arithmetic: 3.45 us -> 1.68 us
  local copies, waits for them, and re-layouts: 5.18 us -> 6.5 us
    ppermute x9, waiting for transfers between devices: 10.2 us -> 5.02 us  [exchange(): return [x] + [lax.ppermute(x, axis, step) for step in steps]]
    ppermute x4, waiting for transfers between devices: 11.7 us -> 16.1 us  [the longest x1 11.8 us: project(): far_chip = lax.ppermute(chip, 'dp', other_y)]
    ppermute x1, waiting for transfers between devices: 0.01 us -> 1.63 us  [project(): core1 = lax.ppermute(narrow(product(turned, 1, 1)), 'dp', other_core)]
    add x2 -> x0, other arithmetic: 1.41 us -> none  [the longest x1 0.72 us: split_body(): update = update + lax.ppermute(update, 'group', [(0, 1), (1, 0)])]
    another operation x5 -> x6, local copies, waits for them, and re-layouts: 1.45 us -> 2.66 us
    ppermute x4, starting transfers between devices: 3.7 us -> 4.61 us  [the longest x1 2.06 us: split_body(): far_side = lax.ppermute(pooled, 'group', other_side)]
    unnamed x35 -> x40, local copies, waits for them, and re-layouts: 3.73 us -> 3.83 us
  transfers between devices with their start and end apart: 16 -> 16, of which waited for: 9 -> 7; matrix products, arithmetic and copies ran while one was open for 8% -> 12% of each run, Pallas kernels for 4% -> 0%
where the time goes in v5:
time: 90.1 us; the launch traced here: 89.5 us
  Pallas kernels  29.9 us (33%)
  waiting for transfers between devices  22.8 us (25%)
  starting transfers between devices  15.7 us (17%)
  matrix products  10.9 us (12%)
  local copies, waits for them, and re-layouts  6.5 us (7%)
  between operations  2.15 us (2%)
  other arithmetic  1.68 us (2%)
    pallas_call x1, Pallas kernels, project(): pl.pallas_call(functools.partial(gather_kernel, base=base), out_shape=[ja...  17.9 us
    ppermute x1, waiting for transfers between devices, project(): far_chip = lax.ppermute(chip, 'dp', other_y)  11.8 us
    dot_general x4, matrix products, mm(): return lax.dot_general(a, b, dims, preferred_element_type=jnp.float32)  10.9 us
    ppermute x9, starting transfers between devices, exchange(): return [x] + [lax.ppermute(x, axis, step) for step in steps]  7.41 us
    ppermute x9, waiting for transfers between devices, exchange(): return [x] + [lax.ppermute(x, axis, step) for step in steps]  5.02 us
    pallas_call x1, Pallas kernels, split_body(): pl.pallas_call(functools.partial(pool_kernel, model_width=float(features...  4.14 us
    unnamed x40, local copies, waits for them, and re-layouts  3.83 us
    pallas_call x1, Pallas kernels, project(): pl.pallas_call(statistics_kernel, out_shape=[jax.ShapeDtypeStruct((extra_...  3.71 us
  transfers between devices with their start and end apart: 16, of which 7 were waited for; matrix products, arithmetic and copies ran while one was open for 12% of the time, Pallas kernels for 0%

profile of v5, /device:TPU:0, one launch (start us, length us, event | category | flops | bytes accessed | tf_op | source)
XLA Modules:
  0.0 89.5 jit_solution(6143963975610399947)
XLA Ops:
  1.3 17.9 %gather.3 = (bf16[1024,1152]{1,0:T(8,128)(2,1)}, bf16[1152,128]{1,0:T(8,128)(2,1)}) custom-call(s32[12,128]{1,0:T(8,128)S(1)} %bitcast.12, bf16[1024,16384]{1,0:T(8,128)(2,1)} %vocab_ref.1), custom_call_target="tpu_custom_call" | custom-call | tf_op jit(solution)/shard_map/gather/pallas_call | solution.py:543
  19.2 2.7 %convolution_convert_fusion.5 = bf16[1152,256]{1,0:T(8,128)(2,1)S(1)} fusion(bf16[1024,1152]{1,0:T(8,128)(2,1)} %get-tuple-element.39.turned, bf16[1024,1024]{1,0:T(8,128)(2,1)} %param.12, s32[]{:T(128)S(6)} %select_n.25), kind=kOutput, calls=%fused_computation.16 | convolution fusion | flops 604274688 | bytes 3473412 | tf_op jit(solution)/shard_map/dot_general | solution.py:127
  22.5 1.6 %collective-permute-done.5 = bf16[1152,256]{1,0:T(8,128)(2,1)S(1)} collective-permute-done((bf16[1152,256]{1,0:T(8,128)(2,1)S(1)}, bf16[1152,256]{1,0:T(8,128)(2,1)S(1)}, u32[]{:S(2)}, u32[]{:S(2)}) %collective-permute-start.5) | collective-permute-done | bytes 589856 | tf_op jit(solution)/shard_map/ppermute | solution.py:570
  24.1 2.7 %add_convert_fusion.2 = bf16[1152,256]{1,0:T(8,128)(2,1)} fusion(bf16[1152,256]{1,0:T(8,128)(2,1)S(1)} %collective-permute-done.5, bf16[1024,1152]{1,0:T(8,128)(2,1)S(1)} %copy-done, bf16[1024,1024]{1,0:T(8,128)(2,1)} %param.12, s32[]{:T(128)S(6)} %select_n.24), kind=kOutput, calls=%fused_computation.17 | convolution fusion | flops 604864512 | bytes 4063236 | tf_op jit(solution)/shard_map/dot_general | solution.py:127
  26.8 3.7 %statistics.3 = (bf16[160,256]{1,0:T(8,128)(2,1)}, s32[1]{0:T(128)}) custom-call(s32[12,128]{1,0:T(8,128)S(1)} %bitcast.13, bf16[1024,1152]{1,0:T(8,128)(2,1)} %get-tuple-element.39.turned, bf16[1152,128]{1,0:T(8,128)(2,1)} %get-tuple-element.40.member_ref, s32[3,7]{1,0:T(4,128)S(1)} %copy-done.20, bf16[16,4096]{1,0:T(8,128)(2,1)} %lower_ref.1), custom_call_target="tpu_custom_call" | custom-call | flops 339738624 | bytes 2359296 | tf_op jit(solution)/shard_map/statistics/pallas_call | solution.py:574
  31.0 2.7 %convolution_convert_fusion.3 = bf16[1152,256]{1,0:T(8,128)(2,1)} fusion(bf16[1024,1152]{1,0:T(8,128)(2,1)S(1)} %copy-done.1, bf16[1024,1024]{1,0:T(8,128)(2,1)} %param.12, s32[]{:T(128)S(6)} %select_n.27), kind=kOutput, calls=%fused_computation.14 | convolution fusion | flops 604274688 | bytes 3473412 | tf_op jit(solution)/shard_map/dot_general | solution.py:127
  34.6 2.7 %conditional.1 = (bf16[384,256]{1,0:T(8,128)(2,1)S(1)}, bf16[384,256]{1,0:T(8,128)(2,1)}, bf16[384,256]{1,0:T(8,128)(2,1)}, bf16[112,256]{1,0:T(8,128)(2,1)}, bf...) conditional(s32[]{:T(128)} %bitcast, () %tuple.18, (s32[12,128]{1,0:T(8,128)S(1)}, ...), branch_computations={%region_0.0_spmd, %region_1.0_spmd} | conditional | flops 919257088 | bytes 13935348 | solution.py:602
  37.2 3.0 %collective-permute-start.7 = (bf16[1152,256]{1,0:T(8,128)(2,1)}, bf16[1152,256]{1,0:T(8,128)(2,1)S(1)}, u32[]{:S(2)}, u32[]{:S(2)}) collective-permute-start(bf16[1152,256]{1,0:T(8,128)(2,1)} %add_convert_fusion.2), channel_id=1, source_target_pairs={{0,8},{4,12},{8,0},{12,4},{1,9},{5,13},{9,1},{13,5},{2,10},{6,14},... | collective-permute-start | bytes 1769480 | tf_op jit(solution)/shard_map/ppermute | solution.py:572
  41.2 2.7 %convolution_convert_fusion.4.own_ref = bf16[1152,256]{1,0:T(8,128)(2,1)} fusion(bf16[1024,1152]{1,0:T(8,128)(2,1)S(1)} %copy-done.1, bf16[1024,1024]{1,0:T(8,128)(2,1)} %param.12, s32[]{:T(128)S(6)} %select_n.26), kind=kOutput, calls=%fused_computation.15 | convolution fusion | flops 604274688 | bytes 3473412 | tf_op jit(solution)/shard_map/dot_general | solution.py:127
  44.0 11.8 %collective-permute-done.9.far_chip_ref = bf16[160,256]{1,0:T(8,128)(2,1)S(1)} collective-permute-done((bf16[160,256]{1,0:T(8,128)(2,1)S(1)}, bf16[160,256]{1,0:T(8,128)(2,1)S(1)}, u32[]{:S(2)}, u32[]{:S(2)}) %collective-permute-start.9) | collective-permute-done | bytes 81952 | tf_op jit(solution)/shard_map/ppermute | solution.py:593
  56.7 4.1 %pool.1 = (bf16[16,256]{1,0:T(8,128)(2,1)}, bf16[192,256]{1,0:T(8,128)(2,1)}, f32[16,256]{1,0:T(8,128)}) custom-call(s32[12,128]{1,0:T(8,128)S(1)} %bitcast.15, bf16[1152,256]{1,0:T(8,128)(2,1)} %convolution_convert_fusion.4.own_ref, bf16[1152,256]{1,0:T(8,128)(2,1)} %collective-permute-done.6.core_ref, bf16[1152,256]{1,0:T(8,128)(2,1)} %copy-done.5, ...), custom_call_target="tpu_custom_call" | custom-call | tf_op jit(solution)/shard_map/pool/pallas_call | solution.py:607
  60.8 2.1 %collective-permute-start.10 = (bf16[16,256]{1,0:T(8,128)(2,1)}, bf16[16,256]{1,0:T(8,128)(2,1)S(1)}, u32[]{:S(2)}, u32[]{:S(2)}) collective-permute-start(bf16[16,256]{1,0:T(8,128)(2,1)} %get-tuple-element.49.near_ref), channel_id=1, source_target_pairs={{0,16},{16,0},{1,17},{17,1},{2,18},{18,2},{3,19},{19,3},{4,20},{20... | collective-permute-start | bytes 24584 | tf_op jit(solution)/shard_map/ppermute | solution.py:625
  62.9 1.8 %collective-permute-done.10.far_ref = bf16[16,256]{1,0:T(8,128)(2,1)S(1)} collective-permute-done((bf16[16,256]{1,0:T(8,128)(2,1)}, bf16[16,256]{1,0:T(8,128)(2,1)S(1)}, u32[]{:S(2)}, u32[]{:S(2)}) %collective-permute-start.10) | collective-permute-done | bytes 8224 | tf_op jit(solution)/shard_map/ppermute | solution.py:625
  65.3 1.7 %dots.1 = (f32[96,128]{1,0:T(8,128)}, bf16[192,256]{1,0:T(8,128)(2,1)}) custom-call(bf16[16,256]{1,0:T(8,128)(2,1)} %get-tuple-element.49.near_ref, bf16[16,256]{1,0:T(8,128)(2,1)} %copy-done.21, bf16[192,256]{1,0:T(8,128)(2,1)} %get-tuple-element.50.slopes_ref), custom_call_target="tpu_custom_call" | custom-call | tf_op jit(solution)/shard_map/dots/pallas_call | solution.py:627
  67.0 1.7 %collective-permute-start.12 = (f32[96,128]{1,0:T(8,128)}, f32[96,128]{1,0:T(8,128)S(1)}, u32[]{:S(2)}, u32[]{:S(2)}) collective-permute-start(f32[96,128]{1,0:T(8,128)} %get-tuple-element.51.packed0), channel_id=1, source_target_pairs={{0,8},{4,12},{8,0},{12,4},{1,9},{5,13},{9,1},{13,5},{2,10},{6,14},... | collective-permute-start | bytes 147464 | tf_op jit(solution)/shard_map/ppermute | solution.py:510
  68.8 2.0 %collective-permute-start.14 = (bf16[192,256]{1,0:T(8,128)(2,1)}, bf16[192,256]{1,0:T(8,128)(2,1)S(1)}, u32[]{:S(2)}, u32[]{:S(2)}) collective-permute-start(bf16[192,256]{1,0:T(8,128)(2,1)} %get-tuple-element.52), channel_id=1, source_target_pairs={{0,16},{16,0},{1,17},{17,1},{2,18},{18,2},{3,19},{19,3},{4,20},{20... | collective-permute-start | bytes 294920 | tf_op jit(solution)/shard_map/ppermute | solution.py:641
  70.8 0.9 %constant_dynamic-update-slice_fusion.1 = bf16[384,256]{1,0:T(8,128)(2,1)S(1)} fusion(bf16[192,256]{1,0:T(8,128)(2,1)} %get-tuple-element.52), kind=kLoop, calls=%fused_computation.29 | loop fusion | bytes 196608
  71.8 2.4 %collective-permute-done.14 = bf16[192,256]{1,0:T(8,128)(2,1)S(1)} collective-permute-done((bf16[192,256]{1,0:T(8,128)(2,1)}, bf16[192,256]{1,0:T(8,128)(2,1)S(1)}, u32[]{:S(2)}, u32[]{:S(2)}) %collective-permute-start.14) | collective-permute-done | bytes 98336 | tf_op jit(solution)/shard_map/ppermute | solution.py:641
  74.5 1.2 %collective-permute-start.16 = (bf16[384,256]{1,0:T(8,128)(2,1)S(1)}, bf16[384,256]{1,0:T(8,128)(2,1)S(1)}, u32[]{:S(2)}, u32[]{:S(2)}) collective-permute-start(bf16[384,256]{1,0:T(8,128)(2,1)S(1)} %constant_dynamic-update-slice_fusion.slopes0), channel_id=1, source_target_pairs={{0,8},{4,12},{8,0},{12,4},{1,9},{5,13},{9,1},{13,5},{2,10},{6,14},... | collective-permute-start | bytes 589832 | tf_op jit(solution)/shard_map/ppermute | solution.py:510
  77.0 3.6 %collective-permute-start.20 = (f32[32,128]{1,0:T(8,128)S(1)}, f32[32,128]{1,0:T(8,128)S(1)}, u32[]{:S(2)}, u32[]{:S(2)}) collective-permute-start(f32[32,128]{1,0:T(8,128)S(1)} %fusion.18.dots0), channel_id=1, source_target_pairs={{0,3},{1,2},{2,1},{3,0},{4,7},{5,6},{6,5},{7,4},{8,11},{9,10},{10,... | collective-permute-start | bytes 49160 | tf_op jit(solution)/shard_map/ppermute | solution.py:510
  80.6 1.9 %collective-permute-done.20.dots3 = f32[32,128]{1,0:T(8,128)S(1)} collective-permute-done((f32[32,128]{1,0:T(8,128)S(1)}, f32[32,128]{1,0:T(8,128)S(1)}, u32[]{:S(2)}, u32[]{:S(2)}) %collective-permute-start.20) | collective-permute-done | bytes 16416 | tf_op jit(solution)/shard_map/ppermute | solution.py:510
  83.2 2.0 %collective-permute-done.19.dots2 = f32[32,128]{1,0:T(8,128)S(1)} collective-permute-done((f32[32,128]{1,0:T(8,128)S(1)}, f32[32,128]{1,0:T(8,128)S(1)}, u32[]{:S(2)}, u32[]{:S(2)}) %collective-permute-start.19) | collective-permute-done | bytes 16416 | tf_op jit(solution)/shard_map/ppermute | solution.py:510
  85.2 1.0 %collective-permute-done.18.dots1 = f32[32,128]{1,0:T(8,128)S(1)} collective-permute-done((f32[32,128]{1,0:T(8,128)S(1)}, f32[32,128]{1,0:T(8,128)S(1)}, u32[]{:S(2)}, u32[]{:S(2)}) %collective-permute-start.18) | collective-permute-done | bytes 16416 | tf_op jit(solution)/shard_map/ppermute | solution.py:510
  87.1 2.5 %score.1 = (bf16[1,3,1024]{2,1,0:T(4,128)(2,1)}, f32[1,3]{1,0:T(1,128)}, f32[16,1024]{1,0:T(8,128)}) custom-call(f32[96,128]{1,0:T(8,128)} %get-tuple-element.51.packed0, f32[96,128]{1,0:T(8,128)} %copy-done.13, f32[96,128]{1,0:T(8,128)} %copy-done.12, f32[96,128]{1,0:T(8,128)} %copy-done.11, bf16[384,256]{1,0:T(8,128)(2,1)} %copy-done.6, ...), custom_call_target="tpu_custom_call" | custom-call | tf_op jit(solution)/shard_map/score/pallas_call | solution.py:643
  (67 shorter events, 9.4 us)
Async XLA Ops:
  19.2 4.9 %copy-start = (bf16[1024,1152]{1,0:T(8,128)(2,1)S(1)}, bf16[1024,1152]{1,0:T(8,128)(2,1)}, u32[]{:S(2)}) copy-start(bf16[1024,1152]{1,0:T(8,128)(2,1)} %get-tuple-element.39.turned) | copy-start | bytes 7077892
  22.0 2.2 %collective-permute-start.5 = (bf16[1152,256]{1,0:T(8,128)(2,1)S(1)}, bf16[1152,256]{1,0:T(8,128)(2,1)S(1)}, u32[]{:S(2)}, u32[]{:S(2)}) collective-permute-start(bf16[1152,256]{1,0:T(8,128)(2,1)S(1)} %convolution_convert_fusion.5), channel_id=1, source_target_pairs={{0,4},{4,0},{8,12},{12,8},{1,5},{5,1},{9,13},{13,9},{2,6},{6,2},{1... | collective-permute-start | bytes 1769480 | tf_op jit(solution)/shard_map/ppermute | solution.py:570
  22.5 4.3 %copy-start.20 = (s32[3,7]{1,0:T(4,128)S(1)}, s32[3,7]{1,0:T(4,128)}, u32[]{:S(2)}) copy-start(s32[3,7]{1,0:T(4,128)} %hard_ref.1) | copy-start | bytes 256
  30.5 9.7 %collective-permute-start.8 = (bf16[160,256]{1,0:T(8,128)(2,1)}, bf16[160,256]{1,0:T(8,128)(2,1)}, u32[]{:S(2)}, u32[]{:S(2)}) collective-permute-start(bf16[160,256]{1,0:T(8,128)(2,1)} %get-tuple-element.41), channel_id=1, source_target_pairs={{0,4},{4,0},{8,12},{12,8},{1,5},{5,1},{9,13},{13,9},{2,6},{6,2},{1... | collective-permute-start | bytes 245768 | tf_op jit(solution)/shard_map/ppermute | solution.py:592
  34.4 21.4 %collective-permute-start.6 = (bf16[1152,256]{1,0:T(8,128)(2,1)}, bf16[1152,256]{1,0:T(8,128)(2,1)}, u32[]{:S(2)}, u32[]{:S(2)}) collective-permute-start(bf16[1152,256]{1,0:T(8,128)(2,1)} %convolution_convert_fusion.3), channel_id=1, source_target_pairs={{0,4},{4,0},{8,12},{12,8},{1,5},{5,1},{9,13},{13,9},{2,6},{6,2},{1... | collective-permute-start | bytes 1769480 | tf_op jit(solution)/shard_map/ppermute | solution.py:594
  34.6 5.6 %copy-start.15 = (bf16[160,256]{1,0:T(8,128)(2,1)S(1)}, bf16[160,256]{1,0:T(8,128)(2,1)}, u32[]{:S(2)}) copy-start(bf16[160,256]{1,0:T(8,128)(2,1)} %get-tuple-element.41) | copy-start | bytes 245764
  37.2 18.6 %collective-permute-start.7 = (bf16[1152,256]{1,0:T(8,128)(2,1)}, bf16[1152,256]{1,0:T(8,128)(2,1)S(1)}, u32[]{:S(2)}, u32[]{:S(2)}) collective-permute-start(bf16[1152,256]{1,0:T(8,128)(2,1)} %add_convert_fusion.2), channel_id=1, source_target_pairs={{0,8},{4,12},{8,0},{12,4},{1,9},{5,13},{9,1},{13,5},{2,10},{6,14},... | collective-permute-start | bytes 1769480 | tf_op jit(solution)/shard_map/ppermute | solution.py:572
  41.1 14.7 %collective-permute-start.9 = (bf16[160,256]{1,0:T(8,128)(2,1)S(1)}, bf16[160,256]{1,0:T(8,128)(2,1)S(1)}, u32[]{:S(2)}, u32[]{:S(2)}) collective-permute-start(bf16[160,256]{1,0:T(8,128)(2,1)S(1)} %add_convert_fusion.3.chip_ref), channel_id=1, source_target_pairs={{0,8},{4,12},{8,0},{12,4},{1,9},{5,13},{9,1},{13,5},{2,10},{6,14},... | collective-permute-start | bytes 245768 | tf_op jit(solution)/shard_map/ppermute | solution.py:593
  60.8 3.9 %collective-permute-start.10 = (bf16[16,256]{1,0:T(8,128)(2,1)}, bf16[16,256]{1,0:T(8,128)(2,1)S(1)}, u32[]{:S(2)}, u32[]{:S(2)}) collective-permute-start(bf16[16,256]{1,0:T(8,128)(2,1)} %get-tuple-element.49.near_ref), channel_id=1, source_target_pairs={{0,16},{16,0},{1,17},{17,1},{2,18},{18,2},{3,19},{19,3},{4,20},{20... | collective-permute-start | bytes 24584 | tf_op jit(solution)/shard_map/ppermute | solution.py:625
  67.0 8.7 %collective-permute-start.13 = (f32[96,128]{1,0:T(8,128)}, f32[96,128]{1,0:T(8,128)S(1)}, u32[]{:S(2)}, u32[]{:S(2)}) collective-permute-start(f32[96,128]{1,0:T(8,128)} %get-tuple-element.51.packed0), channel_id=1, source_target_pairs={{0,12},{4,8},{8,4},{12,0},{1,13},{5,9},{9,5},{13,1},{2,14},{6,10},... | collective-permute-start | bytes 147464 | tf_op jit(solution)/shard_map/ppermute | solution.py:510
  67.0 9.2 %collective-permute-start.12 = (f32[96,128]{1,0:T(8,128)}, f32[96,128]{1,0:T(8,128)S(1)}, u32[]{:S(2)}, u32[]{:S(2)}) collective-permute-start(f32[96,128]{1,0:T(8,128)} %get-tuple-element.51.packed0), channel_id=1, source_target_pairs={{0,8},{4,12},{8,0},{12,4},{1,9},{5,13},{9,1},{13,5},{2,10},{6,14},... | collective-permute-start | bytes 147464 | tf_op jit(solution)/shard_map/ppermute | solution.py:510
  68.7 7.5 %collective-permute-start.11 = (f32[96,128]{1,0:T(8,128)}, f32[96,128]{1,0:T(8,128)S(1)}, u32[]{:S(2)}, u32[]{:S(2)}) collective-permute-start(f32[96,128]{1,0:T(8,128)} %get-tuple-element.51.packed0), channel_id=1, source_target_pairs={{0,4},{4,0},{8,12},{12,8},{1,5},{5,1},{9,13},{13,9},{2,6},{6,2},{1... | collective-permute-start | bytes 147464 | tf_op jit(solution)/shard_map/ppermute | solution.py:510
  68.8 5.4 %collective-permute-start.14 = (bf16[192,256]{1,0:T(8,128)(2,1)}, bf16[192,256]{1,0:T(8,128)(2,1)S(1)}, u32[]{:S(2)}, u32[]{:S(2)}) collective-permute-start(bf16[192,256]{1,0:T(8,128)(2,1)} %get-tuple-element.52), channel_id=1, source_target_pairs={{0,16},{16,0},{1,17},{17,1},{2,18},{18,2},{3,19},{19,3},{4,20},{20... | collective-permute-start | bytes 294920 | tf_op jit(solution)/shard_map/ppermute | solution.py:641
  74.2 12.1 %copy-start.6 = (bf16[384,256]{1,0:T(8,128)(2,1)}, bf16[384,256]{1,0:T(8,128)(2,1)S(1)}, u32[]{:S(2)}) copy-start(bf16[384,256]{1,0:T(8,128)(2,1)S(1)} %constant_dynamic-update-slice_fusion.slopes0) | copy-start | bytes 589828
  74.2 12.0 %collective-permute-start.17 = (bf16[384,256]{1,0:T(8,128)(2,1)S(1)}, bf16[384,256]{1,0:T(8,128)(2,1)S(1)}, u32[]{:S(2)}, u32[]{:S(2)}) collective-permute-start(bf16[384,256]{1,0:T(8,128)(2,1)S(1)} %constant_dynamic-update-slice_fusion.slopes0), channel_id=1, source_target_pairs={{0,12},{4,8},{8,4},{12,0},{1,13},{5,9},{9,5},{13,1},{2,14},{6,10},... | collective-permute-start | bytes 589832 | tf_op jit(solution)/shard_map/ppermute | solution.py:510
  74.5 11.8 %collective-permute-start.16 = (bf16[384,256]{1,0:T(8,128)(2,1)S(1)}, bf16[384,256]{1,0:T(8,128)(2,1)S(1)}, u32[]{:S(2)}, u32[]{:S(2)}) collective-permute-start(bf16[384,256]{1,0:T(8,128)(2,1)S(1)} %constant_dynamic-update-slice_fusion.slopes0), channel_id=1, source_target_pairs={{0,8},{4,12},{8,0},{12,4},{1,9},{5,13},{9,1},{13,5},{2,10},{6,14},... | collective-permute-start | bytes 589832 | tf_op jit(solution)/shard_map/ppermute | solution.py:510
  75.7 10.6 %copy-start.11 = (f32[96,128]{1,0:T(8,128)}, f32[96,128]{1,0:T(8,128)S(1)}, u32[]{:S(2)}) copy-start(f32[96,128]{1,0:T(8,128)S(1)} %collective-permute-done.13.packed3) | copy-start | bytes 147460
  75.7 10.6 %collective-permute-start.15 = (bf16[384,256]{1,0:T(8,128)(2,1)S(1)}, bf16[384,256]{1,0:T(8,128)(2,1)S(1)}, u32[]{:S(2)}, u32[]{:S(2)}) collective-permute-start(bf16[384,256]{1,0:T(8,128)(2,1)S(1)} %constant_dynamic-update-slice_fusion.slopes0), channel_id=1, source_target_pairs={{0,4},{4,0},{8,12},{12,8},{1,5},{5,1},{9,13},{13,9},{2,6},{6,2},{1... | collective-permute-start | bytes 589832 | tf_op jit(solution)/shard_map/ppermute | solution.py:510
  76.2 10.1 %copy-start.12 = (f32[96,128]{1,0:T(8,128)}, f32[96,128]{1,0:T(8,128)S(1)}, u32[]{:S(2)}) copy-start(f32[96,128]{1,0:T(8,128)S(1)} %collective-permute-done.12.packed2) | copy-start | bytes 147460
  76.2 10.1 %copy-start.13 = (f32[96,128]{1,0:T(8,128)}, f32[96,128]{1,0:T(8,128)S(1)}, u32[]{:S(2)}) copy-start(f32[96,128]{1,0:T(8,128)S(1)} %collective-permute-done.11.packed1) | copy-start | bytes 147460
  77.0 9.4 %copy-start.16 = (f32[32,128]{1,0:T(8,128)}, f32[32,128]{1,0:T(8,128)S(1)}, u32[]{:S(2)}) copy-start(f32[32,128]{1,0:T(8,128)S(1)} %fusion.18.dots0) | copy-start | bytes 49156
  77.0 5.5 %collective-permute-start.20 = (f32[32,128]{1,0:T(8,128)S(1)}, f32[32,128]{1,0:T(8,128)S(1)}, u32[]{:S(2)}, u32[]{:S(2)}) collective-permute-start(f32[32,128]{1,0:T(8,128)S(1)} %fusion.18.dots0), channel_id=1, source_target_pairs={{0,3},{1,2},{2,1},{3,0},{4,7},{5,6},{6,5},{7,4},{8,11},{9,10},{10,... | collective-permute-start | bytes 49160 | tf_op jit(solution)/shard_map/ppermute | solution.py:510
  80.6 4.6 %collective-permute-start.19 = (f32[32,128]{1,0:T(8,128)S(1)}, f32[32,128]{1,0:T(8,128)S(1)}, u32[]{:S(2)}, u32[]{:S(2)}) collective-permute-start(f32[32,128]{1,0:T(8,128)S(1)} %fusion.18.dots0), channel_id=1, source_target_pairs={{0,2},{1,3},{2,0},{3,1},{4,6},{5,7},{6,4},{7,5},{8,10},{9,11},{10,... | collective-permute-start | bytes 49160 | tf_op jit(solution)/shard_map/ppermute | solution.py:510
  82.5 3.7 %collective-permute-start.18 = (f32[32,128]{1,0:T(8,128)S(1)}, f32[32,128]{1,0:T(8,128)S(1)}, u32[]{:S(2)}, u32[]{:S(2)}) collective-permute-start(f32[32,128]{1,0:T(8,128)S(1)} %fusion.18.dots0), channel_id=1, source_target_pairs={{0,1},{1,0},{2,3},{3,2},{4,5},{5,4},{6,7},{7,6},{8,9},{9,8},{10,11... | collective-permute-start | bytes 49160 | tf_op jit(solution)/shard_map/ppermute | solution.py:510
  (11 other events, 16.9 us)

commit v6 on v5

--- a/solution.py
+++ b/solution.py
@@ -232,47 +232,49 @@
     def within(place):
         return jnp.clip(place - base, 0, span)
 
-    def take(b, carry):
-        vocab_copy(b).wait()
-        for part in range(IDS_PER_BLOCK // IDS_PER_GROUP):
-            group = b * (IDS_PER_BLOCK // IDS_PER_GROUP) + part
-            first, last = within(bounds[group, 0]), within(bounds[group + 1, 0])
-            begin = lax.shift_right_logical(first, LANE_BITS)
-            end = lax.shift_right_logical(last + LANES - 1, LANE_BITS)
-
-            def window(p, carry):
-                at = pl.ds(pl.multiple_of(p * LANES, LANES), LANES)
-                token = token_ref[pl.ds(p, 1), :] - group * IDS_PER_GROUP
-                token = jnp.broadcast_to(token, (FEATURE_ROWS, LANES))
-                lane = (token & (LANES - 1)).astype(jnp.int16)
-                tile = lax.shift_right_arithmetic(token, LANE_BITS).astype(jnp.int16)
-                pieces = [pl.ds(f, FEATURE_ROWS) for f in range(0, features, FEATURE_ROWS)]
-                fresh = []
-                for rows in pieces:
-                    total = jnp.zeros((FEATURE_ROWS, LANES), jnp.bfloat16)
-                    for j in range(IDS_PER_GROUP // LANES):
-                        columns = pl.ds(part * IDS_PER_GROUP + j * LANES, LANES)
-                        total = jnp.where(tile == j, take_lanes(held[b, rows, columns], lane), total)
-                    fresh.append(total)
-                fresh = [turned[rows, at] + total for rows, total in zip(pieces, fresh)]
-                for rows, total in zip(pieces, fresh):
-                    turned[rows, at] = total
-                return carry
-
-            lax.fori_loop(begin, jnp.where(last > first, end, begin), window, 0)
-        return carry
-
-    lax.fori_loop(0, blocks, take, 0)
-
-
-def statistics_kernel(
-    ids_ref, turned, member_ref, hard_ref, lower_ref, extra_ref, count_ref, small
-):
+    per_block = IDS_PER_BLOCK // IDS_PER_GROUP
+
+    def take(group, carry):
+        b, part = lax.div(group, per_block), lax.rem(group, per_block)
+
+        @pl.when(part == 0)
+        def _():
+            vocab_copy(b).wait()
+
+        first, last = within(bounds[group, 0]), within(bounds[group + 1, 0])
+        begin = lax.shift_right_logical(first, LANE_BITS)
+        end = lax.shift_right_logical(last + LANES - 1, LANE_BITS)
+
+        def window(p, carry):
+            at = pl.ds(pl.multiple_of(p * LANES, LANES), LANES)
+            token = token_ref[pl.ds(p, 1), :] - group * IDS_PER_GROUP
+            token = jnp.broadcast_to(token, (FEATURE_ROWS, LANES))
+            lane = (token & (LANES - 1)).astype(jnp.int16)
+            tile = lax.shift_right_arithmetic(token, LANE_BITS).astype(jnp.int16)
+            pieces = [pl.ds(f, FEATURE_ROWS) for f in range(0, features, FEATURE_ROWS)]
+            fresh = []
+            for rows in pieces:
+                total = jnp.zeros((FEATURE_ROWS, LANES), jnp.bfloat16)
+                for j in range(IDS_PER_GROUP // LANES):
+                    start = pl.multiple_of(part * IDS_PER_GROUP + j * LANES, LANES)
+                    columns = pl.ds(start, LANES)
+                    total = jnp.where(tile == j, take_lanes(held[b, rows, columns], lane), total)
+                fresh.append(total)
+            fresh = [turned[rows, at] + total for rows, total in zip(pieces, fresh)]
+            for rows, total in zip(pieces, fresh):
+                turned[rows, at] = total
+            return carry
+
+        return lax.fori_loop(begin, jnp.where(last > first, end, begin), window, carry)
+
+    lax.fori_loop(0, groups, take, 0)
+
+
+def statistics_kernel(turned, member_ref, hard_ref, lower_ref, extra_ref, small):
     features, span = turned.shape
     stripes = pl.cdiv(span, STRIPE)
     per_shard, negatives = hard_ref.shape
     shard = lax.axis_index("dp")
-    count_ref[0] = jnp.sum((ids_ref[...] != 0).astype(jnp.float32)).astype(jnp.int32)
     small[...] = jnp.zeros_like(small)
     small[0:per_shard, stripes : stripes + negatives] = hard_ref[...].astype(jnp.float32)
     lower = lower_ref[:, pl.ds(pl.multiple_of(shard * features, LANES), features)]
@@ -320,8 +322,7 @@
     far_chip_rest,
     member_rest,
     raise_ref,
-    pooled_ref,
-    slopes_ref,
+    sent_ref,
     misc_ref,
     raised,
     total,
@@ -379,10 +380,10 @@
     counts = jnp.sum(real, axis=1, keepdims=True)
     pooled = total[0:texts] / counts
     pooled = jnp.concatenate([pooled, jnp.zeros((ROWS - texts, width), jnp.float32)])
-    pooled_ref[...] = pooled.astype(jnp.bfloat16)
+    sent_ref[0:ROWS, :] = pooled.astype(jnp.bfloat16)
     for text in range(texts):
-        rows = pl.ds(text * ROWS, ROWS)
-        slopes_ref[rows, :] = (slopes[rows, :] / counts[text : text + 1]).astype(jnp.bfloat16)
+        part = slopes[text * ROWS : (text + 1) * ROWS, :] / counts[text : text + 1]
+        sent_ref[(text + 1) * ROWS : (text + 2) * ROWS, :] = part.astype(jnp.bfloat16)
 
 
 def both_sides(near, far):
@@ -390,15 +391,17 @@
     return jnp.concatenate([jnp.where(queries, near, far), jnp.where(queries, far, near)], axis=0)
 
 
-def dots_kernel(near_ref, far_ref, slopes_ref, packed_ref, slopes_out):
-    block = both_sides(near_ref[...], far_ref[...])
+def dots_kernel(near_ref, far_ref, packed_ref, slopes_ref):
+    block = both_sides(near_ref[0:ROWS], far_ref[0:ROWS])
     rows = 2 * ROWS
     packed_ref[...] = jnp.zeros_like(packed_ref)
     packed_ref[0:rows, 0:rows] = mm(block, block, NT)
     for part in range(block.shape[1] // LANES):
         piece = block[:, part * LANES : (part + 1) * LANES]
         packed_ref[rows + part * rows : rows + (part + 1) * rows, :] = piece.astype(jnp.float32)
-    slopes_out[...] = slopes_ref[...]
+    size = near_ref.shape[0] - ROWS
+    slopes_ref[0:size] = near_ref[ROWS:]
+    slopes_ref[size:] = far_ref[ROWS:]
 
 
 def score_kernel(
@@ -571,14 +574,11 @@
         chip1 = narrow(product(turned, 0, 1) + core1.astype(jnp.float32))
         far = lax.ppermute(chip1, "dp", other_y)
         turned, _ = lax.optimization_barrier((turned, chip1))
-        extra, count = pl.pallas_call(
+        extra = pl.pallas_call(
             statistics_kernel,
-            out_shape=[
-                jax.ShapeDtypeStruct((extra_rows, STRIPE), jnp.bfloat16),
-                jax.ShapeDtypeStruct((1,), jnp.int32),
-            ],
-            in_specs=[vmem_spec()] * 5,
-            out_specs=[vmem_spec(), smem_spec()],
+            out_shape=jax.ShapeDtypeStruct((extra_rows, STRIPE), jnp.bfloat16),
+            in_specs=[vmem_spec()] * 4,
+            out_specs=vmem_spec(),
             scratch_shapes=[pltpu.VMEM((LANES, LANES), jnp.float32)],
             compiler_params=params,
             cost_estimate=pl.CostEstimate(
@@ -587,32 +587,31 @@
                 transcendentals=0,
             ),
             name="statistics",
-        )(ids, turned, member, difficult_distractors, lowering_factor_matrix)
+        )(turned, member, difficult_distractors, lowering_factor_matrix)
         chip = extra.astype(jnp.float32)
         chip = narrow(chip + lax.ppermute(extra, "dp", other_core).astype(jnp.float32))
         far_chip = lax.ppermute(chip, "dp", other_y)
         core0 = lax.ppermute(narrow(product(turned, 1, 0)), "dp", other_core)
         own0 = narrow(product(turned, 0, 0))
-        return (own0, core0, far, chip, far_chip, member), count
-
-    first, count = project(0, FIRST)
-    many = count[0] > FIRST
+        return own0, core0, far, chip, far_chip, member
+
+    first = project(0, FIRST)
+    many = jnp.sum((ids != 0).astype(jnp.int32)) > FIRST
     left = tokens - FIRST
-    shapes = jax.eval_shape(lambda: project(FIRST, left)[0])
+    shapes = jax.eval_shape(lambda: project(FIRST, left))
     rest = lax.cond(
         many,
-        lambda: project(FIRST, left)[0],
+        lambda: project(FIRST, left),
         lambda: tuple(jnp.zeros(x.shape, x.dtype) for x in shapes),
     )
-    pooled, slopes, misc = pl.pallas_call(
+    sent, misc = pl.pallas_call(
         functools.partial(pool_kernel, model_width=float(features * shards)),
         out_shape=[
-            jax.ShapeDtypeStruct((ROWS, width), jnp.bfloat16),
-            jax.ShapeDtypeStruct((texts * ROWS, width), jnp.bfloat16),
+            jax.ShapeDtypeStruct(((texts + 1) * ROWS, width), jnp.bfloat16),
             jax.ShapeDtypeStruct((ROWS, width), jnp.float32),
         ],
         in_specs=[vmem_spec()] * 14,
-        out_specs=[vmem_spec()] * 3,
+        out_specs=[vmem_spec()] * 2,
         scratch_shapes=[
             pltpu.VMEM((LANES, width), jnp.bfloat16),
             pltpu.VMEM((ROWS, width), jnp.float32),
@@ -621,25 +620,29 @@
         compiler_params=params,
         name="pool",
     )(ids, *first, *rest, raising_factor_matrix)
-    other_side = [(0, 1), (1, 0)]
-    far_side = lax.ppermute(pooled, "group", other_side)
+    far_side = lax.ppermute(sent, "group", [(0, 1), (1, 0)])
     rows = 2 * ROWS
     packed, slopes = pl.pallas_call(
         dots_kernel,
         out_shape=[
             jax.ShapeDtypeStruct((rows + width // LANES * rows, LANES), jnp.float32),
-            jax.ShapeDtypeStruct(slopes.shape, slopes.dtype),
+            jax.ShapeDtypeStruct((2 * texts * ROWS, width), jnp.bfloat16),
         ],
-        in_specs=[vmem_spec()] * 3,
+        in_specs=[vmem_spec()] * 2,
         out_specs=[vmem_spec()] * 2,
         compiler_params=params,
         name="dots",
-    )(pooled, far_side, slopes)
+    )(sent, far_side)
     packed = exchange(packed, "dp", shards)
     dots = [x[0:rows] for x in packed]
     dots = exchange((dots[0] + dots[1]) + (dots[2] + dots[3]), "mp", parts)
-    slopes = jnp.concatenate([slopes, lax.ppermute(slopes, "group", other_side)])
-    slopes = exchange(slopes, "dp", shards)
+    over_y = lax.ppermute(slopes, "dp", other_y)
+    slopes = [
+        slopes,
+        lax.ppermute(slopes, "dp", other_core),
+        over_y,
+        lax.ppermute(over_y, "dp", other_core),
+    ]
     embeddings, losses, update = pl.pallas_call(
         functools.partial(
             score_kernel, texts=texts, stripes=pl.cdiv(FIRST, STRIPE), negatives=negatives

time: 90.1 us -> 90.1 us (level)
  starting transfers between devices: 15.7 us -> 13.6 us
  waiting for transfers between devices: 22.8 us -> 24.8 us
    ppermute x2 -> x4, waiting for transfers between devices: 4.27 us -> 6.46 us  [the longest x1 3.25 us: split_body(): far_side = lax.ppermute(sent, 'group', [(0, 1), (1, 0)])]
    ppermute x1, waiting for transfers between devices: 1.63 us -> 0.01 us  [project(): core1 = lax.ppermute(narrow(product(turned, 1, 1)), 'dp', other_core)]
    ppermute x1, waiting for transfers between devices: 11.8 us -> 13.1 us  [project(): far_chip = lax.ppermute(chip, 'dp', other_y)]
    ppermute x9 -> x6, starting transfers between devices: 7.41 us -> 6.31 us  [exchange(): return [x] + [lax.ppermute(x, axis, step) for step in steps]]
    unnamed x40 -> x41, local copies, waits for them, and re-layouts: 3.83 us -> 2.92 us
    ppermute x2 -> x4, starting transfers between devices: 4.07 us -> 3.7 us  [the longest x1 1.72 us: split_body(): far_side = lax.ppermute(sent, 'group', [(0, 1), (1, 0)])]
    ppermute x9 -> x6, waiting for transfers between devices: 5.02 us -> 5.21 us  [exchange(): return [x] + [lax.ppermute(x, axis, step) for step in steps]]
  transfers between devices with their start and end apart: 16 -> 15, of which waited for: 7 -> 6; matrix products, arithmetic and copies ran while one was open for 12% -> 11% of each run, Pallas kernels for 0% -> 0%
where the time goes in v6:
time: 90.1 us; the launch traced here: 89.9 us
  Pallas kernels  30.6 us (34%)
  waiting for transfers between devices  24.8 us (28%)
  starting transfers between devices  13.6 us (15%)
  matrix products  11.7 us (13%)
  local copies, waits for them, and re-layouts  5.6 us (6%)
  between operations  2.15 us (2%)
  other arithmetic  1.4 us (2%)
    pallas_call x1, Pallas kernels, project(): pl.pallas_call(functools.partial(gather_kernel, base=base), out_shape=[ja...  18.7 us
    ppermute x1, waiting for transfers between devices, project(): far_chip = lax.ppermute(chip, 'dp', other_y)  13.1 us
    dot_general x4, matrix products, mm(): return lax.dot_general(a, b, dims, preferred_element_type=jnp.float32)  11.7 us
    ppermute x6, starting transfers between devices, exchange(): return [x] + [lax.ppermute(x, axis, step) for step in steps]  6.31 us
    ppermute x6, waiting for transfers between devices, exchange(): return [x] + [lax.ppermute(x, axis, step) for step in steps]  5.21 us
    pallas_call x1, Pallas kernels, split_body(): pl.pallas_call(functools.partial(pool_kernel, model_width=float(features...  4.14 us
    pallas_call x1, Pallas kernels, project(): pl.pallas_call(statistics_kernel, out_shape=jax.ShapeDtypeStruct((extra_r...  3.59 us
    ppermute x1, waiting for transfers between devices, split_body(): far_side = lax.ppermute(sent, 'group', [(0, 1), (1, 0)])  3.25 us
  transfers between devices with their start and end apart: 15, of which 6 were waited for; matrix products, arithmetic and copies ran while one was open for 11% of the time, Pallas kernels for 0%

profile of v6, /device:TPU:0, one launch (start us, length us, event | category | flops | bytes accessed | tf_op | source)
XLA Modules:
  0.0 89.9 jit_solution(1497459187082247172)
XLA Ops:
  0.6 0.7 copy.14
  1.3 18.7 %gather.3 = (bf16[1024,1152]{1,0:T(8,128)(2,1)}, bf16[1152,128]{1,0:T(8,128)(2,1)}) custom-call(s32[12,128]{1,0:T(8,128)S(1)} %bitcast.13, bf16[1024,16384]{1,0:T(8,128)(2,1)} %vocab_ref.1), custom_call_target="tpu_custom_call" | custom-call | tf_op jit(solution)/shard_map/gather/pallas_call | solution.py:546
  20.1 3.4 %convolution_convert_fusion.5 = bf16[1152,256]{1,0:T(8,128)(2,1)} fusion(bf16[1024,1152]{1,0:T(8,128)(2,1)} %get-tuple-element.35.turned, bf16[1024,1024]{1,0:T(8,128)(2,1)} %param.12, s32[]{:T(128)S(6)} %select_n.25), kind=kOutput, calls=%fused_computation.16 | convolution fusion | flops 604274688 | bytes 3473412 | tf_op jit(solution)/shard_map/dot_general | solution.py:127
  25.3 2.7 %conditional.1 = (bf16[384,256]{1,0:T(8,128)(2,1)S(1)}, bf16[384,256]{1,0:T(8,128)(2,1)}, bf16[384,256]{1,0:T(8,128)(2,1)}, bf16[112,256]{1,0:T(8,128)(2,1)}, bf...) conditional(s32[]{:T(128)} %convert_element_type.63, () %tuple.18, (s32[12,128]{1,0:T(8,128)S(1)}, ...), branch_computations={%region_1.0_spmd, %region_2.0_spmd} | conditional | flops 919257088 | bytes 14459664 | solution.py:602
  25.3 0.7 broadcast.8.clone
  28.0 2.9 %add_convert_fusion.2 = bf16[1152,256]{1,0:T(8,128)(2,1)} fusion(bf16[1152,256]{1,0:T(8,128)(2,1)} %collective-permute-done.5, bf16[1024,1152]{1,0:T(8,128)(2,1)S(1)} %copy-done, bf16[1024,1024]{1,0:T(8,128)(2,1)} %param.12, s32[]{:T(128)S(6)} %select_n.24), kind=kOutput, calls=%fused_computation.17 | convolution fusion | flops 604864512 | bytes 4063236 | tf_op jit(solution)/shard_map/dot_general | solution.py:127
  30.9 3.6 %statistics.3 = bf16[160,256]{1,0:T(8,128)(2,1)} custom-call(bf16[1024,1152]{1,0:T(8,128)(2,1)} %get-tuple-element.35.turned, bf16[1152,128]{1,0:T(8,128)(2,1)} %get-tuple-element.36.member_ref, s32[3,7]{1,0:T(4,128)S(1)} %copy-done.23, bf16[16,4096]{1,0:T(8,128)(2,1)S(1)} %copy-done.6), custom_call_target="tpu_custom_call" | custom-call | flops 339738624 | bytes 2359296 | tf_op jit(solution)/shard_map/statistics/pallas_call | solution.py:577
  34.6 2.7 %convolution_convert_fusion.3 = bf16[1152,256]{1,0:T(8,128)(2,1)} fusion(bf16[1024,1152]{1,0:T(8,128)(2,1)S(1)} %copy-done.1, bf16[1024,1024]{1,0:T(8,128)(2,1)} %param.12, s32[]{:T(128)S(6)} %select_n.27), kind=kOutput, calls=%fused_computation.14 | convolution fusion | flops 604274688 | bytes 3473412 | tf_op jit(solution)/shard_map/dot_general | solution.py:127
  37.7 2.6 %collective-permute-start.7 = (bf16[1152,256]{1,0:T(8,128)(2,1)}, bf16[1152,256]{1,0:T(8,128)(2,1)}, u32[]{:S(2)}, u32[]{:S(2)}) collective-permute-start(bf16[1152,256]{1,0:T(8,128)(2,1)} %add_convert_fusion.2), channel_id=1, source_target_pairs={{0,8},{4,12},{8,0},{12,4},{1,9},{5,13},{9,1},{13,5},{2,10},{6,14},... | collective-permute-start | bytes 1769480 | tf_op jit(solution)/shard_map/ppermute | solution.py:575
  40.4 2.7 %convolution_convert_fusion.4.own_ref = bf16[1152,256]{1,0:T(8,128)(2,1)} fusion(bf16[1024,1152]{1,0:T(8,128)(2,1)S(1)} %copy-done.1, bf16[1024,1024]{1,0:T(8,128)(2,1)} %param.12, s32[]{:T(128)S(6)} %select_n.26), kind=kOutput, calls=%fused_computation.15 | convolution fusion | flops 604274688 | bytes 3473412 | tf_op jit(solution)/shard_map/dot_general | solution.py:127
  43.1 13.1 %collective-permute-done.9.far_chip_ref = bf16[160,256]{1,0:T(8,128)(2,1)S(1)} collective-permute-done((bf16[160,256]{1,0:T(8,128)(2,1)S(1)}, bf16[160,256]{1,0:T(8,128)(2,1)S(1)}, u32[]{:S(2)}, u32[]{:S(2)}) %collective-permute-start.9) | collective-permute-done | bytes 81952 | tf_op jit(solution)/shard_map/ppermute | solution.py:593
  57.0 4.1 %pool.1 = (bf16[208,256]{1,0:T(8,128)(2,1)}, f32[16,256]{1,0:T(8,128)}) custom-call(s32[12,128]{1,0:T(8,128)S(1)} %bitcast.15, bf16[1152,256]{1,0:T(8,128)(2,1)} %convolution_convert_fusion.4.own_ref, bf16[1152,256]{1,0:T(8,128)(2,1)} %copy-done.5, bf16[1152,256]{1,0:T(8,128)(2,1)} %collective-permute-done.7.far_ref, bf16[160,256]{1,0:T(8,128)(2,1)} %copy-done.8, ...), custom_call_target="tpu_custom_call" | custom-call | tf_op jit(solution)/shard_map/pool/pallas_call | solution.py:607
  61.2 1.7 %collective-permute-start.10 = (bf16[208,256]{1,0:T(8,128)(2,1)}, bf16[208,256]{1,0:T(8,128)(2,1)S(1)}, u32[]{:S(2)}, u32[]{:S(2)}) collective-permute-start(bf16[208,256]{1,0:T(8,128)(2,1)} %get-tuple-element.43.near_ref), channel_id=1, source_target_pairs={{0,16},{16,0},{1,17},{17,1},{2,18},{18,2},{3,19},{19,3},{4,20},{20... | collective-permute-start | bytes 319496 | tf_op jit(solution)/shard_map/ppermute | solution.py:623
  62.9 3.2 %collective-permute-done.10.far_ref = bf16[208,256]{1,0:T(8,128)(2,1)S(1)} collective-permute-done((bf16[208,256]{1,0:T(8,128)(2,1)}, bf16[208,256]{1,0:T(8,128)(2,1)S(1)}, u32[]{:S(2)}, u32[]{:S(2)}) %collective-permute-start.10) | collective-permute-done | bytes 106528 | tf_op jit(solution)/shard_map/ppermute | solution.py:623
  66.8 1.7 %dots.1 = (f32[96,128]{1,0:T(8,128)}, bf16[384,256]{1,0:T(8,128)(2,1)}) custom-call(bf16[208,256]{1,0:T(8,128)(2,1)} %get-tuple-element.43.near_ref, bf16[208,256]{1,0:T(8,128)(2,1)} %copy-done.13), custom_call_target="tpu_custom_call" | custom-call | tf_op jit(solution)/shard_map/dots/pallas_call | solution.py:625
  68.5 1.7 %collective-permute-start.15 = (bf16[384,256]{1,0:T(8,128)(2,1)}, bf16[384,256]{1,0:T(8,128)(2,1)S(1)}, u32[]{:S(2)}, u32[]{:S(2)}) collective-permute-start(bf16[384,256]{1,0:T(8,128)(2,1)} %get-tuple-element.45.slopes0), channel_id=1, source_target_pairs={{0,8},{4,12},{8,0},{12,4},{1,9},{5,13},{9,1},{13,5},{2,10},{6,14},... | collective-permute-start | bytes 589832 | tf_op jit(solution)/shard_map/ppermute | solution.py:639
  70.5 1.5 %collective-permute-start.13 = (f32[96,128]{1,0:T(8,128)}, f32[96,128]{1,0:T(8,128)S(1)}, u32[]{:S(2)}, u32[]{:S(2)}) collective-permute-start(f32[96,128]{1,0:T(8,128)} %get-tuple-element.44.packed0), channel_id=1, source_target_pairs={{0,12},{4,8},{8,4},{12,0},{1,13},{5,9},{9,5},{13,1},{2,14},{6,10},... | collective-permute-start | bytes 147464 | tf_op jit(solution)/shard_map/ppermute | solution.py:513
  72.3 3.2 %collective-permute-done.15.slopes2 = bf16[384,256]{1,0:T(8,128)(2,1)S(1)} collective-permute-done((bf16[384,256]{1,0:T(8,128)(2,1)}, bf16[384,256]{1,0:T(8,128)(2,1)S(1)}, u32[]{:S(2)}, u32[]{:S(2)}) %collective-permute-start.15) | collective-permute-done | bytes 196640 | tf_op jit(solution)/shard_map/ppermute | solution.py:639
  76.1 0.7 fusion.18.dots0
  76.9 1.7 %collective-permute-start.17 = (f32[32,128]{1,0:T(8,128)S(1)}, f32[32,128]{1,0:T(8,128)S(1)}, u32[]{:S(2)}, u32[]{:S(2)}) collective-permute-start(f32[32,128]{1,0:T(8,128)S(1)} %fusion.18.dots0), channel_id=1, source_target_pairs={{0,1},{1,0},{2,3},{3,2},{4,5},{5,4},{6,7},{7,6},{8,9},{9,8},{10,11... | collective-permute-start | bytes 49160 | tf_op jit(solution)/shard_map/ppermute | solution.py:513
  78.5 2.6 %collective-permute-start.18 = (f32[32,128]{1,0:T(8,128)S(1)}, f32[32,128]{1,0:T(8,128)S(1)}, u32[]{:S(2)}, u32[]{:S(2)}) collective-permute-start(f32[32,128]{1,0:T(8,128)S(1)} %fusion.18.dots0), channel_id=1, source_target_pairs={{0,2},{1,3},{2,0},{3,1},{4,6},{5,7},{6,4},{7,5},{8,10},{9,11},{10,... | collective-permute-start | bytes 49160 | tf_op jit(solution)/shard_map/ppermute | solution.py:513
  82.0 1.2 %collective-permute-done.18.dots2 = f32[32,128]{1,0:T(8,128)S(1)} collective-permute-done((f32[32,128]{1,0:T(8,128)S(1)}, f32[32,128]{1,0:T(8,128)S(1)}, u32[]{:S(2)}, u32[]{:S(2)}) %collective-permute-start.18) | collective-permute-done | bytes 16416 | tf_op jit(solution)/shard_map/ppermute | solution.py:513
  83.2 3.4 %collective-permute-done.19.dots3 = f32[32,128]{1,0:T(8,128)S(1)} collective-permute-done((f32[32,128]{1,0:T(8,128)S(1)}, f32[32,128]{1,0:T(8,128)S(1)}, u32[]{:S(2)}, u32[]{:S(2)}) %collective-permute-start.19) | collective-permute-done | bytes 16416 | tf_op jit(solution)/shard_map/ppermute | solution.py:513
  87.4 2.5 %score.1 = (bf16[1,3,1024]{2,1,0:T(4,128)(2,1)}, f32[1,3]{1,0:T(1,128)}, f32[16,1024]{1,0:T(8,128)}) custom-call(f32[96,128]{1,0:T(8,128)} %get-tuple-element.44.packed0, f32[96,128]{1,0:T(8,128)} %copy-done.14, f32[96,128]{1,0:T(8,128)} %copy-done.15, f32[96,128]{1,0:T(8,128)} %copy-done.16, bf16[384,256]{1,0:T(8,128)(2,1)} %get-tuple-element.45.slopes0, ...), custom_call_target="tpu_custom_call" | custom-call | tf_op jit(solution)/shard_map/score/pallas_call | solution.py:646
  (66 shorter events, 7.3 us)
Async XLA Ops:
  20.1 3.9 %copy-start.19 = (s32[1,12,128]{2,0,1:T(1,128)S(1)}, s32[1,12,128]{2,0,1:T(1,128)}, u32[]{:S(2)}) copy-start(s32[1,12,128]{2,0,1:T(1,128)} %param.9) | copy-start | bytes 18436
  20.1 5.2 %copy-start.23 = (s32[3,7]{1,0:T(4,128)S(1)}, s32[3,7]{1,0:T(4,128)}, u32[]{:S(2)}) copy-start(s32[3,7]{1,0:T(4,128)} %hard_ref.1) | copy-start | bytes 256
  23.5 4.5 %collective-permute-start.5 = (bf16[1152,256]{1,0:T(8,128)(2,1)}, bf16[1152,256]{1,0:T(8,128)(2,1)}, u32[]{:S(2)}, u32[]{:S(2)}) collective-permute-start(bf16[1152,256]{1,0:T(8,128)(2,1)} %convolution_convert_fusion.5), channel_id=1, source_target_pairs={{0,4},{4,0},{8,12},{12,8},{1,5},{5,1},{9,13},{13,9},{2,6},{6,2},{1... | collective-permute-start | bytes 1769480 | tf_op jit(solution)/shard_map/ppermute | solution.py:573
  34.5 5.8 %copy-start.9 = (bf16[160,256]{1,0:T(8,128)(2,1)S(1)}, bf16[160,256]{1,0:T(8,128)(2,1)}, u32[]{:S(2)}) copy-start(bf16[160,256]{1,0:T(8,128)(2,1)} %statistics.3) | copy-start | bytes 245764
  34.5 5.8 %collective-permute-start.8 = (bf16[160,256]{1,0:T(8,128)(2,1)}, bf16[160,256]{1,0:T(8,128)(2,1)S(1)}, u32[]{:S(2)}, u32[]{:S(2)}) collective-permute-start(bf16[160,256]{1,0:T(8,128)(2,1)} %statistics.3), channel_id=1, source_target_pairs={{0,4},{4,0},{8,12},{12,8},{1,5},{5,1},{9,13},{13,9},{2,6},{6,2},{1... | collective-permute-start | bytes 245768 | tf_op jit(solution)/shard_map/ppermute | solution.py:592
  37.2 18.9 %collective-permute-start.6 = (bf16[1152,256]{1,0:T(8,128)(2,1)}, bf16[1152,256]{1,0:T(8,128)(2,1)S(1)}, u32[]{:S(2)}, u32[]{:S(2)}) collective-permute-start(bf16[1152,256]{1,0:T(8,128)(2,1)} %convolution_convert_fusion.3), channel_id=1, source_target_pairs={{0,4},{4,0},{8,12},{12,8},{1,5},{5,1},{9,13},{13,9},{2,6},{6,2},{1... | collective-permute-start | bytes 1769480 | tf_op jit(solution)/shard_map/ppermute | solution.py:594
  37.7 18.5 %collective-permute-start.7 = (bf16[1152,256]{1,0:T(8,128)(2,1)}, bf16[1152,256]{1,0:T(8,128)(2,1)}, u32[]{:S(2)}, u32[]{:S(2)}) collective-permute-start(bf16[1152,256]{1,0:T(8,128)(2,1)} %add_convert_fusion.2), channel_id=1, source_target_pairs={{0,8},{4,12},{8,0},{12,4},{1,9},{5,13},{9,1},{13,5},{2,10},{6,14},... | collective-permute-start | bytes 1769480 | tf_op jit(solution)/shard_map/ppermute | solution.py:575
  40.3 15.9 %collective-permute-start.9 = (bf16[160,256]{1,0:T(8,128)(2,1)S(1)}, bf16[160,256]{1,0:T(8,128)(2,1)S(1)}, u32[]{:S(2)}, u32[]{:S(2)}) collective-permute-start(bf16[160,256]{1,0:T(8,128)(2,1)S(1)} %add_convert_fusion.3.chip_ref), channel_id=1, source_target_pairs={{0,8},{4,12},{8,0},{12,4},{1,9},{5,13},{9,1},{13,5},{2,10},{6,14},... | collective-permute-start | bytes 245768 | tf_op jit(solution)/shard_map/ppermute | solution.py:593
  61.2 5.0 %collective-permute-start.10 = (bf16[208,256]{1,0:T(8,128)(2,1)}, bf16[208,256]{1,0:T(8,128)(2,1)S(1)}, u32[]{:S(2)}, u32[]{:S(2)}) collective-permute-start(bf16[208,256]{1,0:T(8,128)(2,1)} %get-tuple-element.43.near_ref), channel_id=1, source_target_pairs={{0,16},{16,0},{1,17},{17,1},{2,18},{18,2},{3,19},{19,3},{4,20},{20... | collective-permute-start | bytes 319496 | tf_op jit(solution)/shard_map/ppermute | solution.py:623
  68.5 7.0 %collective-permute-start.15 = (bf16[384,256]{1,0:T(8,128)(2,1)}, bf16[384,256]{1,0:T(8,128)(2,1)S(1)}, u32[]{:S(2)}, u32[]{:S(2)}) collective-permute-start(bf16[384,256]{1,0:T(8,128)(2,1)} %get-tuple-element.45.slopes0), channel_id=1, source_target_pairs={{0,8},{4,12},{8,0},{12,4},{1,9},{5,13},{9,1},{13,5},{2,10},{6,14},... | collective-permute-start | bytes 589832 | tf_op jit(solution)/shard_map/ppermute | solution.py:639
  70.2 5.4 %collective-permute-start.11 = (f32[96,128]{1,0:T(8,128)}, f32[96,128]{1,0:T(8,128)S(1)}, u32[]{:S(2)}, u32[]{:S(2)}) collective-permute-start(f32[96,128]{1,0:T(8,128)} %get-tuple-element.44.packed0), channel_id=1, source_target_pairs={{0,4},{4,0},{8,12},{12,8},{1,5},{5,1},{9,13},{13,9},{2,6},{6,2},{1... | collective-permute-start | bytes 147464 | tf_op jit(solution)/shard_map/ppermute | solution.py:513
  70.2 5.9 %collective-permute-start.12 = (f32[96,128]{1,0:T(8,128)}, f32[96,128]{1,0:T(8,128)S(1)}, u32[]{:S(2)}, u32[]{:S(2)}) collective-permute-start(f32[96,128]{1,0:T(8,128)} %get-tuple-element.44.packed0), channel_id=1, source_target_pairs={{0,8},{4,12},{8,0},{12,4},{1,9},{5,13},{9,1},{13,5},{2,10},{6,14},... | collective-permute-start | bytes 147464 | tf_op jit(solution)/shard_map/ppermute | solution.py:513
  70.5 5.6 %collective-permute-start.13 = (f32[96,128]{1,0:T(8,128)}, f32[96,128]{1,0:T(8,128)S(1)}, u32[]{:S(2)}, u32[]{:S(2)}) collective-permute-start(f32[96,128]{1,0:T(8,128)} %get-tuple-element.44.packed0), channel_id=1, source_target_pairs={{0,12},{4,8},{8,4},{12,0},{1,13},{5,9},{9,5},{13,1},{2,14},{6,10},... | collective-permute-start | bytes 147464 | tf_op jit(solution)/shard_map/ppermute | solution.py:513
  72.0 14.6 %collective-permute-start.14 = (bf16[384,256]{1,0:T(8,128)(2,1)}, bf16[384,256]{1,0:T(8,128)(2,1)S(1)}, u32[]{:S(2)}, u32[]{:S(2)}) collective-permute-start(bf16[384,256]{1,0:T(8,128)(2,1)} %get-tuple-element.45.slopes0), channel_id=1, source_target_pairs={{0,4},{4,0},{8,12},{12,8},{1,5},{5,1},{9,13},{13,9},{2,6},{6,2},{1... | collective-permute-start | bytes 589832 | tf_op jit(solution)/shard_map/ppermute | solution.py:642
  75.5 11.1 %copy-start.10 = (bf16[384,256]{1,0:T(8,128)(2,1)}, bf16[384,256]{1,0:T(8,128)(2,1)S(1)}, u32[]{:S(2)}) copy-start(bf16[384,256]{1,0:T(8,128)(2,1)S(1)} %collective-permute-done.15.slopes2) | copy-start | bytes 589828
  75.5 11.1 %collective-permute-start.16 = (bf16[384,256]{1,0:T(8,128)(2,1)S(1)}, bf16[384,256]{1,0:T(8,128)(2,1)S(1)}, u32[]{:S(2)}, u32[]{:S(2)}) collective-permute-start(bf16[384,256]{1,0:T(8,128)(2,1)S(1)} %collective-permute-done.15.slopes2), channel_id=1, source_target_pairs={{0,4},{4,0},{8,12},{12,8},{1,5},{5,1},{9,13},{13,9},{2,6},{6,2},{1... | collective-permute-start | bytes 589832 | tf_op jit(solution)/shard_map/ppermute | solution.py:644
  75.5 11.1 %copy-start.14 = (f32[96,128]{1,0:T(8,128)}, f32[96,128]{1,0:T(8,128)S(1)}, u32[]{:S(2)}) copy-start(f32[96,128]{1,0:T(8,128)S(1)} %collective-permute-done.11.packed1) | copy-start | bytes 147460
  76.1 10.6 %copy-start.15 = (f32[96,128]{1,0:T(8,128)}, f32[96,128]{1,0:T(8,128)S(1)}, u32[]{:S(2)}) copy-start(f32[96,128]{1,0:T(8,128)S(1)} %collective-permute-done.12.packed2) | copy-start | bytes 147460
  76.1 10.6 %copy-start.16 = (f32[96,128]{1,0:T(8,128)}, f32[96,128]{1,0:T(8,128)S(1)}, u32[]{:S(2)}) copy-start(f32[96,128]{1,0:T(8,128)S(1)} %collective-permute-done.13.packed3) | copy-start | bytes 147460
  76.8 9.8 %copy-start.18 = (f32[32,128]{1,0:T(8,128)}, f32[32,128]{1,0:T(8,128)S(1)}, u32[]{:S(2)}) copy-start(f32[32,128]{1,0:T(8,128)S(1)} %fusion.18.dots0) | copy-start | bytes 49156
  76.9 5.1 %collective-permute-start.17 = (f32[32,128]{1,0:T(8,128)S(1)}, f32[32,128]{1,0:T(8,128)S(1)}, u32[]{:S(2)}, u32[]{:S(2)}) collective-permute-start(f32[32,128]{1,0:T(8,128)S(1)} %fusion.18.dots0), channel_id=1, source_target_pairs={{0,1},{1,0},{2,3},{3,2},{4,5},{5,4},{6,7},{7,6},{8,9},{9,8},{10,11... | collective-permute-start | bytes 49160 | tf_op jit(solution)/shard_map/ppermute | solution.py:513
  78.5 4.7 %collective-permute-start.18 = (f32[32,128]{1,0:T(8,128)S(1)}, f32[32,128]{1,0:T(8,128)S(1)}, u32[]{:S(2)}, u32[]{:S(2)}) collective-permute-start(f32[32,128]{1,0:T(8,128)S(1)} %fusion.18.dots0), channel_id=1, source_target_pairs={{0,2},{1,3},{2,0},{3,1},{4,6},{5,7},{6,4},{7,5},{8,10},{9,11},{10,... | collective-permute-start | bytes 49160 | tf_op jit(solution)/shard_map/ppermute | solution.py:513
  81.1 5.5 %collective-permute-start.19 = (f32[32,128]{1,0:T(8,128)S(1)}, f32[32,128]{1,0:T(8,128)S(1)}, u32[]{:S(2)}, u32[]{:S(2)}) collective-permute-start(f32[32,128]{1,0:T(8,128)S(1)} %fusion.18.dots0), channel_id=1, source_target_pairs={{0,3},{1,2},{2,1},{3,0},{4,7},{5,6},{6,5},{7,4},{8,11},{9,10},{10,... | collective-permute-start | bytes 49160 | tf_op jit(solution)/shard_map/ppermute | solution.py:513
  82.0 4.7 %copy-start.20 = (f32[32,128]{1,0:T(8,128)}, f32[32,128]{1,0:T(8,128)S(1)}, u32[]{:S(2)}) copy-start(f32[32,128]{1,0:T(8,128)S(1)} %collective-permute-done.17.dots1) | copy-start | bytes 49156
  (11 other events, 19.8 us)

commit v7 on v6

--- a/solution.py
+++ b/solution.py
@@ -232,42 +232,37 @@
     def within(place):
         return jnp.clip(place - base, 0, span)
 
-    per_block = IDS_PER_BLOCK // IDS_PER_GROUP
-
-    def take(group, carry):
-        b, part = lax.div(group, per_block), lax.rem(group, per_block)
-
-        @pl.when(part == 0)
-        def _():
-            vocab_copy(b).wait()
-
-        first, last = within(bounds[group, 0]), within(bounds[group + 1, 0])
-        begin = lax.shift_right_logical(first, LANE_BITS)
-        end = lax.shift_right_logical(last + LANES - 1, LANE_BITS)
-
-        def window(p, carry):
-            at = pl.ds(pl.multiple_of(p * LANES, LANES), LANES)
-            token = token_ref[pl.ds(p, 1), :] - group * IDS_PER_GROUP
-            token = jnp.broadcast_to(token, (FEATURE_ROWS, LANES))
-            lane = (token & (LANES - 1)).astype(jnp.int16)
-            tile = lax.shift_right_arithmetic(token, LANE_BITS).astype(jnp.int16)
-            pieces = [pl.ds(f, FEATURE_ROWS) for f in range(0, features, FEATURE_ROWS)]
-            fresh = []
-            for rows in pieces:
-                total = jnp.zeros((FEATURE_ROWS, LANES), jnp.bfloat16)
-                for j in range(IDS_PER_GROUP // LANES):
-                    start = pl.multiple_of(part * IDS_PER_GROUP + j * LANES, LANES)
-                    columns = pl.ds(start, LANES)
-                    total = jnp.where(tile == j, take_lanes(held[b, rows, columns], lane), total)
-                fresh.append(total)
-            fresh = [turned[rows, at] + total for rows, total in zip(pieces, fresh)]
-            for rows, total in zip(pieces, fresh):
-                turned[rows, at] = total
-            return carry
-
-        return lax.fori_loop(begin, jnp.where(last > first, end, begin), window, carry)
-
-    lax.fori_loop(0, groups, take, 0)
+    def take(b, carry):
+        vocab_copy(b).wait()
+        for part in range(IDS_PER_BLOCK // IDS_PER_GROUP):
+            group = b * (IDS_PER_BLOCK // IDS_PER_GROUP) + part
+            first, last = within(bounds[group, 0]), within(bounds[group + 1, 0])
+            begin = lax.shift_right_logical(first, LANE_BITS)
+            end = lax.shift_right_logical(last + LANES - 1, LANE_BITS)
+
+            def window(p, carry):
+                at = pl.ds(pl.multiple_of(p * LANES, LANES), LANES)
+                token = token_ref[pl.ds(p, 1), :] - group * IDS_PER_GROUP
+                token = jnp.broadcast_to(token, (FEATURE_ROWS, LANES))
+                lane = (token & (LANES - 1)).astype(jnp.int16)
+                tile = lax.shift_right_arithmetic(token, LANE_BITS).astype(jnp.int16)
+                pieces = [pl.ds(f, FEATURE_ROWS) for f in range(0, features, FEATURE_ROWS)]
+                fresh = []
+                for rows in pieces:
+                    total = jnp.zeros((FEATURE_ROWS, LANES), jnp.bfloat16)
+                    for j in range(IDS_PER_GROUP // LANES):
+                        columns = pl.ds(part * IDS_PER_GROUP + j * LANES, LANES)
+                        total = jnp.where(tile == j, take_lanes(held[b, rows, columns], lane), total)
+                    fresh.append(total)
+                fresh = [turned[rows, at] + total for rows, total in zip(pieces, fresh)]
+                for rows, total in zip(pieces, fresh):
+                    turned[rows, at] = total
+                return carry
+
+            lax.fori_loop(begin, jnp.where(last > first, end, begin), window, 0)
+        return carry
+
+    lax.fori_loop(0, blocks, take, 0)
 
 
 def statistics_kernel(turned, member_ref, hard_ref, lower_ref, extra_ref, small):
@@ -312,14 +307,12 @@
     own_ref,
     core_ref,
     far_ref,
-    chip_ref,
-    far_chip_ref,
+    extra_ref,
     member_ref,
     own_rest,
     core_rest,
     far_rest,
-    chip_rest,
-    far_chip_rest,
+    extra_rest,
     member_rest,
     raise_ref,
     sent_ref,
@@ -337,26 +330,26 @@
     total[...] = jnp.zeros_like(total)
     slopes[...] = jnp.zeros_like(slopes)
 
-    def add(refs, extras, member_ref, base):
+    def add(refs, extra_ref, member_ref, base):
         span = member_ref.shape[0]
         stripes = pl.cdiv(span, STRIPE)
 
-        def summed(refs, start, size):
+        def summed(start, size):
             return sum(ref[pl.ds(start, size), :].astype(jnp.float32) for ref in refs)
 
-        misc = summed(extras, stripes * ROWS, ROWS)
+        misc = extra_ref[stripes * ROWS : (stripes + 1) * ROWS, :]
         if base == 0:
             misc_ref[...] = misc
         inverse = lax.rsqrt(misc / model_width + 1e-05)
         for k in range(stripes):
             size = min(STRIPE, span - k * STRIPE)
             scale = inverse[k : k + 1]
-            reduced = (summed(extras, k * ROWS, ROWS) * scale).astype(jnp.bfloat16)
+            reduced = (extra_ref[k * ROWS : (k + 1) * ROWS, :] * scale).astype(jnp.bfloat16)
             reduced = reduced.astype(jnp.float32)
             stacked = jnp.concatenate([reduced, jnp.broadcast_to(scale, (LANES - ROWS, STRIPE))])
             turned = stacked[:, 0:size].T
             low = turned.astype(jnp.bfloat16)
-            linear = summed(refs, k * STRIPE, size)
+            linear = summed(k * STRIPE, size)
             linear = linear * turned[:, ROWS : ROWS + 1] + mm(low, raised[...])
             sigma = 1.0 / (1.0 + jnp.exp(-linear))
             slope = (sigma * (1.0 + linear * (1.0 - sigma))).astype(jnp.bfloat16)
@@ -367,15 +360,14 @@
             spread = [reduced[:, 0:size] * member[text : text + 1] for text in range(texts)]
             slopes[...] += mm(jnp.concatenate(spread).astype(jnp.bfloat16), slope)
         start = pl.multiple_of((stripes + 1 + quarter) * ROWS, ROWS)
-        total[...] += summed(extras, start, ROWS)
-
-    add((own_ref, core_ref, far_ref), (chip_ref, far_chip_ref), member_ref, 0)
+        total[...] += extra_ref[pl.ds(start, ROWS), :]
+
+    add((own_ref, core_ref, far_ref), extra_ref, member_ref, 0)
     real = (ids_ref[...] != 0).astype(jnp.float32)
 
     @pl.when(jnp.sum(real) > member_ref.shape[0])
     def _():
-        extras = (chip_rest, far_chip_rest)
-        add((own_rest, core_rest, far_rest), extras, member_rest, member_ref.shape[0])
+        add((own_rest, core_rest, far_rest), extra_rest, member_rest, member_ref.shape[0])
 
     counts = jnp.sum(real, axis=1, keepdims=True)
     pooled = total[0:texts] / counts
@@ -589,11 +581,11 @@
             name="statistics",
         )(turned, member, difficult_distractors, lowering_factor_matrix)
         chip = extra.astype(jnp.float32)
-        chip = narrow(chip + lax.ppermute(extra, "dp", other_core).astype(jnp.float32))
-        far_chip = lax.ppermute(chip, "dp", other_y)
+        chip += lax.ppermute(extra, "dp", other_core).astype(jnp.float32)
+        extra = chip + lax.ppermute(narrow(chip), "dp", other_y).astype(jnp.float32)
         core0 = lax.ppermute(narrow(product(turned, 1, 0)), "dp", other_core)
         own0 = narrow(product(turned, 0, 0))
-        return own0, core0, far, chip, far_chip, member
+        return own0, core0, far, extra, member
 
     first = project(0, FIRST)
     many = jnp.sum((ids != 0).astype(jnp.int32)) > FIRST
@@ -610,7 +602,7 @@
             jax.ShapeDtypeStruct(((texts + 1) * ROWS, width), jnp.bfloat16),
             jax.ShapeDtypeStruct((ROWS, width), jnp.float32),
         ],
-        in_specs=[vmem_spec()] * 14,
+        in_specs=[vmem_spec()] * 12,
         out_specs=[vmem_spec()] * 2,
         scratch_shapes=[
             pltpu.VMEM((LANES, width), jnp.bfloat16),
@@ -635,7 +627,9 @@
     )(sent, far_side)
     packed = exchange(packed, "dp", shards)
     dots = [x[0:rows] for x in packed]
-    dots = exchange((dots[0] + dots[1]) + (dots[2] + dots[3]), "mp", parts)
+    dots = (dots[0] + dots[1]) + (dots[2] + dots[3])
+    slopes, dots = lax.optimization_barrier((slopes, dots))
+    dots = exchange(dots, "mp", parts)
     over_y = lax.ppermute(slopes, "dp", other_y)
     slopes = [
         slopes,

time: 90.1 us -> 88.1 us (0.978)
  Pallas kernels: 30.6 us -> 29.2 us
  starting transfers between devices: 13.6 us -> 12.6 us
    ppermute x2, waiting for transfers between devices: 13.1 us -> 7.06 us  [the longest x1 7.06 us: project(): extra = chip + lax.ppermute(narrow(chip), 'dp', other_y).astype(jnp.float32)]
    ppermute x6, waiting for transfers between devices: 5.21 us -> 8.36 us  [exchange(): return [x] + [lax.ppermute(x, axis, step) for step in steps]]
    ppermute x1, waiting for transfers between devices: 3.21 us -> 6.06 us  [split_body(): over_y = lax.ppermute(slopes, 'dp', other_y)]
    another operation x6 -> x5, local copies, waits for them, and re-layouts: 2.68 us -> 1.46 us
    pallas_call x1, Pallas kernels: 18.7 us -> 17.5 us  [project(): pl.pallas_call(functools.partial(gather_kernel, base=base), out_shape=[ja...]
    unnamed x41 -> x43, local copies, waits for them, and re-layouts: 2.92 us -> 3.92 us
  transfers between devices with their start and end apart: 15 -> 15, of which waited for: 6 -> 7; matrix products, arithmetic and copies ran while one was open for 11% -> 8% of each run, Pallas kernels for 0% -> 4%
where the time goes in v7:
time: 88.1 us; the launch traced here: 87.5 us
  Pallas kernels  29.2 us (33%)
  waiting for transfers between devices  25.1 us (28%)
  starting transfers between devices  12.6 us (14%)
  matrix products  10.8 us (12%)
  local copies, waits for them, and re-layouts  5.38 us (6%)
  between operations  2.17 us (2%)
  other arithmetic  2.09 us (2%)
    pallas_call x1, Pallas kernels, project(): pl.pallas_call(functools.partial(gather_kernel, base=base), out_shape=[ja...  17.5 us
    dot_general x4, matrix products, mm(): return lax.dot_general(a, b, dims, preferred_element_type=jnp.float32)  10.8 us
    ppermute x6, waiting for transfers between devices, exchange(): return [x] + [lax.ppermute(x, axis, step) for step in steps]  8.36 us
    ppermute x1, waiting for transfers between devices, project(): extra = chip + lax.ppermute(narrow(chip), 'dp', other_y).astype(jnp.float32)  7.06 us
    ppermute x6, starting transfers between devices, exchange(): return [x] + [lax.ppermute(x, axis, step) for step in steps]  6.25 us
    ppermute x1, waiting for transfers between devices, split_body(): over_y = lax.ppermute(slopes, 'dp', other_y)  6.06 us
    pallas_call x1, Pallas kernels, split_body(): pl.pallas_call(functools.partial(pool_kernel, model_width=float(features...  4.13 us
    unnamed x43, local copies, waits for them, and re-layouts  3.92 us
  transfers between devices with their start and end apart: 15, of which 7 were waited for; matrix products, arithmetic and copies ran while one was open for 8% of the time, Pallas kernels for 4%

profile of v7, /device:TPU:0, one launch (start us, length us, event | category | flops | bytes accessed | tf_op | source)
XLA Modules:
  0.0 87.5 jit_solution(4235752014225937944)
XLA Ops:
  1.3 17.5 %gather.3 = (bf16[1024,1152]{1,0:T(8,128)(2,1)}, bf16[1152,128]{1,0:T(8,128)(2,1)}) custom-call(s32[12,128]{1,0:T(8,128)S(1)} %bitcast.13, bf16[1024,16384]{1,0:T(8,128)(2,1)} %vocab_ref.1), custom_call_target="tpu_custom_call" | custom-call | tf_op jit(solution)/shard_map/gather/pallas_call | solution.py:538
  18.9 3.4 %convolution_convert_fusion.5 = bf16[1152,256]{1,0:T(8,128)(2,1)} fusion(bf16[1024,1152]{1,0:T(8,128)(2,1)} %get-tuple-element.36.turned, bf16[1024,1024]{1,0:T(8,128)(2,1)} %param.12, s32[]{:T(128)S(6)} %select_n.25), kind=kOutput, calls=%fused_computation.18 | convolution fusion | flops 604274688 | bytes 3473412 | tf_op jit(solution)/shard_map/dot_general | solution.py:127
  24.1 1.5 %conditional.1 = (bf16[384,256]{1,0:T(8,128)(2,1)S(1)}, bf16[384,256]{1,0:T(8,128)(2,1)}, bf16[384,256]{1,0:T(8,128)(2,1)}, f32[112,256]{1,0:T(8,128)S(1)}, bf16[384,128]{1,0:T(8,128)(2,1)S(1)}) conditional(s32[]{:T(128)} %convert_element_type.70, () %tuple.19, (s32[12,128]{1,0:T(8,128)S(1)}, bf16[1024,16384]{1,0:T(8,128)(2,1)}, ...), branch_computations={%region_1.0_spmd, %region_2.0_spmd} | conditional | flops 919400448 | bytes 14976144 | solution.py:594
  25.8 2.9 %add_convert_fusion.1 = bf16[1152,256]{1,0:T(8,128)(2,1)} fusion(bf16[1152,256]{1,0:T(8,128)(2,1)} %collective-permute-done.5, bf16[1024,1152]{1,0:T(8,128)(2,1)S(1)} %copy-done, bf16[1024,1024]{1,0:T(8,128)(2,1)} %param.12, s32[]{:T(128)S(6)} %select_n.24), kind=kOutput, calls=%fused_computation.19 | convolution fusion | flops 604864512 | bytes 4063236 | tf_op jit(solution)/shard_map/dot_general | solution.py:127
  28.7 2.5 %collective-permute-start.7 = (bf16[1152,256]{1,0:T(8,128)(2,1)}, bf16[1152,256]{1,0:T(8,128)(2,1)S(1)}, u32[]{:S(2)}, u32[]{:S(2)}) collective-permute-start(bf16[1152,256]{1,0:T(8,128)(2,1)} %add_convert_fusion.1), channel_id=1, source_target_pairs={{0,8},{4,12},{8,0},{12,4},{1,9},{5,13},{9,1},{13,5},{2,10},{6,14},... | collective-permute-start | bytes 1769480 | tf_op jit(solution)/shard_map/ppermute | solution.py:567
  31.2 3.4 %statistics.3 = bf16[160,256]{1,0:T(8,128)(2,1)} custom-call(bf16[1024,1152]{1,0:T(8,128)(2,1)} %get-tuple-element.36.turned, bf16[1152,128]{1,0:T(8,128)(2,1)} %get-tuple-element.37.member_ref, s32[3,7]{1,0:T(4,128)S(1)} %copy-done.25, bf16[16,4096]{1,0:T(8,128)(2,1)S(1)} %copy-done.8), custom_call_target="tpu_custom_call" | custom-call | flops 339738624 | bytes 2359296 | tf_op jit(solution)/shard_map/statistics/pallas_call | solution.py:569
  34.9 1.9 %convolution_convert_fusion.3 = bf16[1152,256]{1,0:T(8,128)(2,1)S(1)} fusion(bf16[1024,1152]{1,0:T(8,128)(2,1)S(1)} %copy-done.1, bf16[1024,1024]{1,0:T(8,128)(2,1)} %param.12, s32[]{:T(128)S(6)} %select_n.27), kind=kOutput, calls=%fused_computation.16 | convolution fusion | flops 604274688 | bytes 3473412 | tf_op jit(solution)/shard_map/dot_general | solution.py:127
  37.4 2.7 %convolution_convert_fusion.4.own_ref = bf16[1152,256]{1,0:T(8,128)(2,1)} fusion(bf16[1024,1152]{1,0:T(8,128)(2,1)S(1)} %copy-done.1, bf16[1024,1024]{1,0:T(8,128)(2,1)} %param.12, s32[]{:T(128)S(6)} %select_n.26), kind=kOutput, calls=%fused_computation.17 | convolution fusion | flops 604274688 | bytes 3473412 | tf_op jit(solution)/shard_map/dot_general | solution.py:127
  40.1 7.1 %collective-permute-done.9 = bf16[160,256]{1,0:T(8,128)(2,1)S(1)} collective-permute-done((bf16[160,256]{1,0:T(8,128)(2,1)S(1)}, bf16[160,256]{1,0:T(8,128)(2,1)S(1)}, u32[]{:S(2)}, u32[]{:S(2)}) %collective-permute-start.9) | collective-permute-done | bytes 81952 | tf_op jit(solution)/shard_map/ppermute | solution.py:585
  47.8 0.8 copy-done.7
  49.5 4.1 %pool.1 = (bf16[208,256]{1,0:T(8,128)(2,1)}, f32[16,256]{1,0:T(8,128)}) custom-call(s32[12,128]{1,0:T(8,128)S(1)} %bitcast.15, bf16[1152,256]{1,0:T(8,128)(2,1)} %convolution_convert_fusion.4.own_ref, bf16[1152,256]{1,0:T(8,128)(2,1)} %copy-done.7, bf16[1152,256]{1,0:T(8,128)(2,1)} %copy-done.6, f32[160,256]{1,0:T(8,128)} %convert_add_fusion.2.extra_ref, ...), custom_call_target="tpu_custom_call" | custom-call | tf_op jit(solution)/shard_map/pool/pallas_call | solution.py:599
  53.6 1.4 %collective-permute-start.10 = (bf16[208,256]{1,0:T(8,128)(2,1)}, bf16[208,256]{1,0:T(8,128)(2,1)S(1)}, u32[]{:S(2)}, u32[]{:S(2)}) collective-permute-start(bf16[208,256]{1,0:T(8,128)(2,1)} %get-tuple-element.43.near_ref), channel_id=1, source_target_pairs={{0,16},{16,0},{1,17},{17,1},{2,18},{18,2},{3,19},{19,3},{4,20},{20... | collective-permute-start | bytes 319496 | tf_op jit(solution)/shard_map/ppermute | solution.py:615
  55.0 3.6 %collective-permute-done.10.far_ref = bf16[208,256]{1,0:T(8,128)(2,1)S(1)} collective-permute-done((bf16[208,256]{1,0:T(8,128)(2,1)}, bf16[208,256]{1,0:T(8,128)(2,1)S(1)}, u32[]{:S(2)}, u32[]{:S(2)}) %collective-permute-start.10) | collective-permute-done | bytes 106528 | tf_op jit(solution)/shard_map/ppermute | solution.py:615
  59.3 1.7 %dots.1 = (f32[96,128]{1,0:T(8,128)}, bf16[384,256]{1,0:T(8,128)(2,1)}) custom-call(bf16[208,256]{1,0:T(8,128)(2,1)} %get-tuple-element.43.near_ref, bf16[208,256]{1,0:T(8,128)(2,1)} %copy-done.16), custom_call_target="tpu_custom_call" | custom-call | tf_op jit(solution)/shard_map/dots/pallas_call | solution.py:617
  61.0 1.7 %collective-permute-start.12 = (f32[96,128]{1,0:T(8,128)}, f32[96,128]{1,0:T(8,128)S(1)}, u32[]{:S(2)}, u32[]{:S(2)}) collective-permute-start(f32[96,128]{1,0:T(8,128)} %get-tuple-element.44.packed0), channel_id=1, source_target_pairs={{0,8},{4,12},{8,0},{12,4},{1,9},{5,13},{9,1},{13,5},{2,10},{6,14},... | collective-permute-start | bytes 147464 | tf_op jit(solution)/shard_map/ppermute | solution.py:505
  62.8 2.5 %collective-permute-done.12.packed2 = f32[96,128]{1,0:T(8,128)S(1)} collective-permute-done((f32[96,128]{1,0:T(8,128)}, f32[96,128]{1,0:T(8,128)S(1)}, u32[]{:S(2)}, u32[]{:S(2)}) %collective-permute-start.12) | collective-permute-done | bytes 49184 | tf_op jit(solution)/shard_map/ppermute | solution.py:505
  65.3 1.2 %collective-permute-done.13.packed3 = f32[96,128]{1,0:T(8,128)S(1)} collective-permute-done((f32[96,128]{1,0:T(8,128)}, f32[96,128]{1,0:T(8,128)S(1)}, u32[]{:S(2)}, u32[]{:S(2)}) %collective-permute-start.13) | collective-permute-done | bytes 49184 | tf_op jit(solution)/shard_map/ppermute | solution.py:505
  67.3 1.2 %collective-permute-start.15 = (bf16[384,256]{1,0:T(8,128)(2,1)}, bf16[384,256]{1,0:T(8,128)(2,1)S(1)}, u32[]{:S(2)}, u32[]{:S(2)}) collective-permute-start(bf16[384,256]{1,0:T(8,128)(2,1)} %get-tuple-element.46.slopes0), channel_id=1, source_target_pairs={{0,8},{4,12},{8,0},{12,4},{1,9},{5,13},{9,1},{13,5},{2,10},{6,14},... | collective-permute-start | bytes 589832 | tf_op jit(solution)/shard_map/ppermute | solution.py:633
  68.5 6.1 %collective-permute-done.15.slopes2 = bf16[384,256]{1,0:T(8,128)(2,1)S(1)} collective-permute-done((bf16[384,256]{1,0:T(8,128)(2,1)}, bf16[384,256]{1,0:T(8,128)(2,1)S(1)}, u32[]{:S(2)}, u32[]{:S(2)}) %collective-permute-start.15) | collective-permute-done | bytes 196640 | tf_op jit(solution)/shard_map/ppermute | solution.py:633
  74.5 1.6 %collective-permute-start.17 = (f32[32,128]{1,0:T(8,128)S(1)}, f32[32,128]{1,0:T(8,128)S(1)}, u32[]{:S(2)}, u32[]{:S(2)}) collective-permute-start(f32[32,128]{1,0:T(8,128)S(1)} %fusion.20.dots0), channel_id=1, source_target_pairs={{0,1},{1,0},{2,3},{3,2},{4,5},{5,4},{6,7},{7,6},{8,9},{9,8},{10,11... | collective-permute-start | bytes 49160 | tf_op jit(solution)/shard_map/ppermute | solution.py:505
  76.1 2.6 %collective-permute-start.18 = (f32[32,128]{1,0:T(8,128)S(1)}, f32[32,128]{1,0:T(8,128)S(1)}, u32[]{:S(2)}, u32[]{:S(2)}) collective-permute-start(f32[32,128]{1,0:T(8,128)S(1)} %fusion.20.dots0), channel_id=1, source_target_pairs={{0,2},{1,3},{2,0},{3,1},{4,6},{5,7},{6,4},{7,5},{8,10},{9,11},{10,... | collective-permute-start | bytes 49160 | tf_op jit(solution)/shard_map/ppermute | solution.py:505
  79.6 1.2 %collective-permute-done.18.dots2 = f32[32,128]{1,0:T(8,128)S(1)} collective-permute-done((f32[32,128]{1,0:T(8,128)S(1)}, f32[32,128]{1,0:T(8,128)S(1)}, u32[]{:S(2)}, u32[]{:S(2)}) %collective-permute-start.18) | collective-permute-done | bytes 16416 | tf_op jit(solution)/shard_map/ppermute | solution.py:505
  80.8 3.4 %collective-permute-done.19.dots3 = f32[32,128]{1,0:T(8,128)S(1)} collective-permute-done((f32[32,128]{1,0:T(8,128)S(1)}, f32[32,128]{1,0:T(8,128)S(1)}, u32[]{:S(2)}, u32[]{:S(2)}) %collective-permute-start.19) | collective-permute-done | bytes 16416 | tf_op jit(solution)/shard_map/ppermute | solution.py:505
  85.0 2.5 %score.1 = (bf16[1,3,1024]{2,1,0:T(4,128)(2,1)}, f32[1,3]{1,0:T(1,128)}, f32[16,1024]{1,0:T(8,128)}) custom-call(f32[96,128]{1,0:T(8,128)} %get-tuple-element.44.packed0, f32[96,128]{1,0:T(8,128)} %copy-done.17, f32[96,128]{1,0:T(8,128)} %copy-done.18, f32[96,128]{1,0:T(8,128)} %copy-done.19, bf16[384,256]{1,0:T(8,128)(2,1)} %get-tuple-element.46.slopes0, ...), custom_call_target="tpu_custom_call" | custom-call | tf_op jit(solution)/shard_map/score/pallas_call | solution.py:640
  (68 shorter events, 8.4 us)
Async XLA Ops:
  1.3 22.7 %copy-start.14 = (s32[1,12,128]{2,1,0:T(8,128)}, s32[1,12,128]{2,1,0:T(8,128)S(1)}, u32[]{:S(2)}) copy-start(s32[1,12,128]{2,1,0:T(8,128)S(1)} %copy.14) | copy-start | bytes 18436
  22.3 3.3 %collective-permute-start.5 = (bf16[1152,256]{1,0:T(8,128)(2,1)}, bf16[1152,256]{1,0:T(8,128)(2,1)}, u32[]{:S(2)}, u32[]{:S(2)}) collective-permute-start(bf16[1152,256]{1,0:T(8,128)(2,1)} %convolution_convert_fusion.5), channel_id=1, source_target_pairs={{0,4},{4,0},{8,12},{12,8},{1,5},{5,1},{9,13},{13,9},{2,6},{6,2},{1... | collective-permute-start | bytes 1769480 | tf_op jit(solution)/shard_map/ppermute | solution.py:565
  25.6 5.6 %copy-start.8 = (bf16[16,4096]{1,0:T(8,128)(2,1)S(1)}, bf16[16,4096]{1,0:T(8,128)(2,1)}, u32[]{:S(2)}) copy-start(bf16[16,4096]{1,0:T(8,128)(2,1)} %lower_ref.1) | copy-start | bytes 393220
  28.7 6.2 %copy-start.1 = (bf16[1024,1152]{1,0:T(8,128)(2,1)S(1)}, bf16[1024,1152]{1,0:T(8,128)(2,1)}, u32[]{:S(2)}) copy-start(bf16[1024,1152]{1,0:T(8,128)(2,1)} %get-tuple-element.36.turned) | copy-start | bytes 7077892
  28.7 19.2 %collective-permute-start.7 = (bf16[1152,256]{1,0:T(8,128)(2,1)}, bf16[1152,256]{1,0:T(8,128)(2,1)S(1)}, u32[]{:S(2)}, u32[]{:S(2)}) collective-permute-start(bf16[1152,256]{1,0:T(8,128)(2,1)} %add_convert_fusion.1), channel_id=1, source_target_pairs={{0,8},{4,12},{8,0},{12,4},{1,9},{5,13},{9,1},{13,5},{2,10},{6,14},... | collective-permute-start | bytes 1769480 | tf_op jit(solution)/shard_map/ppermute | solution.py:567
  34.6 2.5 %collective-permute-start.8 = (bf16[160,256]{1,0:T(8,128)(2,1)}, bf16[160,256]{1,0:T(8,128)(2,1)S(1)}, u32[]{:S(2)}, u32[]{:S(2)}) collective-permute-start(bf16[160,256]{1,0:T(8,128)(2,1)} %statistics.3), channel_id=1, source_target_pairs={{0,4},{4,0},{8,12},{12,8},{1,5},{5,1},{9,13},{13,9},{2,6},{6,2},{1... | collective-permute-start | bytes 245768 | tf_op jit(solution)/shard_map/ppermute | solution.py:584
  36.7 11.1 %collective-permute-start.6 = (bf16[1152,256]{1,0:T(8,128)(2,1)S(1)}, bf16[1152,256]{1,0:T(8,128)(2,1)S(1)}, u32[]{:S(2)}, u32[]{:S(2)}) collective-permute-start(bf16[1152,256]{1,0:T(8,128)(2,1)S(1)} %convolution_convert_fusion.3), channel_id=1, source_target_pairs={{0,4},{4,0},{8,12},{12,8},{1,5},{5,1},{9,13},{13,9},{2,6},{6,2},{1... | collective-permute-start | bytes 1769480 | tf_op jit(solution)/shard_map/ppermute | solution.py:586
  37.1 12.4 %copy-start.15 = (s32[1,12,128]{2,1,0:T(8,128)S(1)}, s32[1,12,128]{2,1,0:T(8,128)}, u32[]{:S(2)}) copy-start(s32[1,12,128]{2,1,0:T(8,128)} %copy-done.14) | copy-start | bytes 18436
  37.1 10.0 %collective-permute-start.9 = (bf16[160,256]{1,0:T(8,128)(2,1)S(1)}, bf16[160,256]{1,0:T(8,128)(2,1)S(1)}, u32[]{:S(2)}, u32[]{:S(2)}) collective-permute-start(bf16[160,256]{1,0:T(8,128)(2,1)S(1)} %fusion.19), channel_id=1, source_target_pairs={{0,8},{4,12},{8,0},{12,4},{1,9},{5,13},{9,1},{13,5},{2,10},{6,14},... | collective-permute-start | bytes 245768 | tf_op jit(solution)/shard_map/ppermute | solution.py:585
  53.6 5.0 %collective-permute-start.10 = (bf16[208,256]{1,0:T(8,128)(2,1)}, bf16[208,256]{1,0:T(8,128)(2,1)S(1)}, u32[]{:S(2)}, u32[]{:S(2)}) collective-permute-start(bf16[208,256]{1,0:T(8,128)(2,1)} %get-tuple-element.43.near_ref), channel_id=1, source_target_pairs={{0,16},{16,0},{1,17},{17,1},{2,18},{18,2},{3,19},{19,3},{4,20},{20... | collective-permute-start | bytes 319496 | tf_op jit(solution)/shard_map/ppermute | solution.py:615
  61.0 1.9 %collective-permute-start.11 = (f32[96,128]{1,0:T(8,128)}, f32[96,128]{1,0:T(8,128)S(1)}, u32[]{:S(2)}, u32[]{:S(2)}) collective-permute-start(f32[96,128]{1,0:T(8,128)} %get-tuple-element.44.packed0), channel_id=1, source_target_pairs={{0,4},{4,0},{8,12},{12,8},{1,5},{5,1},{9,13},{13,9},{2,6},{6,2},{1... | collective-permute-start | bytes 147464 | tf_op jit(solution)/shard_map/ppermute | solution.py:505
  61.0 4.4 %collective-permute-start.12 = (f32[96,128]{1,0:T(8,128)}, f32[96,128]{1,0:T(8,128)S(1)}, u32[]{:S(2)}, u32[]{:S(2)}) collective-permute-start(f32[96,128]{1,0:T(8,128)} %get-tuple-element.44.packed0), channel_id=1, source_target_pairs={{0,8},{4,12},{8,0},{12,4},{1,9},{5,13},{9,1},{13,5},{2,10},{6,14},... | collective-permute-start | bytes 147464 | tf_op jit(solution)/shard_map/ppermute | solution.py:505
  62.6 3.9 %collective-permute-start.13 = (f32[96,128]{1,0:T(8,128)}, f32[96,128]{1,0:T(8,128)S(1)}, u32[]{:S(2)}, u32[]{:S(2)}) collective-permute-start(f32[96,128]{1,0:T(8,128)} %get-tuple-element.44.packed0), channel_id=1, source_target_pairs={{0,12},{4,8},{8,4},{12,0},{1,13},{5,9},{9,5},{13,1},{2,14},{6,10},... | collective-permute-start | bytes 147464 | tf_op jit(solution)/shard_map/ppermute | solution.py:505
  62.8 21.4 %copy-start.17 = (f32[96,128]{1,0:T(8,128)}, f32[96,128]{1,0:T(8,128)S(1)}, u32[]{:S(2)}) copy-start(f32[96,128]{1,0:T(8,128)S(1)} %collective-permute-done.11.packed1) | copy-start | bytes 147460
  65.3 18.9 %copy-start.18 = (f32[96,128]{1,0:T(8,128)}, f32[96,128]{1,0:T(8,128)S(1)}, u32[]{:S(2)}) copy-start(f32[96,128]{1,0:T(8,128)S(1)} %collective-permute-done.12.packed2) | copy-start | bytes 147460
  66.6 17.7 %copy-start.19 = (f32[96,128]{1,0:T(8,128)}, f32[96,128]{1,0:T(8,128)S(1)}, u32[]{:S(2)}) copy-start(f32[96,128]{1,0:T(8,128)S(1)} %collective-permute-done.13.packed3) | copy-start | bytes 147460
  67.3 17.0 %copy-start.20 = (f32[32,128]{1,0:T(8,128)}, f32[32,128]{1,0:T(8,128)S(1)}, u32[]{:S(2)}) copy-start(f32[32,128]{1,0:T(8,128)S(1)} %fusion.20.dots0) | copy-start | bytes 49156
  67.3 7.2 %collective-permute-start.15 = (bf16[384,256]{1,0:T(8,128)(2,1)}, bf16[384,256]{1,0:T(8,128)(2,1)S(1)}, u32[]{:S(2)}, u32[]{:S(2)}) collective-permute-start(bf16[384,256]{1,0:T(8,128)(2,1)} %get-tuple-element.46.slopes0), channel_id=1, source_target_pairs={{0,8},{4,12},{8,0},{12,4},{1,9},{5,13},{9,1},{13,5},{2,10},{6,14},... | collective-permute-start | bytes 589832 | tf_op jit(solution)/shard_map/ppermute | solution.py:633
  68.5 15.8 %collective-permute-start.14 = (bf16[384,256]{1,0:T(8,128)(2,1)}, bf16[384,256]{1,0:T(8,128)(2,1)S(1)}, u32[]{:S(2)}, u32[]{:S(2)}) collective-permute-start(bf16[384,256]{1,0:T(8,128)(2,1)} %get-tuple-element.46.slopes0), channel_id=1, source_target_pairs={{0,4},{4,0},{8,12},{12,8},{1,5},{5,1},{9,13},{13,9},{2,6},{6,2},{1... | collective-permute-start | bytes 589832 | tf_op jit(solution)/shard_map/ppermute | solution.py:636
  74.5 9.8 %copy-start.11 = (bf16[384,256]{1,0:T(8,128)(2,1)}, bf16[384,256]{1,0:T(8,128)(2,1)S(1)}, u32[]{:S(2)}) copy-start(bf16[384,256]{1,0:T(8,128)(2,1)S(1)} %collective-permute-done.15.slopes2) | copy-start | bytes 589828
  74.5 9.7 %collective-permute-start.16 = (bf16[384,256]{1,0:T(8,128)(2,1)S(1)}, bf16[384,256]{1,0:T(8,128)(2,1)S(1)}, u32[]{:S(2)}, u32[]{:S(2)}) collective-permute-start(bf16[384,256]{1,0:T(8,128)(2,1)S(1)} %collective-permute-done.15.slopes2), channel_id=1, source_target_pairs={{0,4},{4,0},{8,12},{12,8},{1,5},{5,1},{9,13},{13,9},{2,6},{6,2},{1... | collective-permute-start | bytes 589832 | tf_op jit(solution)/shard_map/ppermute | solution.py:638
  74.5 5.0 %collective-permute-start.17 = (f32[32,128]{1,0:T(8,128)S(1)}, f32[32,128]{1,0:T(8,128)S(1)}, u32[]{:S(2)}, u32[]{:S(2)}) collective-permute-start(f32[32,128]{1,0:T(8,128)S(1)} %fusion.20.dots0), channel_id=1, source_target_pairs={{0,1},{1,0},{2,3},{3,2},{4,5},{5,4},{6,7},{7,6},{8,9},{9,8},{10,11... | collective-permute-start | bytes 49160 | tf_op jit(solution)/shard_map/ppermute | solution.py:505
  76.1 4.7 %collective-permute-start.18 = (f32[32,128]{1,0:T(8,128)S(1)}, f32[32,128]{1,0:T(8,128)S(1)}, u32[]{:S(2)}, u32[]{:S(2)}) collective-permute-start(f32[32,128]{1,0:T(8,128)S(1)} %fusion.20.dots0), channel_id=1, source_target_pairs={{0,2},{1,3},{2,0},{3,1},{4,6},{5,7},{6,4},{7,5},{8,10},{9,11},{10,... | collective-permute-start | bytes 49160 | tf_op jit(solution)/shard_map/ppermute | solution.py:505
  78.7 5.5 %collective-permute-start.19 = (f32[32,128]{1,0:T(8,128)S(1)}, f32[32,128]{1,0:T(8,128)S(1)}, u32[]{:S(2)}, u32[]{:S(2)}) collective-permute-start(f32[32,128]{1,0:T(8,128)S(1)} %fusion.20.dots0), channel_id=1, source_target_pairs={{0,3},{1,2},{2,1},{3,0},{4,7},{5,6},{6,5},{7,4},{8,11},{9,10},{10,... | collective-permute-start | bytes 49160 | tf_op jit(solution)/shard_map/ppermute | solution.py:505
  (12 other events, 26.3 us)

commit v8 on v7

--- a/solution.py
+++ b/solution.py
@@ -119,6 +119,7 @@
 LANES = 1 << LANE_BITS
 FEATURE_ROWS = 128
 FIRST = 1152
+TAKEN = 768
 NT = (((1,), (1,)), ((), ()))
 VMEM_BYTES = 60 * 1024 * 1024
 
@@ -246,7 +247,14 @@
                 token = jnp.broadcast_to(token, (FEATURE_ROWS, LANES))
                 lane = (token & (LANES - 1)).astype(jnp.int16)
                 tile = lax.shift_right_arithmetic(token, LANE_BITS).astype(jnp.int16)
-                pieces = [pl.ds(f, FEATURE_ROWS) for f in range(0, features, FEATURE_ROWS)]
+                pieces = [pl.ds(f, FEATURE_ROWS) for f in range(0, TAKEN, FEATURE_ROWS)]
+                short = jnp.broadcast_to(token[0:1], (IDS_PER_GROUP, LANES)).astype(jnp.int16)
+                picked = jnp.where(
+                    short == iota((IDS_PER_GROUP, LANES), 0).astype(jnp.int16), 1.0, 0.0
+                ).astype(jnp.bfloat16)
+                columns = pl.ds(part * IDS_PER_GROUP, IDS_PER_GROUP)
+                rest = pl.ds(TAKEN, features - TAKEN)
+                product = mm(held[b, rest, columns], picked).astype(jnp.bfloat16)
                 fresh = []
                 for rows in pieces:
                     total = jnp.zeros((FEATURE_ROWS, LANES), jnp.bfloat16)
@@ -254,6 +262,8 @@
                         columns = pl.ds(part * IDS_PER_GROUP + j * LANES, LANES)
                         total = jnp.where(tile == j, take_lanes(held[b, rows, columns], lane), total)
                     fresh.append(total)
+                pieces.append(rest)
+                fresh.append(product)
                 fresh = [turned[rows, at] + total for rows, total in zip(pieces, fresh)]
                 for rows, total in zip(pieces, fresh):
                     turned[rows, at] = total
@@ -302,11 +312,19 @@
         )
 
 
+def fetch(pairs, sems):
+    copies = [pltpu.make_async_copy(a, b, sems.at[n]) for n, (a, b) in enumerate(pairs)]
+    for copy in copies:
+        copy.start()
+    for copy in copies:
+        copy.wait()
+
+
 def pool_kernel(
     ids_ref,
     own_ref,
-    core_ref,
-    far_ref,
+    core_any,
+    far_any,
     extra_ref,
     member_ref,
     own_rest,
@@ -320,11 +338,15 @@
     raised,
     total,
     slopes,
+    core_ref,
+    far_ref,
+    sems,
     model_width,
 ):
     texts, length = ids_ref.shape
     width = own_ref.shape[1]
     quarter = quarter_of(lax.axis_index("dp"))
+    fetch([(core_any, core_ref), (far_any, far_ref)], sems)
     raised[...] = jnp.zeros_like(raised)
     raised[0:ROWS, :] = raise_ref[:, pl.ds(pl.multiple_of(quarter * width, LANES), width)]
     total[...] = jnp.zeros_like(total)
@@ -383,7 +405,8 @@
     return jnp.concatenate([jnp.where(queries, near, far), jnp.where(queries, far, near)], axis=0)
 
 
-def dots_kernel(near_ref, far_ref, packed_ref, slopes_ref):
+def dots_kernel(near_ref, far_any, packed_ref, slopes_ref, far_ref, sems):
+    fetch([(far_any, far_ref)], sems)
     block = both_sides(near_ref[0:ROWS], far_ref[0:ROWS])
     rows = 2 * ROWS
     packed_ref[...] = jnp.zeros_like(packed_ref)
@@ -396,28 +419,15 @@
     slopes_ref[size:] = far_ref[ROWS:]
 
 
-def score_kernel(
-    packed0,
-    packed1,
-    packed2,
-    packed3,
-    slopes0,
-    slopes1,
-    slopes2,
-    slopes3,
-    dots0,
-    dots1,
-    dots2,
-    dots3,
-    misc_ref,
-    sharp_ref,
-    embed_ref,
-    loss_ref,
-    up_ref,
-    texts,
-    stripes,
-    negatives,
-):
+def score_kernel(*refs, texts, stripes, negatives):
+    there, (misc_ref, sharp_ref, embed_ref, loss_ref, up_ref), (*here, sems) = (
+        refs[0:12],
+        refs[12:17],
+        refs[17:],
+    )
+    fetch(list(zip(there, here)), sems)
+    packed0, packed1, packed2, packed3, slopes0, slopes1, slopes2, slopes3 = here[0:8]
+    dots0, dots1, dots2, dots3 = here[8:12]
     rows = 2 * ROWS
     per_shard = loss_ref.shape[1]
     group, shard = lax.axis_index("group"), lax.axis_index("dp")
@@ -525,6 +535,7 @@
     part_width = layer_weight_matrix.shape[1]
     width = part_width // shards
     params = pltpu.CompilerParams(vmem_limit_bytes=VMEM_BYTES)
+    modest = pltpu.CompilerParams(vmem_limit_bytes=VMEM_BYTES // 4)
     other_core = [(d, d ^ 1) for d in range(shards)]
     other_y = [(d, d ^ 2) for d in range(shards)]
 
@@ -602,14 +613,17 @@
             jax.ShapeDtypeStruct(((texts + 1) * ROWS, width), jnp.bfloat16),
             jax.ShapeDtypeStruct((ROWS, width), jnp.float32),
         ],
-        in_specs=[vmem_spec()] * 12,
+        in_specs=[vmem_spec()] * 2 + [any_spec()] * 2 + [vmem_spec()] * 8,
         out_specs=[vmem_spec()] * 2,
         scratch_shapes=[
             pltpu.VMEM((LANES, width), jnp.bfloat16),
             pltpu.VMEM((ROWS, width), jnp.float32),
             pltpu.VMEM((texts * ROWS, width), jnp.float32),
+            pltpu.VMEM((FIRST, width), jnp.bfloat16),
+            pltpu.VMEM((FIRST, width), jnp.bfloat16),
+            pltpu.SemaphoreType.DMA((2,)),
         ],
-        compiler_params=params,
+        compiler_params=modest,
         name="pool",
     )(ids, *first, *rest, raising_factor_matrix)
     far_side = lax.ppermute(sent, "group", [(0, 1), (1, 0)])
@@ -620,9 +634,13 @@
             jax.ShapeDtypeStruct((rows + width // LANES * rows, LANES), jnp.float32),
             jax.ShapeDtypeStruct((2 * texts * ROWS, width), jnp.bfloat16),
         ],
-        in_specs=[vmem_spec()] * 2,
+        in_specs=[vmem_spec(), any_spec()],
         out_specs=[vmem_spec()] * 2,
-        compiler_params=params,
+        scratch_shapes=[
+            pltpu.VMEM(sent.shape, sent.dtype),
+            pltpu.SemaphoreType.DMA((1,)),
+        ],
+        compiler_params=modest,
         name="dots",
     )(sent, far_side)
     packed = exchange(packed, "dp", shards)
@@ -630,13 +648,7 @@
     dots = (dots[0] + dots[1]) + (dots[2] + dots[3])
     slopes, dots = lax.optimization_barrier((slopes, dots))
     dots = exchange(dots, "mp", parts)
-    over_y = lax.ppermute(slopes, "dp", other_y)
-    slopes = [
-        slopes,
-        lax.ppermute(slopes, "dp", other_core),
-        over_y,
-        lax.ppermute(over_y, "dp", other_core),
-    ]
+    slopes = exchange(slopes, "dp", shards)
     embeddings, losses, update = pl.pallas_call(
         functools.partial(
             score_kernel, texts=texts, stripes=pl.cdiv(FIRST, STRIPE), negatives=negatives
@@ -646,9 +658,11 @@
             jax.ShapeDtypeStruct((1, per_shard), jnp.float32),
             jax.ShapeDtypeStruct((ROWS, part_width), jnp.float32),
         ],
-        in_specs=[vmem_spec()] * 13 + [smem_spec()],
+        in_specs=[any_spec()] * 12 + [vmem_spec(), smem_spec()],
         out_specs=[vmem_spec()] * 3,
-        compiler_params=params,
+        scratch_shapes=[pltpu.VMEM(x.shape, x.dtype) for x in (*packed, *slopes, *dots)]
+        + [pltpu.SemaphoreType.DMA((12,))],
+        compiler_params=modest,
         name="score",
     )(*packed, *slopes, *dots, misc, logit_sharpness)
     return (embeddings, losses, update)

time: 88.1 us -> 74.2 us (0.84)
  waiting for transfers between devices: 25.1 us -> 16.2 us
  starting transfers between devices: 12.6 us -> 16.8 us
  Pallas kernels: 29.2 us -> 25.4 us
  local copies, waits for them, and re-layouts: 5.38 us -> 2.41 us
  other arithmetic: 2.09 us -> 0.69 us
    ppermute x3 -> x0, waiting for transfers between devices: 6.06 us -> none  [the longest x1 6.06 us: split_body(): over_y = lax.ppermute(slopes, 'dp', other_y)]
    ppermute x6 -> x9, starting transfers between devices: 6.25 us -> 11.2 us  [exchange(): return [x] + [lax.ppermute(x, axis, step) for step in steps]]
    ppermute x6 -> x9, waiting for transfers between devices: 8.36 us -> 5.26 us  [exchange(): return [x] + [lax.ppermute(x, axis, step) for step in steps]]
    unnamed x43 -> x21, local copies, waits for them, and re-layouts: 3.92 us -> 1 us
    pallas_call x1, Pallas kernels: 17.5 us -> 15.9 us  [project(): pl.pallas_call(functools.partial(gather_kernel, base=base), out_shape=[ja...]
    pallas_call x1, Pallas kernels: 1.69 us -> 0.26 us  [split_body(): pl.pallas_call(dots_kernel, out_shape=[jax.ShapeDtypeStruct((rows + width...]
    ppermute x3 -> x0, starting transfers between devices: 1.16 us -> none  [the longest x1 1.16 us: split_body(): over_y = lax.ppermute(slopes, 'dp', other_y)]
    pallas_call x1, Pallas kernels: 4.13 us -> 3.1 us  [split_body(): pl.pallas_call(functools.partial(pool_kernel, model_width=float(features...]
  transfers between devices with their start and end apart: 15 -> 15, of which waited for: 7 -> 5; matrix products, arithmetic and copies ran while one was open for 8% -> 8% of each run, Pallas kernels for 4% -> 5%
where the time goes in v8:
time: 74.2 us; the launch traced here: 73.7 us
  Pallas kernels  25.4 us (34%)
  starting transfers between devices  16.8 us (23%)
  waiting for transfers between devices  16.2 us (22%)
  matrix products  10 us (13%)
  local copies, waits for them, and re-layouts  2.41 us (3%)
  between operations  2.17 us (3%)
    pallas_call x1, Pallas kernels, project(): pl.pallas_call(functools.partial(gather_kernel, base=base), out_shape=[ja...  15.9 us
    ppermute x9, starting transfers between devices, exchange(): return [x] + [lax.ppermute(x, axis, step) for step in steps]  11.2 us
    dot_general x4, matrix products, mm(): return lax.dot_general(a, b, dims, preferred_element_type=jnp.float32)  10 us
    ppermute x1, waiting for transfers between devices, project(): extra = chip + lax.ppermute(narrow(chip), 'dp', other_y).astype(jnp.float32)  7.85 us
    ppermute x9, waiting for transfers between devices, exchange(): return [x] + [lax.ppermute(x, axis, step) for step in steps]  5.26 us
    pallas_call x1, Pallas kernels, project(): pl.pallas_call(statistics_kernel, out_shape=jax.ShapeDtypeStruct((extra_r...  3.44 us
    pallas_call x1, Pallas kernels, split_body(): pl.pallas_call(functools.partial(pool_kernel, model_width=float(features...  3.1 us
    ppermute x1, waiting for transfers between devices, split_body(): far_side = lax.ppermute(sent, 'group', [(0, 1), (1, 0)])  3.09 us
  transfers between devices with their start and end apart: 15, of which 5 were waited for; matrix products, arithmetic and copies ran while one was open for 8% of the time, Pallas kernels for 5%

profile of v8, /device:TPU:0, one launch (start us, length us, event | category | flops | bytes accessed | tf_op | source)
XLA Modules:
  0.0 73.7 jit_solution(8087750617905687073)
XLA Ops:
  0.6 0.7 copy.14
  1.3 15.9 %gather.3 = (bf16[1024,1152]{1,0:T(8,128)(2,1)}, bf16[1152,128]{1,0:T(8,128)(2,1)}) custom-call(s32[12,128]{1,0:T(8,128)S(1)} %bitcast.13, bf16[1024,16384]{1,0:T(8,128)(2,1)} %vocab_ref.1), custom_call_target="tpu_custom_call" | custom-call | tf_op jit(solution)/shard_map/gather/pallas_call | solution.py:549
  17.3 3.4 %convolution_convert_fusion.5 = bf16[1152,256]{1,0:T(8,128)(2,1)} fusion(bf16[1024,1152]{1,0:T(8,128)(2,1)} %get-tuple-element.36.turned, bf16[1024,1024]{1,0:T(8,128)(2,1)} %param.12, s32[]{:T(128)S(6)} %select_n.25), kind=kOutput, calls=%fused_computation.18 | convolution fusion | flops 604274688 | bytes 3473412 | tf_op jit(solution)/shard_map/dot_general | solution.py:128
  22.5 1.4 %conditional.1 = (bf16[384,256]{1,0:T(8,128)(2,1)S(1)}, bf16[384,256]{1,0:T(8,128)(2,1)}, bf16[384,256]{1,0:T(8,128)(2,1)}, f32[112,256]{1,0:T(8,128)S(1)}, bf16[384,128]{1,0:T(8,128)(2,1)S(1)}) conditional(s32[]{:T(128)} %convert_element_type.70, () %tuple.19, (s32[12,128]{1,0:T(8,128)S(1)}, bf16[1024,16384]{1,0:T(8,128)(2,1)}, ...), branch_computations={%region_1.0_spmd, %region_2.0_spmd} | conditional | flops 919400448 | bytes 14976144 | solution.py:605
  22.5 0.7 broadcast.8.clone
  23.2 0.7 broadcast.8.clone.1
  24.2 2.9 %add_convert_fusion.1 = bf16[1152,256]{1,0:T(8,128)(2,1)} fusion(bf16[1152,256]{1,0:T(8,128)(2,1)} %collective-permute-done.5, bf16[1024,1152]{1,0:T(8,128)(2,1)S(1)} %copy-done.2, bf16[1024,1024]{1,0:T(8,128)(2,1)} %param.12, s32[]{:T(128)S(6)} %select_n.24), kind=kOutput, calls=%fused_computation.19 | convolution fusion | flops 604864512 | bytes 4063236 | tf_op jit(solution)/shard_map/dot_general | solution.py:128
  27.1 2.5 %collective-permute-start.7 = (bf16[1152,256]{1,0:T(8,128)(2,1)}, bf16[1152,256]{1,0:T(8,128)(2,1)S(1)}, u32[]{:S(2)}, u32[]{:S(2)}) collective-permute-start(bf16[1152,256]{1,0:T(8,128)(2,1)} %add_convert_fusion.1), channel_id=1, source_target_pairs={{0,8},{4,12},{8,0},{12,4},{1,9},{5,13},{9,1},{13,5},{2,10},{6,14},... | collective-permute-start | bytes 1769480 | tf_op jit(solution)/shard_map/ppermute | solution.py:578
  29.6 3.4 %statistics.3 = bf16[160,256]{1,0:T(8,128)(2,1)} custom-call(bf16[1024,1152]{1,0:T(8,128)(2,1)} %get-tuple-element.36.turned, bf16[1152,128]{1,0:T(8,128)(2,1)} %get-tuple-element.37.member_ref, s32[3,7]{1,0:T(4,128)S(1)} %copy-done.14, bf16[16,4096]{1,0:T(8,128)(2,1)S(1)} %copy-done.8), custom_call_target="tpu_custom_call" | custom-call | flops 339738624 | bytes 2359296 | tf_op jit(solution)/shard_map/statistics/pallas_call | solution.py:580
  33.3 1.9 %convolution_convert_fusion.3 = bf16[1152,256]{1,0:T(8,128)(2,1)S(1)} fusion(bf16[1024,1152]{1,0:T(8,128)(2,1)S(1)} %copy-done.3, bf16[1024,1024]{1,0:T(8,128)(2,1)} %param.12, s32[]{:T(128)S(6)} %select_n.27), kind=kOutput, calls=%fused_computation.16 | convolution fusion | flops 604274688 | bytes 3473412 | tf_op jit(solution)/shard_map/dot_general | solution.py:128
  35.9 1.9 %convolution_convert_fusion.4.own_ref = bf16[1152,256]{1,0:T(8,128)(2,1)S(1)} fusion(bf16[1024,1152]{1,0:T(8,128)(2,1)S(1)} %copy-done.3, bf16[1024,1024]{1,0:T(8,128)(2,1)} %param.12, s32[]{:T(128)S(6)} %select_n.26), kind=kOutput, calls=%fused_computation.17 | convolution fusion | flops 604274688 | bytes 3473412 | tf_op jit(solution)/shard_map/dot_general | solution.py:128
  37.7 7.9 %collective-permute-done.9 = bf16[160,256]{1,0:T(8,128)(2,1)S(1)} collective-permute-done((bf16[160,256]{1,0:T(8,128)(2,1)S(1)}, bf16[160,256]{1,0:T(8,128)(2,1)S(1)}, u32[]{:S(2)}, u32[]{:S(2)}) %collective-permute-start.9) | collective-permute-done | bytes 81952 | tf_op jit(solution)/shard_map/ppermute | solution.py:596
  45.7 3.1 %pool.1 = (bf16[208,256]{1,0:T(8,128)(2,1)S(1)}, f32[16,256]{1,0:T(8,128)S(1)}) custom-call(s32[12,128]{1,0:T(8,128)S(1)} %bitcast.15, bf16[1152,256]{1,0:T(8,128)(2,1)S(1)} %convolution_convert_fusion.4.own_ref, bf16[1152,256]{1,0:T(8,128)(2,1)S(1)} %collective-permute-done.6.core_any, bf16[1152,256]{1,0:T(8,128)(2,1)S(1)} %collective-permute-done.7.far_any, ...), custom_call_target="tpu_custom_call" | custom-call | tf_op jit(solution)/shard_map/pool/pallas_call | solution.py:610
  48.8 1.8 %collective-permute-start.10 = (bf16[208,256]{1,0:T(8,128)(2,1)S(1)}, bf16[208,256]{1,0:T(8,128)(2,1)S(1)}, u32[]{:S(2)}, u32[]{:S(2)}) collective-permute-start(bf16[208,256]{1,0:T(8,128)(2,1)S(1)} %get-tuple-element.43.near_ref), channel_id=1, source_target_pairs={{0,16},{16,0},{1,17},{17,1},{2,18},{18,2},{3,19},{19,3},{4,20},{20... | collective-permute-start | bytes 319496 | tf_op jit(solution)/shard_map/ppermute | solution.py:629
  50.6 3.1 %collective-permute-done.10.far_any = bf16[208,256]{1,0:T(8,128)(2,1)S(1)} collective-permute-done((bf16[208,256]{1,0:T(8,128)(2,1)S(1)}, bf16[208,256]{1,0:T(8,128)(2,1)S(1)}, u32[]{:S(2)}, u32[]{:S(2)}) %collective-permute-start.10) | collective-permute-done | bytes 106528 | tf_op jit(solution)/shard_map/ppermute | solution.py:629
  54.0 1.7 %collective-permute-start.12 = (f32[96,128]{1,0:T(8,128)S(1)}, f32[96,128]{1,0:T(8,128)S(1)}, u32[]{:S(2)}, u32[]{:S(2)}) collective-permute-start(f32[96,128]{1,0:T(8,128)S(1)} %get-tuple-element.44.refs_0_), channel_id=1, source_target_pairs={{0,8},{4,12},{8,0},{12,4},{1,9},{5,13},{9,1},{13,5},{2,10},{6,14},... | collective-permute-start | bytes 147464 | tf_op jit(solution)/shard_map/ppermute | solution.py:515
  55.9 2.3 %collective-permute-done.12.refs_2_ = f32[96,128]{1,0:T(8,128)S(1)} collective-permute-done((f32[96,128]{1,0:T(8,128)S(1)}, f32[96,128]{1,0:T(8,128)S(1)}, u32[]{:S(2)}, u32[]{:S(2)}) %collective-permute-start.12) | collective-permute-done | bytes 49184 | tf_op jit(solution)/shard_map/ppermute | solution.py:515
  58.2 1.2 %collective-permute-done.13.refs_3_ = f32[96,128]{1,0:T(8,128)S(1)} collective-permute-done((f32[96,128]{1,0:T(8,128)S(1)}, f32[96,128]{1,0:T(8,128)S(1)}, u32[]{:S(2)}, u32[]{:S(2)}) %collective-permute-start.13) | collective-permute-done | bytes 49184 | tf_op jit(solution)/shard_map/ppermute | solution.py:515
  59.6 1.1 %collective-permute-start.15 = (bf16[384,256]{1,0:T(8,128)(2,1)S(1)}, bf16[384,256]{1,0:T(8,128)(2,1)S(1)}, u32[]{:S(2)}, u32[]{:S(2)}) collective-permute-start(bf16[384,256]{1,0:T(8,128)(2,1)S(1)} %get-tuple-element.46.refs_4_), channel_id=1, source_target_pairs={{0,8},{4,12},{8,0},{12,4},{1,9},{5,13},{9,1},{13,5},{2,10},{6,14},... | collective-permute-start | bytes 589832 | tf_op jit(solution)/shard_map/ppermute | solution.py:515
  61.3 1.6 %collective-permute-start.17 = (f32[32,128]{1,0:T(8,128)S(1)}, f32[32,128]{1,0:T(8,128)S(1)}, u32[]{:S(2)}, u32[]{:S(2)}) collective-permute-start(f32[32,128]{1,0:T(8,128)S(1)} %fusion.20.refs_8_), channel_id=1, source_target_pairs={{0,1},{1,0},{2,3},{3,2},{4,5},{5,4},{6,7},{7,6},{8,9},{9,8},{10,11... | collective-permute-start | bytes 49160 | tf_op jit(solution)/shard_map/ppermute | solution.py:515
  62.9 2.6 %collective-permute-start.18 = (f32[32,128]{1,0:T(8,128)S(1)}, f32[32,128]{1,0:T(8,128)S(1)}, u32[]{:S(2)}, u32[]{:S(2)}) collective-permute-start(f32[32,128]{1,0:T(8,128)S(1)} %fusion.20.refs_8_), channel_id=1, source_target_pairs={{0,2},{1,3},{2,0},{3,1},{4,6},{5,7},{6,4},{7,5},{8,10},{9,11},{10,... | collective-permute-start | bytes 49160 | tf_op jit(solution)/shard_map/ppermute | solution.py:515
  65.5 3.2 %collective-permute-start.19 = (f32[32,128]{1,0:T(8,128)S(1)}, f32[32,128]{1,0:T(8,128)S(1)}, u32[]{:S(2)}, u32[]{:S(2)}) collective-permute-start(f32[32,128]{1,0:T(8,128)S(1)} %fusion.20.refs_8_), channel_id=1, source_target_pairs={{0,3},{1,2},{2,1},{3,0},{4,7},{5,6},{6,5},{7,4},{8,11},{9,10},{10,... | collective-permute-start | bytes 49160 | tf_op jit(solution)/shard_map/ppermute | solution.py:515
  69.3 1.7 %collective-permute-done.19.refs_11_ = f32[32,128]{1,0:T(8,128)S(1)} collective-permute-done((f32[32,128]{1,0:T(8,128)S(1)}, f32[32,128]{1,0:T(8,128)S(1)}, u32[]{:S(2)}, u32[]{:S(2)}) %collective-permute-start.19) | collective-permute-done | bytes 16416 | tf_op jit(solution)/shard_map/ppermute | solution.py:515
  71.1 2.6 %score.1 = (bf16[1,3,1024]{2,1,0:T(4,128)(2,1)}, f32[1,3]{1,0:T(1,128)}, f32[16,1024]{1,0:T(8,128)}) custom-call(f32[96,128]{1,0:T(8,128)S(1)} %get-tuple-element.44.refs_0_, f32[96,128]{1,0:T(8,128)S(1)} %collective-permute-done.11.refs_1_, f32[96,128]{1,0:T(8,128)S(1)} %collective-permute-done.12.refs_2_, f32[96,128]{1,0:T(8,128)S(1)} %collective-permute-done.13.refs_3_, ...), custom_call_target="tpu_custom_call" | custom-call | tf_op jit(solution)/shard_map/score/pallas_call | solution.py:652
  (46 shorter events, 3.7 us)
Async XLA Ops:
  1.3 21.1 %copy-start.11 = (s32[1,12,128]{2,1,0:T(8,128)}, s32[1,12,128]{2,1,0:T(8,128)S(1)}, u32[]{:S(2)}) copy-start(s32[1,12,128]{2,1,0:T(8,128)S(1)} %copy.14) | copy-start | bytes 18436
  17.3 3.9 %copy-start.13 = (s32[1,12,128]{2,0,1:T(1,128)S(1)}, s32[1,12,128]{2,0,1:T(1,128)}, u32[]{:S(2)}) copy-start(s32[1,12,128]{2,0,1:T(1,128)} %param.9) | copy-start | bytes 18436
  20.7 3.3 %collective-permute-start.5 = (bf16[1152,256]{1,0:T(8,128)(2,1)}, bf16[1152,256]{1,0:T(8,128)(2,1)}, u32[]{:S(2)}, u32[]{:S(2)}) collective-permute-start(bf16[1152,256]{1,0:T(8,128)(2,1)} %convolution_convert_fusion.5), channel_id=1, source_target_pairs={{0,4},{4,0},{8,12},{12,8},{1,5},{5,1},{9,13},{13,9},{2,6},{6,2},{1... | collective-permute-start | bytes 1769480 | tf_op jit(solution)/shard_map/ppermute | solution.py:576
  23.9 5.7 %copy-start.8 = (bf16[16,4096]{1,0:T(8,128)(2,1)S(1)}, bf16[16,4096]{1,0:T(8,128)(2,1)}, u32[]{:S(2)}) copy-start(bf16[16,4096]{1,0:T(8,128)(2,1)} %lower_ref.1) | copy-start | bytes 393220
  24.0 5.7 %copy-start.14 = (s32[3,7]{1,0:T(4,128)S(1)}, s32[3,7]{1,0:T(4,128)}, u32[]{:S(2)}) copy-start(s32[3,7]{1,0:T(4,128)} %hard_ref.1) | copy-start | bytes 256
  27.1 6.2 %copy-start.3 = (bf16[1024,1152]{1,0:T(8,128)(2,1)S(1)}, bf16[1024,1152]{1,0:T(8,128)(2,1)}, u32[]{:S(2)}) copy-start(bf16[1024,1152]{1,0:T(8,128)(2,1)} %get-tuple-element.36.turned) | copy-start | bytes 7077892
  27.1 18.5 %collective-permute-start.7 = (bf16[1152,256]{1,0:T(8,128)(2,1)}, bf16[1152,256]{1,0:T(8,128)(2,1)S(1)}, u32[]{:S(2)}, u32[]{:S(2)}) collective-permute-start(bf16[1152,256]{1,0:T(8,128)(2,1)} %add_convert_fusion.1), channel_id=1, source_target_pairs={{0,8},{4,12},{8,0},{12,4},{1,9},{5,13},{9,1},{13,5},{2,10},{6,14},... | collective-permute-start | bytes 1769480 | tf_op jit(solution)/shard_map/ppermute | solution.py:578
  33.1 2.5 %copy-start.7 = (bf16[160,256]{1,0:T(8,128)(2,1)S(1)}, bf16[160,256]{1,0:T(8,128)(2,1)}, u32[]{:S(2)}) copy-start(bf16[160,256]{1,0:T(8,128)(2,1)} %statistics.3) | copy-start | bytes 245764
  33.1 2.5 %collective-permute-start.8 = (bf16[160,256]{1,0:T(8,128)(2,1)}, bf16[160,256]{1,0:T(8,128)(2,1)S(1)}, u32[]{:S(2)}, u32[]{:S(2)}) collective-permute-start(bf16[160,256]{1,0:T(8,128)(2,1)} %statistics.3), channel_id=1, source_target_pairs={{0,4},{4,0},{8,12},{12,8},{1,5},{5,1},{9,13},{13,9},{2,6},{6,2},{1... | collective-permute-start | bytes 245768 | tf_op jit(solution)/shard_map/ppermute | solution.py:595
  35.2 10.4 %collective-permute-start.6 = (bf16[1152,256]{1,0:T(8,128)(2,1)S(1)}, bf16[1152,256]{1,0:T(8,128)(2,1)S(1)}, u32[]{:S(2)}, u32[]{:S(2)}) collective-permute-start(bf16[1152,256]{1,0:T(8,128)(2,1)S(1)} %convolution_convert_fusion.3), channel_id=1, source_target_pairs={{0,4},{4,0},{8,12},{12,8},{1,5},{5,1},{9,13},{13,9},{2,6},{6,2},{1... | collective-permute-start | bytes 1769480 | tf_op jit(solution)/shard_map/ppermute | solution.py:597
  35.6 10.1 %copy-start = (bf16[1152,128]{1,0:T(8,128)(2,1)S(1)}, bf16[1152,128]{1,0:T(8,128)(2,1)}, u32[]{:S(2)}) copy-start(bf16[1152,128]{1,0:T(8,128)(2,1)} %get-tuple-element.37.member_ref) | copy-start | bytes 884740
  35.6 10.1 %copy-start.1 = (bf16[16,1024]{1,0:T(8,128)(2,1)S(1)}, bf16[16,1024]{1,0:T(8,128)(2,1)}, u32[]{:S(2)}) copy-start(bf16[16,1024]{1,0:T(8,128)(2,1)} %raise_ref.1) | copy-start | bytes 98308
  35.6 10.1 %copy-start.12 = (s32[1,12,128]{2,1,0:T(8,128)S(1)}, s32[1,12,128]{2,1,0:T(8,128)}, u32[]{:S(2)}) copy-start(s32[1,12,128]{2,1,0:T(8,128)} %copy-done.11) | copy-start | bytes 18436
  35.6 10.0 %collective-permute-start.9 = (bf16[160,256]{1,0:T(8,128)(2,1)S(1)}, bf16[160,256]{1,0:T(8,128)(2,1)S(1)}, u32[]{:S(2)}, u32[]{:S(2)}) collective-permute-start(bf16[160,256]{1,0:T(8,128)(2,1)S(1)} %fusion.19), channel_id=1, source_target_pairs={{0,8},{4,12},{8,0},{12,4},{1,9},{5,13},{9,1},{13,5},{2,10},{6,14},... | collective-permute-start | bytes 245768 | tf_op jit(solution)/shard_map/ppermute | solution.py:596
  48.8 4.9 %collective-permute-start.10 = (bf16[208,256]{1,0:T(8,128)(2,1)S(1)}, bf16[208,256]{1,0:T(8,128)(2,1)S(1)}, u32[]{:S(2)}, u32[]{:S(2)}) collective-permute-start(bf16[208,256]{1,0:T(8,128)(2,1)S(1)} %get-tuple-element.43.near_ref), channel_id=1, source_target_pairs={{0,16},{16,0},{1,17},{17,1},{2,18},{18,2},{3,19},{19,3},{4,20},{20... | collective-permute-start | bytes 319496 | tf_op jit(solution)/shard_map/ppermute | solution.py:629
  53.9 1.9 %collective-permute-start.11 = (f32[96,128]{1,0:T(8,128)S(1)}, f32[96,128]{1,0:T(8,128)S(1)}, u32[]{:S(2)}, u32[]{:S(2)}) collective-permute-start(f32[96,128]{1,0:T(8,128)S(1)} %get-tuple-element.44.refs_0_), channel_id=1, source_target_pairs={{0,4},{4,0},{8,12},{12,8},{1,5},{5,1},{9,13},{13,9},{2,6},{6,2},{1... | collective-permute-start | bytes 147464 | tf_op jit(solution)/shard_map/ppermute | solution.py:515
  54.0 4.2 %collective-permute-start.12 = (f32[96,128]{1,0:T(8,128)S(1)}, f32[96,128]{1,0:T(8,128)S(1)}, u32[]{:S(2)}, u32[]{:S(2)}) collective-permute-start(f32[96,128]{1,0:T(8,128)S(1)} %get-tuple-element.44.refs_0_), channel_id=1, source_target_pairs={{0,8},{4,12},{8,0},{12,4},{1,9},{5,13},{9,1},{13,5},{2,10},{6,14},... | collective-permute-start | bytes 147464 | tf_op jit(solution)/shard_map/ppermute | solution.py:515
  55.7 3.7 %collective-permute-start.13 = (f32[96,128]{1,0:T(8,128)S(1)}, f32[96,128]{1,0:T(8,128)S(1)}, u32[]{:S(2)}, u32[]{:S(2)}) collective-permute-start(f32[96,128]{1,0:T(8,128)S(1)} %get-tuple-element.44.refs_0_), channel_id=1, source_target_pairs={{0,12},{4,8},{8,4},{12,0},{1,13},{5,9},{9,5},{13,1},{2,14},{6,10},... | collective-permute-start | bytes 147464 | tf_op jit(solution)/shard_map/ppermute | solution.py:515
  59.4 11.6 %collective-permute-start.14 = (bf16[384,256]{1,0:T(8,128)(2,1)S(1)}, bf16[384,256]{1,0:T(8,128)(2,1)S(1)}, u32[]{:S(2)}, u32[]{:S(2)}) collective-permute-start(bf16[384,256]{1,0:T(8,128)(2,1)S(1)} %get-tuple-element.46.refs_4_), channel_id=1, source_target_pairs={{0,4},{4,0},{8,12},{12,8},{1,5},{5,1},{9,13},{13,9},{2,6},{6,2},{1... | collective-permute-start | bytes 589832 | tf_op jit(solution)/shard_map/ppermute | solution.py:515
  59.6 11.4 %collective-permute-start.15 = (bf16[384,256]{1,0:T(8,128)(2,1)S(1)}, bf16[384,256]{1,0:T(8,128)(2,1)S(1)}, u32[]{:S(2)}, u32[]{:S(2)}) collective-permute-start(bf16[384,256]{1,0:T(8,128)(2,1)S(1)} %get-tuple-element.46.refs_4_), channel_id=1, source_target_pairs={{0,8},{4,12},{8,0},{12,4},{1,9},{5,13},{9,1},{13,5},{2,10},{6,14},... | collective-permute-start | bytes 589832 | tf_op jit(solution)/shard_map/ppermute | solution.py:515
  60.7 10.3 %collective-permute-start.16 = (bf16[384,256]{1,0:T(8,128)(2,1)S(1)}, bf16[384,256]{1,0:T(8,128)(2,1)S(1)}, u32[]{:S(2)}, u32[]{:S(2)}) collective-permute-start(bf16[384,256]{1,0:T(8,128)(2,1)S(1)} %get-tuple-element.46.refs_4_), channel_id=1, source_target_pairs={{0,12},{4,8},{8,4},{12,0},{1,13},{5,9},{9,5},{13,1},{2,14},{6,10},... | collective-permute-start | bytes 589832 | tf_op jit(solution)/shard_map/ppermute | solution.py:515
  61.3 4.2 %collective-permute-start.17 = (f32[32,128]{1,0:T(8,128)S(1)}, f32[32,128]{1,0:T(8,128)S(1)}, u32[]{:S(2)}, u32[]{:S(2)}) collective-permute-start(f32[32,128]{1,0:T(8,128)S(1)} %fusion.20.refs_8_), channel_id=1, source_target_pairs={{0,1},{1,0},{2,3},{3,2},{4,5},{5,4},{6,7},{7,6},{8,9},{9,8},{10,11... | collective-permute-start | bytes 49160 | tf_op jit(solution)/shard_map/ppermute | solution.py:515
  62.9 6.4 %collective-permute-start.18 = (f32[32,128]{1,0:T(8,128)S(1)}, f32[32,128]{1,0:T(8,128)S(1)}, u32[]{:S(2)}, u32[]{:S(2)}) collective-permute-start(f32[32,128]{1,0:T(8,128)S(1)} %fusion.20.refs_8_), channel_id=1, source_target_pairs={{0,2},{1,3},{2,0},{3,1},{4,6},{5,7},{6,4},{7,5},{8,10},{9,11},{10,... | collective-permute-start | bytes 49160 | tf_op jit(solution)/shard_map/ppermute | solution.py:515
  65.5 5.5 %collective-permute-start.19 = (f32[32,128]{1,0:T(8,128)S(1)}, f32[32,128]{1,0:T(8,128)S(1)}, u32[]{:S(2)}, u32[]{:S(2)}) collective-permute-start(f32[32,128]{1,0:T(8,128)S(1)} %fusion.20.refs_8_), channel_id=1, source_target_pairs={{0,3},{1,2},{2,1},{3,0},{4,7},{5,6},{6,5},{7,4},{8,11},{9,10},{10,... | collective-permute-start | bytes 49160 | tf_op jit(solution)/shard_map/ppermute | solution.py:515
  (1 other events, 1.8 us)

commit v9 on v8

--- a/solution.py
+++ b/solution.py
@@ -121,7 +121,7 @@
 FIRST = 1152
 TAKEN = 768
 NT = (((1,), (1,)), ((), ()))
-VMEM_BYTES = 60 * 1024 * 1024
+LARGE_VMEM, MODEST_VMEM = 44 * 1024 * 1024, 15 * 1024 * 1024
 
 
 def mm(a, b, dims=(((1,), (0,)), ((), ()))):
@@ -159,9 +159,19 @@
     return lax.gather(x, lanes[..., None], numbers, slice_sizes=(1, 1), mode=mode)
 
 
+def fetch(pairs, sems):
+    copies = [pltpu.make_async_copy(a, b, sems.at[n]) for n, (a, b) in enumerate(pairs)]
+    for copy in copies:
+        copy.start()
+    for copy in copies:
+        copy.wait()
+
+
 def gather_kernel(
     ids_ref,
     vocab_ref,
+    turned_any,
+    member_any,
     turned,
     member_ref,
     held,
@@ -171,6 +181,7 @@
     bounds,
     held_sems,
     bounds_sem,
+    out_sems,
     base,
 ):
     texts, length = ids_ref.shape
@@ -273,9 +284,13 @@
         return carry
 
     lax.fori_loop(0, blocks, take, 0)
-
-
-def statistics_kernel(turned, member_ref, hard_ref, lower_ref, extra_ref, small):
+    fetch([(turned, turned_any), (member_ref, member_any)], out_sems)
+
+
+def statistics_kernel(
+    turned_any, member_any, hard_ref, lower_ref, extra_ref, small, turned, member_ref, spread, sems
+):
+    fetch([(turned_any, turned), (member_any, member_ref)], sems)
     features, span = turned.shape
     stripes = pl.cdiv(span, STRIPE)
     per_shard, negatives = hard_ref.shape
@@ -305,19 +320,11 @@
         misc += jnp.where(iota((ROWS, STRIPE), 1) == shard * per_shard + i, hard[:, i : i + 1], 0.0)
     extra_ref[stripes * ROWS : (stripes + 1) * ROWS, :] = misc.astype(jnp.bfloat16)
     residual = jnp.where(lax.axis_index("mp") == shard, residual.T[0:ROWS], 0.0)
-    for q in range(features // STRIPE):
+    spread[...] = residual
+    for q in range(4):
         start = (stripes + 1 + q) * ROWS
-        extra_ref[start : start + ROWS, :] = residual[:, q * STRIPE : (q + 1) * STRIPE].astype(
-            jnp.bfloat16
-        )
-
-
-def fetch(pairs, sems):
-    copies = [pltpu.make_async_copy(a, b, sems.at[n]) for n, (a, b) in enumerate(pairs)]
-    for copy in copies:
-        copy.start()
-    for copy in copies:
-        copy.wait()
+        quarter = pl.multiple_of(split_quarter(q // 2, q % 2) * STRIPE, LANES)
+        extra_ref[start : start + ROWS, :] = spread[:, pl.ds(quarter, STRIPE)].astype(jnp.bfloat16)
 
 
 def pool_kernel(
@@ -381,8 +388,7 @@
             total[...] += mm(chosen, high) + mm(chosen, rest)
             spread = [reduced[:, 0:size] * member[text : text + 1] for text in range(texts)]
             slopes[...] += mm(jnp.concatenate(spread).astype(jnp.bfloat16), slope)
-        start = pl.multiple_of((stripes + 1 + quarter) * ROWS, ROWS)
-        total[...] += extra_ref[pl.ds(start, ROWS), :]
+        total[...] += extra_ref[(stripes + 1) * ROWS : (stripes + 2) * ROWS, :]
 
     add((own_ref, core_ref, far_ref), extra_ref, member_ref, 0)
     real = (ids_ref[...] != 0).astype(jnp.float32)
@@ -421,13 +427,13 @@
 
 def score_kernel(*refs, texts, stripes, negatives):
     there, (misc_ref, sharp_ref, embed_ref, loss_ref, up_ref), (*here, sems) = (
-        refs[0:12],
-        refs[12:17],
-        refs[17:],
+        refs[0:10],
+        refs[10:15],
+        refs[15:],
     )
     fetch(list(zip(there, here)), sems)
-    packed0, packed1, packed2, packed3, slopes0, slopes1, slopes2, slopes3 = here[0:8]
-    dots0, dots1, dots2, dots3 = here[8:12]
+    packed0, packed1, packed2, packed3, slopes0, slopes2 = here[0:6]
+    dots0, dots1, dots2, dots3 = here[6:10]
     rows = 2 * ROWS
     per_shard = loss_ref.shape[1]
     group, shard = lax.axis_index("group"), lax.axis_index("dp")
@@ -472,16 +478,22 @@
     rnorm_own = jnp.where(group == 0, rnorm_col[0:ROWS], rnorm_col[ROWS:rows])
     chosen = iota((ROWS, ROWS), 1) == iota((ROWS, ROWS), 0) + first
     chosen = jnp.where(chosen & (iota((ROWS, ROWS), 0) < per_shard), 1.0, 0.0).astype(jnp.bfloat16)
-    blocks = ((packed0, slopes0), (packed1, slopes1), (packed2, slopes2), (packed3, slopes3))
+    blocks = ((packed0, slopes0), (packed1, None), (packed2, slopes2), (packed3, None))
     for o, (packed, slopes) in enumerate(blocks):
         parts = packed.shape[0] // rows - 1
         width = parts * LANES
         halves = [packed[rows * (part + 1) : rows * (part + 2), :] for part in range(parts)]
         block = jnp.concatenate(halves, axis=1)
+        queries = group == 0
+        at = pl.multiple_of(quarter_of(shard ^ o) * width, LANES)
+        own = jnp.where(queries, block[0:ROWS], block[ROWS:rows]) * rnorm_own
+        picked = mm(chosen, own.astype(jnp.bfloat16)).astype(jnp.bfloat16)
+        embed_ref[0, :, pl.ds(at, width)] = picked[0:per_shard]
+        if slopes is None:
+            continue
         along = mm(along_rows, block.astype(jnp.bfloat16))
         grad = sharpness * (along - radial_col * block)
         near, far = slopes[0 : slopes.shape[0] // 2], slopes[slopes.shape[0] // 2 :]
-        queries = group == 0
         grad_near = jnp.where(queries, grad[0:ROWS], grad[ROWS:rows])
         grad_far = jnp.where(queries, grad[ROWS:rows], grad[0:ROWS])
         update = []
@@ -491,11 +503,8 @@
                 slope = side[text * ROWS : (text + 1) * ROWS].astype(jnp.float32)
                 total += side_grad[text : text + 1] * slope
             update.append(total)
-        at = pl.multiple_of(quarter_of(shard ^ o) * width, LANES)
+        at = pl.multiple_of((lax.div(shard, 2) ^ (o // 2)) * width, LANES)
         up_ref[:, pl.ds(at, width)] = update[0] + update[1]
-        own = jnp.where(queries, block[0:ROWS], block[ROWS:rows]) * rnorm_own
-        picked = mm(chosen, own.astype(jnp.bfloat16)).astype(jnp.bfloat16)
-        embed_ref[0, :, pl.ds(at, width)] = picked[0:per_shard]
 
 
 def any_spec():
@@ -534,8 +543,8 @@
     per_shard, negatives = difficult_distractors.shape
     part_width = layer_weight_matrix.shape[1]
     width = part_width // shards
-    params = pltpu.CompilerParams(vmem_limit_bytes=VMEM_BYTES)
-    modest = pltpu.CompilerParams(vmem_limit_bytes=VMEM_BYTES // 4)
+    params = pltpu.CompilerParams(vmem_limit_bytes=LARGE_VMEM)
+    modest = pltpu.CompilerParams(vmem_limit_bytes=MODEST_VMEM)
     other_core = [(d, d ^ 1) for d in range(shards)]
     other_y = [(d, d ^ 2) for d in range(shards)]
 
@@ -553,8 +562,10 @@
                 jax.ShapeDtypeStruct((span, LANES), jnp.bfloat16),
             ],
             in_specs=[vmem_spec(), any_spec()],
-            out_specs=[vmem_spec()] * 2,
+            out_specs=[any_spec()] * 2,
             scratch_shapes=[
+                pltpu.VMEM((features, span), jnp.bfloat16),
+                pltpu.VMEM((span, LANES), jnp.bfloat16),
                 pltpu.VMEM((blocks, features, IDS_PER_BLOCK), jnp.bfloat16),
                 pltpu.VMEM((8 * pl.cdiv(span // LANES, 8), LANES), jnp.int32),
                 pltpu.VMEM((texts, length), jnp.float32),
@@ -562,6 +573,7 @@
                 pltpu.SMEM((group_rows, length), jnp.int32),
                 pltpu.SemaphoreType.DMA((blocks,)),
                 pltpu.SemaphoreType.DMA,
+                pltpu.SemaphoreType.DMA((2,)),
             ],
             compiler_params=params,
             name="gather",
@@ -580,10 +592,16 @@
         extra = pl.pallas_call(
             statistics_kernel,
             out_shape=jax.ShapeDtypeStruct((extra_rows, STRIPE), jnp.bfloat16),
-            in_specs=[vmem_spec()] * 4,
+            in_specs=[any_spec()] * 2 + [vmem_spec()] * 2,
             out_specs=vmem_spec(),
-            scratch_shapes=[pltpu.VMEM((LANES, LANES), jnp.float32)],
-            compiler_params=params,
+            scratch_shapes=[
+                pltpu.VMEM((LANES, LANES), jnp.float32),
+                pltpu.VMEM(turned.shape, turned.dtype),
+                pltpu.VMEM(member.shape, member.dtype),
+                pltpu.VMEM((ROWS, features), jnp.float32),
+                pltpu.SemaphoreType.DMA((2,)),
+            ],
+            compiler_params=modest,
             cost_estimate=pl.CostEstimate(
                 flops=2 * features * span * (ROWS + LANES),
                 bytes_accessed=2 * features * span,
@@ -591,15 +609,21 @@
             ),
             name="statistics",
         )(turned, member, difficult_distractors, lowering_factor_matrix)
-        chip = extra.astype(jnp.float32)
-        chip += lax.ppermute(extra, "dp", other_core).astype(jnp.float32)
-        extra = chip + lax.ppermute(narrow(chip), "dp", other_y).astype(jnp.float32)
+        common = (stripes + 1) * ROWS
+        near = extra.astype(jnp.float32)
+        across = lax.ppermute(extra, "dp", other_core).astype(jnp.float32)
+        chip = near[0:common] + across[0:common]
+        inputs = near[common : common + 2 * ROWS] + across[common + 2 * ROWS :]
+        sent = narrow(jnp.concatenate([chip, inputs[ROWS:]]))
+        sent = lax.ppermute(sent, "dp", other_y).astype(jnp.float32)
+        extra = jnp.concatenate([chip, inputs[0:ROWS]]) + sent
         core0 = lax.ppermute(narrow(product(turned, 1, 0)), "dp", other_core)
         own0 = narrow(product(turned, 0, 0))
         return own0, core0, far, extra, member
 
     first = project(0, FIRST)
-    many = jnp.sum((ids != 0).astype(jnp.int32)) > FIRST
+    later, _ = lax.optimization_barrier((ids, first[0]))
+    many = jnp.sum((later != 0).astype(jnp.int32)) > FIRST
     left = tokens - FIRST
     shapes = jax.eval_shape(lambda: project(FIRST, left))
     rest = lax.cond(
@@ -648,7 +672,7 @@
     dots = (dots[0] + dots[1]) + (dots[2] + dots[3])
     slopes, dots = lax.optimization_barrier((slopes, dots))
     dots = exchange(dots, "mp", parts)
-    slopes = exchange(slopes, "dp", shards)
+    slopes = [slopes, lax.ppermute(slopes, "dp", other_y)]
     embeddings, losses, update = pl.pallas_call(
         functools.partial(
             score_kernel, texts=texts, stripes=pl.cdiv(FIRST, STRIPE), negatives=negatives
@@ -656,16 +680,19 @@
         out_shape=[
             jax.ShapeDtypeStruct((1, per_shard, part_width), jnp.bfloat16),
             jax.ShapeDtypeStruct((1, per_shard), jnp.float32),
-            jax.ShapeDtypeStruct((ROWS, part_width), jnp.float32),
+            jax.ShapeDtypeStruct((ROWS, part_width // 2), jnp.float32),
         ],
-        in_specs=[any_spec()] * 12 + [vmem_spec(), smem_spec()],
+        in_specs=[any_spec()] * 10 + [vmem_spec(), smem_spec()],
         out_specs=[vmem_spec()] * 3,
         scratch_shapes=[pltpu.VMEM(x.shape, x.dtype) for x in (*packed, *slopes, *dots)]
-        + [pltpu.SemaphoreType.DMA((12,))],
+        + [pltpu.SemaphoreType.DMA((10,))],
         compiler_params=modest,
         name="score",
     )(*packed, *slopes, *dots, misc, logit_sharpness)
-    return (embeddings, losses, update)
+    other = lax.ppermute(update, "dp", other_core)
+    core = lax.rem(lax.axis_index("dp"), 2)
+    halves = [jnp.where(core == 0, update, other), jnp.where(core == 0, other, update)]
+    return (embeddings, losses, jnp.concatenate(halves, axis=1))
 
 
 def body(words, hard, vocabulary, weight, lowering, raising, sharpness):

time: 74.2 us -> 70.1 us (0.945)
  waiting for transfers between devices: 16.2 us -> 20.5 us
  Pallas kernels: 25.4 us -> 21.3 us
  starting transfers between devices: 16.8 us -> 13.2 us
  matrix products: 10 us -> 8.09 us
  other arithmetic: 0.69 us -> 2.23 us
    ppermute x9 -> x6, starting transfers between devices: 11.2 us -> 6.33 us  [exchange(): return [x] + [lax.ppermute(x, axis, step) for step in steps]]
    ppermute x2 -> x4, starting transfers between devices: 0.5 us -> 2.59 us  [the longest x1 1.71 us: split_body(): slopes = [slopes, lax.ppermute(slopes, 'dp', other_y)]]
    pallas_call x1, Pallas kernels: 3.44 us -> 1.41 us  [project(): pl.pallas_call(statistics_kernel, out_shape=jax.ShapeDtypeStruct((extra_r...]
    dot_general x4, matrix products: 10 us -> 8.09 us  [mm(): return lax.dot_general(a, b, dims, preferred_element_type=jnp.float32)]
    ppermute x1, waiting for transfers between devices: 0.01 us -> 1.76 us  [project(): core1 = lax.ppermute(narrow(product(turned, 1, 1)), 'dp', other_core)]
    pallas_call x1, Pallas kernels: 15.9 us -> 14.7 us  [project(): pl.pallas_call(functools.partial(gather_kernel, base=base), out_shape=[ja...]
    ppermute x2 -> x4, waiting for transfers between devices: 7.86 us -> 8.89 us  [the longest x1 7.7 us: project(): sent = lax.ppermute(sent, 'dp', other_y).astype(jnp.float32)]
    ppermute x1, starting transfers between devices: 1.78 us -> 0.86 us  [split_body(): far_side = lax.ppermute(sent, 'group', [(0, 1), (1, 0)])]
  transfers between devices with their start and end apart: 15 -> 14, of which waited for: 5 -> 8; matrix products, arithmetic and copies ran while one was open for 8% -> 9% of each run, Pallas kernels for 5% -> 0%
where the time goes in v9:
time: 70.1 us; the launch traced here: 69.7 us
  Pallas kernels  21.3 us (30%)
  waiting for transfers between devices  20.5 us (29%)
  starting transfers between devices  13.2 us (19%)
  matrix products  8.09 us (12%)
  other arithmetic  2.23 us (3%)
  between operations  2.14 us (3%)
  local copies, waits for them, and re-layouts  2.13 us (3%)
    pallas_call x1, Pallas kernels, project(): pl.pallas_call(functools.partial(gather_kernel, base=base), out_shape=[ja...  14.7 us
    dot_general x4, matrix products, mm(): return lax.dot_general(a, b, dims, preferred_element_type=jnp.float32)  8.09 us
    ppermute x1, waiting for transfers between devices, project(): sent = lax.ppermute(sent, 'dp', other_y).astype(jnp.float32)  7.7 us
    ppermute x6, starting transfers between devices, exchange(): return [x] + [lax.ppermute(x, axis, step) for step in steps]  6.33 us
    ppermute x6, waiting for transfers between devices, exchange(): return [x] + [lax.ppermute(x, axis, step) for step in steps]  5.98 us
    ppermute x1, waiting for transfers between devices, split_body(): far_side = lax.ppermute(sent, 'group', [(0, 1), (1, 0)])  3.91 us
    pallas_call x1, Pallas kernels, split_body(): pl.pallas_call(functools.partial(pool_kernel, model_width=float(features...  3.1 us
    ppermute x1, starting transfers between devices, project(): far = lax.ppermute(chip1, 'dp', other_y)  2.73 us
  transfers between devices with their start and end apart: 14, of which 8 were waited for; matrix products, arithmetic and copies ran while one was open for 9% of the time, Pallas kernels for 0%

profile of v9, /device:TPU:0, one launch (start us, length us, event | category | flops | bytes accessed | tf_op | source)
XLA Modules:
  0.0 69.7 jit_solution(514604989279409588)
XLA Ops:
  0.6 0.7 copy.12
  1.3 14.7 %gather.3 = (bf16[1024,1152]{1,0:T(8,128)(2,1)S(1)}, bf16[1152,128]{1,0:T(8,128)(2,1)S(1)}) custom-call(s32[12,128]{1,0:T(8,128)S(1)} %bitcast.11, bf16[1024,16384]{1,0:T(8,128)(2,1)} %vocab_ref.1), custom_call_target="tpu_custom_call" | custom-call | tf_op jit(solution)/shard_map/gather/pallas_call | solution.py:558
  16.0 1.9 %convolution_convert_fusion.5 = bf16[1152,256]{1,0:T(8,128)(2,1)S(1)} fusion(bf16[1024,1152]{1,0:T(8,128)(2,1)S(1)} %get-tuple-element.40.turned_any, bf16[1024,1024]{1,0:T(8,128)(2,1)} %param.12, s32[]{:T(128)S(6)} %select_n.37), kind=kOutput, calls=%fused_computation.20 | convolution fusion | flops 604274688 | bytes 3473412 | tf_op jit(solution)/shard_map/dot_general | solution.py:128
  18.4 1.8 %collective-permute-done.5 = bf16[1152,256]{1,0:T(8,128)(2,1)} collective-permute-done((bf16[1152,256]{1,0:T(8,128)(2,1)S(1)}, bf16[1152,256]{1,0:T(8,128)(2,1)}, u32[]{:S(2)}, u32[]{:S(2)}) %collective-permute-start.5) | collective-permute-done | bytes 589856 | tf_op jit(solution)/shard_map/ppermute | solution.py:588
  20.2 2.9 %add_convert_fusion.1 = bf16[1152,256]{1,0:T(8,128)(2,1)} fusion(bf16[1152,256]{1,0:T(8,128)(2,1)} %collective-permute-done.5, bf16[1024,1152]{1,0:T(8,128)(2,1)S(1)} %get-tuple-element.40.turned_any, bf16[1024,1024]{1,0:T(8,128)(2,1)} %param.12, s32[]{:T(128)S(6)} %select_n.36), kind=kOutput, calls=%fused_computation.21 | convolution fusion | flops 604864512 | bytes 4063236 | tf_op jit(solution)/shard_map/dot_general | solution.py:128
  23.0 1.4 %statistics.3 = bf16[160,256]{1,0:T(8,128)(2,1)S(1)} custom-call(bf16[1024,1152]{1,0:T(8,128)(2,1)S(1)} %get-tuple-element.40.turned_any, bf16[1152,128]{1,0:T(8,128)(2,1)S(1)} %get-tuple-element.41.member_any.member_ref, s32[3,7]{1,0:T(4,128)S(1)} %copy-done.6, bf16[16,4096]{1,0:T(8,128)(2,1)S(1)} %copy-done.4), custom_call_target="tpu_custom_call" | custom-call | flops 339738624 | bytes 2359296 | tf_op jit(solution)/shard_map/statistics/pallas_call | solution.py:592
  24.9 2.7 %collective-permute-start.7 = (bf16[1152,256]{1,0:T(8,128)(2,1)}, bf16[1152,256]{1,0:T(8,128)(2,1)S(1)}, u32[]{:S(2)}, u32[]{:S(2)}) collective-permute-start(bf16[1152,256]{1,0:T(8,128)(2,1)} %add_convert_fusion.1), channel_id=1, source_target_pairs={{0,8},{4,12},{8,0},{12,4},{1,9},{5,13},{9,1},{13,5},{2,10},{6,14},... | collective-permute-start | bytes 1769480 | tf_op jit(solution)/shard_map/ppermute | solution.py:590
  27.6 1.7 %convolution_convert_fusion.4.own_ref = bf16[1152,256]{1,0:T(8,128)(2,1)} fusion(bf16[1024,1152]{1,0:T(8,128)(2,1)S(1)} %get-tuple-element.40.turned_any, bf16[1024,1024]{1,0:T(8,128)(2,1)S(1)} %copy-done.7, s32[]{:T(128)S(6)} %select_n.38), kind=kOutput, calls=%fused_computation.19 | convolution fusion | flops 604274688 | bytes 3473412 | tf_op jit(solution)/shard_map/dot_general | solution.py:128
  29.3 1.7 %convolution_convert_fusion.3 = bf16[1152,256]{1,0:T(8,128)(2,1)} fusion(bf16[1024,1152]{1,0:T(8,128)(2,1)S(1)} %get-tuple-element.40.turned_any, bf16[1024,1024]{1,0:T(8,128)(2,1)S(1)} %copy-done.7, s32[]{:T(128)S(6)} %select_n.39), kind=kOutput, calls=%fused_computation.18 | convolution fusion | flops 604274688 | bytes 3473412 | tf_op jit(solution)/shard_map/dot_general | solution.py:128
  32.3 1.4 %conditional.1 = (bf16[384,256]{1,0:T(8,128)(2,1)S(1)}, bf16[384,256]{1,0:T(8,128)(2,1)}, bf16[384,256]{1,0:T(8,128)(2,1)}, f32[64,256]{1,0:T(8,128)S(1)}, bf16[384,128]{1,0:T(8,128)(2,1)S(1)}) conditional(s32[]{:T(128)} %convert_element_type.65, () %tuple.22, (s32[12,128]{1,0:T(8,128)S(1)}, bf16[1024,16384]{1,0:T(8,128)(2,1)}, ...), branch_computations={%region_1.0_spmd, %region_2.0_spmd} | conditional | flops 919347200 | bytes 20325128 | solution.py:629
  33.9 0.9 %convert_element_type.62 = f32[160,256]{1,0:T(8,128)S(1)} convert(bf16[160,256]{1,0:T(8,128)(2,1)} %collective-permute-done.8) | non-fusion elementwise | flops 40960 | bytes 245760 | tf_op jit(solution)/shard_map/convert_element_type | solution.py:614
  35.2 7.7 %collective-permute-done.9 = bf16[112,256]{1,0:T(8,128)(2,1)S(1)} collective-permute-done((bf16[112,256]{1,0:T(8,128)(2,1)S(1)}, bf16[112,256]{1,0:T(8,128)(2,1)S(1)}, u32[]{:S(2)}, u32[]{:S(2)}) %collective-permute-start.9) | collective-permute-done | bytes 57376 | tf_op jit(solution)/shard_map/ppermute | solution.py:618
  43.0 3.1 %pool.1 = (bf16[208,256]{1,0:T(8,128)(2,1)S(1)}, f32[16,256]{1,0:T(8,128)S(1)}) custom-call(s32[12,128]{1,0:T(8,128)S(1)} %bitcast.14, bf16[1152,256]{1,0:T(8,128)(2,1)S(1)} %copy-done, bf16[1152,256]{1,0:T(8,128)(2,1)S(1)} %collective-permute-done.6.core_any, bf16[1152,256]{1,0:T(8,128)(2,1)S(1)} %collective-permute-done.7.far_any, ...), custom_call_target="tpu_custom_call" | custom-call | tf_op jit(solution)/shard_map/pool/pallas_call | solution.py:634
  46.1 0.9 %collective-permute-start.10 = (bf16[208,256]{1,0:T(8,128)(2,1)S(1)}, bf16[208,256]{1,0:T(8,128)(2,1)S(1)}, u32[]{:S(2)}, u32[]{:S(2)}) collective-permute-start(bf16[208,256]{1,0:T(8,128)(2,1)S(1)} %get-tuple-element.48.near_ref), channel_id=1, source_target_pairs={{0,16},{16,0},{1,17},{17,1},{2,18},{18,2},{3,19},{19,3},{4,20},{20... | collective-permute-start | bytes 319496 | tf_op jit(solution)/shard_map/ppermute | solution.py:653
  46.9 3.9 %collective-permute-done.10.far_any = bf16[208,256]{1,0:T(8,128)(2,1)S(1)} collective-permute-done((bf16[208,256]{1,0:T(8,128)(2,1)S(1)}, bf16[208,256]{1,0:T(8,128)(2,1)S(1)}, u32[]{:S(2)}, u32[]{:S(2)}) %collective-permute-start.10) | collective-permute-done | bytes 106528 | tf_op jit(solution)/shard_map/ppermute | solution.py:653
  51.2 1.8 %collective-permute-start.12 = (f32[96,128]{1,0:T(8,128)S(1)}, f32[96,128]{1,0:T(8,128)S(1)}, u32[]{:S(2)}, u32[]{:S(2)}) collective-permute-start(f32[96,128]{1,0:T(8,128)S(1)} %get-tuple-element.49.refs_0_), channel_id=1, source_target_pairs={{0,8},{4,12},{8,0},{12,4},{1,9},{5,13},{9,1},{13,5},{2,10},{6,14},... | collective-permute-start | bytes 147464 | tf_op jit(solution)/shard_map/ppermute | solution.py:524
  53.1 1.9 %collective-permute-done.13.refs_3_ = f32[96,128]{1,0:T(8,128)S(1)} collective-permute-done((f32[96,128]{1,0:T(8,128)S(1)}, f32[96,128]{1,0:T(8,128)S(1)}, u32[]{:S(2)}, u32[]{:S(2)}) %collective-permute-start.13) | collective-permute-done | bytes 49184 | tf_op jit(solution)/shard_map/ppermute | solution.py:524
  54.9 0.9 %collective-permute-done.12.refs_2_ = f32[96,128]{1,0:T(8,128)S(1)} collective-permute-done((f32[96,128]{1,0:T(8,128)S(1)}, f32[96,128]{1,0:T(8,128)S(1)}, u32[]{:S(2)}, u32[]{:S(2)}) %collective-permute-start.12) | collective-permute-done | bytes 49184 | tf_op jit(solution)/shard_map/ppermute | solution.py:524
  55.9 1.7 %collective-permute-start.14 = (bf16[384,256]{1,0:T(8,128)(2,1)S(1)}, bf16[384,256]{1,0:T(8,128)(2,1)S(1)}, u32[]{:S(2)}, u32[]{:S(2)}) collective-permute-start(bf16[384,256]{1,0:T(8,128)(2,1)S(1)} %get-tuple-element.51.refs_4_), channel_id=1, source_target_pairs={{0,8},{4,12},{8,0},{12,4},{1,9},{5,13},{9,1},{13,5},{2,10},{6,14},... | collective-permute-start | bytes 589832 | tf_op jit(solution)/shard_map/ppermute | solution.py:675
  57.6 3.6 %collective-permute-start.17 = (f32[32,128]{1,0:T(8,128)S(1)}, f32[32,128]{1,0:T(8,128)S(1)}, u32[]{:S(2)}, u32[]{:S(2)}) collective-permute-start(f32[32,128]{1,0:T(8,128)S(1)} %fusion.18.refs_6_), channel_id=1, source_target_pairs={{0,3},{1,2},{2,1},{3,0},{4,7},{5,6},{6,5},{7,4},{8,11},{9,10},{10,... | collective-permute-start | bytes 49160 | tf_op jit(solution)/shard_map/ppermute | solution.py:524
  61.2 0.8 %collective-permute-start.15 = (f32[32,128]{1,0:T(8,128)S(1)}, f32[32,128]{1,0:T(8,128)S(1)}, u32[]{:S(2)}, u32[]{:S(2)}) collective-permute-start(f32[32,128]{1,0:T(8,128)S(1)} %fusion.18.refs_6_), channel_id=1, source_target_pairs={{0,1},{1,0},{2,3},{3,2},{4,5},{5,4},{6,7},{7,6},{8,9},{9,8},{10,11... | collective-permute-start | bytes 49160 | tf_op jit(solution)/shard_map/ppermute | solution.py:524
  63.1 2.7 %collective-permute-done.16.refs_8_ = f32[32,128]{1,0:T(8,128)S(1)} collective-permute-done((f32[32,128]{1,0:T(8,128)S(1)}, f32[32,128]{1,0:T(8,128)S(1)}, u32[]{:S(2)}, u32[]{:S(2)}) %collective-permute-start.16) | collective-permute-done | bytes 16416 | tf_op jit(solution)/shard_map/ppermute | solution.py:524
  65.8 1.9 %score.1 = (bf16[1,3,1024]{2,1,0:T(4,128)(2,1)}, f32[1,3]{1,0:T(1,128)}, f32[16,512]{1,0:T(8,128)S(1)}) custom-call(f32[96,128]{1,0:T(8,128)S(1)} %get-tuple-element.49.refs_0_, f32[96,128]{1,0:T(8,128)S(1)} %collective-permute-done.11.refs_1_, f32[96,128]{1,0:T(8,128)S(1)} %collective-permute-done.12.refs_2_, ...), custom_call_target="tpu_custom_call" | custom-call | tf_op jit(solution)/shard_map/score/pallas_call | solution.py:676
  67.8 1.2 %collective-permute-done.18 = f32[16,512]{1,0:T(8,128)S(1)} collective-permute-done((f32[16,512]{1,0:T(8,128)S(1)}, f32[16,512]{1,0:T(8,128)S(1)}, u32[]{:S(2)}, u32[]{:S(2)}) %collective-permute-start.18) | collective-permute-done | bytes 32800 | tf_op jit(solution)/shard_map/ppermute | solution.py:692
  (42 shorter events, 5.2 us)
Async XLA Ops:
  17.9 2.3 %collective-permute-start.5 = (bf16[1152,256]{1,0:T(8,128)(2,1)S(1)}, bf16[1152,256]{1,0:T(8,128)(2,1)}, u32[]{:S(2)}, u32[]{:S(2)}) collective-permute-start(bf16[1152,256]{1,0:T(8,128)(2,1)S(1)} %convolution_convert_fusion.5), channel_id=1, source_target_pairs={{0,4},{4,0},{8,12},{12,8},{1,5},{5,1},{9,13},{13,9},{2,6},{6,2},{1... | collective-permute-start | bytes 1769480 | tf_op jit(solution)/shard_map/ppermute | solution.py:588
  18.4 4.6 %copy-start.4 = (bf16[16,4096]{1,0:T(8,128)(2,1)S(1)}, bf16[16,4096]{1,0:T(8,128)(2,1)}, u32[]{:S(2)}) copy-start(bf16[16,4096]{1,0:T(8,128)(2,1)} %lower_ref.1) | copy-start | bytes 393220
  18.4 4.6 %copy-start.6 = (s32[3,7]{1,0:T(4,128)S(1)}, s32[3,7]{1,0:T(4,128)}, u32[]{:S(2)}) copy-start(s32[3,7]{1,0:T(4,128)} %hard_ref.1) | copy-start | bytes 256
  23.0 4.6 %copy-start.7 = (bf16[1024,1024]{1,0:T(8,128)(2,1)S(1)}, bf16[1024,1024]{1,0:T(8,128)(2,1)}, u32[]{:S(2)}) copy-start(bf16[1024,1024]{1,0:T(8,128)(2,1)} %param.12) | copy-start | bytes 6291460
  24.5 9.4 %collective-permute-start.8 = (bf16[160,256]{1,0:T(8,128)(2,1)S(1)}, bf16[160,256]{1,0:T(8,128)(2,1)}, u32[]{:S(2)}, u32[]{:S(2)}) collective-permute-start(bf16[160,256]{1,0:T(8,128)(2,1)S(1)} %statistics.3), channel_id=1, source_target_pairs={{0,4},{4,0},{8,12},{12,8},{1,5},{5,1},{9,13},{13,9},{2,6},{6,2},{1... | collective-permute-start | bytes 245768 | tf_op jit(solution)/shard_map/ppermute | solution.py:614
  24.9 18.0 %collective-permute-start.7 = (bf16[1152,256]{1,0:T(8,128)(2,1)}, bf16[1152,256]{1,0:T(8,128)(2,1)S(1)}, u32[]{:S(2)}, u32[]{:S(2)}) collective-permute-start(bf16[1152,256]{1,0:T(8,128)(2,1)} %add_convert_fusion.1), channel_id=1, source_target_pairs={{0,8},{4,12},{8,0},{12,4},{1,9},{5,13},{9,1},{13,5},{2,10},{6,14},... | collective-permute-start | bytes 1769480 | tf_op jit(solution)/shard_map/ppermute | solution.py:590
  32.3 10.7 %copy-start = (bf16[1152,256]{1,0:T(8,128)(2,1)S(1)}, bf16[1152,256]{1,0:T(8,128)(2,1)}, u32[]{:S(2)}) copy-start(bf16[1152,256]{1,0:T(8,128)(2,1)} %convolution_convert_fusion.4.own_ref) | copy-start | bytes 1769476
  32.3 10.7 %copy-start.1 = (bf16[16,1024]{1,0:T(8,128)(2,1)S(1)}, bf16[16,1024]{1,0:T(8,128)(2,1)}, u32[]{:S(2)}) copy-start(bf16[16,1024]{1,0:T(8,128)(2,1)} %raise_ref.1) | copy-start | bytes 98308
  33.7 9.2 %collective-permute-start.6 = (bf16[1152,256]{1,0:T(8,128)(2,1)}, bf16[1152,256]{1,0:T(8,128)(2,1)S(1)}, u32[]{:S(2)}, u32[]{:S(2)}) collective-permute-start(bf16[1152,256]{1,0:T(8,128)(2,1)} %convolution_convert_fusion.3), channel_id=1, source_target_pairs={{0,4},{4,0},{8,12},{12,8},{1,5},{5,1},{9,13},{13,9},{2,6},{6,2},{1... | collective-permute-start | bytes 1769480 | tf_op jit(solution)/shard_map/ppermute | solution.py:620
  34.9 8.1 %collective-permute-start.9 = (bf16[112,256]{1,0:T(8,128)(2,1)S(1)}, bf16[112,256]{1,0:T(8,128)(2,1)S(1)}, u32[]{:S(2)}, u32[]{:S(2)}) collective-permute-start(bf16[112,256]{1,0:T(8,128)(2,1)S(1)} %pad_maximum_fusion.2), channel_id=1, source_target_pairs={{0,8},{4,12},{8,0},{12,4},{1,9},{5,13},{9,1},{13,5},{2,10},{6,14},... | collective-permute-start | bytes 172040 | tf_op jit(solution)/shard_map/ppermute | solution.py:618
  46.1 4.8 %collective-permute-start.10 = (bf16[208,256]{1,0:T(8,128)(2,1)S(1)}, bf16[208,256]{1,0:T(8,128)(2,1)S(1)}, u32[]{:S(2)}, u32[]{:S(2)}) collective-permute-start(bf16[208,256]{1,0:T(8,128)(2,1)S(1)} %get-tuple-element.48.near_ref), channel_id=1, source_target_pairs={{0,16},{16,0},{1,17},{17,1},{2,18},{18,2},{3,19},{19,3},{4,20},{20... | collective-permute-start | bytes 319496 | tf_op jit(solution)/shard_map/ppermute | solution.py:653
  51.1 3.8 %collective-permute-start.13 = (f32[96,128]{1,0:T(8,128)S(1)}, f32[96,128]{1,0:T(8,128)S(1)}, u32[]{:S(2)}, u32[]{:S(2)}) collective-permute-start(f32[96,128]{1,0:T(8,128)S(1)} %get-tuple-element.49.refs_0_), channel_id=1, source_target_pairs={{0,12},{4,8},{8,4},{12,0},{1,13},{5,9},{9,5},{13,1},{2,14},{6,10},... | collective-permute-start | bytes 147464 | tf_op jit(solution)/shard_map/ppermute | solution.py:524
  51.2 4.6 %collective-permute-start.12 = (f32[96,128]{1,0:T(8,128)S(1)}, f32[96,128]{1,0:T(8,128)S(1)}, u32[]{:S(2)}, u32[]{:S(2)}) collective-permute-start(f32[96,128]{1,0:T(8,128)S(1)} %get-tuple-element.49.refs_0_), channel_id=1, source_target_pairs={{0,8},{4,12},{8,0},{12,4},{1,9},{5,13},{9,1},{13,5},{2,10},{6,14},... | collective-permute-start | bytes 147464 | tf_op jit(solution)/shard_map/ppermute | solution.py:524
  53.0 2.8 %collective-permute-start.11 = (f32[96,128]{1,0:T(8,128)S(1)}, f32[96,128]{1,0:T(8,128)S(1)}, u32[]{:S(2)}, u32[]{:S(2)}) collective-permute-start(f32[96,128]{1,0:T(8,128)S(1)} %get-tuple-element.49.refs_0_), channel_id=1, source_target_pairs={{0,4},{4,0},{8,12},{12,8},{1,5},{5,1},{9,13},{13,9},{2,6},{6,2},{1... | collective-permute-start | bytes 147464 | tf_op jit(solution)/shard_map/ppermute | solution.py:524
  55.9 10.0 %collective-permute-start.14 = (bf16[384,256]{1,0:T(8,128)(2,1)S(1)}, bf16[384,256]{1,0:T(8,128)(2,1)S(1)}, u32[]{:S(2)}, u32[]{:S(2)}) collective-permute-start(bf16[384,256]{1,0:T(8,128)(2,1)S(1)} %get-tuple-element.51.refs_4_), channel_id=1, source_target_pairs={{0,8},{4,12},{8,0},{12,4},{1,9},{5,13},{9,1},{13,5},{2,10},{6,14},... | collective-permute-start | bytes 589832 | tf_op jit(solution)/shard_map/ppermute | solution.py:675
  57.6 5.5 %collective-permute-start.17 = (f32[32,128]{1,0:T(8,128)S(1)}, f32[32,128]{1,0:T(8,128)S(1)}, u32[]{:S(2)}, u32[]{:S(2)}) collective-permute-start(f32[32,128]{1,0:T(8,128)S(1)} %fusion.18.refs_6_), channel_id=1, source_target_pairs={{0,3},{1,2},{2,1},{3,0},{4,7},{5,6},{6,5},{7,4},{8,11},{9,10},{10,... | collective-permute-start | bytes 49160 | tf_op jit(solution)/shard_map/ppermute | solution.py:524
  61.2 4.6 %collective-permute-start.16 = (f32[32,128]{1,0:T(8,128)S(1)}, f32[32,128]{1,0:T(8,128)S(1)}, u32[]{:S(2)}, u32[]{:S(2)}) collective-permute-start(f32[32,128]{1,0:T(8,128)S(1)} %fusion.18.refs_6_), channel_id=1, source_target_pairs={{0,2},{1,3},{2,0},{3,1},{4,6},{5,7},{6,4},{7,5},{8,10},{9,11},{10,... | collective-permute-start | bytes 49160 | tf_op jit(solution)/shard_map/ppermute | solution.py:524
  61.2 4.6 %collective-permute-start.15 = (f32[32,128]{1,0:T(8,128)S(1)}, f32[32,128]{1,0:T(8,128)S(1)}, u32[]{:S(2)}, u32[]{:S(2)}) collective-permute-start(f32[32,128]{1,0:T(8,128)S(1)} %fusion.18.refs_6_), channel_id=1, source_target_pairs={{0,1},{1,0},{2,3},{3,2},{4,5},{5,4},{6,7},{7,6},{8,9},{9,8},{10,11... | collective-permute-start | bytes 49160 | tf_op jit(solution)/shard_map/ppermute | solution.py:524
  67.7 1.3 %collective-permute-start.18 = (f32[16,512]{1,0:T(8,128)S(1)}, f32[16,512]{1,0:T(8,128)S(1)}, u32[]{:S(2)}, u32[]{:S(2)}) collective-permute-start(f32[16,512]{1,0:T(8,128)S(1)} %get-tuple-element.56), channel_id=1, source_target_pairs={{0,4},{4,0},{8,12},{12,8},{1,5},{5,1},{9,13},{13,9},{2,6},{6,2},{1... | collective-permute-start | bytes 98312 | tf_op jit(solution)/shard_map/ppermute | solution.py:692

commit v10 on v9

--- a/solution.py
+++ b/solution.py
@@ -119,7 +119,7 @@
 LANES = 1 << LANE_BITS
 FEATURE_ROWS = 128
 FIRST = 1152
-TAKEN = 768
+TAKEN = 512
 NT = (((1,), (1,)), ((), ()))
 LARGE_VMEM, MODEST_VMEM = 44 * 1024 * 1024, 15 * 1024 * 1024
 
@@ -157,6 +157,10 @@
     )
     mode = lax.GatherScatterMode.PROMISE_IN_BOUNDS
     return lax.gather(x, lanes[..., None], numbers, slice_sizes=(1, 1), mode=mode)
+
+
+def load_ids(ref):
+    return jnp.concatenate([ref[text] for text in range(ref.shape[0])], axis=0)
 
 
 def fetch(pairs, sems):
@@ -184,7 +188,7 @@
     out_sems,
     base,
 ):
-    texts, length = ids_ref.shape
+    texts, _, length = ids_ref.shape
     features, vocab = vocab_ref.shape
     blocks = vocab // IDS_PER_BLOCK
     groups = vocab // IDS_PER_GROUP
@@ -198,7 +202,7 @@
     for b in range(1, blocks):
         vocab_copy(b).start()
 
-    ids = ids_ref[...]
+    ids = load_ids(ids_ref)
     valid = ids != 0
     group_of = jnp.where(valid, lax.shift_right_logical(ids, GROUP_BITS), groups)
     group_rows = counted.shape[0]
@@ -327,17 +331,32 @@
         extra_ref[start : start + ROWS, :] = spread[:, pl.ds(quarter, STRIPE)].astype(jnp.bfloat16)
 
 
+def join_kernel(own_any, core_any, extra_ref, core_extra_ref, chip_ref, inputs_ref, own, core, sems):
+    fetch([(own_any, own), (core_any, core)], sems)
+    span = own.shape[0]
+    common = extra_ref.shape[0] - 4 * ROWS
+    near, across = extra_ref[...].astype(jnp.float32), core_extra_ref[...].astype(jnp.float32)
+    chip_ref[0:span, :] = (own[...] + core[...].astype(jnp.float32)).astype(jnp.bfloat16)
+    chip = near[0:common] + across[0:common]
+    inputs = near[common : common + 2 * ROWS] + across[common + 2 * ROWS :]
+    sent = jnp.concatenate([chip, inputs[ROWS:]]).astype(jnp.bfloat16)
+    chip_ref[span : span + common + ROWS, :] = sent
+    inputs_ref[...] = inputs[0:ROWS]
+
+
 def pool_kernel(
     ids_ref,
     own_ref,
     core_any,
     far_any,
-    extra_ref,
+    chip_any,
+    inputs_ref,
     member_ref,
     own_rest,
     core_rest,
     far_rest,
-    extra_rest,
+    chip_rest,
+    inputs_rest,
     member_rest,
     raise_ref,
     sent_ref,
@@ -347,33 +366,41 @@
     slopes,
     core_ref,
     far_ref,
+    chip_ref,
     sems,
+    *rest,
     model_width,
 ):
-    texts, length = ids_ref.shape
+    texts, _, length = ids_ref.shape
     width = own_ref.shape[1]
     quarter = quarter_of(lax.axis_index("dp"))
-    fetch([(core_any, core_ref), (far_any, far_ref)], sems)
+    extra_rows = far_ref.shape[0] - own_ref.shape[0]
+    chip_extra = chip_any.at[pl.ds(own_ref.shape[0], extra_rows)]
+    fetch([(core_any, core_ref), (far_any, far_ref), (chip_extra, chip_ref)], sems)
     raised[...] = jnp.zeros_like(raised)
     raised[0:ROWS, :] = raise_ref[:, pl.ds(pl.multiple_of(quarter * width, LANES), width)]
     total[...] = jnp.zeros_like(total)
     slopes[...] = jnp.zeros_like(slopes)
 
-    def add(refs, extra_ref, member_ref, base):
+    def add(refs, far_ref, chip_ref, inputs_ref, member_ref, base):
         span = member_ref.shape[0]
         stripes = pl.cdiv(span, STRIPE)
 
         def summed(start, size):
             return sum(ref[pl.ds(start, size), :].astype(jnp.float32) for ref in refs)
 
-        misc = extra_ref[stripes * ROWS : (stripes + 1) * ROWS, :]
+        def extra(row):
+            near, far = chip_ref[pl.ds(row, ROWS), :], far_ref[pl.ds(span + row, ROWS), :]
+            return near.astype(jnp.float32) + far.astype(jnp.float32)
+
+        misc = extra(stripes * ROWS)
         if base == 0:
             misc_ref[...] = misc
         inverse = lax.rsqrt(misc / model_width + 1e-05)
         for k in range(stripes):
             size = min(STRIPE, span - k * STRIPE)
             scale = inverse[k : k + 1]
-            reduced = (extra_ref[k * ROWS : (k + 1) * ROWS, :] * scale).astype(jnp.bfloat16)
+            reduced = (extra(k * ROWS) * scale).astype(jnp.bfloat16)
             reduced = reduced.astype(jnp.float32)
             stacked = jnp.concatenate([reduced, jnp.broadcast_to(scale, (LANES - ROWS, STRIPE))])
             turned = stacked[:, 0:size].T
@@ -388,14 +415,21 @@
             total[...] += mm(chosen, high) + mm(chosen, rest)
             spread = [reduced[:, 0:size] * member[text : text + 1] for text in range(texts)]
             slopes[...] += mm(jnp.concatenate(spread).astype(jnp.bfloat16), slope)
-        total[...] += extra_ref[(stripes + 1) * ROWS : (stripes + 2) * ROWS, :]
-
-    add((own_ref, core_ref, far_ref), extra_ref, member_ref, 0)
-    real = (ids_ref[...] != 0).astype(jnp.float32)
+        far_inputs = far_ref[pl.ds(span + (stripes + 1) * ROWS, ROWS), :]
+        total[...] += inputs_ref[...] + far_inputs.astype(jnp.float32)
+
+    add((own_ref, core_ref, far_ref), far_ref, chip_ref, inputs_ref, member_ref, 0)
+    real = (load_ids(ids_ref) != 0).astype(jnp.float32)
 
     @pl.when(jnp.sum(real) > member_ref.shape[0])
     def _():
-        add((own_rest, core_rest, far_rest), extra_rest, member_rest, member_ref.shape[0])
+        *here, rest_sems = rest
+        span = member_rest.shape[0]
+        chip_extra = chip_rest.at[pl.ds(span, here[3].shape[0])]
+        there = (own_rest, core_rest, far_rest, chip_extra, inputs_rest, member_rest)
+        fetch(list(zip(there, here)), rest_sems)
+        own, core, far, chip, inputs, member = here
+        add((own, core, far), far, chip, inputs, member, member_ref.shape[0])
 
     counts = jnp.sum(real, axis=1, keepdims=True)
     pooled = total[0:texts] / counts
@@ -534,8 +568,8 @@
     logit_sharpness,
 ):
     shards, parts = lax.axis_size("dp"), lax.axis_size("mp")
-    ids = query_passage_words[0]
-    texts, length = ids.shape
+    texts, length = query_passage_words.shape[1:]
+    ids = query_passage_words.reshape(texts, 1, length)
     tokens = texts * length
     features, vocab = vocabulary_vectors.shape
     blocks = vocab // IDS_PER_BLOCK
@@ -586,9 +620,7 @@
             return x.astype(jnp.bfloat16)
 
         core1 = lax.ppermute(narrow(product(turned, 1, 1)), "dp", other_core)
-        chip1 = narrow(product(turned, 0, 1) + core1.astype(jnp.float32))
-        far = lax.ppermute(chip1, "dp", other_y)
-        turned, _ = lax.optimization_barrier((turned, chip1))
+        own1 = lax.optimization_barrier(product(turned, 0, 1))
         extra = pl.pallas_call(
             statistics_kernel,
             out_shape=jax.ShapeDtypeStruct((extra_rows, STRIPE), jnp.bfloat16),
@@ -609,17 +641,29 @@
             ),
             name="statistics",
         )(turned, member, difficult_distractors, lowering_factor_matrix)
-        common = (stripes + 1) * ROWS
-        near = extra.astype(jnp.float32)
-        across = lax.ppermute(extra, "dp", other_core).astype(jnp.float32)
-        chip = near[0:common] + across[0:common]
-        inputs = near[common : common + 2 * ROWS] + across[common + 2 * ROWS :]
-        sent = narrow(jnp.concatenate([chip, inputs[ROWS:]]))
-        sent = lax.ppermute(sent, "dp", other_y).astype(jnp.float32)
-        extra = jnp.concatenate([chip, inputs[0:ROWS]]) + sent
+        core_extra = lax.ppermute(extra, "dp", other_core)
+        joined = span + extra_rows - 3 * ROWS
+        chip, inputs = pl.pallas_call(
+            join_kernel,
+            out_shape=[
+                jax.ShapeDtypeStruct((joined, width), jnp.bfloat16),
+                jax.ShapeDtypeStruct((ROWS, width), jnp.float32),
+            ],
+            in_specs=[any_spec()] * 2 + [vmem_spec()] * 2,
+            out_specs=[vmem_spec()] * 2,
+            scratch_shapes=[
+                pltpu.VMEM(own1.shape, own1.dtype),
+                pltpu.VMEM(core1.shape, core1.dtype),
+                pltpu.SemaphoreType.DMA((2,)),
+            ],
+            compiler_params=modest,
+            name="join",
+        )(own1, core1, extra, core_extra)
+        far = lax.ppermute(chip, "dp", other_y)
+        turned, _ = lax.optimization_barrier((turned, chip))
         core0 = lax.ppermute(narrow(product(turned, 1, 0)), "dp", other_core)
         own0 = narrow(product(turned, 0, 0))
-        return own0, core0, far, extra, member
+        return own0, core0, far, chip, inputs, member
 
     first = project(0, FIRST)
     later, _ = lax.optimization_barrier((ids, first[0]))
@@ -637,15 +681,23 @@
             jax.ShapeDtypeStruct(((texts + 1) * ROWS, width), jnp.bfloat16),
             jax.ShapeDtypeStruct((ROWS, width), jnp.float32),
         ],
-        in_specs=[vmem_spec()] * 2 + [any_spec()] * 2 + [vmem_spec()] * 8,
+        in_specs=[vmem_spec()] * 2
+        + [any_spec()] * 3
+        + [vmem_spec()] * 2
+        + [any_spec()] * 6
+        + [vmem_spec()],
         out_specs=[vmem_spec()] * 2,
         scratch_shapes=[
             pltpu.VMEM((LANES, width), jnp.bfloat16),
             pltpu.VMEM((ROWS, width), jnp.float32),
             pltpu.VMEM((texts * ROWS, width), jnp.float32),
-            pltpu.VMEM((FIRST, width), jnp.bfloat16),
-            pltpu.VMEM((FIRST, width), jnp.bfloat16),
-            pltpu.SemaphoreType.DMA((2,)),
+            *[pltpu.VMEM(x.shape, x.dtype) for x in first[1:3]],
+            pltpu.VMEM((first[2].shape[0] - FIRST, width), jnp.bfloat16),
+            pltpu.SemaphoreType.DMA((3,)),
+            *[pltpu.VMEM(x.shape, x.dtype) for x in rest[0:3]],
+            pltpu.VMEM((rest[2].shape[0] - left, width), jnp.bfloat16),
+            *[pltpu.VMEM(x.shape, x.dtype) for x in rest[4:6]],
+            pltpu.SemaphoreType.DMA((6,)),
         ],
         compiler_params=modest,
         name="pool",

time: 70.1 us -> 75.4 us (1.076)
  Pallas kernels: 21.3 us -> 27.7 us
  matrix products: 8.09 us -> 10.1 us
  waiting for transfers between devices: 20.5 us -> 18.8 us
  other arithmetic: 2.23 us -> 1.29 us
    pallas_call x0 -> x1, Pallas kernels: none -> 3.19 us  [project(): pl.pallas_call(join_kernel, out_shape=[jax.ShapeDtypeStruct((joined, widt...]
    pallas_call x1, Pallas kernels: 14.7 us -> 17.3 us  [project(): pl.pallas_call(functools.partial(gather_kernel, base=base), out_shape=[ja...]
    ppermute x6, waiting for transfers between devices: 5.98 us -> 8.28 us  [exchange(): return [x] + [lax.ppermute(x, axis, step) for step in steps]]
    dot_general x4, matrix products: 8.09 us -> 10.1 us  [mm(): return lax.dot_general(a, b, dims, preferred_element_type=jnp.float32)]
    ppermute x1, waiting for transfers between devices: 1.76 us -> 0.01 us  [project(): core1 = lax.ppermute(narrow(product(turned, 1, 1)), 'dp', other_core)]
    ppermute x3 -> x2, waiting for transfers between devices: 7.7 us -> 6.01 us  [the longest x1 6.01 us: project(): far = lax.ppermute(chip, 'dp', other_y)]
    convert_element_type x2 -> x0, other arithmetic: 0.91 us -> none  [the longest x1 0.9 us: project(): across = lax.ppermute(extra, 'dp', other_core).astype(jnp.float32)]
    another operation x5 -> x6, local copies, waits for them, and re-layouts: 1.41 us -> 2.12 us
  transfers between devices with their start and end apart: 14 -> 13, of which waited for: 8 -> 7; matrix products, arithmetic and copies ran while one was open for 9% -> 13% of each run, Pallas kernels for 0% -> 3%
where the time goes in v10:
time: 75.4 us; the launch traced here: 74.8 us
  Pallas kernels  27.7 us (37%)
  waiting for transfers between devices  18.8 us (25%)
  starting transfers between devices  12.5 us (17%)
  matrix products  10.1 us (13%)
  between operations  2.17 us (3%)
  local copies, waits for them, and re-layouts  2.16 us (3%)
  other arithmetic  1.29 us (2%)
    pallas_call x1, Pallas kernels, project(): pl.pallas_call(functools.partial(gather_kernel, base=base), out_shape=[ja...  17.3 us
    dot_general x4, matrix products, mm(): return lax.dot_general(a, b, dims, preferred_element_type=jnp.float32)  10.1 us
    ppermute x6, waiting for transfers between devices, exchange(): return [x] + [lax.ppermute(x, axis, step) for step in steps]  8.28 us
    ppermute x6, starting transfers between devices, exchange(): return [x] + [lax.ppermute(x, axis, step) for step in steps]  6.33 us
    ppermute x1, waiting for transfers between devices, project(): far = lax.ppermute(chip, 'dp', other_y)  6.01 us
    ppermute x1, waiting for transfers between devices, split_body(): far_side = lax.ppermute(sent, 'group', [(0, 1), (1, 0)])  3.34 us
    pallas_call x1, Pallas kernels, project(): pl.pallas_call(join_kernel, out_shape=[jax.ShapeDtypeStruct((joined, widt...  3.19 us
    ppermute x1, starting transfers between devices, project(): far = lax.ppermute(chip, 'dp', other_y)  3.03 us
  transfers between devices with their start and end apart: 13, of which 7 were waited for; matrix products, arithmetic and copies ran while one was open for 13% of the time, Pallas kernels for 3%

profile of v10, /device:TPU:0, one launch (start us, length us, event | category | flops | bytes accessed | tf_op | source)
XLA Modules:
  0.0 74.8 jit_solution(2624105560706613669)
XLA Ops:
  0.6 17.3 %gather.3 = (bf16[1024,1152]{1,0:T(8,128)(2,1)S(1)}, bf16[1152,128]{1,0:T(8,128)(2,1)S(1)}) custom-call(s32[12,1,128]{2,1,0:T(1,128)} %bitcast.9, bf16[1024,16384]{1,0:T(8,128)(2,1)} %vocab_ref.1), custom_call_target="tpu_custom_call" | custom-call | tf_op jit(solution)/shard_map/gather/pallas_call | solution.py:592
  18.0 2.8 %convolution_convert_fusion.5 = bf16[1152,256]{1,0:T(8,128)(2,1)} fusion(bf16[1024,1152]{1,0:T(8,128)(2,1)S(1)} %get-tuple-element.47.turned_any, bf16[1024,1024]{1,0:T(8,128)(2,1)} %param.12, s32[]{:T(128)S(6)} %select_n.37), kind=kOutput, calls=%fused_computation.14 | convolution fusion | flops 604274688 | bytes 3473412 | tf_op jit(solution)/shard_map/dot_general | solution.py:128
  21.3 2.0 %statistics.3.extra_ref = bf16[160,256]{1,0:T(8,128)(2,1)} custom-call(bf16[1024,1152]{1,0:T(8,128)(2,1)S(1)} %get-tuple-element.47.turned_any, bf16[1152,128]{1,0:T(8,128)(2,1)S(1)} %get-tuple-element.45.member_any.member_ref, s32[3,7]{1,0:T(4,128)S(1)} %copy-done.9, bf16[16,4096]{1,0:T(8,128)(2,1)S(1)} %copy-done.6), custom_call_target="tpu_custom_call" | custom-call | flops 339738624 | bytes 2359296 | tf_op jit(solution)/shard_map/statistics/pallas_call | solution.py:624
  23.5 1.9 %fusion.12.own_any = f32[1152,256]{1,0:T(8,128)S(1)} fusion(bf16[1024,1152]{1,0:T(8,128)(2,1)S(1)} %get-tuple-element.47.turned_any, bf16[1024,1024]{1,0:T(8,128)(2,1)} %param.12, s32[]{:T(128)S(6)} %select_n.36), kind=kOutput, calls=%fused_computation.18 | convolution fusion | flops 603979776 | bytes 4063236 | tf_op jit(solution)/shard_map/dot_general | solution.py:128
  25.4 3.2 %join.3 = (bf16[1264,256]{1,0:T(8,128)(2,1)}, f32[16,256]{1,0:T(8,128)S(1)}) custom-call(f32[1152,256]{1,0:T(8,128)S(1)} %fusion.12.own_any, bf16[1152,256]{1,0:T(8,128)(2,1)} %collective-permute-done.4.core_any, bf16[160,256]{1,0:T(8,128)(2,1)} %statistics.3.extra_ref, bf16[160,256]{1,0:T(8,128)(2,1)} %collective-permute-done.5.core_extra_ref), custom_call_target="tpu_custom_call" | custom-call | tf_op jit(solution)/shard_map/join/pallas_call | solution.py:646
  28.6 3.0 %collective-permute-start.7 = (bf16[1264,256]{1,0:T(8,128)(2,1)}, bf16[1264,256]{1,0:T(8,128)(2,1)S(1)}, u32[]{:S(2)}, u32[]{:S(2)}) collective-permute-start(bf16[1264,256]{1,0:T(8,128)(2,1)} %get-tuple-element.46.chip_any), channel_id=1, source_target_pairs={{0,8},{4,12},{8,0},{12,4},{1,9},{5,13},{9,1},{13,5},{2,10},{6,14},... | collective-permute-start | bytes 1941512 | tf_op jit(solution)/shard_map/ppermute | solution.py:662
  31.6 2.7 %convolution_convert_fusion.3 = bf16[1152,256]{1,0:T(8,128)(2,1)} fusion(bf16[1024,1152]{1,0:T(8,128)(2,1)S(1)} %get-tuple-element.47.turned_any, bf16[1024,1024]{1,0:T(8,128)(2,1)} %param.12, s32[]{:T(128)S(6)} %select_n.39), kind=kOutput, calls=%fused_computation.12 | convolution fusion | flops 604274688 | bytes 3473412 | tf_op jit(solution)/shard_map/dot_general | solution.py:128
  34.3 2.8 %convolution_convert_fusion.4.own_ref = bf16[1152,256]{1,0:T(8,128)(2,1)} fusion(bf16[1024,1152]{1,0:T(8,128)(2,1)S(1)} %get-tuple-element.47.turned_any, bf16[1024,1024]{1,0:T(8,128)(2,1)} %param.12, s32[]{:T(128)S(6)} %select_n.38), kind=kOutput, calls=%fused_computation.13 | convolution fusion | flops 604274688 | bytes 3473412 | tf_op jit(solution)/shard_map/dot_general | solution.py:128
  38.4 2.1 %conditional.1 = (bf16[384,256]{1,0:T(8,128)(2,1)S(1)}, bf16[384,256]{1,0:T(8,128)(2,1)}, bf16[448,256]{1,0:T(8,128)(2,1)}, bf16[448,256]{1,0:T(8,128)(2,1)}, f3...) conditional(s32[]{:T(128)} %convert_element_type.28, () %tuple.22, (s32[12,1,128]{2,1,0:T(1,128)S(1)}, ...), branch_computations={%region_1.0_spmd, %region_2.0_spmd} | conditional | flops 918847488 | bytes 10519216 | solution.py:673
  39.1 0.7 broadcast.11
  40.6 6.0 %collective-permute-done.7.far_any = bf16[1264,256]{1,0:T(8,128)(2,1)S(1)} collective-permute-done((bf16[1264,256]{1,0:T(8,128)(2,1)}, bf16[1264,256]{1,0:T(8,128)(2,1)S(1)}, u32[]{:S(2)}, u32[]{:S(2)}) %collective-permute-start.7) | collective-permute-done | bytes 647200 | tf_op jit(solution)/shard_map/ppermute | solution.py:662
  46.6 3.0 %pool.1 = (bf16[208,256]{1,0:T(8,128)(2,1)S(1)}, f32[16,256]{1,0:T(8,128)S(1)}) custom-call(s32[12,1,128]{2,1,0:T(1,128)S(1)} %bitcast.12, bf16[1152,256]{1,0:T(8,128)(2,1)S(1)} %copy-done.2, bf16[1152,256]{1,0:T(8,128)(2,1)} %collective-permute-done.6.core_any, bf16[1264,256]{1,0:T(8,128)(2,1)S(1)} %collective-permute-done.7.far_any, ...), custom_call_target="tpu_custom_call" | custom-call | tf_op jit(solution)/shard_map/pool/pallas_call | solution.py:678
  49.6 1.4 %collective-permute-start.8 = (bf16[208,256]{1,0:T(8,128)(2,1)S(1)}, bf16[208,256]{1,0:T(8,128)(2,1)S(1)}, u32[]{:S(2)}, u32[]{:S(2)}) collective-permute-start(bf16[208,256]{1,0:T(8,128)(2,1)S(1)} %get-tuple-element.56.near_ref), channel_id=1, source_target_pairs={{0,16},{16,0},{1,17},{17,1},{2,18},{18,2},{3,19},{19,3},{4,20},{20... | collective-permute-start | bytes 319496 | tf_op jit(solution)/shard_map/ppermute | solution.py:705
  51.0 3.3 %collective-permute-done.8.far_any = bf16[208,256]{1,0:T(8,128)(2,1)S(1)} collective-permute-done((bf16[208,256]{1,0:T(8,128)(2,1)S(1)}, bf16[208,256]{1,0:T(8,128)(2,1)S(1)}, u32[]{:S(2)}, u32[]{:S(2)}) %collective-permute-start.8) | collective-permute-done | bytes 106528 | tf_op jit(solution)/shard_map/ppermute | solution.py:705
  54.7 1.8 %collective-permute-start.10 = (f32[96,128]{1,0:T(8,128)S(1)}, f32[96,128]{1,0:T(8,128)S(1)}, u32[]{:S(2)}, u32[]{:S(2)}) collective-permute-start(f32[96,128]{1,0:T(8,128)S(1)} %get-tuple-element.57.refs_0_), channel_id=1, source_target_pairs={{0,8},{4,12},{8,0},{12,4},{1,9},{5,13},{9,1},{13,5},{2,10},{6,14},... | collective-permute-start | bytes 147464 | tf_op jit(solution)/shard_map/ppermute | solution.py:558
  56.5 2.3 %collective-permute-done.10.refs_2_ = f32[96,128]{1,0:T(8,128)S(1)} collective-permute-done((f32[96,128]{1,0:T(8,128)S(1)}, f32[96,128]{1,0:T(8,128)S(1)}, u32[]{:S(2)}, u32[]{:S(2)}) %collective-permute-start.10) | collective-permute-done | bytes 49184 | tf_op jit(solution)/shard_map/ppermute | solution.py:558
  58.8 1.3 %collective-permute-done.11.refs_3_ = f32[96,128]{1,0:T(8,128)S(1)} collective-permute-done((f32[96,128]{1,0:T(8,128)S(1)}, f32[96,128]{1,0:T(8,128)S(1)}, u32[]{:S(2)}, u32[]{:S(2)}) %collective-permute-start.11) | collective-permute-done | bytes 49184 | tf_op jit(solution)/shard_map/ppermute | solution.py:558
  60.2 1.1 %collective-permute-start.12 = (bf16[384,256]{1,0:T(8,128)(2,1)S(1)}, bf16[384,256]{1,0:T(8,128)(2,1)S(1)}, u32[]{:S(2)}, u32[]{:S(2)}) collective-permute-start(bf16[384,256]{1,0:T(8,128)(2,1)S(1)} %get-tuple-element.59.refs_4_), channel_id=1, source_target_pairs={{0,8},{4,12},{8,0},{12,4},{1,9},{5,13},{9,1},{13,5},{2,10},{6,14},... | collective-permute-start | bytes 589832 | tf_op jit(solution)/shard_map/ppermute | solution.py:727
  61.2 1.6 %collective-permute-start.13 = (f32[32,128]{1,0:T(8,128)S(1)}, f32[32,128]{1,0:T(8,128)S(1)}, u32[]{:S(2)}, u32[]{:S(2)}) collective-permute-start(f32[32,128]{1,0:T(8,128)S(1)} %fusion.14.refs_6_), channel_id=1, source_target_pairs={{0,1},{1,0},{2,3},{3,2},{4,5},{5,4},{6,7},{7,6},{8,9},{9,8},{10,11... | collective-permute-start | bytes 49160 | tf_op jit(solution)/shard_map/ppermute | solution.py:558
  62.8 2.6 %collective-permute-start.14 = (f32[32,128]{1,0:T(8,128)S(1)}, f32[32,128]{1,0:T(8,128)S(1)}, u32[]{:S(2)}, u32[]{:S(2)}) collective-permute-start(f32[32,128]{1,0:T(8,128)S(1)} %fusion.14.refs_6_), channel_id=1, source_target_pairs={{0,2},{1,3},{2,0},{3,1},{4,6},{5,7},{6,4},{7,5},{8,10},{9,11},{10,... | collective-permute-start | bytes 49160 | tf_op jit(solution)/shard_map/ppermute | solution.py:558
  66.3 1.4 %collective-permute-done.14.refs_8_ = f32[32,128]{1,0:T(8,128)S(1)} collective-permute-done((f32[32,128]{1,0:T(8,128)S(1)}, f32[32,128]{1,0:T(8,128)S(1)}, u32[]{:S(2)}, u32[]{:S(2)}) %collective-permute-start.14) | collective-permute-done | bytes 16416 | tf_op jit(solution)/shard_map/ppermute | solution.py:558
  67.7 3.3 %collective-permute-done.15.refs_9_ = f32[32,128]{1,0:T(8,128)S(1)} collective-permute-done((f32[32,128]{1,0:T(8,128)S(1)}, f32[32,128]{1,0:T(8,128)S(1)}, u32[]{:S(2)}, u32[]{:S(2)}) %collective-permute-start.15) | collective-permute-done | bytes 16416 | tf_op jit(solution)/shard_map/ppermute | solution.py:558
  70.9 1.9 %score.1 = (bf16[1,3,1024]{2,1,0:T(4,128)(2,1)}, f32[1,3]{1,0:T(1,128)}, f32[16,512]{1,0:T(8,128)S(1)}) custom-call(f32[96,128]{1,0:T(8,128)S(1)} %get-tuple-element.57.refs_0_, f32[96,128]{1,0:T(8,128)S(1)} %collective-permute-done.9.refs_1_, f32[96,128]{1,0:T(8,128)S(1)} %collective-permute-done.10.refs_2_, f32[96,128]{1,0:T(8,128)S(1)} %collective-permute-done.11.refs_3_, ...), custom_call_target="tpu_custom_call" | custom-call | tf_op jit(solution)/shard_map/score/pallas_call | solution.py:728
  72.9 1.2 %collective-permute-done.16 = f32[16,512]{1,0:T(8,128)S(1)} collective-permute-done((f32[16,512]{1,0:T(8,128)S(1)}, f32[16,512]{1,0:T(8,128)S(1)}, u32[]{:S(2)}, u32[]{:S(2)}) %collective-permute-start.16) | collective-permute-done | bytes 32800 | tf_op jit(solution)/shard_map/ppermute | solution.py:744
  (41 shorter events, 4.0 us)
Async XLA Ops:
  18.0 3.3 %copy-start = (bf16[1152,128]{1,0:T(8,128)(2,1)}, bf16[1152,128]{1,0:T(8,128)(2,1)S(1)}, u32[]{:S(2)}) copy-start(bf16[1152,128]{1,0:T(8,128)(2,1)S(1)} %get-tuple-element.45.member_any.member_ref) | copy-start | bytes 884740
  18.0 3.3 %copy-start.6 = (bf16[16,4096]{1,0:T(8,128)(2,1)S(1)}, bf16[16,4096]{1,0:T(8,128)(2,1)}, u32[]{:S(2)}) copy-start(bf16[16,4096]{1,0:T(8,128)(2,1)} %lower_ref.1) | copy-start | bytes 393220
  18.0 3.3 %copy-start.9 = (s32[3,7]{1,0:T(4,128)S(1)}, s32[3,7]{1,0:T(4,128)}, u32[]{:S(2)}) copy-start(s32[3,7]{1,0:T(4,128)} %hard_ref.1) | copy-start | bytes 256
  20.9 4.5 %collective-permute-start.4 = (bf16[1152,256]{1,0:T(8,128)(2,1)}, bf16[1152,256]{1,0:T(8,128)(2,1)}, u32[]{:S(2)}, u32[]{:S(2)}) collective-permute-start(bf16[1152,256]{1,0:T(8,128)(2,1)} %convolution_convert_fusion.5), channel_id=1, source_target_pairs={{0,4},{4,0},{8,12},{12,8},{1,5},{5,1},{9,13},{13,9},{2,6},{6,2},{1... | collective-permute-start | bytes 1769480 | tf_op jit(solution)/shard_map/ppermute | solution.py:622
  23.4 2.0 %collective-permute-start.5 = (bf16[160,256]{1,0:T(8,128)(2,1)}, bf16[160,256]{1,0:T(8,128)(2,1)}, u32[]{:S(2)}, u32[]{:S(2)}) collective-permute-start(bf16[160,256]{1,0:T(8,128)(2,1)} %statistics.3.extra_ref), channel_id=1, source_target_pairs={{0,4},{4,0},{8,12},{12,8},{1,5},{5,1},{9,13},{13,9},{2,6},{6,2},{1... | collective-permute-start | bytes 245768 | tf_op jit(solution)/shard_map/ppermute | solution.py:644
  28.6 18.0 %collective-permute-start.7 = (bf16[1264,256]{1,0:T(8,128)(2,1)}, bf16[1264,256]{1,0:T(8,128)(2,1)S(1)}, u32[]{:S(2)}, u32[]{:S(2)}) collective-permute-start(bf16[1264,256]{1,0:T(8,128)(2,1)} %get-tuple-element.46.chip_any), channel_id=1, source_target_pairs={{0,8},{4,12},{8,0},{12,4},{1,9},{5,13},{9,1},{13,5},{2,10},{6,14},... | collective-permute-start | bytes 1941512 | tf_op jit(solution)/shard_map/ppermute | solution.py:662
  34.3 6.3 %collective-permute-start.6 = (bf16[1152,256]{1,0:T(8,128)(2,1)}, bf16[1152,256]{1,0:T(8,128)(2,1)}, u32[]{:S(2)}, u32[]{:S(2)}) collective-permute-start(bf16[1152,256]{1,0:T(8,128)(2,1)} %convolution_convert_fusion.3), channel_id=1, source_target_pairs={{0,4},{4,0},{8,12},{12,8},{1,5},{5,1},{9,13},{13,9},{2,6},{6,2},{1... | collective-permute-start | bytes 1769480 | tf_op jit(solution)/shard_map/ppermute | solution.py:664
  34.3 2.8 %copy-start.8 = (s32[1,12,128]{2,0,1:T(1,128)S(1)}, s32[1,12,128]{2,0,1:T(1,128)}, u32[]{:S(2)}) copy-start(s32[1,12,128]{2,0,1:T(1,128)} %param.9) | copy-start | bytes 18436
  34.3 4.1 %copy-start.7 = (bf16[16,4096]{1,0:T(8,128)(2,1)S(1)}, bf16[16,4096]{1,0:T(8,128)(2,1)}, u32[]{:S(2)}) copy-start(bf16[16,4096]{1,0:T(8,128)(2,1)} %lower_ref.1) | copy-start | bytes 393220
  34.3 4.1 %copy-start.10 = (s32[3,7]{1,0:T(4,128)S(1)}, s32[3,7]{1,0:T(4,128)}, u32[]{:S(2)}) copy-start(s32[3,7]{1,0:T(4,128)} %hard_ref.1) | copy-start | bytes 256
  38.4 8.2 %copy-start.1 = (bf16[1152,128]{1,0:T(8,128)(2,1)S(1)}, bf16[1152,128]{1,0:T(8,128)(2,1)}, u32[]{:S(2)}) copy-start(bf16[1152,128]{1,0:T(8,128)(2,1)} %copy-done) | copy-start | bytes 884740
  38.4 8.2 %copy-start.2 = (bf16[1152,256]{1,0:T(8,128)(2,1)S(1)}, bf16[1152,256]{1,0:T(8,128)(2,1)}, u32[]{:S(2)}) copy-start(bf16[1152,256]{1,0:T(8,128)(2,1)} %convolution_convert_fusion.4.own_ref) | copy-start | bytes 1769476
  38.4 8.2 %copy-start.3 = (bf16[16,1024]{1,0:T(8,128)(2,1)S(1)}, bf16[16,1024]{1,0:T(8,128)(2,1)}, u32[]{:S(2)}) copy-start(bf16[16,1024]{1,0:T(8,128)(2,1)} %raise_ref.1) | copy-start | bytes 98308
  49.6 4.8 %collective-permute-start.8 = (bf16[208,256]{1,0:T(8,128)(2,1)S(1)}, bf16[208,256]{1,0:T(8,128)(2,1)S(1)}, u32[]{:S(2)}, u32[]{:S(2)}) collective-permute-start(bf16[208,256]{1,0:T(8,128)(2,1)S(1)} %get-tuple-element.56.near_ref), channel_id=1, source_target_pairs={{0,16},{16,0},{1,17},{17,1},{2,18},{18,2},{3,19},{19,3},{4,20},{20... | collective-permute-start | bytes 319496 | tf_op jit(solution)/shard_map/ppermute | solution.py:705
  54.6 2.0 %collective-permute-start.9 = (f32[96,128]{1,0:T(8,128)S(1)}, f32[96,128]{1,0:T(8,128)S(1)}, u32[]{:S(2)}, u32[]{:S(2)}) collective-permute-start(f32[96,128]{1,0:T(8,128)S(1)} %get-tuple-element.57.refs_0_), channel_id=1, source_target_pairs={{0,4},{4,0},{8,12},{12,8},{1,5},{5,1},{9,13},{13,9},{2,6},{6,2},{1... | collective-permute-start | bytes 147464 | tf_op jit(solution)/shard_map/ppermute | solution.py:558
  54.7 4.2 %collective-permute-start.10 = (f32[96,128]{1,0:T(8,128)S(1)}, f32[96,128]{1,0:T(8,128)S(1)}, u32[]{:S(2)}, u32[]{:S(2)}) collective-permute-start(f32[96,128]{1,0:T(8,128)S(1)} %get-tuple-element.57.refs_0_), channel_id=1, source_target_pairs={{0,8},{4,12},{8,0},{12,4},{1,9},{5,13},{9,1},{13,5},{2,10},{6,14},... | collective-permute-start | bytes 147464 | tf_op jit(solution)/shard_map/ppermute | solution.py:558
  56.5 3.7 %collective-permute-start.11 = (f32[96,128]{1,0:T(8,128)S(1)}, f32[96,128]{1,0:T(8,128)S(1)}, u32[]{:S(2)}, u32[]{:S(2)}) collective-permute-start(f32[96,128]{1,0:T(8,128)S(1)} %get-tuple-element.57.refs_0_), channel_id=1, source_target_pairs={{0,12},{4,8},{8,4},{12,0},{1,13},{5,9},{9,5},{13,1},{2,14},{6,10},... | collective-permute-start | bytes 147464 | tf_op jit(solution)/shard_map/ppermute | solution.py:558
  60.2 10.8 %collective-permute-start.12 = (bf16[384,256]{1,0:T(8,128)(2,1)S(1)}, bf16[384,256]{1,0:T(8,128)(2,1)S(1)}, u32[]{:S(2)}, u32[]{:S(2)}) collective-permute-start(bf16[384,256]{1,0:T(8,128)(2,1)S(1)} %get-tuple-element.59.refs_4_), channel_id=1, source_target_pairs={{0,8},{4,12},{8,0},{12,4},{1,9},{5,13},{9,1},{13,5},{2,10},{6,14},... | collective-permute-start | bytes 589832 | tf_op jit(solution)/shard_map/ppermute | solution.py:727
  61.2 5.0 %collective-permute-start.13 = (f32[32,128]{1,0:T(8,128)S(1)}, f32[32,128]{1,0:T(8,128)S(1)}, u32[]{:S(2)}, u32[]{:S(2)}) collective-permute-start(f32[32,128]{1,0:T(8,128)S(1)} %fusion.14.refs_6_), channel_id=1, source_target_pairs={{0,1},{1,0},{2,3},{3,2},{4,5},{5,4},{6,7},{7,6},{8,9},{9,8},{10,11... | collective-permute-start | bytes 49160 | tf_op jit(solution)/shard_map/ppermute | solution.py:558
  62.8 4.9 %collective-permute-start.14 = (f32[32,128]{1,0:T(8,128)S(1)}, f32[32,128]{1,0:T(8,128)S(1)}, u32[]{:S(2)}, u32[]{:S(2)}) collective-permute-start(f32[32,128]{1,0:T(8,128)S(1)} %fusion.14.refs_6_), channel_id=1, source_target_pairs={{0,2},{1,3},{2,0},{3,1},{4,6},{5,7},{6,4},{7,5},{8,10},{9,11},{10,... | collective-permute-start | bytes 49160 | tf_op jit(solution)/shard_map/ppermute | solution.py:558
  65.4 5.5 %collective-permute-start.15 = (f32[32,128]{1,0:T(8,128)S(1)}, f32[32,128]{1,0:T(8,128)S(1)}, u32[]{:S(2)}, u32[]{:S(2)}) collective-permute-start(f32[32,128]{1,0:T(8,128)S(1)} %fusion.14.refs_6_), channel_id=1, source_target_pairs={{0,3},{1,2},{2,1},{3,0},{4,7},{5,6},{6,5},{7,4},{8,11},{9,10},{10,... | collective-permute-start | bytes 49160 | tf_op jit(solution)/shard_map/ppermute | solution.py:558
  72.9 1.3 %collective-permute-start.16 = (f32[16,512]{1,0:T(8,128)S(1)}, f32[16,512]{1,0:T(8,128)S(1)}, u32[]{:S(2)}, u32[]{:S(2)}) collective-permute-start(f32[16,512]{1,0:T(8,128)S(1)} %get-tuple-element.64), channel_id=1, source_target_pairs={{0,4},{4,0},{8,12},{12,8},{1,5},{5,1},{9,13},{13,9},{2,6},{6,2},{1... | collective-permute-start | bytes 98312 | tf_op jit(solution)/shard_map/ppermute | solution.py:744

commit v11 on v10

--- a/solution.py
+++ b/solution.py
@@ -119,7 +119,7 @@
 LANES = 1 << LANE_BITS
 FEATURE_ROWS = 128
 FIRST = 1152
-TAKEN = 512
+TAKEN = 768
 NT = (((1,), (1,)), ((), ()))
 LARGE_VMEM, MODEST_VMEM = 44 * 1024 * 1024, 15 * 1024 * 1024
 
@@ -163,19 +163,9 @@
     return jnp.concatenate([ref[text] for text in range(ref.shape[0])], axis=0)
 
 
-def fetch(pairs, sems):
-    copies = [pltpu.make_async_copy(a, b, sems.at[n]) for n, (a, b) in enumerate(pairs)]
-    for copy in copies:
-        copy.start()
-    for copy in copies:
-        copy.wait()
-
-
 def gather_kernel(
     ids_ref,
     vocab_ref,
-    turned_any,
-    member_any,
     turned,
     member_ref,
     held,
@@ -185,7 +175,6 @@
     bounds,
     held_sems,
     bounds_sem,
-    out_sems,
     base,
 ):
     texts, _, length = ids_ref.shape
@@ -288,13 +277,9 @@
         return carry
 
     lax.fori_loop(0, blocks, take, 0)
-    fetch([(turned, turned_any), (member_ref, member_any)], out_sems)
-
-
-def statistics_kernel(
-    turned_any, member_any, hard_ref, lower_ref, extra_ref, small, turned, member_ref, spread, sems
-):
-    fetch([(turned_any, turned), (member_any, member_ref)], sems)
+
+
+def statistics_kernel(turned, member_ref, hard_ref, lower_ref, extra_ref, small, spread):
     features, span = turned.shape
     stripes = pl.cdiv(span, STRIPE)
     per_shard, negatives = hard_ref.shape
@@ -331,8 +316,7 @@
         extra_ref[start : start + ROWS, :] = spread[:, pl.ds(quarter, STRIPE)].astype(jnp.bfloat16)
 
 
-def join_kernel(own_any, core_any, extra_ref, core_extra_ref, chip_ref, inputs_ref, own, core, sems):
-    fetch([(own_any, own), (core_any, core)], sems)
+def join_kernel(own, core, extra_ref, core_extra_ref, chip_ref, inputs_ref):
     span = own.shape[0]
     common = extra_ref.shape[0] - 4 * ROWS
     near, across = extra_ref[...].astype(jnp.float32), core_extra_ref[...].astype(jnp.float32)
@@ -347,9 +331,9 @@
 def pool_kernel(
     ids_ref,
     own_ref,
-    core_any,
-    far_any,
-    chip_any,
+    core_ref,
+    far_ref,
+    chip_ref,
     inputs_ref,
     member_ref,
     own_rest,
@@ -364,19 +348,11 @@
     raised,
     total,
     slopes,
-    core_ref,
-    far_ref,
-    chip_ref,
-    sems,
-    *rest,
     model_width,
 ):
     texts, _, length = ids_ref.shape
     width = own_ref.shape[1]
     quarter = quarter_of(lax.axis_index("dp"))
-    extra_rows = far_ref.shape[0] - own_ref.shape[0]
-    chip_extra = chip_any.at[pl.ds(own_ref.shape[0], extra_rows)]
-    fetch([(core_any, core_ref), (far_any, far_ref), (chip_extra, chip_ref)], sems)
     raised[...] = jnp.zeros_like(raised)
     raised[0:ROWS, :] = raise_ref[:, pl.ds(pl.multiple_of(quarter * width, LANES), width)]
     total[...] = jnp.zeros_like(total)
@@ -390,7 +366,8 @@
             return sum(ref[pl.ds(start, size), :].astype(jnp.float32) for ref in refs)
 
         def extra(row):
-            near, far = chip_ref[pl.ds(row, ROWS), :], far_ref[pl.ds(span + row, ROWS), :]
+            rows = pl.ds(span + row, ROWS)
+            near, far = chip_ref[rows, :], far_ref[rows, :]
             return near.astype(jnp.float32) + far.astype(jnp.float32)
 
         misc = extra(stripes * ROWS)
@@ -423,13 +400,8 @@
 
     @pl.when(jnp.sum(real) > member_ref.shape[0])
     def _():
-        *here, rest_sems = rest
-        span = member_rest.shape[0]
-        chip_extra = chip_rest.at[pl.ds(span, here[3].shape[0])]
-        there = (own_rest, core_rest, far_rest, chip_extra, inputs_rest, member_rest)
-        fetch(list(zip(there, here)), rest_sems)
-        own, core, far, chip, inputs, member = here
-        add((own, core, far), far, chip, inputs, member, member_ref.shape[0])
+        refs = (own_rest, core_rest, far_rest)
+        add(refs, far_rest, chip_rest, inputs_rest, member_rest, member_ref.shape[0])
 
     counts = jnp.sum(real, axis=1, keepdims=True)
     pooled = total[0:texts] / counts
@@ -445,8 +417,7 @@
     return jnp.concatenate([jnp.where(queries, near, far), jnp.where(queries, far, near)], axis=0)
 
 
-def dots_kernel(near_ref, far_any, packed_ref, slopes_ref, far_ref, sems):
-    fetch([(far_any, far_ref)], sems)
+def dots_kernel(near_ref, far_ref, packed_ref, slopes_ref):
     block = both_sides(near_ref[0:ROWS], far_ref[0:ROWS])
     rows = 2 * ROWS
     packed_ref[...] = jnp.zeros_like(packed_ref)
@@ -460,14 +431,9 @@
 
 
 def score_kernel(*refs, texts, stripes, negatives):
-    there, (misc_ref, sharp_ref, embed_ref, loss_ref, up_ref), (*here, sems) = (
-        refs[0:10],
-        refs[10:15],
-        refs[15:],
-    )
-    fetch(list(zip(there, here)), sems)
-    packed0, packed1, packed2, packed3, slopes0, slopes2 = here[0:6]
-    dots0, dots1, dots2, dots3 = here[6:10]
+    packed0, packed1, packed2, packed3, slopes0, slopes2 = refs[0:6]
+    dots0, dots1, dots2, dots3, misc_ref, sharp_ref = refs[6:12]
+    embed_ref, loss_ref, up_ref = refs[12:15]
     rows = 2 * ROWS
     per_shard = loss_ref.shape[1]
     group, shard = lax.axis_index("group"), lax.axis_index("dp")
@@ -596,10 +562,8 @@
                 jax.ShapeDtypeStruct((span, LANES), jnp.bfloat16),
             ],
             in_specs=[vmem_spec(), any_spec()],
-            out_specs=[any_spec()] * 2,
+            out_specs=[vmem_spec()] * 2,
             scratch_shapes=[
-                pltpu.VMEM((features, span), jnp.bfloat16),
-                pltpu.VMEM((span, LANES), jnp.bfloat16),
                 pltpu.VMEM((blocks, features, IDS_PER_BLOCK), jnp.bfloat16),
                 pltpu.VMEM((8 * pl.cdiv(span // LANES, 8), LANES), jnp.int32),
                 pltpu.VMEM((texts, length), jnp.float32),
@@ -607,7 +571,6 @@
                 pltpu.SMEM((group_rows, length), jnp.int32),
                 pltpu.SemaphoreType.DMA((blocks,)),
                 pltpu.SemaphoreType.DMA,
-                pltpu.SemaphoreType.DMA((2,)),
             ],
             compiler_params=params,
             name="gather",
@@ -624,14 +587,11 @@
         extra = pl.pallas_call(
             statistics_kernel,
             out_shape=jax.ShapeDtypeStruct((extra_rows, STRIPE), jnp.bfloat16),
-            in_specs=[any_spec()] * 2 + [vmem_spec()] * 2,
+            in_specs=[vmem_spec()] * 4,
             out_specs=vmem_spec(),
             scratch_shapes=[
                 pltpu.VMEM((LANES, LANES), jnp.float32),
-                pltpu.VMEM(turned.shape, turned.dtype),
-                pltpu.VMEM(member.shape, member.dtype),
                 pltpu.VMEM((ROWS, features), jnp.float32),
-                pltpu.SemaphoreType.DMA((2,)),
             ],
             compiler_params=modest,
             cost_estimate=pl.CostEstimate(
@@ -649,13 +609,8 @@
                 jax.ShapeDtypeStruct((joined, width), jnp.bfloat16),
                 jax.ShapeDtypeStruct((ROWS, width), jnp.float32),
             ],
-            in_specs=[any_spec()] * 2 + [vmem_spec()] * 2,
+            in_specs=[vmem_spec()] * 4,
             out_specs=[vmem_spec()] * 2,
-            scratch_shapes=[
-                pltpu.VMEM(own1.shape, own1.dtype),
-                pltpu.VMEM(core1.shape, core1.dtype),
-                pltpu.SemaphoreType.DMA((2,)),
-            ],
             compiler_params=modest,
             name="join",
         )(own1, core1, extra, core_extra)
@@ -681,23 +636,12 @@
             jax.ShapeDtypeStruct(((texts + 1) * ROWS, width), jnp.bfloat16),
             jax.ShapeDtypeStruct((ROWS, width), jnp.float32),
         ],
-        in_specs=[vmem_spec()] * 2
-        + [any_spec()] * 3
-        + [vmem_spec()] * 2
-        + [any_spec()] * 6
-        + [vmem_spec()],
+        in_specs=[vmem_spec()] * 14,
         out_specs=[vmem_spec()] * 2,
         scratch_shapes=[
             pltpu.VMEM((LANES, width), jnp.bfloat16),
             pltpu.VMEM((ROWS, width), jnp.float32),
             pltpu.VMEM((texts * ROWS, width), jnp.float32),
-            *[pltpu.VMEM(x.shape, x.dtype) for x in first[1:3]],
-            pltpu.VMEM((first[2].shape[0] - FIRST, width), jnp.bfloat16),
-            pltpu.SemaphoreType.DMA((3,)),
-            *[pltpu.VMEM(x.shape, x.dtype) for x in rest[0:3]],
-            pltpu.VMEM((rest[2].shape[0] - left, width), jnp.bfloat16),
-            *[pltpu.VMEM(x.shape, x.dtype) for x in rest[4:6]],
-            pltpu.SemaphoreType.DMA((6,)),
         ],
         compiler_params=modest,
         name="pool",
@@ -710,12 +654,8 @@
             jax.ShapeDtypeStruct((rows + width // LANES * rows, LANES), jnp.float32),
             jax.ShapeDtypeStruct((2 * texts * ROWS, width), jnp.bfloat16),
         ],
-        in_specs=[vmem_spec(), any_spec()],
+        in_specs=[vmem_spec()] * 2,
         out_specs=[vmem_spec()] * 2,
-        scratch_shapes=[
-            pltpu.VMEM(sent.shape, sent.dtype),
-            pltpu.SemaphoreType.DMA((1,)),
-        ],
         compiler_params=modest,
         name="dots",
     )(sent, far_side)
@@ -734,10 +674,8 @@
             jax.ShapeDtypeStruct((1, per_shard), jnp.float32),
             jax.ShapeDtypeStruct((ROWS, part_width // 2), jnp.float32),
         ],
-        in_specs=[any_spec()] * 10 + [vmem_spec(), smem_spec()],
+        in_specs=[vmem_spec()] * 11 + [smem_spec()],
         out_specs=[vmem_spec()] * 3,
-        scratch_shapes=[pltpu.VMEM(x.shape, x.dtype) for x in (*packed, *slopes, *dots)]
-        + [pltpu.SemaphoreType.DMA((10,))],
         compiler_params=modest,
         name="score",
     )(*packed, *slopes, *dots, misc, logit_sharpness)

time: 75.4 us -> 70.7 us (0.938)
  Pallas kernels: 27.7 us -> 23.3 us
    pallas_call x1, Pallas kernels: 17.3 us -> 15.1 us  [project(): pl.pallas_call(functools.partial(gather_kernel, base=base), out_shape=[ja...]
    pallas_call x1, Pallas kernels: 3.19 us -> 2.07 us  [project(): pl.pallas_call(join_kernel, out_shape=[jax.ShapeDtypeStruct((joined, widt...]
    pallas_call x1, Pallas kernels: 1.9 us -> 0.99 us  [split_body(): pl.pallas_call(functools.partial(score_kernel, texts=texts, stripes=pl.cd...]
  transfers between devices with their start and end apart: 13 -> 13, of which waited for: 7 -> 7; matrix products, arithmetic and copies ran while one was open for 13% -> 14% of each run, Pallas kernels for 3% -> 3%
where the time goes in v11:
time: 70.7 us; the launch traced here: 70.1 us
  Pallas kernels  23.3 us (33%)
  waiting for transfers between devices  18.5 us (26%)
  starting transfers between devices  12.6 us (18%)
  matrix products  10.1 us (14%)
  local copies, waits for them, and re-layouts  2.16 us (3%)
  between operations  2.12 us (3%)
  other arithmetic  1.29 us (2%)
    pallas_call x1, Pallas kernels, project(): pl.pallas_call(functools.partial(gather_kernel, base=base), out_shape=[ja...  15.1 us
    dot_general x4, matrix products, mm(): return lax.dot_general(a, b, dims, preferred_element_type=jnp.float32)  10.1 us
    ppermute x6, waiting for transfers between devices, exchange(): return [x] + [lax.ppermute(x, axis, step) for step in steps]  8.28 us
    ppermute x6, starting transfers between devices, exchange(): return [x] + [lax.ppermute(x, axis, step) for step in steps]  6.28 us
    ppermute x1, waiting for transfers between devices, project(): far = lax.ppermute(chip, 'dp', other_y)  5.98 us
    pallas_call x1, Pallas kernels, split_body(): pl.pallas_call(functools.partial(pool_kernel, model_width=float(features...  3.27 us
    ppermute x1, waiting for transfers between devices, split_body(): far_side = lax.ppermute(sent, 'group', [(0, 1), (1, 0)])  2.99 us
    ppermute x1, starting transfers between devices, project(): far = lax.ppermute(chip, 'dp', other_y)  2.97 us
  transfers between devices with their start and end apart: 13, of which 7 were waited for; matrix products, arithmetic and copies ran while one was open for 14% of the time, Pallas kernels for 3%

profile of v11, /device:TPU:0, one launch (start us, length us, event | category | flops | bytes accessed | tf_op | source)
XLA Modules:
  0.0 70.1 jit_solution(12959115604792486159)
XLA Ops:
  0.6 15.1 %gather.3 = (bf16[1024,1152]{1,0:T(8,128)(2,1)S(1)}, bf16[1152,128]{1,0:T(8,128)(2,1)S(1)}) custom-call(s32[12,1,128]{2,1,0:T(1,128)} %bitcast.9, bf16[1024,16384]{1,0:T(8,128)(2,1)} %vocab_ref.1), custom_call_target="tpu_custom_call" | custom-call | tf_op jit(solution)/shard_map/gather/pallas_call | solution.py:558
  15.8 2.8 %convolution_convert_fusion.5 = bf16[1152,256]{1,0:T(8,128)(2,1)} fusion(bf16[1024,1152]{1,0:T(8,128)(2,1)S(1)} %get-tuple-element.47.turned, bf16[1024,1024]{1,0:T(8,128)(2,1)} %param.12, s32[]{:T(128)S(6)} %select_n.37), kind=kOutput, calls=%fused_computation.14 | convolution fusion | flops 604274688 | bytes 3473412 | tf_op jit(solution)/shard_map/dot_general | solution.py:128
  19.1 1.8 %statistics.3.extra_ref = bf16[160,256]{1,0:T(8,128)(2,1)} custom-call(bf16[1024,1152]{1,0:T(8,128)(2,1)S(1)} %get-tuple-element.47.turned, bf16[1152,128]{1,0:T(8,128)(2,1)S(1)} %get-tuple-element.45.member_ref, s32[3,7]{1,0:T(4,128)S(1)} %copy-done.9, bf16[16,4096]{1,0:T(8,128)(2,1)S(1)} %copy-done.6), custom_call_target="tpu_custom_call" | custom-call | flops 339738624 | bytes 2359296 | tf_op jit(solution)/shard_map/statistics/pallas_call | solution.py:587
  20.9 1.9 %fusion.12.own = f32[1152,256]{1,0:T(8,128)S(1)} fusion(bf16[1024,1152]{1,0:T(8,128)(2,1)S(1)} %get-tuple-element.47.turned, bf16[1024,1024]{1,0:T(8,128)(2,1)} %param.12, s32[]{:T(128)S(6)} %select_n.36), kind=kOutput, calls=%fused_computation.18 | convolution fusion | flops 603979776 | bytes 4063236 | tf_op jit(solution)/shard_map/dot_general | solution.py:128
  22.8 2.1 %join.3 = (bf16[1264,256]{1,0:T(8,128)(2,1)}, f32[16,256]{1,0:T(8,128)S(1)}) custom-call(f32[1152,256]{1,0:T(8,128)S(1)} %fusion.12.own, bf16[1152,256]{1,0:T(8,128)(2,1)} %collective-permute-done.4.core, bf16[160,256]{1,0:T(8,128)(2,1)} %statistics.3.extra_ref, bf16[160,256]{1,0:T(8,128)(2,1)} %collective-permute-done.5.core_extra_ref), custom_call_target="tpu_custom_call" | custom-call | tf_op jit(solution)/shard_map/join/pallas_call | solution.py:606
  24.9 3.0 %collective-permute-start.7 = (bf16[1264,256]{1,0:T(8,128)(2,1)}, bf16[1264,256]{1,0:T(8,128)(2,1)S(1)}, u32[]{:S(2)}, u32[]{:S(2)}) collective-permute-start(bf16[1264,256]{1,0:T(8,128)(2,1)} %get-tuple-element.46.chip_ref), channel_id=1, source_target_pairs={{0,8},{4,12},{8,0},{12,4},{1,9},{5,13},{9,1},{13,5},{2,10},{6,14},... | collective-permute-start | bytes 1941512 | tf_op jit(solution)/shard_map/ppermute | solution.py:617
  27.9 2.7 %convolution_convert_fusion.3 = bf16[1152,256]{1,0:T(8,128)(2,1)} fusion(bf16[1024,1152]{1,0:T(8,128)(2,1)S(1)} %get-tuple-element.47.turned, bf16[1024,1024]{1,0:T(8,128)(2,1)} %param.12, s32[]{:T(128)S(6)} %select_n.39), kind=kOutput, calls=%fused_computation.12 | convolution fusion | flops 604274688 | bytes 3473412 | tf_op jit(solution)/shard_map/dot_general | solution.py:128
  30.5 2.8 %convolution_convert_fusion.4.own_ref = bf16[1152,256]{1,0:T(8,128)(2,1)} fusion(bf16[1024,1152]{1,0:T(8,128)(2,1)S(1)} %get-tuple-element.47.turned, bf16[1024,1024]{1,0:T(8,128)(2,1)} %param.12, s32[]{:T(128)S(6)} %select_n.38), kind=kOutput, calls=%fused_computation.13 | convolution fusion | flops 604274688 | bytes 3473412 | tf_op jit(solution)/shard_map/dot_general | solution.py:128
  34.6 2.1 %conditional.1 = (bf16[384,256]{1,0:T(8,128)(2,1)S(1)}, bf16[384,256]{1,0:T(8,128)(2,1)}, bf16[448,256]{1,0:T(8,128)(2,1)}, bf16[448,256]{1,0:T(8,128)(2,1)}, f3...) conditional(s32[]{:T(128)} %convert_element_type.28, () %tuple.22, (s32[12,1,128]{2,1,0:T(1,128)S(1)}, ...), branch_computations={%region_1.0_spmd, %region_2.0_spmd} | conditional | flops 918847488 | bytes 10519216 | solution.py:628
  35.4 0.7 %broadcast.11 = bf16[448,256]{1,0:T(8,128)(2,1)} broadcast(bf16[]{:T(256)} %constant.16.clone), dimensions={} | broadcast | bytes 229378 | tf_op jit(solution)/shard_map/broadcast.6
  36.8 6.0 %collective-permute-done.7.far_ref = bf16[1264,256]{1,0:T(8,128)(2,1)S(1)} collective-permute-done((bf16[1264,256]{1,0:T(8,128)(2,1)}, bf16[1264,256]{1,0:T(8,128)(2,1)S(1)}, u32[]{:S(2)}, u32[]{:S(2)}) %collective-permute-start.7) | collective-permute-done | bytes 647200 | tf_op jit(solution)/shard_map/ppermute | solution.py:617
  42.8 3.3 %pool.1 = (bf16[208,256]{1,0:T(8,128)(2,1)S(1)}, f32[16,256]{1,0:T(8,128)S(1)}) custom-call(s32[12,1,128]{2,1,0:T(1,128)S(1)} %bitcast.12, bf16[1152,256]{1,0:T(8,128)(2,1)S(1)} %copy-done.2, bf16[1152,256]{1,0:T(8,128)(2,1)} %collective-permute-done.6.core_ref, bf16[1264,256]{1,0:T(8,128)(2,1)S(1)} %collective-permute-done.7.far_ref, ...), custom_call_target="tpu_custom_call" | custom-call | tf_op jit(solution)/shard_map/pool/pallas_call | solution.py:633
  46.1 1.8 %collective-permute-start.8 = (bf16[208,256]{1,0:T(8,128)(2,1)S(1)}, bf16[208,256]{1,0:T(8,128)(2,1)S(1)}, u32[]{:S(2)}, u32[]{:S(2)}) collective-permute-start(bf16[208,256]{1,0:T(8,128)(2,1)S(1)} %get-tuple-element.56.near_ref), channel_id=1, source_target_pairs={{0,16},{16,0},{1,17},{17,1},{2,18},{18,2},{3,19},{19,3},{4,20},{20... | collective-permute-start | bytes 319496 | tf_op jit(solution)/shard_map/ppermute | solution.py:649
  47.9 3.0 %collective-permute-done.8.far_ref = bf16[208,256]{1,0:T(8,128)(2,1)S(1)} collective-permute-done((bf16[208,256]{1,0:T(8,128)(2,1)S(1)}, bf16[208,256]{1,0:T(8,128)(2,1)S(1)}, u32[]{:S(2)}, u32[]{:S(2)}) %collective-permute-start.8) | collective-permute-done | bytes 106528 | tf_op jit(solution)/shard_map/ppermute | solution.py:649
  51.0 1.8 %collective-permute-start.10 = (f32[96,128]{1,0:T(8,128)S(1)}, f32[96,128]{1,0:T(8,128)S(1)}, u32[]{:S(2)}, u32[]{:S(2)}) collective-permute-start(f32[96,128]{1,0:T(8,128)S(1)} %get-tuple-element.57.refs_0_), channel_id=1, source_target_pairs={{0,8},{4,12},{8,0},{12,4},{1,9},{5,13},{9,1},{13,5},{2,10},{6,14},... | collective-permute-start | bytes 147464 | tf_op jit(solution)/shard_map/ppermute | solution.py:524
  52.9 2.3 %collective-permute-done.10.refs_2_ = f32[96,128]{1,0:T(8,128)S(1)} collective-permute-done((f32[96,128]{1,0:T(8,128)S(1)}, f32[96,128]{1,0:T(8,128)S(1)}, u32[]{:S(2)}, u32[]{:S(2)}) %collective-permute-start.10) | collective-permute-done | bytes 49184 | tf_op jit(solution)/shard_map/ppermute | solution.py:524
  55.1 1.4 %collective-permute-done.11.refs_3_ = f32[96,128]{1,0:T(8,128)S(1)} collective-permute-done((f32[96,128]{1,0:T(8,128)S(1)}, f32[96,128]{1,0:T(8,128)S(1)}, u32[]{:S(2)}, u32[]{:S(2)}) %collective-permute-start.11) | collective-permute-done | bytes 49184 | tf_op jit(solution)/shard_map/ppermute | solution.py:524
  56.5 1.1 %collective-permute-start.12 = (bf16[384,256]{1,0:T(8,128)(2,1)S(1)}, bf16[384,256]{1,0:T(8,128)(2,1)S(1)}, u32[]{:S(2)}, u32[]{:S(2)}) collective-permute-start(bf16[384,256]{1,0:T(8,128)(2,1)S(1)} %get-tuple-element.59.refs_4_), channel_id=1, source_target_pairs={{0,8},{4,12},{8,0},{12,4},{1,9},{5,13},{9,1},{13,5},{2,10},{6,14},... | collective-permute-start | bytes 589832 | tf_op jit(solution)/shard_map/ppermute | solution.py:667
  57.6 1.6 %collective-permute-start.13 = (f32[32,128]{1,0:T(8,128)S(1)}, f32[32,128]{1,0:T(8,128)S(1)}, u32[]{:S(2)}, u32[]{:S(2)}) collective-permute-start(f32[32,128]{1,0:T(8,128)S(1)} %fusion.14.refs_6_), channel_id=1, source_target_pairs={{0,1},{1,0},{2,3},{3,2},{4,5},{5,4},{6,7},{7,6},{8,9},{9,8},{10,11... | collective-permute-start | bytes 49160 | tf_op jit(solution)/shard_map/ppermute | solution.py:524
  59.2 2.6 %collective-permute-start.14 = (f32[32,128]{1,0:T(8,128)S(1)}, f32[32,128]{1,0:T(8,128)S(1)}, u32[]{:S(2)}, u32[]{:S(2)}) collective-permute-start(f32[32,128]{1,0:T(8,128)S(1)} %fusion.14.refs_6_), channel_id=1, source_target_pairs={{0,2},{1,3},{2,0},{3,1},{4,6},{5,7},{6,4},{7,5},{8,10},{9,11},{10,... | collective-permute-start | bytes 49160 | tf_op jit(solution)/shard_map/ppermute | solution.py:524
  62.6 1.4 %collective-permute-done.14.refs_8_ = f32[32,128]{1,0:T(8,128)S(1)} collective-permute-done((f32[32,128]{1,0:T(8,128)S(1)}, f32[32,128]{1,0:T(8,128)S(1)}, u32[]{:S(2)}, u32[]{:S(2)}) %collective-permute-start.14) | collective-permute-done | bytes 16416 | tf_op jit(solution)/shard_map/ppermute | solution.py:524
  64.0 3.3 %collective-permute-done.15.refs_9_ = f32[32,128]{1,0:T(8,128)S(1)} collective-permute-done((f32[32,128]{1,0:T(8,128)S(1)}, f32[32,128]{1,0:T(8,128)S(1)}, u32[]{:S(2)}, u32[]{:S(2)}) %collective-permute-start.15) | collective-permute-done | bytes 16416 | tf_op jit(solution)/shard_map/ppermute | solution.py:524
  67.3 1.0 %score.1 = (bf16[1,3,1024]{2,1,0:T(4,128)(2,1)}, f32[1,3]{1,0:T(1,128)}, f32[16,512]{1,0:T(8,128)S(1)}) custom-call(f32[96,128]{1,0:T(8,128)S(1)} %get-tuple-element.57.refs_0_, f32[96,128]{1,0:T(8,128)S(1)} %collective-permute-done.9.refs_1_, f32[96,128]{1,0:T(8,128)S(1)} %collective-permute-done.10.refs_2_, f32[96,128]{1,0:T(8,128)S(1)} %collective-permute-done.11.refs_3_, ...), custom_call_target="tpu_custom_call" | custom-call | tf_op jit(solution)/shard_map/score/pallas_call | solution.py:668
  68.3 1.2 %collective-permute-done.16 = f32[16,512]{1,0:T(8,128)S(1)} collective-permute-done((f32[16,512]{1,0:T(8,128)S(1)}, f32[16,512]{1,0:T(8,128)S(1)}, u32[]{:S(2)}, u32[]{:S(2)}) %collective-permute-start.16) | collective-permute-done | bytes 32800 | tf_op jit(solution)/shard_map/ppermute | solution.py:682
  (41 shorter events, 3.8 us)
Async XLA Ops:
  15.7 3.3 %copy-start = (bf16[1152,128]{1,0:T(8,128)(2,1)}, bf16[1152,128]{1,0:T(8,128)(2,1)S(1)}, u32[]{:S(2)}) copy-start(bf16[1152,128]{1,0:T(8,128)(2,1)S(1)} %get-tuple-element.45.member_ref) | copy-start | bytes 884740
  15.8 3.3 %copy-start.6 = (bf16[16,4096]{1,0:T(8,128)(2,1)S(1)}, bf16[16,4096]{1,0:T(8,128)(2,1)}, u32[]{:S(2)}) copy-start(bf16[16,4096]{1,0:T(8,128)(2,1)} %lower_ref.1) | copy-start | bytes 393220
  15.8 3.3 %copy-start.9 = (s32[3,7]{1,0:T(4,128)S(1)}, s32[3,7]{1,0:T(4,128)}, u32[]{:S(2)}) copy-start(s32[3,7]{1,0:T(4,128)} %hard_ref.1) | copy-start | bytes 256
  18.6 4.2 %collective-permute-start.4 = (bf16[1152,256]{1,0:T(8,128)(2,1)}, bf16[1152,256]{1,0:T(8,128)(2,1)}, u32[]{:S(2)}, u32[]{:S(2)}) collective-permute-start(bf16[1152,256]{1,0:T(8,128)(2,1)} %convolution_convert_fusion.5), channel_id=1, source_target_pairs={{0,4},{4,0},{8,12},{12,8},{1,5},{5,1},{9,13},{13,9},{2,6},{6,2},{1... | collective-permute-start | bytes 1769480 | tf_op jit(solution)/shard_map/ppermute | solution.py:585
  20.9 1.9 %collective-permute-start.5 = (bf16[160,256]{1,0:T(8,128)(2,1)}, bf16[160,256]{1,0:T(8,128)(2,1)}, u32[]{:S(2)}, u32[]{:S(2)}) collective-permute-start(bf16[160,256]{1,0:T(8,128)(2,1)} %statistics.3.extra_ref), channel_id=1, source_target_pairs={{0,4},{4,0},{8,12},{12,8},{1,5},{5,1},{9,13},{13,9},{2,6},{6,2},{1... | collective-permute-start | bytes 245768 | tf_op jit(solution)/shard_map/ppermute | solution.py:604
  24.9 17.9 %collective-permute-start.7 = (bf16[1264,256]{1,0:T(8,128)(2,1)}, bf16[1264,256]{1,0:T(8,128)(2,1)S(1)}, u32[]{:S(2)}, u32[]{:S(2)}) collective-permute-start(bf16[1264,256]{1,0:T(8,128)(2,1)} %get-tuple-element.46.chip_ref), channel_id=1, source_target_pairs={{0,8},{4,12},{8,0},{12,4},{1,9},{5,13},{9,1},{13,5},{2,10},{6,14},... | collective-permute-start | bytes 1941512 | tf_op jit(solution)/shard_map/ppermute | solution.py:617
  30.5 6.3 %collective-permute-start.6 = (bf16[1152,256]{1,0:T(8,128)(2,1)}, bf16[1152,256]{1,0:T(8,128)(2,1)}, u32[]{:S(2)}, u32[]{:S(2)}) collective-permute-start(bf16[1152,256]{1,0:T(8,128)(2,1)} %convolution_convert_fusion.3), channel_id=1, source_target_pairs={{0,4},{4,0},{8,12},{12,8},{1,5},{5,1},{9,13},{13,9},{2,6},{6,2},{1... | collective-permute-start | bytes 1769480 | tf_op jit(solution)/shard_map/ppermute | solution.py:619
  30.5 2.8 %copy-start.8 = (s32[1,12,128]{2,0,1:T(1,128)S(1)}, s32[1,12,128]{2,0,1:T(1,128)}, u32[]{:S(2)}) copy-start(s32[1,12,128]{2,0,1:T(1,128)} %param.9) | copy-start | bytes 18436
  30.5 4.1 %copy-start.7 = (bf16[16,4096]{1,0:T(8,128)(2,1)S(1)}, bf16[16,4096]{1,0:T(8,128)(2,1)}, u32[]{:S(2)}) copy-start(bf16[16,4096]{1,0:T(8,128)(2,1)} %lower_ref.1) | copy-start | bytes 393220
  30.5 4.1 %copy-start.10 = (s32[3,7]{1,0:T(4,128)S(1)}, s32[3,7]{1,0:T(4,128)}, u32[]{:S(2)}) copy-start(s32[3,7]{1,0:T(4,128)} %hard_ref.1) | copy-start | bytes 256
  34.6 8.2 %copy-start.1 = (bf16[1152,128]{1,0:T(8,128)(2,1)S(1)}, bf16[1152,128]{1,0:T(8,128)(2,1)}, u32[]{:S(2)}) copy-start(bf16[1152,128]{1,0:T(8,128)(2,1)} %copy-done) | copy-start | bytes 884740
  34.6 8.2 %copy-start.2 = (bf16[1152,256]{1,0:T(8,128)(2,1)S(1)}, bf16[1152,256]{1,0:T(8,128)(2,1)}, u32[]{:S(2)}) copy-start(bf16[1152,256]{1,0:T(8,128)(2,1)} %convolution_convert_fusion.4.own_ref) | copy-start | bytes 1769476
  34.6 8.2 %copy-start.3 = (bf16[16,1024]{1,0:T(8,128)(2,1)S(1)}, bf16[16,1024]{1,0:T(8,128)(2,1)}, u32[]{:S(2)}) copy-start(bf16[16,1024]{1,0:T(8,128)(2,1)} %raise_ref.1) | copy-start | bytes 98308
  46.1 4.8 %collective-permute-start.8 = (bf16[208,256]{1,0:T(8,128)(2,1)S(1)}, bf16[208,256]{1,0:T(8,128)(2,1)S(1)}, u32[]{:S(2)}, u32[]{:S(2)}) collective-permute-start(bf16[208,256]{1,0:T(8,128)(2,1)S(1)} %get-tuple-element.56.near_ref), channel_id=1, source_target_pairs={{0,16},{16,0},{1,17},{17,1},{2,18},{18,2},{3,19},{19,3},{4,20},{20... | collective-permute-start | bytes 319496 | tf_op jit(solution)/shard_map/ppermute | solution.py:649
  51.0 1.9 %collective-permute-start.9 = (f32[96,128]{1,0:T(8,128)S(1)}, f32[96,128]{1,0:T(8,128)S(1)}, u32[]{:S(2)}, u32[]{:S(2)}) collective-permute-start(f32[96,128]{1,0:T(8,128)S(1)} %get-tuple-element.57.refs_0_), channel_id=1, source_target_pairs={{0,4},{4,0},{8,12},{12,8},{1,5},{5,1},{9,13},{13,9},{2,6},{6,2},{1... | collective-permute-start | bytes 147464 | tf_op jit(solution)/shard_map/ppermute | solution.py:524
  51.0 4.2 %collective-permute-start.10 = (f32[96,128]{1,0:T(8,128)S(1)}, f32[96,128]{1,0:T(8,128)S(1)}, u32[]{:S(2)}, u32[]{:S(2)}) collective-permute-start(f32[96,128]{1,0:T(8,128)S(1)} %get-tuple-element.57.refs_0_), channel_id=1, source_target_pairs={{0,8},{4,12},{8,0},{12,4},{1,9},{5,13},{9,1},{13,5},{2,10},{6,14},... | collective-permute-start | bytes 147464 | tf_op jit(solution)/shard_map/ppermute | solution.py:524
  52.8 3.7 %collective-permute-start.11 = (f32[96,128]{1,0:T(8,128)S(1)}, f32[96,128]{1,0:T(8,128)S(1)}, u32[]{:S(2)}, u32[]{:S(2)}) collective-permute-start(f32[96,128]{1,0:T(8,128)S(1)} %get-tuple-element.57.refs_0_), channel_id=1, source_target_pairs={{0,12},{4,8},{8,4},{12,0},{1,13},{5,9},{9,5},{13,1},{2,14},{6,10},... | collective-permute-start | bytes 147464 | tf_op jit(solution)/shard_map/ppermute | solution.py:524
  56.5 10.8 %collective-permute-start.12 = (bf16[384,256]{1,0:T(8,128)(2,1)S(1)}, bf16[384,256]{1,0:T(8,128)(2,1)S(1)}, u32[]{:S(2)}, u32[]{:S(2)}) collective-permute-start(bf16[384,256]{1,0:T(8,128)(2,1)S(1)} %get-tuple-element.59.refs_4_), channel_id=1, source_target_pairs={{0,8},{4,12},{8,0},{12,4},{1,9},{5,13},{9,1},{13,5},{2,10},{6,14},... | collective-permute-start | bytes 589832 | tf_op jit(solution)/shard_map/ppermute | solution.py:667
  57.6 5.0 %collective-permute-start.13 = (f32[32,128]{1,0:T(8,128)S(1)}, f32[32,128]{1,0:T(8,128)S(1)}, u32[]{:S(2)}, u32[]{:S(2)}) collective-permute-start(f32[32,128]{1,0:T(8,128)S(1)} %fusion.14.refs_6_), channel_id=1, source_target_pairs={{0,1},{1,0},{2,3},{3,2},{4,5},{5,4},{6,7},{7,6},{8,9},{9,8},{10,11... | collective-permute-start | bytes 49160 | tf_op jit(solution)/shard_map/ppermute | solution.py:524
  59.2 4.9 %collective-permute-start.14 = (f32[32,128]{1,0:T(8,128)S(1)}, f32[32,128]{1,0:T(8,128)S(1)}, u32[]{:S(2)}, u32[]{:S(2)}) collective-permute-start(f32[32,128]{1,0:T(8,128)S(1)} %fusion.14.refs_6_), channel_id=1, source_target_pairs={{0,2},{1,3},{2,0},{3,1},{4,6},{5,7},{6,4},{7,5},{8,10},{9,11},{10,... | collective-permute-start | bytes 49160 | tf_op jit(solution)/shard_map/ppermute | solution.py:524
  61.7 5.5 %collective-permute-start.15 = (f32[32,128]{1,0:T(8,128)S(1)}, f32[32,128]{1,0:T(8,128)S(1)}, u32[]{:S(2)}, u32[]{:S(2)}) collective-permute-start(f32[32,128]{1,0:T(8,128)S(1)} %fusion.14.refs_6_), channel_id=1, source_target_pairs={{0,3},{1,2},{2,1},{3,0},{4,7},{5,6},{6,5},{7,4},{8,11},{9,10},{10,... | collective-permute-start | bytes 49160 | tf_op jit(solution)/shard_map/ppermute | solution.py:524
  68.3 1.2 %collective-permute-start.16 = (f32[16,512]{1,0:T(8,128)S(1)}, f32[16,512]{1,0:T(8,128)S(1)}, u32[]{:S(2)}, u32[]{:S(2)}) collective-permute-start(f32[16,512]{1,0:T(8,128)S(1)} %get-tuple-element.64), channel_id=1, source_target_pairs={{0,4},{4,0},{8,12},{12,8},{1,5},{5,1},{9,13},{13,9},{2,6},{6,2},{1... | collective-permute-start | bytes 98312 | tf_op jit(solution)/shard_map/ppermute | solution.py:682

commit v12 on v9

--- a/solution.py
+++ b/solution.py
@@ -172,6 +172,7 @@
     vocab_ref,
     turned_any,
     member_any,
+    count_ref,
     turned,
     member_ref,
     held,
@@ -240,6 +241,7 @@
 
     lax.fori_loop(0, span // LANES, place, 0)
     bounds_copy.wait()
+    count_ref[0] = bounds[groups, 0]
 
     def within(place):
         return jnp.clip(place - base, 0, span)
@@ -411,8 +413,7 @@
     return jnp.concatenate([jnp.where(queries, near, far), jnp.where(queries, far, near)], axis=0)
 
 
-def dots_kernel(near_ref, far_any, packed_ref, slopes_ref, far_ref, sems):
-    fetch([(far_any, far_ref)], sems)
+def dots_kernel(near_ref, far_ref, packed_ref, slopes_ref):
     block = both_sides(near_ref[0:ROWS], far_ref[0:ROWS])
     rows = 2 * ROWS
     packed_ref[...] = jnp.zeros_like(packed_ref)
@@ -426,14 +427,9 @@
 
 
 def score_kernel(*refs, texts, stripes, negatives):
-    there, (misc_ref, sharp_ref, embed_ref, loss_ref, up_ref), (*here, sems) = (
-        refs[0:10],
-        refs[10:15],
-        refs[15:],
-    )
-    fetch(list(zip(there, here)), sems)
-    packed0, packed1, packed2, packed3, slopes0, slopes2 = here[0:6]
-    dots0, dots1, dots2, dots3 = here[6:10]
+    packed0, packed1, packed2, packed3, slopes0, slopes2 = refs[0:6]
+    dots0, dots1, dots2, dots3, misc_ref, sharp_ref = refs[6:12]
+    embed_ref, loss_ref, up_ref = refs[12:15]
     rows = 2 * ROWS
     per_shard = loss_ref.shape[1]
     group, shard = lax.axis_index("group"), lax.axis_index("dp")
@@ -555,14 +551,15 @@
     def project(base, span):
         stripes = pl.cdiv(span, STRIPE)
         extra_rows = (stripes + 1 + shards) * ROWS
-        turned, member = pl.pallas_call(
+        turned, member, count = pl.pallas_call(
             functools.partial(gather_kernel, base=base),
             out_shape=[
                 jax.ShapeDtypeStruct((features, span), jnp.bfloat16),
                 jax.ShapeDtypeStruct((span, LANES), jnp.bfloat16),
+                jax.ShapeDtypeStruct((1,), jnp.int32),
             ],
             in_specs=[vmem_spec(), any_spec()],
-            out_specs=[any_spec()] * 2,
+            out_specs=[any_spec()] * 2 + [smem_spec()],
             scratch_shapes=[
                 pltpu.VMEM((features, span), jnp.bfloat16),
                 pltpu.VMEM((span, LANES), jnp.bfloat16),
@@ -586,7 +583,8 @@
             return x.astype(jnp.bfloat16)
 
         core1 = lax.ppermute(narrow(product(turned, 1, 1)), "dp", other_core)
-        chip1 = narrow(product(turned, 0, 1) + core1.astype(jnp.float32))
+        own1 = lax.optimization_barrier(narrow(product(turned, 0, 1)))
+        chip1 = narrow(own1.astype(jnp.float32) + core1.astype(jnp.float32))
         far = lax.ppermute(chip1, "dp", other_y)
         turned, _ = lax.optimization_barrier((turned, chip1))
         extra = pl.pallas_call(
@@ -619,16 +617,15 @@
         extra = jnp.concatenate([chip, inputs[0:ROWS]]) + sent
         core0 = lax.ppermute(narrow(product(turned, 1, 0)), "dp", other_core)
         own0 = narrow(product(turned, 0, 0))
-        return own0, core0, far, extra, member
-
-    first = project(0, FIRST)
-    later, _ = lax.optimization_barrier((ids, first[0]))
-    many = jnp.sum((later != 0).astype(jnp.int32)) > FIRST
+        return (own0, core0, far, extra, member), count
+
+    first, count = project(0, FIRST)
+    many = count[0] > FIRST
     left = tokens - FIRST
-    shapes = jax.eval_shape(lambda: project(FIRST, left))
+    shapes = jax.eval_shape(lambda: project(FIRST, left)[0])
     rest = lax.cond(
         many,
-        lambda: project(FIRST, left),
+        lambda: project(FIRST, left)[0],
         lambda: tuple(jnp.zeros(x.shape, x.dtype) for x in shapes),
     )
     sent, misc = pl.pallas_call(
@@ -658,12 +655,8 @@
             jax.ShapeDtypeStruct((rows + width // LANES * rows, LANES), jnp.float32),
             jax.ShapeDtypeStruct((2 * texts * ROWS, width), jnp.bfloat16),
         ],
-        in_specs=[vmem_spec(), any_spec()],
+        in_specs=[vmem_spec()] * 2,
         out_specs=[vmem_spec()] * 2,
-        scratch_shapes=[
-            pltpu.VMEM(sent.shape, sent.dtype),
-            pltpu.SemaphoreType.DMA((1,)),
-        ],
         compiler_params=modest,
         name="dots",
     )(sent, far_side)
@@ -682,10 +675,8 @@
             jax.ShapeDtypeStruct((1, per_shard), jnp.float32),
             jax.ShapeDtypeStruct((ROWS, part_width // 2), jnp.float32),
         ],
-        in_specs=[any_spec()] * 10 + [vmem_spec(), smem_spec()],
+        in_specs=[vmem_spec()] * 11 + [smem_spec()],
         out_specs=[vmem_spec()] * 3,
-        scratch_shapes=[pltpu.VMEM(x.shape, x.dtype) for x in (*packed, *slopes, *dots)]
-        + [pltpu.SemaphoreType.DMA((10,))],
         compiler_params=modest,
         name="score",
     )(*packed, *slopes, *dots, misc, logit_sharpness)

time: 70.1 us -> 73.3 us (1.046)
  waiting for transfers between devices: 20.5 us -> 22.9 us
  local copies, waits for them, and re-layouts: 2.13 us -> 3.43 us
  matrix products: 8.09 us -> 7.06 us
  Pallas kernels: 21.3 us -> 22.1 us
    ppermute x1, waiting for transfers between devices: 7.7 us -> 12.8 us  [project(): sent = lax.ppermute(sent, 'dp', other_y).astype(jnp.float32)]
    ppermute x1, waiting for transfers between devices: 1.76 us -> 0.01 us  [project(): core1 = lax.ppermute(narrow(product(turned, 1, 1)), 'dp', other_core)]
    convert_element_type x0 -> x1, other arithmetic: none -> 1.54 us  [narrow(): return x.astype(jnp.bfloat16)]
    dot_general x4, matrix products: 8.09 us -> 7.06 us  [mm(): return lax.dot_general(a, b, dims, preferred_element_type=jnp.float32)]
    pallas_call x1, Pallas kernels: 1.91 us -> 0.99 us  [split_body(): pl.pallas_call(functools.partial(score_kernel, texts=texts, stripes=pl.cd...]
    ppermute x1, waiting for transfers between devices: 3.91 us -> 2.99 us  [split_body(): far_side = lax.ppermute(sent, 'group', [(0, 1), (1, 0)])]
    ppermute x1, starting transfers between devices: 0.86 us -> 1.78 us  [split_body(): far_side = lax.ppermute(sent, 'group', [(0, 1), (1, 0)])]
    pallas_call x1, Pallas kernels: 1.41 us -> 2.31 us  [project(): pl.pallas_call(statistics_kernel, out_shape=jax.ShapeDtypeStruct((extra_r...]
  transfers between devices with their start and end apart: 14 -> 14, of which waited for: 8 -> 7; matrix products, arithmetic and copies ran while one was open for 9% -> 9% of each run, Pallas kernels for 0% -> 0%
where the time goes in v12:
time: 73.3 us; the launch traced here: 73.5 us
  waiting for transfers between devices  22.9 us (31%)
  Pallas kernels  22.1 us (30%)
  starting transfers between devices  13.5 us (18%)
  matrix products  7.06 us (10%)
  local copies, waits for them, and re-layouts  3.43 us (5%)
  other arithmetic  2.25 us (3%)
  between operations  2.14 us (3%)
    pallas_call x1, Pallas kernels, project(): pl.pallas_call(functools.partial(gather_kernel, base=base), out_shape=[ja...  15.5 us
    ppermute x1, waiting for transfers between devices, project(): sent = lax.ppermute(sent, 'dp', other_y).astype(jnp.float32)  12.8 us
    dot_general x4, matrix products, mm(): return lax.dot_general(a, b, dims, preferred_element_type=jnp.float32)  7.06 us
    ppermute x6, starting transfers between devices, exchange(): return [x] + [lax.ppermute(x, axis, step) for step in steps]  6.28 us
    ppermute x6, waiting for transfers between devices, exchange(): return [x] + [lax.ppermute(x, axis, step) for step in steps]  5.97 us
    pallas_call x1, Pallas kernels, split_body(): pl.pallas_call(functools.partial(pool_kernel, model_width=float(features...  3.19 us
    ppermute x1, starting transfers between devices, project(): far = lax.ppermute(chip1, 'dp', other_y)  3.03 us
    ppermute x1, waiting for transfers between devices, split_body(): far_side = lax.ppermute(sent, 'group', [(0, 1), (1, 0)])  2.99 us
  transfers between devices with their start and end apart: 14, of which 7 were waited for; matrix products, arithmetic and copies ran while one was open for 9% of the time, Pallas kernels for 0%

profile of v12, /device:TPU:0, one launch (start us, length us, event | category | flops | bytes accessed | tf_op | source)
XLA Modules:
  0.0 73.5 jit_solution(16144000328908022945)
XLA Ops:
  0.6 0.7 copy.12
  1.3 15.5 %gather.3 = (bf16[1024,1152]{1,0:T(8,128)(2,1)S(1)}, bf16[1152,128]{1,0:T(8,128)(2,1)S(1)}, s32[1]{0:T(128)}) custom-call(s32[12,128]{1,0:T(8,128)S(1)} %bitcast.12, bf16[1024,16384]{1,0:T(8,128)(2,1)} %vocab_ref.1), custom_call_target="tpu_custom_call" | custom-call | tf_op jit(solution)/shard_map/gather/pallas_call | solution.py:554
  16.8 2.7 %convolution_convert_fusion.6 = bf16[1152,256]{1,0:T(8,128)(2,1)} fusion(bf16[1024,1152]{1,0:T(8,128)(2,1)S(1)} %get-tuple-element.40.turned_any, bf16[1024,1024]{1,0:T(8,128)(2,1)} %param.12, s32[]{:T(128)S(6)} %select_n.37), kind=kOutput, calls=%fused_computation.20 | convolution fusion | flops 604274688 | bytes 3473412 | tf_op jit(solution)/shard_map/dot_general | solution.py:128
  20.6 2.7 %convolution_convert_fusion.7 = bf16[1152,256]{1,0:T(8,128)(2,1)} fusion(bf16[1024,1152]{1,0:T(8,128)(2,1)S(1)} %get-tuple-element.40.turned_any, bf16[1024,1024]{1,0:T(8,128)(2,1)} %param.12, s32[]{:T(128)S(6)} %select_n.36), kind=kOutput, calls=%fused_computation.21 | convolution fusion | flops 604274688 | bytes 3473412 | tf_op jit(solution)/shard_map/dot_general | solution.py:128
  23.3 2.1 %conditional.1 = (bf16[384,256]{1,0:T(8,128)(2,1)}, bf16[384,256]{1,0:T(8,128)(2,1)}, bf16[384,256]{1,0:T(8,128)(2,1)}, f32[64,256]{1,0:T(8,128)S(1)}, bf16[384,128]{1,0:T(8,128)(2,1)S(1)}) conditional(s32[]{:T(128)} %bitcast, () %tuple.20, (s32[12,128]{1,0:T(8,128)S(1)}, bf16[1024,16384]{1,0:T(8,128)(2,1)}, bf16[1024,1024]{1,0:T(8,128)(2,1)}, ...), branch_computations={%region_0.0_spmd, %region_1.0_spmd} | conditional | flops 919543808 | bytes 11805392 | solution.py:626
  23.4 0.7 broadcast.8.clone.1
  26.1 1.5 %add_convert_fusion.1 = bf16[1152,256]{1,0:T(8,128)(2,1)S(1)} fusion(bf16[1152,256]{1,0:T(8,128)(2,1)} %collective-permute-done.5, bf16[1152,256]{1,0:T(8,128)(2,1)} %convolution_convert_fusion.7), kind=kLoop, calls=%fused_computation.22 | loop fusion | flops 1179648 | bytes 1769472 | tf_op jit(solution)/shard_map/convert_element_type | solution.py:583
  27.6 2.3 %statistics.3 = bf16[160,256]{1,0:T(8,128)(2,1)S(1)} custom-call(bf16[1024,1152]{1,0:T(8,128)(2,1)S(1)} %get-tuple-element.40.turned_any, bf16[1152,128]{1,0:T(8,128)(2,1)S(1)} %get-tuple-element.41.member_any.member_ref, s32[3,7]{1,0:T(4,128)S(1)} %copy-done.5, bf16[16,4096]{1,0:T(8,128)(2,1)} %lower_ref.1), custom_call_target="tpu_custom_call" | custom-call | flops 339738624 | bytes 2359296 | tf_op jit(solution)/shard_map/statistics/pallas_call | solution.py:590
  30.1 3.0 %collective-permute-start.7 = (bf16[1152,256]{1,0:T(8,128)(2,1)S(1)}, bf16[1152,256]{1,0:T(8,128)(2,1)S(1)}, u32[]{:S(2)}, u32[]{:S(2)}) collective-permute-start(bf16[1152,256]{1,0:T(8,128)(2,1)S(1)} %add_convert_fusion.1), channel_id=1, source_target_pairs={{0,8},{4,12},{8,0},{12,4},{1,9},{5,13},{9,1},{13,5},{2,10},{6,14},... | collective-permute-start | bytes 1769480 | tf_op jit(solution)/shard_map/ppermute | solution.py:588
  33.1 0.8 %convolution_convert_fusion.4 = bf16[1152,256]{1,0:T(8,128)(2,1)S(1)} fusion(bf16[1024,1152]{1,0:T(8,128)(2,1)S(1)} %get-tuple-element.40.turned_any, bf16[1024,1024]{1,0:T(8,128)(2,1)S(1)} %copy-done.6, s32[]{:T(128)S(6)} %select_n.39), kind=kOutput, calls=%fused_computation.18 | convolution fusion | flops 604274688 | bytes 3473412 | tf_op jit(solution)/shard_map/dot_general | solution.py:128
  34.2 0.8 %convolution_convert_fusion.5.own_ref = bf16[1152,256]{1,0:T(8,128)(2,1)S(1)} fusion(bf16[1024,1152]{1,0:T(8,128)(2,1)S(1)} %get-tuple-element.40.turned_any, bf16[1024,1024]{1,0:T(8,128)(2,1)S(1)} %copy-done.6, s32[]{:T(128)S(6)} %select_n.38), kind=kOutput, calls=%fused_computation.19 | convolution fusion | flops 604274688 | bytes 3473412 | tf_op jit(solution)/shard_map/dot_general | solution.py:128
  35.1 12.8 %collective-permute-done.9 = bf16[112,256]{1,0:T(8,128)(2,1)S(1)} collective-permute-done((bf16[112,256]{1,0:T(8,128)(2,1)S(1)}, bf16[112,256]{1,0:T(8,128)(2,1)S(1)}, u32[]{:S(2)}, u32[]{:S(2)}) %collective-permute-start.9) | collective-permute-done | bytes 57376 | tf_op jit(solution)/shard_map/ppermute | solution.py:616
  47.9 3.2 %pool.1 = (bf16[208,256]{1,0:T(8,128)(2,1)S(1)}, f32[16,256]{1,0:T(8,128)S(1)}) custom-call(s32[12,128]{1,0:T(8,128)S(1)} %bitcast.14, bf16[1152,256]{1,0:T(8,128)(2,1)S(1)} %convolution_convert_fusion.5.own_ref, bf16[1152,256]{1,0:T(8,128)(2,1)S(1)} %collective-permute-done.6.core_any, bf16[1152,256]{1,0:T(8,128)(2,1)S(1)} %collective-permute-done.7.far_any, ...), custom_call_target="tpu_custom_call" | custom-call | tf_op jit(solution)/shard_map/pool/pallas_call | solution.py:631
  51.1 1.8 %collective-permute-start.10 = (bf16[208,256]{1,0:T(8,128)(2,1)S(1)}, bf16[208,256]{1,0:T(8,128)(2,1)S(1)}, u32[]{:S(2)}, u32[]{:S(2)}) collective-permute-start(bf16[208,256]{1,0:T(8,128)(2,1)S(1)} %get-tuple-element.48.near_ref), channel_id=1, source_target_pairs={{0,16},{16,0},{1,17},{17,1},{2,18},{18,2},{3,19},{19,3},{4,20},{20... | collective-permute-start | bytes 319496 | tf_op jit(solution)/shard_map/ppermute | solution.py:650
  52.9 3.0 %collective-permute-done.10.far_ref = bf16[208,256]{1,0:T(8,128)(2,1)S(1)} collective-permute-done((bf16[208,256]{1,0:T(8,128)(2,1)S(1)}, bf16[208,256]{1,0:T(8,128)(2,1)S(1)}, u32[]{:S(2)}, u32[]{:S(2)}) %collective-permute-start.10) | collective-permute-done | bytes 106528 | tf_op jit(solution)/shard_map/ppermute | solution.py:650
  56.0 1.8 %collective-permute-start.12 = (f32[96,128]{1,0:T(8,128)S(1)}, f32[96,128]{1,0:T(8,128)S(1)}, u32[]{:S(2)}, u32[]{:S(2)}) collective-permute-start(f32[96,128]{1,0:T(8,128)S(1)} %get-tuple-element.49.refs_0_), channel_id=1, source_target_pairs={{0,8},{4,12},{8,0},{12,4},{1,9},{5,13},{9,1},{13,5},{2,10},{6,14},... | collective-permute-start | bytes 147464 | tf_op jit(solution)/shard_map/ppermute | solution.py:520
  57.9 1.9 %collective-permute-done.13.refs_3_ = f32[96,128]{1,0:T(8,128)S(1)} collective-permute-done((f32[96,128]{1,0:T(8,128)S(1)}, f32[96,128]{1,0:T(8,128)S(1)}, u32[]{:S(2)}, u32[]{:S(2)}) %collective-permute-start.13) | collective-permute-done | bytes 49184 | tf_op jit(solution)/shard_map/ppermute | solution.py:520
  59.8 0.9 %collective-permute-done.12.refs_2_ = f32[96,128]{1,0:T(8,128)S(1)} collective-permute-done((f32[96,128]{1,0:T(8,128)S(1)}, f32[96,128]{1,0:T(8,128)S(1)}, u32[]{:S(2)}, u32[]{:S(2)}) %collective-permute-start.12) | collective-permute-done | bytes 49184 | tf_op jit(solution)/shard_map/ppermute | solution.py:520
  60.7 1.7 %collective-permute-start.14 = (bf16[384,256]{1,0:T(8,128)(2,1)S(1)}, bf16[384,256]{1,0:T(8,128)(2,1)S(1)}, u32[]{:S(2)}, u32[]{:S(2)}) collective-permute-start(bf16[384,256]{1,0:T(8,128)(2,1)S(1)} %get-tuple-element.51.refs_4_), channel_id=1, source_target_pairs={{0,8},{4,12},{8,0},{12,4},{1,9},{5,13},{9,1},{13,5},{2,10},{6,14},... | collective-permute-start | bytes 589832 | tf_op jit(solution)/shard_map/ppermute | solution.py:668
  62.4 3.6 %collective-permute-start.17 = (f32[32,128]{1,0:T(8,128)S(1)}, f32[32,128]{1,0:T(8,128)S(1)}, u32[]{:S(2)}, u32[]{:S(2)}) collective-permute-start(f32[32,128]{1,0:T(8,128)S(1)} %fusion.12.refs_6_), channel_id=1, source_target_pairs={{0,3},{1,2},{2,1},{3,0},{4,7},{5,6},{6,5},{7,4},{8,11},{9,10},{10,... | collective-permute-start | bytes 49160 | tf_op jit(solution)/shard_map/ppermute | solution.py:520
  66.0 0.8 %collective-permute-start.15 = (f32[32,128]{1,0:T(8,128)S(1)}, f32[32,128]{1,0:T(8,128)S(1)}, u32[]{:S(2)}, u32[]{:S(2)}) collective-permute-start(f32[32,128]{1,0:T(8,128)S(1)} %fusion.12.refs_6_), channel_id=1, source_target_pairs={{0,1},{1,0},{2,3},{3,2},{4,5},{5,4},{6,7},{7,6},{8,9},{9,8},{10,11... | collective-permute-start | bytes 49160 | tf_op jit(solution)/shard_map/ppermute | solution.py:520
  67.9 2.7 %collective-permute-done.16.refs_8_ = f32[32,128]{1,0:T(8,128)S(1)} collective-permute-done((f32[32,128]{1,0:T(8,128)S(1)}, f32[32,128]{1,0:T(8,128)S(1)}, u32[]{:S(2)}, u32[]{:S(2)}) %collective-permute-start.16) | collective-permute-done | bytes 16416 | tf_op jit(solution)/shard_map/ppermute | solution.py:520
  70.6 1.0 %score.1 = (bf16[1,3,1024]{2,1,0:T(4,128)(2,1)}, f32[1,3]{1,0:T(1,128)}, f32[16,512]{1,0:T(8,128)S(1)}) custom-call(f32[96,128]{1,0:T(8,128)S(1)} %get-tuple-element.49.refs_0_, f32[96,128]{1,0:T(8,128)S(1)} %collective-permute-done.11.refs_1_, f32[96,128]{1,0:T(8,128)S(1)} %collective-permute-done.12.refs_2_, ...), custom_call_target="tpu_custom_call" | custom-call | tf_op jit(solution)/shard_map/score/pallas_call | solution.py:669
  71.6 1.2 %collective-permute-done.18 = f32[16,512]{1,0:T(8,128)S(1)} collective-permute-done((f32[16,512]{1,0:T(8,128)S(1)}, f32[16,512]{1,0:T(8,128)S(1)}, u32[]{:S(2)}, u32[]{:S(2)}) %collective-permute-start.18) | collective-permute-done | bytes 32800 | tf_op jit(solution)/shard_map/ppermute | solution.py:683
  (42 shorter events, 4.2 us)
Async XLA Ops:
  19.5 6.6 %collective-permute-start.5 = (bf16[1152,256]{1,0:T(8,128)(2,1)}, bf16[1152,256]{1,0:T(8,128)(2,1)}, u32[]{:S(2)}, u32[]{:S(2)}) collective-permute-start(bf16[1152,256]{1,0:T(8,128)(2,1)} %convolution_convert_fusion.6), channel_id=1, source_target_pairs={{0,4},{4,0},{8,12},{12,8},{1,5},{5,1},{9,13},{13,9},{2,6},{6,2},{1... | collective-permute-start | bytes 1769480 | tf_op jit(solution)/shard_map/ppermute | solution.py:585
  20.6 2.7 %copy-start.5 = (s32[3,7]{1,0:T(4,128)S(1)}, s32[3,7]{1,0:T(4,128)}, u32[]{:S(2)}) copy-start(s32[3,7]{1,0:T(4,128)} %hard_ref.1) | copy-start | bytes 256
  25.4 0.6 copy-start.3
  26.1 7.0 %copy-start.6 = (bf16[1024,1024]{1,0:T(8,128)(2,1)S(1)}, bf16[1024,1024]{1,0:T(8,128)(2,1)}, u32[]{:S(2)}) copy-start(bf16[1024,1024]{1,0:T(8,128)(2,1)} %param.12) | copy-start | bytes 6291460
  29.9 4.1 %collective-permute-start.8 = (bf16[160,256]{1,0:T(8,128)(2,1)S(1)}, bf16[160,256]{1,0:T(8,128)(2,1)S(1)}, u32[]{:S(2)}, u32[]{:S(2)}) collective-permute-start(bf16[160,256]{1,0:T(8,128)(2,1)S(1)} %statistics.3), channel_id=1, source_target_pairs={{0,4},{4,0},{8,12},{12,8},{1,5},{5,1},{9,13},{13,9},{2,6},{6,2},{1... | collective-permute-start | bytes 245768 | tf_op jit(solution)/shard_map/ppermute | solution.py:612
  30.1 17.8 %collective-permute-start.7 = (bf16[1152,256]{1,0:T(8,128)(2,1)S(1)}, bf16[1152,256]{1,0:T(8,128)(2,1)S(1)}, u32[]{:S(2)}, u32[]{:S(2)}) collective-permute-start(bf16[1152,256]{1,0:T(8,128)(2,1)S(1)} %add_convert_fusion.1), channel_id=1, source_target_pairs={{0,8},{4,12},{8,0},{12,4},{1,9},{5,13},{9,1},{13,5},{2,10},{6,14},... | collective-permute-start | bytes 1769480 | tf_op jit(solution)/shard_map/ppermute | solution.py:588
  33.9 13.9 %collective-permute-start.6 = (bf16[1152,256]{1,0:T(8,128)(2,1)S(1)}, bf16[1152,256]{1,0:T(8,128)(2,1)S(1)}, u32[]{:S(2)}, u32[]{:S(2)}) collective-permute-start(bf16[1152,256]{1,0:T(8,128)(2,1)S(1)} %convolution_convert_fusion.4), channel_id=1, source_target_pairs={{0,4},{4,0},{8,12},{12,8},{1,5},{5,1},{9,13},{13,9},{2,6},{6,2},{1... | collective-permute-start | bytes 1769480 | tf_op jit(solution)/shard_map/ppermute | solution.py:618
  34.1 13.8 %copy-start = (bf16[16,1024]{1,0:T(8,128)(2,1)S(1)}, bf16[16,1024]{1,0:T(8,128)(2,1)}, u32[]{:S(2)}) copy-start(bf16[16,1024]{1,0:T(8,128)(2,1)} %raise_ref.1) | copy-start | bytes 98308
  34.1 13.8 %copy-start.4 = (f32[64,256]{1,0:T(8,128)S(1)}, f32[64,256]{1,0:T(8,128)}, u32[]{:S(2)}) copy-start(f32[64,256]{1,0:T(8,128)} %copy-done.3) | copy-start | bytes 196612
  34.1 13.7 %collective-permute-start.9 = (bf16[112,256]{1,0:T(8,128)(2,1)S(1)}, bf16[112,256]{1,0:T(8,128)(2,1)S(1)}, u32[]{:S(2)}, u32[]{:S(2)}) collective-permute-start(bf16[112,256]{1,0:T(8,128)(2,1)S(1)} %pad_maximum_fusion.2), channel_id=1, source_target_pairs={{0,8},{4,12},{8,0},{12,4},{1,9},{5,13},{9,1},{13,5},{2,10},{6,14},... | collective-permute-start | bytes 172040 | tf_op jit(solution)/shard_map/ppermute | solution.py:616
  51.1 4.8 %collective-permute-start.10 = (bf16[208,256]{1,0:T(8,128)(2,1)S(1)}, bf16[208,256]{1,0:T(8,128)(2,1)S(1)}, u32[]{:S(2)}, u32[]{:S(2)}) collective-permute-start(bf16[208,256]{1,0:T(8,128)(2,1)S(1)} %get-tuple-element.48.near_ref), channel_id=1, source_target_pairs={{0,16},{16,0},{1,17},{17,1},{2,18},{18,2},{3,19},{19,3},{4,20},{20... | collective-permute-start | bytes 319496 | tf_op jit(solution)/shard_map/ppermute | solution.py:650
  56.0 3.8 %collective-permute-start.13 = (f32[96,128]{1,0:T(8,128)S(1)}, f32[96,128]{1,0:T(8,128)S(1)}, u32[]{:S(2)}, u32[]{:S(2)}) collective-permute-start(f32[96,128]{1,0:T(8,128)S(1)} %get-tuple-element.49.refs_0_), channel_id=1, source_target_pairs={{0,12},{4,8},{8,4},{12,0},{1,13},{5,9},{9,5},{13,1},{2,14},{6,10},... | collective-permute-start | bytes 147464 | tf_op jit(solution)/shard_map/ppermute | solution.py:520
  56.0 4.7 %collective-permute-start.12 = (f32[96,128]{1,0:T(8,128)S(1)}, f32[96,128]{1,0:T(8,128)S(1)}, u32[]{:S(2)}, u32[]{:S(2)}) collective-permute-start(f32[96,128]{1,0:T(8,128)S(1)} %get-tuple-element.49.refs_0_), channel_id=1, source_target_pairs={{0,8},{4,12},{8,0},{12,4},{1,9},{5,13},{9,1},{13,5},{2,10},{6,14},... | collective-permute-start | bytes 147464 | tf_op jit(solution)/shard_map/ppermute | solution.py:520
  57.8 2.9 %collective-permute-start.11 = (f32[96,128]{1,0:T(8,128)S(1)}, f32[96,128]{1,0:T(8,128)S(1)}, u32[]{:S(2)}, u32[]{:S(2)}) collective-permute-start(f32[96,128]{1,0:T(8,128)S(1)} %get-tuple-element.49.refs_0_), channel_id=1, source_target_pairs={{0,4},{4,0},{8,12},{12,8},{1,5},{5,1},{9,13},{13,9},{2,6},{6,2},{1... | collective-permute-start | bytes 147464 | tf_op jit(solution)/shard_map/ppermute | solution.py:520
  60.7 10.0 %collective-permute-start.14 = (bf16[384,256]{1,0:T(8,128)(2,1)S(1)}, bf16[384,256]{1,0:T(8,128)(2,1)S(1)}, u32[]{:S(2)}, u32[]{:S(2)}) collective-permute-start(bf16[384,256]{1,0:T(8,128)(2,1)S(1)} %get-tuple-element.51.refs_4_), channel_id=1, source_target_pairs={{0,8},{4,12},{8,0},{12,4},{1,9},{5,13},{9,1},{13,5},{2,10},{6,14},... | collective-permute-start | bytes 589832 | tf_op jit(solution)/shard_map/ppermute | solution.py:668
  62.4 5.5 %collective-permute-start.17 = (f32[32,128]{1,0:T(8,128)S(1)}, f32[32,128]{1,0:T(8,128)S(1)}, u32[]{:S(2)}, u32[]{:S(2)}) collective-permute-start(f32[32,128]{1,0:T(8,128)S(1)} %fusion.12.refs_6_), channel_id=1, source_target_pairs={{0,3},{1,2},{2,1},{3,0},{4,7},{5,6},{6,5},{7,4},{8,11},{9,10},{10,... | collective-permute-start | bytes 49160 | tf_op jit(solution)/shard_map/ppermute | solution.py:520
  66.0 4.6 %collective-permute-start.16 = (f32[32,128]{1,0:T(8,128)S(1)}, f32[32,128]{1,0:T(8,128)S(1)}, u32[]{:S(2)}, u32[]{:S(2)}) collective-permute-start(f32[32,128]{1,0:T(8,128)S(1)} %fusion.12.refs_6_), channel_id=1, source_target_pairs={{0,2},{1,3},{2,0},{3,1},{4,6},{5,7},{6,4},{7,5},{8,10},{9,11},{10,... | collective-permute-start | bytes 49160 | tf_op jit(solution)/shard_map/ppermute | solution.py:520
  66.0 4.6 %collective-permute-start.15 = (f32[32,128]{1,0:T(8,128)S(1)}, f32[32,128]{1,0:T(8,128)S(1)}, u32[]{:S(2)}, u32[]{:S(2)}) collective-permute-start(f32[32,128]{1,0:T(8,128)S(1)} %fusion.12.refs_6_), channel_id=1, source_target_pairs={{0,1},{1,0},{2,3},{3,2},{4,5},{5,4},{6,7},{7,6},{8,9},{9,8},{10,11... | collective-permute-start | bytes 49160 | tf_op jit(solution)/shard_map/ppermute | solution.py:520
  71.6 1.2 %collective-permute-start.18 = (f32[16,512]{1,0:T(8,128)S(1)}, f32[16,512]{1,0:T(8,128)S(1)}, u32[]{:S(2)}, u32[]{:S(2)}) collective-permute-start(f32[16,512]{1,0:T(8,128)S(1)} %get-tuple-element.56), channel_id=1, source_target_pairs={{0,4},{4,0},{8,12},{12,8},{1,5},{5,1},{9,13},{13,9},{2,6},{6,2},{1... | collective-permute-start | bytes 98312 | tf_op jit(solution)/shard_map/ppermute | solution.py:683

commit v13 on v12

--- a/solution.py
+++ b/solution.py
@@ -191,12 +191,17 @@
     groups = vocab // IDS_PER_GROUP
     span = member_ref.shape[0]
 
+    slots = held.shape[0]
+
+    def slot(b):
+        return b if slots == blocks else lax.rem(b, slots)
+
     def vocab_copy(b):
         columns = pl.ds(pl.multiple_of(b * IDS_PER_BLOCK, LANES), IDS_PER_BLOCK)
-        return pltpu.make_async_copy(vocab_ref.at[:, columns], held.at[b], held_sems.at[b])
+        return pltpu.make_async_copy(vocab_ref.at[:, columns], held.at[slot(b)], held_sems.at[slot(b)])
 
     vocab_copy(0).start()
-    for b in range(1, blocks):
+    for b in range(1, slots):
         vocab_copy(b).start()
 
     ids = ids_ref[...]
@@ -267,13 +272,13 @@
                 ).astype(jnp.bfloat16)
                 columns = pl.ds(part * IDS_PER_GROUP, IDS_PER_GROUP)
                 rest = pl.ds(TAKEN, features - TAKEN)
-                product = mm(held[b, rest, columns], picked).astype(jnp.bfloat16)
+                product = mm(held[slot(b), rest, columns], picked).astype(jnp.bfloat16)
                 fresh = []
                 for rows in pieces:
                     total = jnp.zeros((FEATURE_ROWS, LANES), jnp.bfloat16)
                     for j in range(IDS_PER_GROUP // LANES):
                         columns = pl.ds(part * IDS_PER_GROUP + j * LANES, LANES)
-                        total = jnp.where(tile == j, take_lanes(held[b, rows, columns], lane), total)
+                        total = jnp.where(tile == j, take_lanes(held[slot(b), rows, columns], lane), total)
                     fresh.append(total)
                 pieces.append(rest)
                 fresh.append(product)
@@ -283,6 +288,12 @@
                 return carry
 
             lax.fori_loop(begin, jnp.where(last > first, end, begin), window, 0)
+        if slots < blocks:
+
+            @pl.when(b + slots < blocks)
+            def _():
+                vocab_copy(b + slots).start()
+
         return carry
 
     lax.fori_loop(0, blocks, take, 0)
@@ -548,7 +559,7 @@
         start = split_quarter(i, j) * width
         return lax.dynamic_slice(layer_weight_matrix, (0, start), (features, width))
 
-    def project(base, span):
+    def project(base, span, slots, grant):
         stripes = pl.cdiv(span, STRIPE)
         extra_rows = (stripes + 1 + shards) * ROWS
         turned, member, count = pl.pallas_call(
@@ -563,16 +574,16 @@
             scratch_shapes=[
                 pltpu.VMEM((features, span), jnp.bfloat16),
                 pltpu.VMEM((span, LANES), jnp.bfloat16),
-                pltpu.VMEM((blocks, features, IDS_PER_BLOCK), jnp.bfloat16),
+                pltpu.VMEM((slots, features, IDS_PER_BLOCK), jnp.bfloat16),
                 pltpu.VMEM((8 * pl.cdiv(span // LANES, 8), LANES), jnp.int32),
                 pltpu.VMEM((texts, length), jnp.float32),
                 pltpu.VMEM((group_rows, length), jnp.int32),
                 pltpu.SMEM((group_rows, length), jnp.int32),
-                pltpu.SemaphoreType.DMA((blocks,)),
+                pltpu.SemaphoreType.DMA((slots,)),
                 pltpu.SemaphoreType.DMA,
                 pltpu.SemaphoreType.DMA((2,)),
             ],
-            compiler_params=params,
+            compiler_params=grant,
             name="gather",
         )(ids, vocabulary_vectors)
 
@@ -619,13 +630,13 @@
         own0 = narrow(product(turned, 0, 0))
         return (own0, core0, far, extra, member), count
 
-    first, count = project(0, FIRST)
+    first, count = project(0, FIRST, blocks, params)
     many = count[0] > FIRST
     left = tokens - FIRST
-    shapes = jax.eval_shape(lambda: project(FIRST, left)[0])
+    shapes = jax.eval_shape(lambda: project(FIRST, left, min(blocks, 4), modest)[0])
     rest = lax.cond(
         many,
-        lambda: project(FIRST, left)[0],
+        lambda: project(FIRST, left, min(blocks, 4), modest)[0],
         lambda: tuple(jnp.zeros(x.shape, x.dtype) for x in shapes),
     )
     sent, misc = pl.pallas_call(

time: 73.3 us -> 73.9 us (level)
  no operation moved by 1% of the time
where the time goes in v13:
time: 73.9 us; the launch traced here: 73.5 us
  waiting for transfers between devices  22.6 us (31%)
  Pallas kernels  22.1 us (30%)
  starting transfers between devices  13.8 us (19%)
  matrix products  7.05 us (10%)
  local copies, waits for them, and re-layouts  3.43 us (5%)
  other arithmetic  2.25 us (3%)
  between operations  2.14 us (3%)
    pallas_call x1, Pallas kernels, project(): pl.pallas_call(functools.partial(gather_kernel, base=base), out_shape=[ja...  15.5 us
    ppermute x1, waiting for transfers between devices, project(): sent = lax.ppermute(sent, 'dp', other_y).astype(jnp.float32)  12.8 us
    dot_general x4, matrix products, mm(): return lax.dot_general(a, b, dims, preferred_element_type=jnp.float32)  7.05 us
    ppermute x6, starting transfers between devices, exchange(): return [x] + [lax.ppermute(x, axis, step) for step in steps]  6.28 us
    ppermute x6, waiting for transfers between devices, exchange(): return [x] + [lax.ppermute(x, axis, step) for step in steps]  5.97 us
    pallas_call x1, Pallas kernels, split_body(): pl.pallas_call(functools.partial(pool_kernel, model_width=float(features...  3.19 us
    ppermute x1, starting transfers between devices, project(): far = lax.ppermute(chip1, 'dp', other_y)  3.03 us
    ppermute x1, waiting for transfers between devices, split_body(): far_side = lax.ppermute(sent, 'group', [(0, 1), (1, 0)])  2.69 us
  transfers between devices with their start and end apart: 14, of which 7 were waited for; matrix products, arithmetic and copies ran while one was open for 9% of the time, Pallas kernels for 0%

profile of v13, /device:TPU:0, one launch (start us, length us, event | category | flops | bytes accessed | tf_op | source)
XLA Modules:
  0.0 73.5 jit_solution(15496300680596965477)
XLA Ops:
  0.6 0.7 copy.12
  1.3 15.5 %gather.3 = (bf16[1024,1152]{1,0:T(8,128)(2,1)S(1)}, bf16[1152,128]{1,0:T(8,128)(2,1)S(1)}, s32[1]{0:T(128)}) custom-call(s32[12,128]{1,0:T(8,128)S(1)} %bitcast.12, bf16[1024,16384]{1,0:T(8,128)(2,1)} %vocab_ref.1), custom_call_target="tpu_custom_call" | custom-call | tf_op jit(solution)/shard_map/gather/pallas_call | solution.py:565
  16.8 2.7 %convolution_convert_fusion.6 = bf16[1152,256]{1,0:T(8,128)(2,1)} fusion(bf16[1024,1152]{1,0:T(8,128)(2,1)S(1)} %get-tuple-element.40.turned_any, bf16[1024,1024]{1,0:T(8,128)(2,1)} %param.12, s32[]{:T(128)S(6)} %select_n.37), kind=kOutput, calls=%fused_computation.20 | convolution fusion | flops 604274688 | bytes 3473412 | tf_op jit(solution)/shard_map/dot_general | solution.py:128
  20.6 2.7 %convolution_convert_fusion.7 = bf16[1152,256]{1,0:T(8,128)(2,1)} fusion(bf16[1024,1152]{1,0:T(8,128)(2,1)S(1)} %get-tuple-element.40.turned_any, bf16[1024,1024]{1,0:T(8,128)(2,1)} %param.12, s32[]{:T(128)S(6)} %select_n.36), kind=kOutput, calls=%fused_computation.21 | convolution fusion | flops 604274688 | bytes 3473412 | tf_op jit(solution)/shard_map/dot_general | solution.py:128
  23.3 2.1 %conditional.1 = (bf16[384,256]{1,0:T(8,128)(2,1)}, bf16[384,256]{1,0:T(8,128)(2,1)}, bf16[384,256]{1,0:T(8,128)(2,1)}, f32[64,256]{1,0:T(8,128)S(1)}, bf16[384,128]{1,0:T(8,128)(2,1)S(1)}) conditional(s32[]{:T(128)} %bitcast, () %tuple.20, (s32[12,128]{1,0:T(8,128)S(1)}, bf16[1024,16384]{1,0:T(8,128)(2,1)}, bf16[1024,1024]{1,0:T(8,128)(2,1)}, ...), branch_computations={%region_0.0_spmd, %region_1.0_spmd} | conditional | flops 919543808 | bytes 11805392 | solution.py:637
  23.4 0.7 broadcast.8.clone.1
  26.1 1.5 %add_convert_fusion.1 = bf16[1152,256]{1,0:T(8,128)(2,1)S(1)} fusion(bf16[1152,256]{1,0:T(8,128)(2,1)} %collective-permute-done.5, bf16[1152,256]{1,0:T(8,128)(2,1)} %convolution_convert_fusion.7), kind=kLoop, calls=%fused_computation.22 | loop fusion | flops 1179648 | bytes 1769472 | tf_op jit(solution)/shard_map/convert_element_type | solution.py:594
  27.6 2.3 %statistics.3 = bf16[160,256]{1,0:T(8,128)(2,1)S(1)} custom-call(bf16[1024,1152]{1,0:T(8,128)(2,1)S(1)} %get-tuple-element.40.turned_any, bf16[1152,128]{1,0:T(8,128)(2,1)S(1)} %get-tuple-element.41.member_any.member_ref, s32[3,7]{1,0:T(4,128)S(1)} %copy-done.5, bf16[16,4096]{1,0:T(8,128)(2,1)} %lower_ref.1), custom_call_target="tpu_custom_call" | custom-call | flops 339738624 | bytes 2359296 | tf_op jit(solution)/shard_map/statistics/pallas_call | solution.py:601
  30.1 3.0 %collective-permute-start.7 = (bf16[1152,256]{1,0:T(8,128)(2,1)S(1)}, bf16[1152,256]{1,0:T(8,128)(2,1)S(1)}, u32[]{:S(2)}, u32[]{:S(2)}) collective-permute-start(bf16[1152,256]{1,0:T(8,128)(2,1)S(1)} %add_convert_fusion.1), channel_id=1, source_target_pairs={{0,8},{4,12},{8,0},{12,4},{1,9},{5,13},{9,1},{13,5},{2,10},{6,14},... | collective-permute-start | bytes 1769480 | tf_op jit(solution)/shard_map/ppermute | solution.py:599
  33.1 0.8 %convolution_convert_fusion.4 = bf16[1152,256]{1,0:T(8,128)(2,1)S(1)} fusion(bf16[1024,1152]{1,0:T(8,128)(2,1)S(1)} %get-tuple-element.40.turned_any, bf16[1024,1024]{1,0:T(8,128)(2,1)S(1)} %copy-done.6, s32[]{:T(128)S(6)} %select_n.39), kind=kOutput, calls=%fused_computation.18 | convolution fusion | flops 604274688 | bytes 3473412 | tf_op jit(solution)/shard_map/dot_general | solution.py:128
  34.2 0.8 %convolution_convert_fusion.5.own_ref = bf16[1152,256]{1,0:T(8,128)(2,1)S(1)} fusion(bf16[1024,1152]{1,0:T(8,128)(2,1)S(1)} %get-tuple-element.40.turned_any, bf16[1024,1024]{1,0:T(8,128)(2,1)S(1)} %copy-done.6, s32[]{:T(128)S(6)} %select_n.38), kind=kOutput, calls=%fused_computation.19 | convolution fusion | flops 604274688 | bytes 3473412 | tf_op jit(solution)/shard_map/dot_general | solution.py:128
  35.1 12.8 %collective-permute-done.9 = bf16[112,256]{1,0:T(8,128)(2,1)S(1)} collective-permute-done((bf16[112,256]{1,0:T(8,128)(2,1)S(1)}, bf16[112,256]{1,0:T(8,128)(2,1)S(1)}, u32[]{:S(2)}, u32[]{:S(2)}) %collective-permute-start.9) | collective-permute-done | bytes 57376 | tf_op jit(solution)/shard_map/ppermute | solution.py:627
  47.9 3.2 %pool.1 = (bf16[208,256]{1,0:T(8,128)(2,1)S(1)}, f32[16,256]{1,0:T(8,128)S(1)}) custom-call(s32[12,128]{1,0:T(8,128)S(1)} %bitcast.14, bf16[1152,256]{1,0:T(8,128)(2,1)S(1)} %convolution_convert_fusion.5.own_ref, bf16[1152,256]{1,0:T(8,128)(2,1)S(1)} %collective-permute-done.6.core_any, bf16[1152,256]{1,0:T(8,128)(2,1)S(1)} %collective-permute-done.7.far_any, ...), custom_call_target="tpu_custom_call" | custom-call | tf_op jit(solution)/shard_map/pool/pallas_call | solution.py:642
  51.1 2.1 %collective-permute-start.10 = (bf16[208,256]{1,0:T(8,128)(2,1)S(1)}, bf16[208,256]{1,0:T(8,128)(2,1)S(1)}, u32[]{:S(2)}, u32[]{:S(2)}) collective-permute-start(bf16[208,256]{1,0:T(8,128)(2,1)S(1)} %get-tuple-element.48.near_ref), channel_id=1, source_target_pairs={{0,16},{16,0},{1,17},{17,1},{2,18},{18,2},{3,19},{19,3},{4,20},{20... | collective-permute-start | bytes 319496 | tf_op jit(solution)/shard_map/ppermute | solution.py:661
  53.2 2.7 %collective-permute-done.10.far_ref = bf16[208,256]{1,0:T(8,128)(2,1)S(1)} collective-permute-done((bf16[208,256]{1,0:T(8,128)(2,1)S(1)}, bf16[208,256]{1,0:T(8,128)(2,1)S(1)}, u32[]{:S(2)}, u32[]{:S(2)}) %collective-permute-start.10) | collective-permute-done | bytes 106528 | tf_op jit(solution)/shard_map/ppermute | solution.py:661
  56.0 1.8 %collective-permute-start.12 = (f32[96,128]{1,0:T(8,128)S(1)}, f32[96,128]{1,0:T(8,128)S(1)}, u32[]{:S(2)}, u32[]{:S(2)}) collective-permute-start(f32[96,128]{1,0:T(8,128)S(1)} %get-tuple-element.49.refs_0_), channel_id=1, source_target_pairs={{0,8},{4,12},{8,0},{12,4},{1,9},{5,13},{9,1},{13,5},{2,10},{6,14},... | collective-permute-start | bytes 147464 | tf_op jit(solution)/shard_map/ppermute | solution.py:531
  57.9 1.9 %collective-permute-done.13.refs_3_ = f32[96,128]{1,0:T(8,128)S(1)} collective-permute-done((f32[96,128]{1,0:T(8,128)S(1)}, f32[96,128]{1,0:T(8,128)S(1)}, u32[]{:S(2)}, u32[]{:S(2)}) %collective-permute-start.13) | collective-permute-done | bytes 49184 | tf_op jit(solution)/shard_map/ppermute | solution.py:531
  59.8 0.9 %collective-permute-done.12.refs_2_ = f32[96,128]{1,0:T(8,128)S(1)} collective-permute-done((f32[96,128]{1,0:T(8,128)S(1)}, f32[96,128]{1,0:T(8,128)S(1)}, u32[]{:S(2)}, u32[]{:S(2)}) %collective-permute-start.12) | collective-permute-done | bytes 49184 | tf_op jit(solution)/shard_map/ppermute | solution.py:531
  60.7 1.7 %collective-permute-start.14 = (bf16[384,256]{1,0:T(8,128)(2,1)S(1)}, bf16[384,256]{1,0:T(8,128)(2,1)S(1)}, u32[]{:S(2)}, u32[]{:S(2)}) collective-permute-start(bf16[384,256]{1,0:T(8,128)(2,1)S(1)} %get-tuple-element.51.refs_4_), channel_id=1, source_target_pairs={{0,8},{4,12},{8,0},{12,4},{1,9},{5,13},{9,1},{13,5},{2,10},{6,14},... | collective-permute-start | bytes 589832 | tf_op jit(solution)/shard_map/ppermute | solution.py:679
  62.4 3.6 %collective-permute-start.17 = (f32[32,128]{1,0:T(8,128)S(1)}, f32[32,128]{1,0:T(8,128)S(1)}, u32[]{:S(2)}, u32[]{:S(2)}) collective-permute-start(f32[32,128]{1,0:T(8,128)S(1)} %fusion.12.refs_6_), channel_id=1, source_target_pairs={{0,3},{1,2},{2,1},{3,0},{4,7},{5,6},{6,5},{7,4},{8,11},{9,10},{10,... | collective-permute-start | bytes 49160 | tf_op jit(solution)/shard_map/ppermute | solution.py:531
  66.0 0.8 %collective-permute-start.15 = (f32[32,128]{1,0:T(8,128)S(1)}, f32[32,128]{1,0:T(8,128)S(1)}, u32[]{:S(2)}, u32[]{:S(2)}) collective-permute-start(f32[32,128]{1,0:T(8,128)S(1)} %fusion.12.refs_6_), channel_id=1, source_target_pairs={{0,1},{1,0},{2,3},{3,2},{4,5},{5,4},{6,7},{7,6},{8,9},{9,8},{10,11... | collective-permute-start | bytes 49160 | tf_op jit(solution)/shard_map/ppermute | solution.py:531
  67.9 2.7 %collective-permute-done.16.refs_8_ = f32[32,128]{1,0:T(8,128)S(1)} collective-permute-done((f32[32,128]{1,0:T(8,128)S(1)}, f32[32,128]{1,0:T(8,128)S(1)}, u32[]{:S(2)}, u32[]{:S(2)}) %collective-permute-start.16) | collective-permute-done | bytes 16416 | tf_op jit(solution)/shard_map/ppermute | solution.py:531
  70.6 1.0 %score.1 = (bf16[1,3,1024]{2,1,0:T(4,128)(2,1)}, f32[1,3]{1,0:T(1,128)}, f32[16,512]{1,0:T(8,128)S(1)}) custom-call(f32[96,128]{1,0:T(8,128)S(1)} %get-tuple-element.49.refs_0_, f32[96,128]{1,0:T(8,128)S(1)} %collective-permute-done.11.refs_1_, f32[96,128]{1,0:T(8,128)S(1)} %collective-permute-done.12.refs_2_, ...), custom_call_target="tpu_custom_call" | custom-call | tf_op jit(solution)/shard_map/score/pallas_call | solution.py:680
  71.6 1.2 %collective-permute-done.18 = f32[16,512]{1,0:T(8,128)S(1)} collective-permute-done((f32[16,512]{1,0:T(8,128)S(1)}, f32[16,512]{1,0:T(8,128)S(1)}, u32[]{:S(2)}, u32[]{:S(2)}) %collective-permute-start.18) | collective-permute-done | bytes 32800 | tf_op jit(solution)/shard_map/ppermute | solution.py:694
  (42 shorter events, 4.3 us)
Async XLA Ops:
  19.5 6.6 %collective-permute-start.5 = (bf16[1152,256]{1,0:T(8,128)(2,1)}, bf16[1152,256]{1,0:T(8,128)(2,1)}, u32[]{:S(2)}, u32[]{:S(2)}) collective-permute-start(bf16[1152,256]{1,0:T(8,128)(2,1)} %convolution_convert_fusion.6), channel_id=1, source_target_pairs={{0,4},{4,0},{8,12},{12,8},{1,5},{5,1},{9,13},{13,9},{2,6},{6,2},{1... | collective-permute-start | bytes 1769480 | tf_op jit(solution)/shard_map/ppermute | solution.py:596
  20.6 2.7 %copy-start.5 = (s32[3,7]{1,0:T(4,128)S(1)}, s32[3,7]{1,0:T(4,128)}, u32[]{:S(2)}) copy-start(s32[3,7]{1,0:T(4,128)} %hard_ref.1) | copy-start | bytes 256
  25.4 0.6 copy-start.3
  26.1 7.0 %copy-start.6 = (bf16[1024,1024]{1,0:T(8,128)(2,1)S(1)}, bf16[1024,1024]{1,0:T(8,128)(2,1)}, u32[]{:S(2)}) copy-start(bf16[1024,1024]{1,0:T(8,128)(2,1)} %param.12) | copy-start | bytes 6291460
  29.9 4.1 %collective-permute-start.8 = (bf16[160,256]{1,0:T(8,128)(2,1)S(1)}, bf16[160,256]{1,0:T(8,128)(2,1)S(1)}, u32[]{:S(2)}, u32[]{:S(2)}) collective-permute-start(bf16[160,256]{1,0:T(8,128)(2,1)S(1)} %statistics.3), channel_id=1, source_target_pairs={{0,4},{4,0},{8,12},{12,8},{1,5},{5,1},{9,13},{13,9},{2,6},{6,2},{1... | collective-permute-start | bytes 245768 | tf_op jit(solution)/shard_map/ppermute | solution.py:623
  30.1 17.8 %collective-permute-start.7 = (bf16[1152,256]{1,0:T(8,128)(2,1)S(1)}, bf16[1152,256]{1,0:T(8,128)(2,1)S(1)}, u32[]{:S(2)}, u32[]{:S(2)}) collective-permute-start(bf16[1152,256]{1,0:T(8,128)(2,1)S(1)} %add_convert_fusion.1), channel_id=1, source_target_pairs={{0,8},{4,12},{8,0},{12,4},{1,9},{5,13},{9,1},{13,5},{2,10},{6,14},... | collective-permute-start | bytes 1769480 | tf_op jit(solution)/shard_map/ppermute | solution.py:599
  33.9 13.9 %collective-permute-start.6 = (bf16[1152,256]{1,0:T(8,128)(2,1)S(1)}, bf16[1152,256]{1,0:T(8,128)(2,1)S(1)}, u32[]{:S(2)}, u32[]{:S(2)}) collective-permute-start(bf16[1152,256]{1,0:T(8,128)(2,1)S(1)} %convolution_convert_fusion.4), channel_id=1, source_target_pairs={{0,4},{4,0},{8,12},{12,8},{1,5},{5,1},{9,13},{13,9},{2,6},{6,2},{1... | collective-permute-start | bytes 1769480 | tf_op jit(solution)/shard_map/ppermute | solution.py:629
  34.1 13.8 %copy-start = (bf16[16,1024]{1,0:T(8,128)(2,1)S(1)}, bf16[16,1024]{1,0:T(8,128)(2,1)}, u32[]{:S(2)}) copy-start(bf16[16,1024]{1,0:T(8,128)(2,1)} %raise_ref.1) | copy-start | bytes 98308
  34.1 13.8 %copy-start.4 = (f32[64,256]{1,0:T(8,128)S(1)}, f32[64,256]{1,0:T(8,128)}, u32[]{:S(2)}) copy-start(f32[64,256]{1,0:T(8,128)} %copy-done.3) | copy-start | bytes 196612
  34.1 13.7 %collective-permute-start.9 = (bf16[112,256]{1,0:T(8,128)(2,1)S(1)}, bf16[112,256]{1,0:T(8,128)(2,1)S(1)}, u32[]{:S(2)}, u32[]{:S(2)}) collective-permute-start(bf16[112,256]{1,0:T(8,128)(2,1)S(1)} %pad_maximum_fusion.2), channel_id=1, source_target_pairs={{0,8},{4,12},{8,0},{12,4},{1,9},{5,13},{9,1},{13,5},{2,10},{6,14},... | collective-permute-start | bytes 172040 | tf_op jit(solution)/shard_map/ppermute | solution.py:627
  51.1 4.8 %collective-permute-start.10 = (bf16[208,256]{1,0:T(8,128)(2,1)S(1)}, bf16[208,256]{1,0:T(8,128)(2,1)S(1)}, u32[]{:S(2)}, u32[]{:S(2)}) collective-permute-start(bf16[208,256]{1,0:T(8,128)(2,1)S(1)} %get-tuple-element.48.near_ref), channel_id=1, source_target_pairs={{0,16},{16,0},{1,17},{17,1},{2,18},{18,2},{3,19},{19,3},{4,20},{20... | collective-permute-start | bytes 319496 | tf_op jit(solution)/shard_map/ppermute | solution.py:661
  56.0 3.8 %collective-permute-start.13 = (f32[96,128]{1,0:T(8,128)S(1)}, f32[96,128]{1,0:T(8,128)S(1)}, u32[]{:S(2)}, u32[]{:S(2)}) collective-permute-start(f32[96,128]{1,0:T(8,128)S(1)} %get-tuple-element.49.refs_0_), channel_id=1, source_target_pairs={{0,12},{4,8},{8,4},{12,0},{1,13},{5,9},{9,5},{13,1},{2,14},{6,10},... | collective-permute-start | bytes 147464 | tf_op jit(solution)/shard_map/ppermute | solution.py:531
  56.0 4.7 %collective-permute-start.12 = (f32[96,128]{1,0:T(8,128)S(1)}, f32[96,128]{1,0:T(8,128)S(1)}, u32[]{:S(2)}, u32[]{:S(2)}) collective-permute-start(f32[96,128]{1,0:T(8,128)S(1)} %get-tuple-element.49.refs_0_), channel_id=1, source_target_pairs={{0,8},{4,12},{8,0},{12,4},{1,9},{5,13},{9,1},{13,5},{2,10},{6,14},... | collective-permute-start | bytes 147464 | tf_op jit(solution)/shard_map/ppermute | solution.py:531
  57.8 2.9 %collective-permute-start.11 = (f32[96,128]{1,0:T(8,128)S(1)}, f32[96,128]{1,0:T(8,128)S(1)}, u32[]{:S(2)}, u32[]{:S(2)}) collective-permute-start(f32[96,128]{1,0:T(8,128)S(1)} %get-tuple-element.49.refs_0_), channel_id=1, source_target_pairs={{0,4},{4,0},{8,12},{12,8},{1,5},{5,1},{9,13},{13,9},{2,6},{6,2},{1... | collective-permute-start | bytes 147464 | tf_op jit(solution)/shard_map/ppermute | solution.py:531
  60.7 10.0 %collective-permute-start.14 = (bf16[384,256]{1,0:T(8,128)(2,1)S(1)}, bf16[384,256]{1,0:T(8,128)(2,1)S(1)}, u32[]{:S(2)}, u32[]{:S(2)}) collective-permute-start(bf16[384,256]{1,0:T(8,128)(2,1)S(1)} %get-tuple-element.51.refs_4_), channel_id=1, source_target_pairs={{0,8},{4,12},{8,0},{12,4},{1,9},{5,13},{9,1},{13,5},{2,10},{6,14},... | collective-permute-start | bytes 589832 | tf_op jit(solution)/shard_map/ppermute | solution.py:679
  62.4 5.5 %collective-permute-start.17 = (f32[32,128]{1,0:T(8,128)S(1)}, f32[32,128]{1,0:T(8,128)S(1)}, u32[]{:S(2)}, u32[]{:S(2)}) collective-permute-start(f32[32,128]{1,0:T(8,128)S(1)} %fusion.12.refs_6_), channel_id=1, source_target_pairs={{0,3},{1,2},{2,1},{3,0},{4,7},{5,6},{6,5},{7,4},{8,11},{9,10},{10,... | collective-permute-start | bytes 49160 | tf_op jit(solution)/shard_map/ppermute | solution.py:531
  66.0 4.6 %collective-permute-start.16 = (f32[32,128]{1,0:T(8,128)S(1)}, f32[32,128]{1,0:T(8,128)S(1)}, u32[]{:S(2)}, u32[]{:S(2)}) collective-permute-start(f32[32,128]{1,0:T(8,128)S(1)} %fusion.12.refs_6_), channel_id=1, source_target_pairs={{0,2},{1,3},{2,0},{3,1},{4,6},{5,7},{6,4},{7,5},{8,10},{9,11},{10,... | collective-permute-start | bytes 49160 | tf_op jit(solution)/shard_map/ppermute | solution.py:531
  66.0 4.6 %collective-permute-start.15 = (f32[32,128]{1,0:T(8,128)S(1)}, f32[32,128]{1,0:T(8,128)S(1)}, u32[]{:S(2)}, u32[]{:S(2)}) collective-permute-start(f32[32,128]{1,0:T(8,128)S(1)} %fusion.12.refs_6_), channel_id=1, source_target_pairs={{0,1},{1,0},{2,3},{3,2},{4,5},{5,4},{6,7},{7,6},{8,9},{9,8},{10,11... | collective-permute-start | bytes 49160 | tf_op jit(solution)/shard_map/ppermute | solution.py:531
  71.6 1.2 %collective-permute-start.18 = (f32[16,512]{1,0:T(8,128)S(1)}, f32[16,512]{1,0:T(8,128)S(1)}, u32[]{:S(2)}, u32[]{:S(2)}) collective-permute-start(f32[16,512]{1,0:T(8,128)S(1)} %get-tuple-element.56), channel_id=1, source_target_pairs={{0,4},{4,0},{8,12},{12,8},{1,5},{5,1},{9,13},{13,9},{2,6},{6,2},{1... | collective-permute-start | bytes 98312 | tf_op jit(solution)/shard_map/ppermute | solution.py:694

commit v14 on v12

--- a/solution.py
+++ b/solution.py
@@ -172,7 +172,6 @@
     vocab_ref,
     turned_any,
     member_any,
-    count_ref,
     turned,
     member_ref,
     held,
@@ -241,7 +240,6 @@
 
     lax.fori_loop(0, span // LANES, place, 0)
     bounds_copy.wait()
-    count_ref[0] = bounds[groups, 0]
 
     def within(place):
         return jnp.clip(place - base, 0, span)
@@ -551,15 +549,14 @@
     def project(base, span):
         stripes = pl.cdiv(span, STRIPE)
         extra_rows = (stripes + 1 + shards) * ROWS
-        turned, member, count = pl.pallas_call(
+        turned, member = pl.pallas_call(
             functools.partial(gather_kernel, base=base),
             out_shape=[
                 jax.ShapeDtypeStruct((features, span), jnp.bfloat16),
                 jax.ShapeDtypeStruct((span, LANES), jnp.bfloat16),
-                jax.ShapeDtypeStruct((1,), jnp.int32),
             ],
             in_specs=[vmem_spec(), any_spec()],
-            out_specs=[any_spec()] * 2 + [smem_spec()],
+            out_specs=[any_spec()] * 2,
             scratch_shapes=[
                 pltpu.VMEM((features, span), jnp.bfloat16),
                 pltpu.VMEM((span, LANES), jnp.bfloat16),
@@ -617,15 +614,16 @@
         extra = jnp.concatenate([chip, inputs[0:ROWS]]) + sent
         core0 = lax.ppermute(narrow(product(turned, 1, 0)), "dp", other_core)
         own0 = narrow(product(turned, 0, 0))
-        return (own0, core0, far, extra, member), count
-
-    first, count = project(0, FIRST)
-    many = count[0] > FIRST
+        return own0, core0, far, extra, member
+
+    first = project(0, FIRST)
+    later, _ = lax.optimization_barrier((ids, first[0]))
+    many = jnp.sum((later != 0).astype(jnp.int32)) > FIRST
     left = tokens - FIRST
-    shapes = jax.eval_shape(lambda: project(FIRST, left)[0])
+    shapes = jax.eval_shape(lambda: project(FIRST, left))
     rest = lax.cond(
         many,
-        lambda: project(FIRST, left)[0],
+        lambda: project(FIRST, left),
         lambda: tuple(jnp.zeros(x.shape, x.dtype) for x in shapes),
     )
     sent, misc = pl.pallas_call(

time: 73.3 us -> 69.5 us (0.948)
  waiting for transfers between devices: 22.9 us -> 17.9 us
  other arithmetic: 2.25 us -> 4.41 us
  Pallas kernels: 22.1 us -> 20.3 us
  matrix products: 7.06 us -> 8.75 us
  local copies, waits for them, and re-layouts: 3.43 us -> 2.15 us
    ppermute x1, waiting for transfers between devices: 12.8 us -> 7.68 us  [project(): sent = lax.ppermute(sent, 'dp', other_y).astype(jnp.float32)]
    dot_general x4, matrix products: 7.06 us -> 8.75 us  [mm(): return lax.dot_general(a, b, dims, preferred_element_type=jnp.float32)]
    pallas_call x1, Pallas kernels: 2.31 us -> 1.4 us  [project(): pl.pallas_call(statistics_kernel, out_shape=jax.ShapeDtypeStruct((extra_r...]
    convert_element_type x1, other arithmetic: 0.01 us -> 0.9 us  [project(): across = lax.ppermute(extra, 'dp', other_core).astype(jnp.float32)]
    pallas_call x1, Pallas kernels: 15.5 us -> 14.7 us  [project(): pl.pallas_call(functools.partial(gather_kernel, base=base), out_shape=[ja...]
  transfers between devices with their start and end apart: 14 -> 14, of which waited for: 7 -> 7; matrix products, arithmetic and copies ran while one was open for 9% -> 13% of each run, Pallas kernels for 0% -> 0%
where the time goes in v14:
time: 69.5 us; the launch traced here: 69.2 us
  Pallas kernels  20.3 us (29%)
  waiting for transfers between devices  17.9 us (26%)
  starting transfers between devices  13.5 us (19%)
  matrix products  8.75 us (13%)
  other arithmetic  4.41 us (6%)
  local copies, waits for them, and re-layouts  2.15 us (3%)
  between operations  2.11 us (3%)
    pallas_call x1, Pallas kernels, project(): pl.pallas_call(functools.partial(gather_kernel, base=base), out_shape=[ja...  14.7 us
    dot_general x4, matrix products, mm(): return lax.dot_general(a, b, dims, preferred_element_type=jnp.float32)  8.75 us
    ppermute x1, waiting for transfers between devices, project(): sent = lax.ppermute(sent, 'dp', other_y).astype(jnp.float32)  7.68 us
    ppermute x6, starting transfers between devices, exchange(): return [x] + [lax.ppermute(x, axis, step) for step in steps]  6.28 us
    ppermute x6, waiting for transfers between devices, exchange(): return [x] + [lax.ppermute(x, axis, step) for step in steps]  5.98 us
    pallas_call x1, Pallas kernels, split_body(): pl.pallas_call(functools.partial(pool_kernel, model_width=float(features...  3.1 us
    ppermute x1, starting transfers between devices, project(): far = lax.ppermute(chip1, 'dp', other_y)  3.03 us
    ppermute x1, waiting for transfers between devices, split_body(): far_side = lax.ppermute(sent, 'group', [(0, 1), (1, 0)])  3 us
  transfers between devices with their start and end apart: 14, of which 7 were waited for; matrix products, arithmetic and copies ran while one was open for 13% of the time, Pallas kernels for 0%

profile of v14, /device:TPU:0, one launch (start us, length us, event | category | flops | bytes accessed | tf_op | source)
XLA Modules:
  0.0 69.2 jit_solution(15660341063236905417)
XLA Ops:
  1.3 14.7 %gather.3 = (bf16[1024,1152]{1,0:T(8,128)(2,1)S(1)}, bf16[1152,128]{1,0:T(8,128)(2,1)S(1)}) custom-call(s32[12,128]{1,0:T(8,128)S(1)} %bitcast.11, bf16[1024,16384]{1,0:T(8,128)(2,1)} %vocab_ref.1), custom_call_target="tpu_custom_call" | custom-call | tf_op jit(solution)/shard_map/gather/pallas_call | solution.py:552
  16.0 2.7 %convolution_convert_fusion.6 = bf16[1152,256]{1,0:T(8,128)(2,1)} fusion(bf16[1024,1152]{1,0:T(8,128)(2,1)S(1)} %get-tuple-element.40.turned_any, bf16[1024,1024]{1,0:T(8,128)(2,1)} %param.12, s32[]{:T(128)S(6)} %select_n.37), kind=kOutput, calls=%fused_computation.20 | convolution fusion | flops 604274688 | bytes 3473412 | tf_op jit(solution)/shard_map/dot_general | solution.py:128
  19.2 2.7 %convolution_convert_fusion.7 = bf16[1152,256]{1,0:T(8,128)(2,1)} fusion(bf16[1024,1152]{1,0:T(8,128)(2,1)S(1)} %get-tuple-element.40.turned_any, bf16[1024,1024]{1,0:T(8,128)(2,1)} %param.12, s32[]{:T(128)S(6)} %select_n.36), kind=kOutput, calls=%fused_computation.21 | convolution fusion | flops 604274688 | bytes 3473412 | tf_op jit(solution)/shard_map/dot_general | solution.py:128
  21.9 2.2 %add_convert_fusion.1 = bf16[1152,256]{1,0:T(8,128)(2,1)} fusion(bf16[1152,256]{1,0:T(8,128)(2,1)S(1)} %collective-permute-done.5, bf16[1152,256]{1,0:T(8,128)(2,1)} %convolution_convert_fusion.7), kind=kLoop, calls=%fused_computation.22 | loop fusion | flops 1179648 | bytes 1769472 | tf_op jit(solution)/shard_map/convert_element_type | solution.py:580
  24.1 1.4 %statistics.3 = bf16[160,256]{1,0:T(8,128)(2,1)S(1)} custom-call(bf16[1024,1152]{1,0:T(8,128)(2,1)S(1)} %get-tuple-element.40.turned_any, bf16[1152,128]{1,0:T(8,128)(2,1)S(1)} %get-tuple-element.41.member_any.member_ref, s32[3,7]{1,0:T(4,128)S(1)} %copy-done.6, bf16[16,4096]{1,0:T(8,128)(2,1)S(1)} %copy-done.4), custom_call_target="tpu_custom_call" | custom-call | flops 339738624 | bytes 2359296 | tf_op jit(solution)/shard_map/statistics/pallas_call | solution.py:587
  25.6 3.0 %collective-permute-start.7 = (bf16[1152,256]{1,0:T(8,128)(2,1)}, bf16[1152,256]{1,0:T(8,128)(2,1)S(1)}, u32[]{:S(2)}, u32[]{:S(2)}) collective-permute-start(bf16[1152,256]{1,0:T(8,128)(2,1)} %add_convert_fusion.1), channel_id=1, source_target_pairs={{0,8},{4,12},{8,0},{12,4},{1,9},{5,13},{9,1},{13,5},{2,10},{6,14},... | collective-permute-start | bytes 1769480 | tf_op jit(solution)/shard_map/ppermute | solution.py:585
  28.6 1.6 %convolution_convert_fusion.5.own_ref = bf16[1152,256]{1,0:T(8,128)(2,1)} fusion(bf16[1024,1152]{1,0:T(8,128)(2,1)S(1)} %get-tuple-element.40.turned_any, bf16[1024,1024]{1,0:T(8,128)(2,1)S(1)} %copy-done.7, s32[]{:T(128)S(6)} %select_n.38), kind=kOutput, calls=%fused_computation.19 | convolution fusion | flops 604274688 | bytes 3473412 | tf_op jit(solution)/shard_map/dot_general | solution.py:128
  30.3 1.7 %convolution_convert_fusion.4 = bf16[1152,256]{1,0:T(8,128)(2,1)} fusion(bf16[1024,1152]{1,0:T(8,128)(2,1)S(1)} %get-tuple-element.40.turned_any, bf16[1024,1024]{1,0:T(8,128)(2,1)S(1)} %copy-done.7, s32[]{:T(128)S(6)} %select_n.39), kind=kOutput, calls=%fused_computation.18 | convolution fusion | flops 604274688 | bytes 3473412 | tf_op jit(solution)/shard_map/dot_general | solution.py:128
  33.3 1.5 %conditional.1 = (bf16[384,256]{1,0:T(8,128)(2,1)S(1)}, bf16[384,256]{1,0:T(8,128)(2,1)}, bf16[384,256]{1,0:T(8,128)(2,1)}, f32[64,256]{1,0:T(8,128)S(1)}, bf16[384,128]{1,0:T(8,128)(2,1)S(1)}) conditional(s32[]{:T(128)} %convert_element_type.79, () %tuple.22, (s32[12,128]{1,0:T(8,128)S(1)}, bf16[1024,16384]{1,0:T(8,128)(2,1)}, ...), branch_computations={%region_1.0_spmd, %region_2.0_spmd} | conditional | flops 919543808 | bytes 12329708 | solution.py:624
  33.3 0.7 %broadcast.8.clone.1 = bf16[384,256]{1,0:T(8,128)(2,1)} broadcast(bf16[]{:T(256)} %constant.15.clone), dimensions={} | broadcast | bytes 196610 | tf_op jit(solution)/shard_map/broadcast.5
  34.9 0.9 %convert_element_type.76 = f32[160,256]{1,0:T(8,128)S(1)} convert(bf16[160,256]{1,0:T(8,128)(2,1)} %collective-permute-done.8) | non-fusion elementwise | flops 40960 | bytes 245760 | tf_op jit(solution)/shard_map/convert_element_type | solution.py:609
  35.9 7.7 %collective-permute-done.9 = bf16[112,256]{1,0:T(8,128)(2,1)S(1)} collective-permute-done((bf16[112,256]{1,0:T(8,128)(2,1)S(1)}, bf16[112,256]{1,0:T(8,128)(2,1)S(1)}, u32[]{:S(2)}, u32[]{:S(2)}) %collective-permute-start.9) | collective-permute-done | bytes 57376 | tf_op jit(solution)/shard_map/ppermute | solution.py:613
  43.7 3.1 %pool.1 = (bf16[208,256]{1,0:T(8,128)(2,1)S(1)}, f32[16,256]{1,0:T(8,128)S(1)}) custom-call(s32[12,128]{1,0:T(8,128)S(1)} %bitcast.14, bf16[1152,256]{1,0:T(8,128)(2,1)S(1)} %copy-done, bf16[1152,256]{1,0:T(8,128)(2,1)S(1)} %collective-permute-done.6.core_any, bf16[1152,256]{1,0:T(8,128)(2,1)S(1)} %collective-permute-done.7.far_any, ...), custom_call_target="tpu_custom_call" | custom-call | tf_op jit(solution)/shard_map/pool/pallas_call | solution.py:629
  46.8 1.8 %collective-permute-start.10 = (bf16[208,256]{1,0:T(8,128)(2,1)S(1)}, bf16[208,256]{1,0:T(8,128)(2,1)S(1)}, u32[]{:S(2)}, u32[]{:S(2)}) collective-permute-start(bf16[208,256]{1,0:T(8,128)(2,1)S(1)} %get-tuple-element.48.near_ref), channel_id=1, source_target_pairs={{0,16},{16,0},{1,17},{17,1},{2,18},{18,2},{3,19},{19,3},{4,20},{20... | collective-permute-start | bytes 319496 | tf_op jit(solution)/shard_map/ppermute | solution.py:648
  48.5 3.0 %collective-permute-done.10.far_ref = bf16[208,256]{1,0:T(8,128)(2,1)S(1)} collective-permute-done((bf16[208,256]{1,0:T(8,128)(2,1)S(1)}, bf16[208,256]{1,0:T(8,128)(2,1)S(1)}, u32[]{:S(2)}, u32[]{:S(2)}) %collective-permute-start.10) | collective-permute-done | bytes 106528 | tf_op jit(solution)/shard_map/ppermute | solution.py:648
  51.7 1.8 %collective-permute-start.12 = (f32[96,128]{1,0:T(8,128)S(1)}, f32[96,128]{1,0:T(8,128)S(1)}, u32[]{:S(2)}, u32[]{:S(2)}) collective-permute-start(f32[96,128]{1,0:T(8,128)S(1)} %get-tuple-element.49.refs_0_), channel_id=1, source_target_pairs={{0,8},{4,12},{8,0},{12,4},{1,9},{5,13},{9,1},{13,5},{2,10},{6,14},... | collective-permute-start | bytes 147464 | tf_op jit(solution)/shard_map/ppermute | solution.py:518
  53.6 1.9 %collective-permute-done.13.refs_3_ = f32[96,128]{1,0:T(8,128)S(1)} collective-permute-done((f32[96,128]{1,0:T(8,128)S(1)}, f32[96,128]{1,0:T(8,128)S(1)}, u32[]{:S(2)}, u32[]{:S(2)}) %collective-permute-start.13) | collective-permute-done | bytes 49184 | tf_op jit(solution)/shard_map/ppermute | solution.py:518
  55.4 0.9 %collective-permute-done.12.refs_2_ = f32[96,128]{1,0:T(8,128)S(1)} collective-permute-done((f32[96,128]{1,0:T(8,128)S(1)}, f32[96,128]{1,0:T(8,128)S(1)}, u32[]{:S(2)}, u32[]{:S(2)}) %collective-permute-start.12) | collective-permute-done | bytes 49184 | tf_op jit(solution)/shard_map/ppermute | solution.py:518
  56.4 1.7 %collective-permute-start.14 = (bf16[384,256]{1,0:T(8,128)(2,1)S(1)}, bf16[384,256]{1,0:T(8,128)(2,1)S(1)}, u32[]{:S(2)}, u32[]{:S(2)}) collective-permute-start(bf16[384,256]{1,0:T(8,128)(2,1)S(1)} %get-tuple-element.51.refs_4_), channel_id=1, source_target_pairs={{0,8},{4,12},{8,0},{12,4},{1,9},{5,13},{9,1},{13,5},{2,10},{6,14},... | collective-permute-start | bytes 589832 | tf_op jit(solution)/shard_map/ppermute | solution.py:666
  58.1 3.6 %collective-permute-start.17 = (f32[32,128]{1,0:T(8,128)S(1)}, f32[32,128]{1,0:T(8,128)S(1)}, u32[]{:S(2)}, u32[]{:S(2)}) collective-permute-start(f32[32,128]{1,0:T(8,128)S(1)} %fusion.12.refs_6_), channel_id=1, source_target_pairs={{0,3},{1,2},{2,1},{3,0},{4,7},{5,6},{6,5},{7,4},{8,11},{9,10},{10,... | collective-permute-start | bytes 49160 | tf_op jit(solution)/shard_map/ppermute | solution.py:518
  61.7 0.8 %collective-permute-start.15 = (f32[32,128]{1,0:T(8,128)S(1)}, f32[32,128]{1,0:T(8,128)S(1)}, u32[]{:S(2)}, u32[]{:S(2)}) collective-permute-start(f32[32,128]{1,0:T(8,128)S(1)} %fusion.12.refs_6_), channel_id=1, source_target_pairs={{0,1},{1,0},{2,3},{3,2},{4,5},{5,4},{6,7},{7,6},{8,9},{9,8},{10,11... | collective-permute-start | bytes 49160 | tf_op jit(solution)/shard_map/ppermute | solution.py:518
  63.6 2.7 %collective-permute-done.16.refs_8_ = f32[32,128]{1,0:T(8,128)S(1)} collective-permute-done((f32[32,128]{1,0:T(8,128)S(1)}, f32[32,128]{1,0:T(8,128)S(1)}, u32[]{:S(2)}, u32[]{:S(2)}) %collective-permute-start.16) | collective-permute-done | bytes 16416 | tf_op jit(solution)/shard_map/ppermute | solution.py:518
  66.3 1.0 %score.1 = (bf16[1,3,1024]{2,1,0:T(4,128)(2,1)}, f32[1,3]{1,0:T(1,128)}, f32[16,512]{1,0:T(8,128)S(1)}) custom-call(f32[96,128]{1,0:T(8,128)S(1)} %get-tuple-element.49.refs_0_, f32[96,128]{1,0:T(8,128)S(1)} %collective-permute-done.11.refs_1_, f32[96,128]{1,0:T(8,128)S(1)} %collective-permute-done.12.refs_2_, ...), custom_call_target="tpu_custom_call" | custom-call | tf_op jit(solution)/shard_map/score/pallas_call | solution.py:667
  67.3 1.2 %collective-permute-done.18 = f32[16,512]{1,0:T(8,128)S(1)} collective-permute-done((f32[16,512]{1,0:T(8,128)S(1)}, f32[16,512]{1,0:T(8,128)S(1)}, u32[]{:S(2)}, u32[]{:S(2)}) %collective-permute-start.18) | collective-permute-done | bytes 32800 | tf_op jit(solution)/shard_map/ppermute | solution.py:681
  (43 shorter events, 4.3 us)
Async XLA Ops:
  18.7 3.2 %collective-permute-start.5 = (bf16[1152,256]{1,0:T(8,128)(2,1)}, bf16[1152,256]{1,0:T(8,128)(2,1)S(1)}, u32[]{:S(2)}, u32[]{:S(2)}) collective-permute-start(bf16[1152,256]{1,0:T(8,128)(2,1)} %convolution_convert_fusion.6), channel_id=1, source_target_pairs={{0,4},{4,0},{8,12},{12,8},{1,5},{5,1},{9,13},{13,9},{2,6},{6,2},{1... | collective-permute-start | bytes 1769480 | tf_op jit(solution)/shard_map/ppermute | solution.py:582
  19.2 4.9 %copy-start.4 = (bf16[16,4096]{1,0:T(8,128)(2,1)S(1)}, bf16[16,4096]{1,0:T(8,128)(2,1)}, u32[]{:S(2)}) copy-start(bf16[16,4096]{1,0:T(8,128)(2,1)} %lower_ref.1) | copy-start | bytes 393220
  19.2 4.9 %copy-start.6 = (s32[3,7]{1,0:T(4,128)S(1)}, s32[3,7]{1,0:T(4,128)}, u32[]{:S(2)}) copy-start(s32[3,7]{1,0:T(4,128)} %hard_ref.1) | copy-start | bytes 256
  21.9 6.8 %copy-start.7 = (bf16[1024,1024]{1,0:T(8,128)(2,1)S(1)}, bf16[1024,1024]{1,0:T(8,128)(2,1)}, u32[]{:S(2)}) copy-start(bf16[1024,1024]{1,0:T(8,128)(2,1)} %param.12) | copy-start | bytes 6291460
  25.5 9.4 %collective-permute-start.8 = (bf16[160,256]{1,0:T(8,128)(2,1)S(1)}, bf16[160,256]{1,0:T(8,128)(2,1)}, u32[]{:S(2)}, u32[]{:S(2)}) collective-permute-start(bf16[160,256]{1,0:T(8,128)(2,1)S(1)} %statistics.3), channel_id=1, source_target_pairs={{0,4},{4,0},{8,12},{12,8},{1,5},{5,1},{9,13},{13,9},{2,6},{6,2},{1... | collective-permute-start | bytes 245768 | tf_op jit(solution)/shard_map/ppermute | solution.py:609
  25.6 18.0 %collective-permute-start.7 = (bf16[1152,256]{1,0:T(8,128)(2,1)}, bf16[1152,256]{1,0:T(8,128)(2,1)S(1)}, u32[]{:S(2)}, u32[]{:S(2)}) collective-permute-start(bf16[1152,256]{1,0:T(8,128)(2,1)} %add_convert_fusion.1), channel_id=1, source_target_pairs={{0,8},{4,12},{8,0},{12,4},{1,9},{5,13},{9,1},{13,5},{2,10},{6,14},... | collective-permute-start | bytes 1769480 | tf_op jit(solution)/shard_map/ppermute | solution.py:585
  33.3 10.4 %copy-start = (bf16[1152,256]{1,0:T(8,128)(2,1)S(1)}, bf16[1152,256]{1,0:T(8,128)(2,1)}, u32[]{:S(2)}) copy-start(bf16[1152,256]{1,0:T(8,128)(2,1)} %convolution_convert_fusion.5.own_ref) | copy-start | bytes 1769476
  33.3 10.4 %copy-start.1 = (bf16[16,1024]{1,0:T(8,128)(2,1)S(1)}, bf16[16,1024]{1,0:T(8,128)(2,1)}, u32[]{:S(2)}) copy-start(bf16[16,1024]{1,0:T(8,128)(2,1)} %raise_ref.1) | copy-start | bytes 98308
  34.8 8.8 %collective-permute-start.6 = (bf16[1152,256]{1,0:T(8,128)(2,1)}, bf16[1152,256]{1,0:T(8,128)(2,1)S(1)}, u32[]{:S(2)}, u32[]{:S(2)}) collective-permute-start(bf16[1152,256]{1,0:T(8,128)(2,1)} %convolution_convert_fusion.4), channel_id=1, source_target_pairs={{0,4},{4,0},{8,12},{12,8},{1,5},{5,1},{9,13},{13,9},{2,6},{6,2},{1... | collective-permute-start | bytes 1769480 | tf_op jit(solution)/shard_map/ppermute | solution.py:615
  35.8 7.8 %collective-permute-start.9 = (bf16[112,256]{1,0:T(8,128)(2,1)S(1)}, bf16[112,256]{1,0:T(8,128)(2,1)S(1)}, u32[]{:S(2)}, u32[]{:S(2)}) collective-permute-start(bf16[112,256]{1,0:T(8,128)(2,1)S(1)} %pad_maximum_fusion.2), channel_id=1, source_target_pairs={{0,8},{4,12},{8,0},{12,4},{1,9},{5,13},{9,1},{13,5},{2,10},{6,14},... | collective-permute-start | bytes 172040 | tf_op jit(solution)/shard_map/ppermute | solution.py:613
  46.8 4.8 %collective-permute-start.10 = (bf16[208,256]{1,0:T(8,128)(2,1)S(1)}, bf16[208,256]{1,0:T(8,128)(2,1)S(1)}, u32[]{:S(2)}, u32[]{:S(2)}) collective-permute-start(bf16[208,256]{1,0:T(8,128)(2,1)S(1)} %get-tuple-element.48.near_ref), channel_id=1, source_target_pairs={{0,16},{16,0},{1,17},{17,1},{2,18},{18,2},{3,19},{19,3},{4,20},{20... | collective-permute-start | bytes 319496 | tf_op jit(solution)/shard_map/ppermute | solution.py:648
  51.7 3.8 %collective-permute-start.13 = (f32[96,128]{1,0:T(8,128)S(1)}, f32[96,128]{1,0:T(8,128)S(1)}, u32[]{:S(2)}, u32[]{:S(2)}) collective-permute-start(f32[96,128]{1,0:T(8,128)S(1)} %get-tuple-element.49.refs_0_), channel_id=1, source_target_pairs={{0,12},{4,8},{8,4},{12,0},{1,13},{5,9},{9,5},{13,1},{2,14},{6,10},... | collective-permute-start | bytes 147464 | tf_op jit(solution)/shard_map/ppermute | solution.py:518
  51.7 4.7 %collective-permute-start.12 = (f32[96,128]{1,0:T(8,128)S(1)}, f32[96,128]{1,0:T(8,128)S(1)}, u32[]{:S(2)}, u32[]{:S(2)}) collective-permute-start(f32[96,128]{1,0:T(8,128)S(1)} %get-tuple-element.49.refs_0_), channel_id=1, source_target_pairs={{0,8},{4,12},{8,0},{12,4},{1,9},{5,13},{9,1},{13,5},{2,10},{6,14},... | collective-permute-start | bytes 147464 | tf_op jit(solution)/shard_map/ppermute | solution.py:518
  53.5 2.9 %collective-permute-start.11 = (f32[96,128]{1,0:T(8,128)S(1)}, f32[96,128]{1,0:T(8,128)S(1)}, u32[]{:S(2)}, u32[]{:S(2)}) collective-permute-start(f32[96,128]{1,0:T(8,128)S(1)} %get-tuple-element.49.refs_0_), channel_id=1, source_target_pairs={{0,4},{4,0},{8,12},{12,8},{1,5},{5,1},{9,13},{13,9},{2,6},{6,2},{1... | collective-permute-start | bytes 147464 | tf_op jit(solution)/shard_map/ppermute | solution.py:518
  56.4 10.0 %collective-permute-start.14 = (bf16[384,256]{1,0:T(8,128)(2,1)S(1)}, bf16[384,256]{1,0:T(8,128)(2,1)S(1)}, u32[]{:S(2)}, u32[]{:S(2)}) collective-permute-start(bf16[384,256]{1,0:T(8,128)(2,1)S(1)} %get-tuple-element.51.refs_4_), channel_id=1, source_target_pairs={{0,8},{4,12},{8,0},{12,4},{1,9},{5,13},{9,1},{13,5},{2,10},{6,14},... | collective-permute-start | bytes 589832 | tf_op jit(solution)/shard_map/ppermute | solution.py:666
  58.1 5.5 %collective-permute-start.17 = (f32[32,128]{1,0:T(8,128)S(1)}, f32[32,128]{1,0:T(8,128)S(1)}, u32[]{:S(2)}, u32[]{:S(2)}) collective-permute-start(f32[32,128]{1,0:T(8,128)S(1)} %fusion.12.refs_6_), channel_id=1, source_target_pairs={{0,3},{1,2},{2,1},{3,0},{4,7},{5,6},{6,5},{7,4},{8,11},{9,10},{10,... | collective-permute-start | bytes 49160 | tf_op jit(solution)/shard_map/ppermute | solution.py:518
  61.7 4.6 %collective-permute-start.16 = (f32[32,128]{1,0:T(8,128)S(1)}, f32[32,128]{1,0:T(8,128)S(1)}, u32[]{:S(2)}, u32[]{:S(2)}) collective-permute-start(f32[32,128]{1,0:T(8,128)S(1)} %fusion.12.refs_6_), channel_id=1, source_target_pairs={{0,2},{1,3},{2,0},{3,1},{4,6},{5,7},{6,4},{7,5},{8,10},{9,11},{10,... | collective-permute-start | bytes 49160 | tf_op jit(solution)/shard_map/ppermute | solution.py:518
  61.7 4.6 %collective-permute-start.15 = (f32[32,128]{1,0:T(8,128)S(1)}, f32[32,128]{1,0:T(8,128)S(1)}, u32[]{:S(2)}, u32[]{:S(2)}) collective-permute-start(f32[32,128]{1,0:T(8,128)S(1)} %fusion.12.refs_6_), channel_id=1, source_target_pairs={{0,1},{1,0},{2,3},{3,2},{4,5},{5,4},{6,7},{7,6},{8,9},{9,8},{10,11... | collective-permute-start | bytes 49160 | tf_op jit(solution)/shard_map/ppermute | solution.py:518
  67.3 1.2 %collective-permute-start.18 = (f32[16,512]{1,0:T(8,128)S(1)}, f32[16,512]{1,0:T(8,128)S(1)}, u32[]{:S(2)}, u32[]{:S(2)}) collective-permute-start(f32[16,512]{1,0:T(8,128)S(1)} %get-tuple-element.56), channel_id=1, source_target_pairs={{0,4},{4,0},{8,12},{12,8},{1,5},{5,1},{9,13},{13,9},{2,6},{6,2},{1... | collective-permute-start | bytes 98312 | tf_op jit(solution)/shard_map/ppermute | solution.py:681

commit v15 on v14

--- a/solution.py
+++ b/solution.py
@@ -170,8 +170,10 @@
 def gather_kernel(
     ids_ref,
     vocab_ref,
+    weight_ref,
     turned_any,
     member_any,
+    weight_any,
     turned,
     member_ref,
     held,
@@ -182,6 +184,7 @@
     held_sems,
     bounds_sem,
     out_sems,
+    weight_sem,
     base,
 ):
     texts, length = ids_ref.shape
@@ -194,7 +197,9 @@
         columns = pl.ds(pl.multiple_of(b * IDS_PER_BLOCK, LANES), IDS_PER_BLOCK)
         return pltpu.make_async_copy(vocab_ref.at[:, columns], held.at[b], held_sems.at[b])
 
+    weight_copy = pltpu.make_async_copy(weight_ref, weight_any, weight_sem)
     vocab_copy(0).start()
+    weight_copy.start()
     for b in range(1, blocks):
         vocab_copy(b).start()
 
@@ -285,6 +290,7 @@
 
     lax.fori_loop(0, blocks, take, 0)
     fetch([(turned, turned_any), (member_ref, member_any)], out_sems)
+    weight_copy.wait()
 
 
 def statistics_kernel(
@@ -542,21 +548,21 @@
     other_core = [(d, d ^ 1) for d in range(shards)]
     other_y = [(d, d ^ 2) for d in range(shards)]
 
-    def columns(i, j):
-        start = split_quarter(i, j) * width
-        return lax.dynamic_slice(layer_weight_matrix, (0, start), (features, width))
+    def columns(weight, i, j):
+        return lax.dynamic_slice(weight, (0, split_quarter(i, j) * width), (features, width))
 
     def project(base, span):
         stripes = pl.cdiv(span, STRIPE)
         extra_rows = (stripes + 1 + shards) * ROWS
-        turned, member = pl.pallas_call(
+        turned, member, weight = pl.pallas_call(
             functools.partial(gather_kernel, base=base),
             out_shape=[
                 jax.ShapeDtypeStruct((features, span), jnp.bfloat16),
                 jax.ShapeDtypeStruct((span, LANES), jnp.bfloat16),
+                jax.ShapeDtypeStruct(layer_weight_matrix.shape, jnp.bfloat16),
             ],
-            in_specs=[vmem_spec(), any_spec()],
-            out_specs=[any_spec()] * 2,
+            in_specs=[vmem_spec()] + [any_spec()] * 2,
+            out_specs=[any_spec()] * 3,
             scratch_shapes=[
                 pltpu.VMEM((features, span), jnp.bfloat16),
                 pltpu.VMEM((span, LANES), jnp.bfloat16),
@@ -568,13 +574,14 @@
                 pltpu.SemaphoreType.DMA((blocks,)),
                 pltpu.SemaphoreType.DMA,
                 pltpu.SemaphoreType.DMA((2,)),
+                pltpu.SemaphoreType.DMA,
             ],
             compiler_params=params,
             name="gather",
-        )(ids, vocabulary_vectors)
+        )(ids, vocabulary_vectors, layer_weight_matrix)
 
         def product(turned, i, j):
-            return mm(turned, columns(i, j), (((0,), (0,)), ((), ())))
+            return mm(turned, columns(weight, i, j), (((0,), (0,)), ((), ())))
 
         def narrow(x):
             return x.astype(jnp.bfloat16)

time: 69.5 us -> 70 us (level)
  local copies, waits for them, and re-layouts: 2.15 us -> 3.48 us
  matrix products: 8.75 us -> 7.72 us
    ppermute x6, waiting for transfers between devices: 5.98 us -> 8.14 us  [exchange(): return [x] + [lax.ppermute(x, axis, step) for step in steps]]
    ppermute x1, waiting for transfers between devices: 7.68 us -> 6.18 us  [project(): sent = lax.ppermute(sent, 'dp', other_y).astype(jnp.float32)]
    unnamed x11 -> x13, local copies, waits for them, and re-layouts: 0.72 us -> 2.05 us
    dot_general x4, matrix products: 8.75 us -> 7.72 us  [mm(): return lax.dot_general(a, b, dims, preferred_element_type=jnp.float32)]
  transfers between devices with their start and end apart: 14 -> 14, of which waited for: 7 -> 7; matrix products, arithmetic and copies ran while one was open for 13% -> 13% of each run, Pallas kernels for 0% -> 2%
where the time goes in v15:
time: 70 us; the launch traced here: 69.6 us
  Pallas kernels  20.3 us (29%)
  waiting for transfers between devices  18.4 us (26%)
  starting transfers between devices  13.1 us (19%)
  matrix products  7.72 us (11%)
  other arithmetic  4.41 us (6%)
  local copies, waits for them, and re-layouts  3.48 us (5%)
  between operations  2.11 us (3%)
    pallas_call x1, Pallas kernels, project(): pl.pallas_call(functools.partial(gather_kernel, base=base), out_shape=[ja...  14.7 us
    ppermute x6, waiting for transfers between devices, exchange(): return [x] + [lax.ppermute(x, axis, step) for step in steps]  8.14 us
    dot_general x4, matrix products, mm(): return lax.dot_general(a, b, dims, preferred_element_type=jnp.float32)  7.72 us
    ppermute x6, starting transfers between devices, exchange(): return [x] + [lax.ppermute(x, axis, step) for step in steps]  6.25 us
    ppermute x1, waiting for transfers between devices, project(): sent = lax.ppermute(sent, 'dp', other_y).astype(jnp.float32)  6.18 us
    pallas_call x1, Pallas kernels, split_body(): pl.pallas_call(functools.partial(pool_kernel, model_width=float(features...  3.1 us
    ppermute x1, waiting for transfers between devices, split_body(): far_side = lax.ppermute(sent, 'group', [(0, 1), (1, 0)])  2.85 us
    ppermute x1, starting transfers between devices, project(): far = lax.ppermute(chip1, 'dp', other_y)  2.52 us
  transfers between devices with their start and end apart: 14, of which 7 were waited for; matrix products, arithmetic and copies ran while one was open for 13% of the time, Pallas kernels for 2%

profile of v15, /device:TPU:0, one launch (start us, length us, event | category | flops | bytes accessed | tf_op | source)
XLA Modules:
  0.0 69.6 jit_solution(3553880917096752285)
XLA Ops:
  1.3 14.7 %gather.3 = (bf16[1024,1152]{1,0:T(8,128)(2,1)S(1)}, bf16[1152,128]{1,0:T(8,128)(2,1)S(1)}, bf16[1024,1024]{1,0:T(8,128)(2,1)S(1)}) custom-call(s32[12,128]{1,0:T(8,128)S(1)} %bitcast.11, bf16[1024,16384]{1,0:T(8,128)(2,1)} %vocab_ref.1, bf16[1024,1024]{1,0:T(8,128)(2,1)} %weight_ref.1), custom_call_target="tpu_custom_call" | custom-call | tf_op jit(solution)/shard_map/gather/pallas_call | solution.py:557
  16.0 1.3 %copy-done.2 = bf16[1024,1024]{1,0:T(8,128)(2,1)} copy-done((bf16[1024,1024]{1,0:T(8,128)(2,1)}, bf16[1024,1024]{1,0:T(8,128)(2,1)S(1)}, u32[]{:S(2)}) %copy-start.2) | copy-done | bytes 2097176
  17.4 1.7 %convolution_convert_fusion.6 = bf16[1152,256]{1,0:T(8,128)(2,1)} fusion(bf16[1024,1152]{1,0:T(8,128)(2,1)S(1)} %get-tuple-element.43.turned_any, bf16[1024,1024]{1,0:T(8,128)(2,1)S(1)} %get-tuple-element.42, s32[]{:T(128)S(6)} %select_n.37), kind=kOutput, calls=%fused_computation.20 | convolution fusion | flops 604274688 | bytes 3473412 | tf_op jit(solution)/shard_map/dot_general | solution.py:128
  19.5 2.7 %convolution_convert_fusion.7 = bf16[1152,256]{1,0:T(8,128)(2,1)} fusion(bf16[1024,1152]{1,0:T(8,128)(2,1)S(1)} %get-tuple-element.43.turned_any, bf16[1024,1024]{1,0:T(8,128)(2,1)} %copy-done.2, s32[]{:T(128)S(6)} %select_n.36), kind=kOutput, calls=%fused_computation.21 | convolution fusion | flops 604274688 | bytes 3473412 | tf_op jit(solution)/shard_map/dot_general | solution.py:128
  22.2 2.2 %add_convert_fusion.1 = bf16[1152,256]{1,0:T(8,128)(2,1)} fusion(bf16[1152,256]{1,0:T(8,128)(2,1)S(1)} %collective-permute-done.5, bf16[1152,256]{1,0:T(8,128)(2,1)} %convolution_convert_fusion.7), kind=kLoop, calls=%fused_computation.22 | loop fusion | flops 1179648 | bytes 1769472 | tf_op jit(solution)/shard_map/convert_element_type | solution.py:587
  24.4 2.5 %collective-permute-start.7 = (bf16[1152,256]{1,0:T(8,128)(2,1)}, bf16[1152,256]{1,0:T(8,128)(2,1)S(1)}, u32[]{:S(2)}, u32[]{:S(2)}) collective-permute-start(bf16[1152,256]{1,0:T(8,128)(2,1)} %add_convert_fusion.1), channel_id=1, source_target_pairs={{0,8},{4,12},{8,0},{12,4},{1,9},{5,13},{9,1},{13,5},{2,10},{6,14},... | collective-permute-start | bytes 1769480 | tf_op jit(solution)/shard_map/ppermute | solution.py:592
  26.9 1.4 %statistics.3 = bf16[160,256]{1,0:T(8,128)(2,1)S(1)} custom-call(bf16[1024,1152]{1,0:T(8,128)(2,1)S(1)} %get-tuple-element.43.turned_any, bf16[1152,128]{1,0:T(8,128)(2,1)S(1)} %get-tuple-element.44.member_any.member_ref, s32[3,7]{1,0:T(4,128)S(1)} %copy-done.8, bf16[16,4096]{1,0:T(8,128)(2,1)S(1)} %copy-done.6), custom_call_target="tpu_custom_call" | custom-call | flops 339738624 | bytes 2359296 | tf_op jit(solution)/shard_map/statistics/pallas_call | solution.py:594
  28.6 1.7 %convolution_convert_fusion.5.own_ref = bf16[1152,256]{1,0:T(8,128)(2,1)} fusion(bf16[1024,1152]{1,0:T(8,128)(2,1)S(1)} %get-tuple-element.43.turned_any, bf16[1024,1024]{1,0:T(8,128)(2,1)S(1)} %copy-done.3, s32[]{:T(128)S(6)} %select_n.38), kind=kOutput, calls=%fused_computation.19 | convolution fusion | flops 604274688 | bytes 3473412 | tf_op jit(solution)/shard_map/dot_general | solution.py:128
  30.3 1.7 %convolution_convert_fusion.4 = bf16[1152,256]{1,0:T(8,128)(2,1)} fusion(bf16[1024,1152]{1,0:T(8,128)(2,1)S(1)} %get-tuple-element.43.turned_any, bf16[1024,1024]{1,0:T(8,128)(2,1)S(1)} %copy-done.3, s32[]{:T(128)S(6)} %select_n.39), kind=kOutput, calls=%fused_computation.18 | convolution fusion | flops 604274688 | bytes 3473412 | tf_op jit(solution)/shard_map/dot_general | solution.py:128
  33.3 1.4 %conditional.1 = (bf16[384,256]{1,0:T(8,128)(2,1)S(1)}, bf16[384,256]{1,0:T(8,128)(2,1)}, bf16[384,256]{1,0:T(8,128)(2,1)}, f32[64,256]{1,0:T(8,128)S(1)}, bf16[384,128]{1,0:T(8,128)(2,1)S(1)}) conditional(s32[]{:T(128)} %convert_element_type.79, () %tuple.22, (s32[12,128]{1,0:T(8,128)S(1)}, bf16[1024,16384]{1,0:T(8,128)(2,1)}, ...), branch_computations={%region_1.0_spmd, %region_2.0_spmd} | conditional | flops 919543808 | bytes 12329708 | solution.py:631
  36.2 6.2 %collective-permute-done.9 = bf16[112,256]{1,0:T(8,128)(2,1)S(1)} collective-permute-done((bf16[112,256]{1,0:T(8,128)(2,1)S(1)}, bf16[112,256]{1,0:T(8,128)(2,1)S(1)}, u32[]{:S(2)}, u32[]{:S(2)}) %collective-permute-start.9) | collective-permute-done | bytes 57376 | tf_op jit(solution)/shard_map/ppermute | solution.py:620
  42.4 3.1 %pool.1 = (bf16[208,256]{1,0:T(8,128)(2,1)S(1)}, f32[16,256]{1,0:T(8,128)S(1)}) custom-call(s32[12,128]{1,0:T(8,128)S(1)} %bitcast.14, bf16[1152,256]{1,0:T(8,128)(2,1)S(1)} %copy-done, bf16[1152,256]{1,0:T(8,128)(2,1)S(1)} %collective-permute-done.6.core_any, bf16[1152,256]{1,0:T(8,128)(2,1)S(1)} %collective-permute-done.7.far_any, ...), custom_call_target="tpu_custom_call" | custom-call | tf_op jit(solution)/shard_map/pool/pallas_call | solution.py:636
  45.5 2.1 %collective-permute-start.10 = (bf16[208,256]{1,0:T(8,128)(2,1)S(1)}, bf16[208,256]{1,0:T(8,128)(2,1)S(1)}, u32[]{:S(2)}, u32[]{:S(2)}) collective-permute-start(bf16[208,256]{1,0:T(8,128)(2,1)S(1)} %get-tuple-element.51.near_ref), channel_id=1, source_target_pairs={{0,16},{16,0},{1,17},{17,1},{2,18},{18,2},{3,19},{19,3},{4,20},{20... | collective-permute-start | bytes 319496 | tf_op jit(solution)/shard_map/ppermute | solution.py:655
  47.6 2.9 %collective-permute-done.10.far_ref = bf16[208,256]{1,0:T(8,128)(2,1)S(1)} collective-permute-done((bf16[208,256]{1,0:T(8,128)(2,1)S(1)}, bf16[208,256]{1,0:T(8,128)(2,1)S(1)}, u32[]{:S(2)}, u32[]{:S(2)}) %collective-permute-start.10) | collective-permute-done | bytes 106528 | tf_op jit(solution)/shard_map/ppermute | solution.py:655
  50.6 1.6 %collective-permute-start.12 = (f32[96,128]{1,0:T(8,128)S(1)}, f32[96,128]{1,0:T(8,128)S(1)}, u32[]{:S(2)}, u32[]{:S(2)}) collective-permute-start(f32[96,128]{1,0:T(8,128)S(1)} %get-tuple-element.52.refs_0_), channel_id=1, source_target_pairs={{0,8},{4,12},{8,0},{12,4},{1,9},{5,13},{9,1},{13,5},{2,10},{6,14},... | collective-permute-start | bytes 147464 | tf_op jit(solution)/shard_map/ppermute | solution.py:524
  52.4 2.3 %collective-permute-done.12.refs_2_ = f32[96,128]{1,0:T(8,128)S(1)} collective-permute-done((f32[96,128]{1,0:T(8,128)S(1)}, f32[96,128]{1,0:T(8,128)S(1)}, u32[]{:S(2)}, u32[]{:S(2)}) %collective-permute-start.12) | collective-permute-done | bytes 49184 | tf_op jit(solution)/shard_map/ppermute | solution.py:524
  54.7 1.2 %collective-permute-done.13.refs_3_ = f32[96,128]{1,0:T(8,128)S(1)} collective-permute-done((f32[96,128]{1,0:T(8,128)S(1)}, f32[96,128]{1,0:T(8,128)S(1)}, u32[]{:S(2)}, u32[]{:S(2)}) %collective-permute-start.13) | collective-permute-done | bytes 49184 | tf_op jit(solution)/shard_map/ppermute | solution.py:524
  55.9 1.1 %collective-permute-start.14 = (bf16[384,256]{1,0:T(8,128)(2,1)S(1)}, bf16[384,256]{1,0:T(8,128)(2,1)S(1)}, u32[]{:S(2)}, u32[]{:S(2)}) collective-permute-start(bf16[384,256]{1,0:T(8,128)(2,1)S(1)} %get-tuple-element.54.refs_4_), channel_id=1, source_target_pairs={{0,8},{4,12},{8,0},{12,4},{1,9},{5,13},{9,1},{13,5},{2,10},{6,14},... | collective-permute-start | bytes 589832 | tf_op jit(solution)/shard_map/ppermute | solution.py:673
  57.0 1.6 %collective-permute-start.15 = (f32[32,128]{1,0:T(8,128)S(1)}, f32[32,128]{1,0:T(8,128)S(1)}, u32[]{:S(2)}, u32[]{:S(2)}) collective-permute-start(f32[32,128]{1,0:T(8,128)S(1)} %fusion.12.refs_6_), channel_id=1, source_target_pairs={{0,1},{1,0},{2,3},{3,2},{4,5},{5,4},{6,7},{7,6},{8,9},{9,8},{10,11... | collective-permute-start | bytes 49160 | tf_op jit(solution)/shard_map/ppermute | solution.py:524
  58.6 2.6 %collective-permute-start.16 = (f32[32,128]{1,0:T(8,128)S(1)}, f32[32,128]{1,0:T(8,128)S(1)}, u32[]{:S(2)}, u32[]{:S(2)}) collective-permute-start(f32[32,128]{1,0:T(8,128)S(1)} %fusion.12.refs_6_), channel_id=1, source_target_pairs={{0,2},{1,3},{2,0},{3,1},{4,6},{5,7},{6,4},{7,5},{8,10},{9,11},{10,... | collective-permute-start | bytes 49160 | tf_op jit(solution)/shard_map/ppermute | solution.py:524
  62.1 1.4 %collective-permute-done.16.refs_8_ = f32[32,128]{1,0:T(8,128)S(1)} collective-permute-done((f32[32,128]{1,0:T(8,128)S(1)}, f32[32,128]{1,0:T(8,128)S(1)}, u32[]{:S(2)}, u32[]{:S(2)}) %collective-permute-start.16) | collective-permute-done | bytes 16416 | tf_op jit(solution)/shard_map/ppermute | solution.py:524
  63.5 3.3 %collective-permute-done.17.refs_9_ = f32[32,128]{1,0:T(8,128)S(1)} collective-permute-done((f32[32,128]{1,0:T(8,128)S(1)}, f32[32,128]{1,0:T(8,128)S(1)}, u32[]{:S(2)}, u32[]{:S(2)}) %collective-permute-start.17) | collective-permute-done | bytes 16416 | tf_op jit(solution)/shard_map/ppermute | solution.py:524
  66.7 1.0 %score.1 = (bf16[1,3,1024]{2,1,0:T(4,128)(2,1)}, f32[1,3]{1,0:T(1,128)}, f32[16,512]{1,0:T(8,128)S(1)}) custom-call(f32[96,128]{1,0:T(8,128)S(1)} %get-tuple-element.52.refs_0_, f32[96,128]{1,0:T(8,128)S(1)} %collective-permute-done.11.refs_1_, f32[96,128]{1,0:T(8,128)S(1)} %collective-permute-done.12.refs_2_, ...), custom_call_target="tpu_custom_call" | custom-call | tf_op jit(solution)/shard_map/score/pallas_call | solution.py:674
  67.7 1.2 %collective-permute-done.18 = f32[16,512]{1,0:T(8,128)S(1)} collective-permute-done((f32[16,512]{1,0:T(8,128)S(1)}, f32[16,512]{1,0:T(8,128)S(1)}, u32[]{:S(2)}, u32[]{:S(2)}) %collective-permute-start.18) | collective-permute-done | bytes 32800 | tf_op jit(solution)/shard_map/ppermute | solution.py:688
  (45 shorter events, 6.2 us)
Async XLA Ops:
  16.0 1.3 %copy-start.2 = (bf16[1024,1024]{1,0:T(8,128)(2,1)}, bf16[1024,1024]{1,0:T(8,128)(2,1)S(1)}, u32[]{:S(2)}) copy-start(bf16[1024,1024]{1,0:T(8,128)(2,1)S(1)} %get-tuple-element.42) | copy-start | bytes 6291460
  19.0 3.2 %collective-permute-start.5 = (bf16[1152,256]{1,0:T(8,128)(2,1)}, bf16[1152,256]{1,0:T(8,128)(2,1)S(1)}, u32[]{:S(2)}, u32[]{:S(2)}) collective-permute-start(bf16[1152,256]{1,0:T(8,128)(2,1)} %convolution_convert_fusion.6), channel_id=1, source_target_pairs={{0,4},{4,0},{8,12},{12,8},{1,5},{5,1},{9,13},{13,9},{2,6},{6,2},{1... | collective-permute-start | bytes 1769480 | tf_op jit(solution)/shard_map/ppermute | solution.py:589
  19.5 7.4 %copy-start.6 = (bf16[16,4096]{1,0:T(8,128)(2,1)S(1)}, bf16[16,4096]{1,0:T(8,128)(2,1)}, u32[]{:S(2)}) copy-start(bf16[16,4096]{1,0:T(8,128)(2,1)} %lower_ref.1) | copy-start | bytes 393220
  19.5 7.4 %copy-start.8 = (s32[3,7]{1,0:T(4,128)S(1)}, s32[3,7]{1,0:T(4,128)}, u32[]{:S(2)}) copy-start(s32[3,7]{1,0:T(4,128)} %hard_ref.1) | copy-start | bytes 256
  22.2 6.4 %copy-start.3 = (bf16[1024,1024]{1,0:T(8,128)(2,1)S(1)}, bf16[1024,1024]{1,0:T(8,128)(2,1)}, u32[]{:S(2)}) copy-start(bf16[1024,1024]{1,0:T(8,128)(2,1)} %copy-done.2) | copy-start | bytes 6291460
  24.4 18.0 %collective-permute-start.7 = (bf16[1152,256]{1,0:T(8,128)(2,1)}, bf16[1152,256]{1,0:T(8,128)(2,1)S(1)}, u32[]{:S(2)}, u32[]{:S(2)}) collective-permute-start(bf16[1152,256]{1,0:T(8,128)(2,1)} %add_convert_fusion.1), channel_id=1, source_target_pairs={{0,8},{4,12},{8,0},{12,4},{1,9},{5,13},{9,1},{13,5},{2,10},{6,14},... | collective-permute-start | bytes 1769480 | tf_op jit(solution)/shard_map/ppermute | solution.py:592
  28.3 6.8 %collective-permute-start.8 = (bf16[160,256]{1,0:T(8,128)(2,1)S(1)}, bf16[160,256]{1,0:T(8,128)(2,1)}, u32[]{:S(2)}, u32[]{:S(2)}) collective-permute-start(bf16[160,256]{1,0:T(8,128)(2,1)S(1)} %statistics.3), channel_id=1, source_target_pairs={{0,4},{4,0},{8,12},{12,8},{1,5},{5,1},{9,13},{13,9},{2,6},{6,2},{1... | collective-permute-start | bytes 245768 | tf_op jit(solution)/shard_map/ppermute | solution.py:616
  33.3 9.1 %copy-start = (bf16[1152,256]{1,0:T(8,128)(2,1)S(1)}, bf16[1152,256]{1,0:T(8,128)(2,1)}, u32[]{:S(2)}) copy-start(bf16[1152,256]{1,0:T(8,128)(2,1)} %convolution_convert_fusion.5.own_ref) | copy-start | bytes 1769476
  33.3 9.1 %copy-start.1 = (bf16[16,1024]{1,0:T(8,128)(2,1)S(1)}, bf16[16,1024]{1,0:T(8,128)(2,1)}, u32[]{:S(2)}) copy-start(bf16[16,1024]{1,0:T(8,128)(2,1)} %raise_ref.1) | copy-start | bytes 98308
  34.7 7.6 %collective-permute-start.6 = (bf16[1152,256]{1,0:T(8,128)(2,1)}, bf16[1152,256]{1,0:T(8,128)(2,1)S(1)}, u32[]{:S(2)}, u32[]{:S(2)}) collective-permute-start(bf16[1152,256]{1,0:T(8,128)(2,1)} %convolution_convert_fusion.4), channel_id=1, source_target_pairs={{0,4},{4,0},{8,12},{12,8},{1,5},{5,1},{9,13},{13,9},{2,6},{6,2},{1... | collective-permute-start | bytes 1769480 | tf_op jit(solution)/shard_map/ppermute | solution.py:622
  36.0 6.3 %collective-permute-start.9 = (bf16[112,256]{1,0:T(8,128)(2,1)S(1)}, bf16[112,256]{1,0:T(8,128)(2,1)S(1)}, u32[]{:S(2)}, u32[]{:S(2)}) collective-permute-start(bf16[112,256]{1,0:T(8,128)(2,1)S(1)} %pad_maximum_fusion.2), channel_id=1, source_target_pairs={{0,8},{4,12},{8,0},{12,4},{1,9},{5,13},{9,1},{13,5},{2,10},{6,14},... | collective-permute-start | bytes 172040 | tf_op jit(solution)/shard_map/ppermute | solution.py:620
  45.5 4.9 %collective-permute-start.10 = (bf16[208,256]{1,0:T(8,128)(2,1)S(1)}, bf16[208,256]{1,0:T(8,128)(2,1)S(1)}, u32[]{:S(2)}, u32[]{:S(2)}) collective-permute-start(bf16[208,256]{1,0:T(8,128)(2,1)S(1)} %get-tuple-element.51.near_ref), channel_id=1, source_target_pairs={{0,16},{16,0},{1,17},{17,1},{2,18},{18,2},{3,19},{19,3},{4,20},{20... | collective-permute-start | bytes 319496 | tf_op jit(solution)/shard_map/ppermute | solution.py:655
  50.6 1.9 %collective-permute-start.11 = (f32[96,128]{1,0:T(8,128)S(1)}, f32[96,128]{1,0:T(8,128)S(1)}, u32[]{:S(2)}, u32[]{:S(2)}) collective-permute-start(f32[96,128]{1,0:T(8,128)S(1)} %get-tuple-element.52.refs_0_), channel_id=1, source_target_pairs={{0,4},{4,0},{8,12},{12,8},{1,5},{5,1},{9,13},{13,9},{2,6},{6,2},{1... | collective-permute-start | bytes 147464 | tf_op jit(solution)/shard_map/ppermute | solution.py:524
  50.6 4.2 %collective-permute-start.12 = (f32[96,128]{1,0:T(8,128)S(1)}, f32[96,128]{1,0:T(8,128)S(1)}, u32[]{:S(2)}, u32[]{:S(2)}) collective-permute-start(f32[96,128]{1,0:T(8,128)S(1)} %get-tuple-element.52.refs_0_), channel_id=1, source_target_pairs={{0,8},{4,12},{8,0},{12,4},{1,9},{5,13},{9,1},{13,5},{2,10},{6,14},... | collective-permute-start | bytes 147464 | tf_op jit(solution)/shard_map/ppermute | solution.py:524
  52.2 3.7 %collective-permute-start.13 = (f32[96,128]{1,0:T(8,128)S(1)}, f32[96,128]{1,0:T(8,128)S(1)}, u32[]{:S(2)}, u32[]{:S(2)}) collective-permute-start(f32[96,128]{1,0:T(8,128)S(1)} %get-tuple-element.52.refs_0_), channel_id=1, source_target_pairs={{0,12},{4,8},{8,4},{12,0},{1,13},{5,9},{9,5},{13,1},{2,14},{6,10},... | collective-permute-start | bytes 147464 | tf_op jit(solution)/shard_map/ppermute | solution.py:524
  55.9 10.8 %collective-permute-start.14 = (bf16[384,256]{1,0:T(8,128)(2,1)S(1)}, bf16[384,256]{1,0:T(8,128)(2,1)S(1)}, u32[]{:S(2)}, u32[]{:S(2)}) collective-permute-start(bf16[384,256]{1,0:T(8,128)(2,1)S(1)} %get-tuple-element.54.refs_4_), channel_id=1, source_target_pairs={{0,8},{4,12},{8,0},{12,4},{1,9},{5,13},{9,1},{13,5},{2,10},{6,14},... | collective-permute-start | bytes 589832 | tf_op jit(solution)/shard_map/ppermute | solution.py:673
  57.0 5.0 %collective-permute-start.15 = (f32[32,128]{1,0:T(8,128)S(1)}, f32[32,128]{1,0:T(8,128)S(1)}, u32[]{:S(2)}, u32[]{:S(2)}) collective-permute-start(f32[32,128]{1,0:T(8,128)S(1)} %fusion.12.refs_6_), channel_id=1, source_target_pairs={{0,1},{1,0},{2,3},{3,2},{4,5},{5,4},{6,7},{7,6},{8,9},{9,8},{10,11... | collective-permute-start | bytes 49160 | tf_op jit(solution)/shard_map/ppermute | solution.py:524
  58.6 4.9 %collective-permute-start.16 = (f32[32,128]{1,0:T(8,128)S(1)}, f32[32,128]{1,0:T(8,128)S(1)}, u32[]{:S(2)}, u32[]{:S(2)}) collective-permute-start(f32[32,128]{1,0:T(8,128)S(1)} %fusion.12.refs_6_), channel_id=1, source_target_pairs={{0,2},{1,3},{2,0},{3,1},{4,6},{5,7},{6,4},{7,5},{8,10},{9,11},{10,... | collective-permute-start | bytes 49160 | tf_op jit(solution)/shard_map/ppermute | solution.py:524
  61.2 5.5 %collective-permute-start.17 = (f32[32,128]{1,0:T(8,128)S(1)}, f32[32,128]{1,0:T(8,128)S(1)}, u32[]{:S(2)}, u32[]{:S(2)}) collective-permute-start(f32[32,128]{1,0:T(8,128)S(1)} %fusion.12.refs_6_), channel_id=1, source_target_pairs={{0,3},{1,2},{2,1},{3,0},{4,7},{5,6},{6,5},{7,4},{8,11},{9,10},{10,... | collective-permute-start | bytes 49160 | tf_op jit(solution)/shard_map/ppermute | solution.py:524
  67.7 1.2 %collective-permute-start.18 = (f32[16,512]{1,0:T(8,128)S(1)}, f32[16,512]{1,0:T(8,128)S(1)}, u32[]{:S(2)}, u32[]{:S(2)}) collective-permute-start(f32[16,512]{1,0:T(8,128)S(1)} %get-tuple-element.59), channel_id=1, source_target_pairs={{0,4},{4,0},{8,12},{12,8},{1,5},{5,1},{9,13},{13,9},{2,6},{6,2},{1... | collective-permute-start | bytes 98312 | tf_op jit(solution)/shard_map/ppermute | solution.py:688

commit v16 on v14

--- a/solution.py
+++ b/solution.py
@@ -170,6 +170,7 @@
 def gather_kernel(
     ids_ref,
     vocab_ref,
+    after_any,
     turned_any,
     member_any,
     turned,
@@ -184,6 +185,7 @@
     out_sems,
     base,
 ):
+    del after_any
     texts, length = ids_ref.shape
     features, vocab = vocab_ref.shape
     blocks = vocab // IDS_PER_BLOCK
@@ -514,8 +516,8 @@
 
 
 def exchange(x, axis, size):
-    steps = [[(i, i ^ o) for i in range(size)] for o in range(1, size)]
-    return [x] + [lax.ppermute(x, axis, step) for step in steps]
+    steps = [[(i, i ^ o) for i in range(size)] for o in reversed(range(1, size))]
+    return [x] + [lax.ppermute(x, axis, step) for step in steps][::-1]
 
 
 def split_body(
@@ -546,7 +548,7 @@
         start = split_quarter(i, j) * width
         return lax.dynamic_slice(layer_weight_matrix, (0, start), (features, width))
 
-    def project(base, span):
+    def project(base, span, after):
         stripes = pl.cdiv(span, STRIPE)
         extra_rows = (stripes + 1 + shards) * ROWS
         turned, member = pl.pallas_call(
@@ -555,7 +557,7 @@
                 jax.ShapeDtypeStruct((features, span), jnp.bfloat16),
                 jax.ShapeDtypeStruct((span, LANES), jnp.bfloat16),
             ],
-            in_specs=[vmem_spec(), any_spec()],
+            in_specs=[vmem_spec()] + [any_spec()] * 2,
             out_specs=[any_spec()] * 2,
             scratch_shapes=[
                 pltpu.VMEM((features, span), jnp.bfloat16),
@@ -571,7 +573,7 @@
             ],
             compiler_params=params,
             name="gather",
-        )(ids, vocabulary_vectors)
+        )(ids, vocabulary_vectors, after)
 
         def product(turned, i, j):
             return mm(turned, columns(i, j), (((0,), (0,)), ((), ())))
@@ -616,16 +618,15 @@
         own0 = narrow(product(turned, 0, 0))
         return own0, core0, far, extra, member
 
-    first = project(0, FIRST)
-    later, _ = lax.optimization_barrier((ids, first[0]))
-    many = jnp.sum((later != 0).astype(jnp.int32)) > FIRST
+    many = jnp.sum((ids != 0).astype(jnp.int32)) > FIRST
     left = tokens - FIRST
-    shapes = jax.eval_shape(lambda: project(FIRST, left))
+    shapes = jax.eval_shape(lambda: project(FIRST, left, logit_sharpness))
     rest = lax.cond(
         many,
-        lambda: project(FIRST, left),
+        lambda: project(FIRST, left, logit_sharpness),
         lambda: tuple(jnp.zeros(x.shape, x.dtype) for x in shapes),
     )
+    first = project(0, FIRST, rest[3])
     sent, misc = pl.pallas_call(
         functools.partial(pool_kernel, model_width=float(features * shards)),
         out_shape=[

time: 69.5 us -> 72.5 us (1.043)
  waiting for transfers between devices: 17.9 us -> 23 us
  matrix products: 8.75 us -> 7.13 us
  other arithmetic: 4.41 us -> 3.59 us
    ppermute x1, waiting for transfers between devices: 7.68 us -> 12.8 us  [project(): sent = lax.ppermute(sent, 'dp', other_y).astype(jnp.float32)]
    dot_general x4, matrix products: 8.75 us -> 7.13 us  [mm(): return lax.dot_general(a, b, dims, preferred_element_type=jnp.float32)]
    convert_element_type x1, other arithmetic: 0.9 us -> 0.01 us  [project(): across = lax.ppermute(extra, 'dp', other_core).astype(jnp.float32)]
  transfers between devices with their start and end apart: 14 -> 14, of which waited for: 7 -> 7; matrix products, arithmetic and copies ran while one was open for 13% -> 6% of each run, Pallas kernels for 0% -> 0%
where the time goes in v16:
time: 72.5 us; the launch traced here: 72.2 us
  waiting for transfers between devices  23 us (32%)
  Pallas kernels  20.6 us (28%)
  starting transfers between devices  13.5 us (19%)
  matrix products  7.13 us (10%)
  other arithmetic  3.59 us (5%)
  local copies, waits for them, and re-layouts  2.15 us (3%)
  between operations  2.13 us (3%)
    pallas_call x1, Pallas kernels, project(): pl.pallas_call(functools.partial(gather_kernel, base=base), out_shape=[ja...  15 us
    ppermute x1, waiting for transfers between devices, project(): sent = lax.ppermute(sent, 'dp', other_y).astype(jnp.float32)  12.8 us
    dot_general x4, matrix products, mm(): return lax.dot_general(a, b, dims, preferred_element_type=jnp.float32)  7.13 us
    ppermute x6, starting transfers between devices, exchange(): return [x] + [lax.ppermute(x, axis, step) for step in steps][::-1]  6.28 us
    ppermute x6, waiting for transfers between devices, exchange(): return [x] + [lax.ppermute(x, axis, step) for step in steps][::-1]  5.97 us
    pallas_call x1, Pallas kernels, split_body(): pl.pallas_call(functools.partial(pool_kernel, model_width=float(features...  3.11 us
    ppermute x1, starting transfers between devices, project(): far = lax.ppermute(chip1, 'dp', other_y)  3.03 us
    ppermute x1, waiting for transfers between devices, split_body(): far_side = lax.ppermute(sent, 'group', [(0, 1), (1, 0)])  3 us
  transfers between devices with their start and end apart: 14, of which 7 were waited for; matrix products, arithmetic and copies ran while one was open for 6% of the time, Pallas kernels for 0%

profile of v16, /device:TPU:0, one launch (start us, length us, event | category | flops | bytes accessed | tf_op | source)
XLA Modules:
  0.0 72.2 jit_solution(9904765416969199509)
XLA Ops:
  0.6 1.3 %convert_reduce_fusion = s32[]{:T(128)} fusion(s32[1,12,128]{2,0,1:T(1,128)} %param.9), kind=kLoop, calls=%fused_computation.39 | loop fusion | flops 4607 | bytes 6148 | tf_op jit(solution)/shard_map/reduce_sum | solution.py:621
  3.3 1.5 %conditional.1 = (bf16[384,256]{1,0:T(8,128)(2,1)S(1)}, bf16[384,256]{1,0:T(8,128)(2,1)}, bf16[384,256]{1,0:T(8,128)(2,1)}, f32[64,256]{1,0:T(8,128)S(1)}, bf16[384,128]{1,0:T(8,128)(2,1)S(1)}) conditional(s32[]{:T(128)} %convert_element_type.69, () %tuple.19, (s32[12,128]{1,0:T(8,128)S(1)}, bf16[1024,16384]{1,0:T(8,128)(2,1)}, f32[1]{0:T(128)}, ...), branch_computations={%region_1.0_spmd, %region_2.0_spmd} | conditional | flops 919543808 | bytes 12330072 | solution.py:624
  3.4 0.7 broadcast.8.clone.1
  4.8 15.0 %gather.3 = (bf16[1024,1152]{1,0:T(8,128)(2,1)S(1)}, bf16[1152,128]{1,0:T(8,128)(2,1)S(1)}) custom-call(s32[12,128]{1,0:T(8,128)S(1)} %bitcast.14, bf16[1024,16384]{1,0:T(8,128)(2,1)} %vocab_ref.1, f32[64,256]{1,0:T(8,128)S(1)} %get-tuple-element.41.after_any.extra_rest), custom_call_target="tpu_custom_call" | custom-call | tf_op jit(solution)/shard_map/gather/pallas_call | solution.py:554
  19.8 2.7 %convolution_convert_fusion.6 = bf16[1152,256]{1,0:T(8,128)(2,1)} fusion(bf16[1024,1152]{1,0:T(8,128)(2,1)S(1)} %get-tuple-element.43.turned_any, bf16[1024,1024]{1,0:T(8,128)(2,1)} %param.12, s32[]{:T(128)S(6)} %select_n.37), kind=kOutput, calls=%fused_computation.20 | convolution fusion | flops 604274688 | bytes 3473412 | tf_op jit(solution)/shard_map/dot_general | solution.py:128
  23.0 2.7 %convolution_convert_fusion.7 = bf16[1152,256]{1,0:T(8,128)(2,1)} fusion(bf16[1024,1152]{1,0:T(8,128)(2,1)S(1)} %get-tuple-element.43.turned_any, bf16[1024,1024]{1,0:T(8,128)(2,1)} %param.12, s32[]{:T(128)S(6)} %select_n.36), kind=kOutput, calls=%fused_computation.21 | convolution fusion | flops 604274688 | bytes 3473412 | tf_op jit(solution)/shard_map/dot_general | solution.py:128
  25.7 1.5 %add_convert_fusion.1 = bf16[1152,256]{1,0:T(8,128)(2,1)S(1)} fusion(bf16[1152,256]{1,0:T(8,128)(2,1)} %collective-permute-done.5, bf16[1152,256]{1,0:T(8,128)(2,1)} %convolution_convert_fusion.7), kind=kLoop, calls=%fused_computation.22 | loop fusion | flops 1179648 | bytes 1769472 | tf_op jit(solution)/shard_map/convert_element_type | solution.py:582
  27.3 1.4 %statistics.3 = bf16[160,256]{1,0:T(8,128)(2,1)S(1)} custom-call(bf16[1024,1152]{1,0:T(8,128)(2,1)S(1)} %get-tuple-element.43.turned_any, bf16[1152,128]{1,0:T(8,128)(2,1)S(1)} %get-tuple-element.44.member_any.member_ref, s32[3,7]{1,0:T(4,128)S(1)} %copy-done.5, bf16[16,4096]{1,0:T(8,128)(2,1)S(1)} %copy-done.3), custom_call_target="tpu_custom_call" | custom-call | flops 339738624 | bytes 2359296 | tf_op jit(solution)/shard_map/statistics/pallas_call | solution.py:589
  28.8 3.0 %collective-permute-start.7 = (bf16[1152,256]{1,0:T(8,128)(2,1)S(1)}, bf16[1152,256]{1,0:T(8,128)(2,1)S(1)}, u32[]{:S(2)}, u32[]{:S(2)}) collective-permute-start(bf16[1152,256]{1,0:T(8,128)(2,1)S(1)} %add_convert_fusion.1), channel_id=1, source_target_pairs={{0,8},{4,12},{8,0},{12,4},{1,9},{5,13},{9,1},{13,5},{2,10},{6,14},... | collective-permute-start | bytes 1769480 | tf_op jit(solution)/shard_map/ppermute | solution.py:587
  31.9 0.8 %convolution_convert_fusion.4 = bf16[1152,256]{1,0:T(8,128)(2,1)S(1)} fusion(bf16[1024,1152]{1,0:T(8,128)(2,1)S(1)} %get-tuple-element.43.turned_any, bf16[1024,1024]{1,0:T(8,128)(2,1)S(1)} %copy-done.7, s32[]{:T(128)S(6)} %select_n.39), kind=kOutput, calls=%fused_computation.18 | convolution fusion | flops 604274688 | bytes 3473412 | tf_op jit(solution)/shard_map/dot_general | solution.py:128
  33.0 0.8 %convolution_convert_fusion.5.own_ref = bf16[1152,256]{1,0:T(8,128)(2,1)S(1)} fusion(bf16[1024,1152]{1,0:T(8,128)(2,1)S(1)} %get-tuple-element.43.turned_any, bf16[1024,1024]{1,0:T(8,128)(2,1)S(1)} %copy-done.7, s32[]{:T(128)S(6)} %select_n.38), kind=kOutput, calls=%fused_computation.19 | convolution fusion | flops 604274688 | bytes 3473412 | tf_op jit(solution)/shard_map/dot_general | solution.py:128
  33.8 12.8 %collective-permute-done.9 = bf16[112,256]{1,0:T(8,128)(2,1)S(1)} collective-permute-done((bf16[112,256]{1,0:T(8,128)(2,1)S(1)}, bf16[112,256]{1,0:T(8,128)(2,1)S(1)}, u32[]{:S(2)}, u32[]{:S(2)}) %collective-permute-start.9) | collective-permute-done | bytes 57376 | tf_op jit(solution)/shard_map/ppermute | solution.py:615
  46.7 3.1 %pool.1 = (bf16[208,256]{1,0:T(8,128)(2,1)S(1)}, f32[16,256]{1,0:T(8,128)S(1)}) custom-call(s32[12,128]{1,0:T(8,128)S(1)} %bitcast.15, bf16[1152,256]{1,0:T(8,128)(2,1)S(1)} %convolution_convert_fusion.5.own_ref, bf16[1152,256]{1,0:T(8,128)(2,1)S(1)} %collective-permute-done.6.core_any, bf16[1152,256]{1,0:T(8,128)(2,1)S(1)} %collective-permute-done.7.far_any, ...), custom_call_target="tpu_custom_call" | custom-call | tf_op jit(solution)/shard_map/pool/pallas_call | solution.py:630
  49.8 1.8 %collective-permute-start.10 = (bf16[208,256]{1,0:T(8,128)(2,1)S(1)}, bf16[208,256]{1,0:T(8,128)(2,1)S(1)}, u32[]{:S(2)}, u32[]{:S(2)}) collective-permute-start(bf16[208,256]{1,0:T(8,128)(2,1)S(1)} %get-tuple-element.49.near_ref), channel_id=1, source_target_pairs={{0,16},{16,0},{1,17},{17,1},{2,18},{18,2},{3,19},{19,3},{4,20},{20... | collective-permute-start | bytes 319496 | tf_op jit(solution)/shard_map/ppermute | solution.py:649
  51.5 3.0 %collective-permute-done.10.far_ref = bf16[208,256]{1,0:T(8,128)(2,1)S(1)} collective-permute-done((bf16[208,256]{1,0:T(8,128)(2,1)S(1)}, bf16[208,256]{1,0:T(8,128)(2,1)S(1)}, u32[]{:S(2)}, u32[]{:S(2)}) %collective-permute-start.10) | collective-permute-done | bytes 106528 | tf_op jit(solution)/shard_map/ppermute | solution.py:649
  54.7 1.8 %collective-permute-start.12 = (f32[96,128]{1,0:T(8,128)S(1)}, f32[96,128]{1,0:T(8,128)S(1)}, u32[]{:S(2)}, u32[]{:S(2)}) collective-permute-start(f32[96,128]{1,0:T(8,128)S(1)} %get-tuple-element.50.refs_0_), channel_id=1, source_target_pairs={{0,8},{4,12},{8,0},{12,4},{1,9},{5,13},{9,1},{13,5},{2,10},{6,14},... | collective-permute-start | bytes 147464 | tf_op jit(solution)/shard_map/ppermute | solution.py:520
  56.6 1.9 %collective-permute-done.13.refs_3_ = f32[96,128]{1,0:T(8,128)S(1)} collective-permute-done((f32[96,128]{1,0:T(8,128)S(1)}, f32[96,128]{1,0:T(8,128)S(1)}, u32[]{:S(2)}, u32[]{:S(2)}) %collective-permute-start.13) | collective-permute-done | bytes 49184 | tf_op jit(solution)/shard_map/ppermute | solution.py:520
  58.4 0.9 %collective-permute-done.12.refs_2_ = f32[96,128]{1,0:T(8,128)S(1)} collective-permute-done((f32[96,128]{1,0:T(8,128)S(1)}, f32[96,128]{1,0:T(8,128)S(1)}, u32[]{:S(2)}, u32[]{:S(2)}) %collective-permute-start.12) | collective-permute-done | bytes 49184 | tf_op jit(solution)/shard_map/ppermute | solution.py:520
  59.4 1.7 %collective-permute-start.14 = (bf16[384,256]{1,0:T(8,128)(2,1)S(1)}, bf16[384,256]{1,0:T(8,128)(2,1)S(1)}, u32[]{:S(2)}, u32[]{:S(2)}) collective-permute-start(bf16[384,256]{1,0:T(8,128)(2,1)S(1)} %get-tuple-element.52.refs_4_), channel_id=1, source_target_pairs={{0,8},{4,12},{8,0},{12,4},{1,9},{5,13},{9,1},{13,5},{2,10},{6,14},... | collective-permute-start | bytes 589832 | tf_op jit(solution)/shard_map/ppermute | solution.py:667
  61.1 3.6 %collective-permute-start.17 = (f32[32,128]{1,0:T(8,128)S(1)}, f32[32,128]{1,0:T(8,128)S(1)}, u32[]{:S(2)}, u32[]{:S(2)}) collective-permute-start(f32[32,128]{1,0:T(8,128)S(1)} %fusion.12.refs_6_), channel_id=1, source_target_pairs={{0,3},{1,2},{2,1},{3,0},{4,7},{5,6},{6,5},{7,4},{8,11},{9,10},{10,... | collective-permute-start | bytes 49160 | tf_op jit(solution)/shard_map/ppermute | solution.py:520
  64.7 0.8 %collective-permute-start.15 = (f32[32,128]{1,0:T(8,128)S(1)}, f32[32,128]{1,0:T(8,128)S(1)}, u32[]{:S(2)}, u32[]{:S(2)}) collective-permute-start(f32[32,128]{1,0:T(8,128)S(1)} %fusion.12.refs_6_), channel_id=1, source_target_pairs={{0,1},{1,0},{2,3},{3,2},{4,5},{5,4},{6,7},{7,6},{8,9},{9,8},{10,11... | collective-permute-start | bytes 49160 | tf_op jit(solution)/shard_map/ppermute | solution.py:520
  66.6 2.7 %collective-permute-done.16.refs_8_ = f32[32,128]{1,0:T(8,128)S(1)} collective-permute-done((f32[32,128]{1,0:T(8,128)S(1)}, f32[32,128]{1,0:T(8,128)S(1)}, u32[]{:S(2)}, u32[]{:S(2)}) %collective-permute-start.16) | collective-permute-done | bytes 16416 | tf_op jit(solution)/shard_map/ppermute | solution.py:520
  69.3 1.0 %score.1 = (bf16[1,3,1024]{2,1,0:T(4,128)(2,1)}, f32[1,3]{1,0:T(1,128)}, f32[16,512]{1,0:T(8,128)S(1)}) custom-call(f32[96,128]{1,0:T(8,128)S(1)} %get-tuple-element.50.refs_0_, f32[96,128]{1,0:T(8,128)S(1)} %collective-permute-done.11.refs_1_, f32[96,128]{1,0:T(8,128)S(1)} %collective-permute-done.12.refs_2_, ...), custom_call_target="tpu_custom_call" | custom-call | tf_op jit(solution)/shard_map/score/pallas_call | solution.py:668
  70.3 1.2 %collective-permute-done.18 = f32[16,512]{1,0:T(8,128)S(1)} collective-permute-done((f32[16,512]{1,0:T(8,128)S(1)}, f32[16,512]{1,0:T(8,128)S(1)}, u32[]{:S(2)}, u32[]{:S(2)}) %collective-permute-start.18) | collective-permute-done | bytes 32800 | tf_op jit(solution)/shard_map/ppermute | solution.py:682
  (41 shorter events, 3.6 us)
Async XLA Ops:
  22.5 3.2 %collective-permute-start.5 = (bf16[1152,256]{1,0:T(8,128)(2,1)}, bf16[1152,256]{1,0:T(8,128)(2,1)}, u32[]{:S(2)}, u32[]{:S(2)}) collective-permute-start(bf16[1152,256]{1,0:T(8,128)(2,1)} %convolution_convert_fusion.6), channel_id=1, source_target_pairs={{0,4},{4,0},{8,12},{12,8},{1,5},{5,1},{9,13},{13,9},{2,6},{6,2},{1... | collective-permute-start | bytes 1769480 | tf_op jit(solution)/shard_map/ppermute | solution.py:584
  23.0 4.3 %copy-start.3 = (bf16[16,4096]{1,0:T(8,128)(2,1)S(1)}, bf16[16,4096]{1,0:T(8,128)(2,1)}, u32[]{:S(2)}) copy-start(bf16[16,4096]{1,0:T(8,128)(2,1)} %lower_ref.1) | copy-start | bytes 393220
  23.0 4.3 %copy-start.5 = (s32[3,7]{1,0:T(4,128)S(1)}, s32[3,7]{1,0:T(4,128)}, u32[]{:S(2)}) copy-start(s32[3,7]{1,0:T(4,128)} %hard_ref.1) | copy-start | bytes 256
  25.7 6.2 %copy-start.7 = (bf16[1024,1024]{1,0:T(8,128)(2,1)S(1)}, bf16[1024,1024]{1,0:T(8,128)(2,1)}, u32[]{:S(2)}) copy-start(bf16[1024,1024]{1,0:T(8,128)(2,1)} %param.12) | copy-start | bytes 6291460
  28.7 4.1 %collective-permute-start.8 = (bf16[160,256]{1,0:T(8,128)(2,1)S(1)}, bf16[160,256]{1,0:T(8,128)(2,1)S(1)}, u32[]{:S(2)}, u32[]{:S(2)}) collective-permute-start(bf16[160,256]{1,0:T(8,128)(2,1)S(1)} %statistics.3), channel_id=1, source_target_pairs={{0,4},{4,0},{8,12},{12,8},{1,5},{5,1},{9,13},{13,9},{2,6},{6,2},{1... | collective-permute-start | bytes 245768 | tf_op jit(solution)/shard_map/ppermute | solution.py:611
  28.8 17.8 %collective-permute-start.7 = (bf16[1152,256]{1,0:T(8,128)(2,1)S(1)}, bf16[1152,256]{1,0:T(8,128)(2,1)S(1)}, u32[]{:S(2)}, u32[]{:S(2)}) collective-permute-start(bf16[1152,256]{1,0:T(8,128)(2,1)S(1)} %add_convert_fusion.1), channel_id=1, source_target_pairs={{0,8},{4,12},{8,0},{12,4},{1,9},{5,13},{9,1},{13,5},{2,10},{6,14},... | collective-permute-start | bytes 1769480 | tf_op jit(solution)/shard_map/ppermute | solution.py:587
  32.7 13.9 %collective-permute-start.6 = (bf16[1152,256]{1,0:T(8,128)(2,1)S(1)}, bf16[1152,256]{1,0:T(8,128)(2,1)S(1)}, u32[]{:S(2)}, u32[]{:S(2)}) collective-permute-start(bf16[1152,256]{1,0:T(8,128)(2,1)S(1)} %convolution_convert_fusion.4), channel_id=1, source_target_pairs={{0,4},{4,0},{8,12},{12,8},{1,5},{5,1},{9,13},{13,9},{2,6},{6,2},{1... | collective-permute-start | bytes 1769480 | tf_op jit(solution)/shard_map/ppermute | solution.py:617
  32.9 13.8 %copy-start = (bf16[16,1024]{1,0:T(8,128)(2,1)S(1)}, bf16[16,1024]{1,0:T(8,128)(2,1)}, u32[]{:S(2)}) copy-start(bf16[16,1024]{1,0:T(8,128)(2,1)} %raise_ref.1) | copy-start | bytes 98308
  32.9 13.7 %collective-permute-start.9 = (bf16[112,256]{1,0:T(8,128)(2,1)S(1)}, bf16[112,256]{1,0:T(8,128)(2,1)S(1)}, u32[]{:S(2)}, u32[]{:S(2)}) collective-permute-start(bf16[112,256]{1,0:T(8,128)(2,1)S(1)} %pad_maximum_fusion.2), channel_id=1, source_target_pairs={{0,8},{4,12},{8,0},{12,4},{1,9},{5,13},{9,1},{13,5},{2,10},{6,14},... | collective-permute-start | bytes 172040 | tf_op jit(solution)/shard_map/ppermute | solution.py:615
  49.8 4.8 %collective-permute-start.10 = (bf16[208,256]{1,0:T(8,128)(2,1)S(1)}, bf16[208,256]{1,0:T(8,128)(2,1)S(1)}, u32[]{:S(2)}, u32[]{:S(2)}) collective-permute-start(bf16[208,256]{1,0:T(8,128)(2,1)S(1)} %get-tuple-element.49.near_ref), channel_id=1, source_target_pairs={{0,16},{16,0},{1,17},{17,1},{2,18},{18,2},{3,19},{19,3},{4,20},{20... | collective-permute-start | bytes 319496 | tf_op jit(solution)/shard_map/ppermute | solution.py:649
  54.7 3.8 %collective-permute-start.13 = (f32[96,128]{1,0:T(8,128)S(1)}, f32[96,128]{1,0:T(8,128)S(1)}, u32[]{:S(2)}, u32[]{:S(2)}) collective-permute-start(f32[96,128]{1,0:T(8,128)S(1)} %get-tuple-element.50.refs_0_), channel_id=1, source_target_pairs={{0,12},{4,8},{8,4},{12,0},{1,13},{5,9},{9,5},{13,1},{2,14},{6,10},... | collective-permute-start | bytes 147464 | tf_op jit(solution)/shard_map/ppermute | solution.py:520
  54.7 4.7 %collective-permute-start.12 = (f32[96,128]{1,0:T(8,128)S(1)}, f32[96,128]{1,0:T(8,128)S(1)}, u32[]{:S(2)}, u32[]{:S(2)}) collective-permute-start(f32[96,128]{1,0:T(8,128)S(1)} %get-tuple-element.50.refs_0_), channel_id=1, source_target_pairs={{0,8},{4,12},{8,0},{12,4},{1,9},{5,13},{9,1},{13,5},{2,10},{6,14},... | collective-permute-start | bytes 147464 | tf_op jit(solution)/shard_map/ppermute | solution.py:520
  56.5 2.9 %collective-permute-start.11 = (f32[96,128]{1,0:T(8,128)S(1)}, f32[96,128]{1,0:T(8,128)S(1)}, u32[]{:S(2)}, u32[]{:S(2)}) collective-permute-start(f32[96,128]{1,0:T(8,128)S(1)} %get-tuple-element.50.refs_0_), channel_id=1, source_target_pairs={{0,4},{4,0},{8,12},{12,8},{1,5},{5,1},{9,13},{13,9},{2,6},{6,2},{1... | collective-permute-start | bytes 147464 | tf_op jit(solution)/shard_map/ppermute | solution.py:520
  59.4 10.0 %collective-permute-start.14 = (bf16[384,256]{1,0:T(8,128)(2,1)S(1)}, bf16[384,256]{1,0:T(8,128)(2,1)S(1)}, u32[]{:S(2)}, u32[]{:S(2)}) collective-permute-start(bf16[384,256]{1,0:T(8,128)(2,1)S(1)} %get-tuple-element.52.refs_4_), channel_id=1, source_target_pairs={{0,8},{4,12},{8,0},{12,4},{1,9},{5,13},{9,1},{13,5},{2,10},{6,14},... | collective-permute-start | bytes 589832 | tf_op jit(solution)/shard_map/ppermute | solution.py:667
  61.1 5.5 %collective-permute-start.17 = (f32[32,128]{1,0:T(8,128)S(1)}, f32[32,128]{1,0:T(8,128)S(1)}, u32[]{:S(2)}, u32[]{:S(2)}) collective-permute-start(f32[32,128]{1,0:T(8,128)S(1)} %fusion.12.refs_6_), channel_id=1, source_target_pairs={{0,3},{1,2},{2,1},{3,0},{4,7},{5,6},{6,5},{7,4},{8,11},{9,10},{10,... | collective-permute-start | bytes 49160 | tf_op jit(solution)/shard_map/ppermute | solution.py:520
  64.7 4.6 %collective-permute-start.16 = (f32[32,128]{1,0:T(8,128)S(1)}, f32[32,128]{1,0:T(8,128)S(1)}, u32[]{:S(2)}, u32[]{:S(2)}) collective-permute-start(f32[32,128]{1,0:T(8,128)S(1)} %fusion.12.refs_6_), channel_id=1, source_target_pairs={{0,2},{1,3},{2,0},{3,1},{4,6},{5,7},{6,4},{7,5},{8,10},{9,11},{10,... | collective-permute-start | bytes 49160 | tf_op jit(solution)/shard_map/ppermute | solution.py:520
  64.7 4.6 %collective-permute-start.15 = (f32[32,128]{1,0:T(8,128)S(1)}, f32[32,128]{1,0:T(8,128)S(1)}, u32[]{:S(2)}, u32[]{:S(2)}) collective-permute-start(f32[32,128]{1,0:T(8,128)S(1)} %fusion.12.refs_6_), channel_id=1, source_target_pairs={{0,1},{1,0},{2,3},{3,2},{4,5},{5,4},{6,7},{7,6},{8,9},{9,8},{10,11... | collective-permute-start | bytes 49160 | tf_op jit(solution)/shard_map/ppermute | solution.py:520
  70.3 1.2 %collective-permute-start.18 = (f32[16,512]{1,0:T(8,128)S(1)}, f32[16,512]{1,0:T(8,128)S(1)}, u32[]{:S(2)}, u32[]{:S(2)}) collective-permute-start(f32[16,512]{1,0:T(8,128)S(1)} %get-tuple-element.57), channel_id=1, source_target_pairs={{0,4},{4,0},{8,12},{12,8},{1,5},{5,1},{9,13},{13,9},{2,6},{6,2},{1... | collective-permute-start | bytes 98312 | tf_op jit(solution)/shard_map/ppermute | solution.py:682

commit v17 on v14

--- a/solution.py
+++ b/solution.py
@@ -170,8 +170,11 @@
 def gather_kernel(
     ids_ref,
     vocab_ref,
+    weight_ref,
     turned_any,
     member_any,
+    weight0,
+    weight1,
     turned,
     member_ref,
     held,
@@ -182,6 +185,7 @@
     held_sems,
     bounds_sem,
     out_sems,
+    weight_sems,
     base,
 ):
     texts, length = ids_ref.shape
@@ -194,7 +198,15 @@
         columns = pl.ds(pl.multiple_of(b * IDS_PER_BLOCK, LANES), IDS_PER_BLOCK)
         return pltpu.make_async_copy(vocab_ref.at[:, columns], held.at[b], held_sems.at[b])
 
+    weight_copies = []
+    for i, weight in enumerate((weight0, weight1)):
+        width = weight.shape[1]
+        columns = pl.ds(pl.multiple_of(split_quarter(i, 1) * width, LANES), width)
+        copy = pltpu.make_async_copy(weight_ref.at[:, columns], weight, weight_sems.at[i])
+        weight_copies.append(copy)
     vocab_copy(0).start()
+    for copy in weight_copies:
+        copy.start()
     for b in range(1, blocks):
         vocab_copy(b).start()
 
@@ -285,6 +297,8 @@
 
     lax.fori_loop(0, blocks, take, 0)
     fetch([(turned, turned_any), (member_ref, member_any)], out_sems)
+    for copy in weight_copies:
+        copy.wait()
 
 
 def statistics_kernel(
@@ -514,8 +528,8 @@
 
 
 def exchange(x, axis, size):
-    steps = [[(i, i ^ o) for i in range(size)] for o in range(1, size)]
-    return [x] + [lax.ppermute(x, axis, step) for step in steps]
+    steps = [[(i, i ^ o) for i in range(size)] for o in reversed(range(1, size))]
+    return [x] + [lax.ppermute(x, axis, step) for step in steps][::-1]
 
 
 def split_body(
@@ -549,14 +563,16 @@
     def project(base, span):
         stripes = pl.cdiv(span, STRIPE)
         extra_rows = (stripes + 1 + shards) * ROWS
-        turned, member = pl.pallas_call(
+        turned, member, weight0, weight1 = pl.pallas_call(
             functools.partial(gather_kernel, base=base),
             out_shape=[
                 jax.ShapeDtypeStruct((features, span), jnp.bfloat16),
                 jax.ShapeDtypeStruct((span, LANES), jnp.bfloat16),
+                jax.ShapeDtypeStruct((features, width), jnp.bfloat16),
+                jax.ShapeDtypeStruct((features, width), jnp.bfloat16),
             ],
-            in_specs=[vmem_spec(), any_spec()],
-            out_specs=[any_spec()] * 2,
+            in_specs=[vmem_spec()] + [any_spec()] * 2,
+            out_specs=[any_spec()] * 4,
             scratch_shapes=[
                 pltpu.VMEM((features, span), jnp.bfloat16),
                 pltpu.VMEM((span, LANES), jnp.bfloat16),
@@ -568,19 +584,20 @@
                 pltpu.SemaphoreType.DMA((blocks,)),
                 pltpu.SemaphoreType.DMA,
                 pltpu.SemaphoreType.DMA((2,)),
+                pltpu.SemaphoreType.DMA((2,)),
             ],
             compiler_params=params,
             name="gather",
-        )(ids, vocabulary_vectors)
-
-        def product(turned, i, j):
-            return mm(turned, columns(i, j), (((0,), (0,)), ((), ())))
+        )(ids, vocabulary_vectors, layer_weight_matrix)
+
+        def product(turned, weight):
+            return mm(turned, weight, (((0,), (0,)), ((), ())))
 
         def narrow(x):
             return x.astype(jnp.bfloat16)
 
-        core1 = lax.ppermute(narrow(product(turned, 1, 1)), "dp", other_core)
-        own1 = lax.optimization_barrier(narrow(product(turned, 0, 1)))
+        core1 = lax.ppermute(narrow(product(turned, weight1)), "dp", other_core)
+        own1 = lax.optimization_barrier(narrow(product(turned, weight0)))
         chip1 = narrow(own1.astype(jnp.float32) + core1.astype(jnp.float32))
         far = lax.ppermute(chip1, "dp", other_y)
         turned, _ = lax.optimization_barrier((turned, chip1))
@@ -612,8 +629,8 @@
         sent = narrow(jnp.concatenate([chip, inputs[ROWS:]]))
         sent = lax.ppermute(sent, "dp", other_y).astype(jnp.float32)
         extra = jnp.concatenate([chip, inputs[0:ROWS]]) + sent
-        core0 = lax.ppermute(narrow(product(turned, 1, 0)), "dp", other_core)
-        own0 = narrow(product(turned, 0, 0))
+        core0 = lax.ppermute(narrow(product(turned, columns(1, 0))), "dp", other_core)
+        own0 = narrow(product(turned, columns(0, 0)))
         return own0, core0, far, extra, member
 
     first = project(0, FIRST)

time: 69.5 us -> 68.1 us (0.980)
  matrix products: 8.75 us -> 6.67 us
  starting transfers between devices: 13.5 us -> 14.2 us
    dot_general x4, matrix products: 8.75 us -> 6.67 us  [mm(): return lax.dot_general(a, b, dims, preferred_element_type=jnp.float32)]
    ppermute x1, starting transfers between devices: 1.77 us -> 2.7 us  [split_body(): far_side = lax.ppermute(sent, 'group', [(0, 1), (1, 0)])]
  transfers between devices with their start and end apart: 14 -> 14, of which waited for: 7 -> 8; matrix products, arithmetic and copies ran while one was open for 13% -> 12% of each run, Pallas kernels for 0% -> 0%
where the time goes in v17:
time: 68.1 us; the launch traced here: 67.6 us
  Pallas kernels  19.7 us (29%)
  waiting for transfers between devices  18.1 us (27%)
  starting transfers between devices  14.2 us (21%)
  matrix products  6.67 us (10%)
  other arithmetic  4.61 us (7%)
  local copies, waits for them, and re-layouts  2.13 us (3%)
  between operations  2.11 us (3%)
    pallas_call x1, Pallas kernels, project(): pl.pallas_call(functools.partial(gather_kernel, base=base), out_shape=[ja...  14.1 us
    ppermute x1, waiting for transfers between devices, project(): sent = lax.ppermute(sent, 'dp', other_y).astype(jnp.float32)  7.71 us
    dot_general x4, matrix products, mm(): return lax.dot_general(a, b, dims, preferred_element_type=jnp.float32)  6.67 us
    ppermute x6, starting transfers between devices, exchange(): return [x] + [lax.ppermute(x, axis, step) for step in steps][::-1]  6.25 us
    ppermute x6, waiting for transfers between devices, exchange(): return [x] + [lax.ppermute(x, axis, step) for step in steps][::-1]  6.23 us
    pallas_call x1, Pallas kernels, split_body(): pl.pallas_call(functools.partial(pool_kernel, model_width=float(features...  3.12 us
    ppermute x1, starting transfers between devices, project(): far = lax.ppermute(chip1, 'dp', other_y)  2.83 us
    ppermute x1, starting transfers between devices, split_body(): far_side = lax.ppermute(sent, 'group', [(0, 1), (1, 0)])  2.7 us
  transfers between devices with their start and end apart: 14, of which 8 were waited for; matrix products, arithmetic and copies ran while one was open for 12% of the time, Pallas kernels for 0%

profile of v17, /device:TPU:0, one launch (start us, length us, event | category | flops | bytes accessed | tf_op | source)
XLA Modules:
  0.0 67.6 jit_solution(2471660995005538648)
XLA Ops:
  0.6 0.7 %copy.12 = s32[1,12,128]{2,1,0:T(8,128)S(1)} copy(s32[1,12,128]{2,0,1:T(1,128)} %param.9) | data formatting | bytes 12288
  1.3 14.1 %gather.3 = (bf16[1024,1152]{1,0:T(8,128)(2,1)S(1)}, bf16[1152,128]{1,0:T(8,128)(2,1)S(1)}, bf16[1024,256]{1,0:T(8,128)(2,1)S(1)}, bf16[1024,256]{1,0:T(8,128)(2,1)S(1)}) custom-call(s32[12,128]{1,0:T(8,128)S(1)} %bitcast.15, bf16[1024,16384]{1,0:T(8,128)(2,1)} %vocab_ref.1, bf16[1024,1024]{1,0:T(8,128)(2,1)} %weight_ref.1), custom_call_target="tpu_custom_call" | custom-call | tf_op jit(solution)/shard_map/gather/pallas_call | solution.py:566
  15.4 1.7 %convolution_convert_fusion.6 = bf16[1152,256]{1,0:T(8,128)(2,1)} fusion(bf16[1024,1152]{1,0:T(8,128)(2,1)S(1)} %get-tuple-element.46.turned_any, bf16[1024,256]{1,0:T(8,128)(2,1)S(1)} %get-tuple-element.45), kind=kOutput, calls=%fused_computation.16 | convolution fusion | flops 604274688 | bytes 3473408 | tf_op jit(solution)/shard_map/dot_general | solution.py:128
  17.5 1.7 %convolution_convert_fusion.7 = bf16[1152,256]{1,0:T(8,128)(2,1)} fusion(bf16[1024,1152]{1,0:T(8,128)(2,1)S(1)} %get-tuple-element.46.turned_any, bf16[1024,256]{1,0:T(8,128)(2,1)S(1)} %get-tuple-element.44), kind=kOutput, calls=%fused_computation.17 | convolution fusion | flops 604274688 | bytes 3473408 | tf_op jit(solution)/shard_map/dot_general | solution.py:128
  19.5 2.4 %add_convert_fusion.1 = bf16[1152,256]{1,0:T(8,128)(2,1)} fusion(bf16[1152,256]{1,0:T(8,128)(2,1)} %collective-permute-done.5, bf16[1152,256]{1,0:T(8,128)(2,1)} %convolution_convert_fusion.7), kind=kLoop, calls=%fused_computation.18 | loop fusion | flops 1179648 | bytes 1769472 | tf_op jit(solution)/shard_map/convert_element_type | solution.py:597
  21.9 1.4 %statistics.3 = bf16[160,256]{1,0:T(8,128)(2,1)S(1)} custom-call(bf16[1024,1152]{1,0:T(8,128)(2,1)S(1)} %get-tuple-element.46.turned_any, bf16[1152,128]{1,0:T(8,128)(2,1)S(1)} %get-tuple-element.47.member_any.member_ref, s32[3,7]{1,0:T(4,128)S(1)} %copy-done.8, bf16[16,4096]{1,0:T(8,128)(2,1)S(1)} %copy-done.5), custom_call_target="tpu_custom_call" | custom-call | flops 339738624 | bytes 2359296 | tf_op jit(solution)/shard_map/statistics/pallas_call | solution.py:604
  23.6 2.8 %collective-permute-start.7 = (bf16[1152,256]{1,0:T(8,128)(2,1)}, bf16[1152,256]{1,0:T(8,128)(2,1)S(1)}, u32[]{:S(2)}, u32[]{:S(2)}) collective-permute-start(bf16[1152,256]{1,0:T(8,128)(2,1)} %add_convert_fusion.1), channel_id=1, source_target_pairs={{0,8},{4,12},{8,0},{12,4},{1,9},{5,13},{9,1},{13,5},{2,10},{6,14},... | collective-permute-start | bytes 1769480 | tf_op jit(solution)/shard_map/ppermute | solution.py:602
  26.5 1.6 %convolution_convert_fusion.5.own_ref = bf16[1152,256]{1,0:T(8,128)(2,1)} fusion(bf16[1024,1152]{1,0:T(8,128)(2,1)S(1)} %get-tuple-element.46.turned_any, bf16[1024,1024]{1,0:T(8,128)(2,1)S(1)} %copy-done.2, s32[]{:T(128)S(6)} %select_n.24), kind=kOutput, calls=%fused_computation.15 | convolution fusion | flops 604274688 | bytes 3473412 | tf_op jit(solution)/shard_map/dot_general | solution.py:128
  28.1 1.7 %convolution_convert_fusion.4 = bf16[1152,256]{1,0:T(8,128)(2,1)} fusion(bf16[1024,1152]{1,0:T(8,128)(2,1)S(1)} %get-tuple-element.46.turned_any, bf16[1024,1024]{1,0:T(8,128)(2,1)S(1)} %copy-done.2, s32[]{:T(128)S(6)} %select_n.25), kind=kOutput, calls=%fused_computation.14 | convolution fusion | flops 604274688 | bytes 3473412 | tf_op jit(solution)/shard_map/dot_general | solution.py:128
  31.1 1.4 %conditional.1 = (bf16[384,256]{1,0:T(8,128)(2,1)S(1)}, bf16[384,256]{1,0:T(8,128)(2,1)}, bf16[384,256]{1,0:T(8,128)(2,1)}, f32[64,256]{1,0:T(8,128)S(1)}, bf16[384,128]{1,0:T(8,128)(2,1)S(1)}) conditional(s32[]{:T(128)} %convert_element_type.79, () %tuple.22, (s32[12,128]{1,0:T(8,128)S(1)}, bf16[1024,16384]{1,0:T(8,128)(2,1)}, ...), branch_computations={%region_1.0_spmd, %region_2.0_spmd} | conditional | flops 919543808 | bytes 12329936 | solution.py:641
  32.6 0.9 %convert_element_type.76 = f32[160,256]{1,0:T(8,128)S(1)} convert(bf16[160,256]{1,0:T(8,128)(2,1)} %collective-permute-done.8) | non-fusion elementwise | flops 40960 | bytes 245760 | tf_op jit(solution)/shard_map/convert_element_type | solution.py:626
  33.9 7.7 %collective-permute-done.9 = bf16[112,256]{1,0:T(8,128)(2,1)S(1)} collective-permute-done((bf16[112,256]{1,0:T(8,128)(2,1)S(1)}, bf16[112,256]{1,0:T(8,128)(2,1)S(1)}, u32[]{:S(2)}, u32[]{:S(2)}) %collective-permute-start.9) | collective-permute-done | bytes 57376 | tf_op jit(solution)/shard_map/ppermute | solution.py:630
  41.7 3.1 %pool.1 = (bf16[208,256]{1,0:T(8,128)(2,1)S(1)}, f32[16,256]{1,0:T(8,128)S(1)}) custom-call(s32[12,128]{1,0:T(8,128)} %bitcast.18, bf16[1152,256]{1,0:T(8,128)(2,1)S(1)} %copy-done, bf16[1152,256]{1,0:T(8,128)(2,1)S(1)} %collective-permute-done.6.core_any, bf16[1152,256]{1,0:T(8,128)(2,1)S(1)} %collective-permute-done.7.far_any, ...), custom_call_target="tpu_custom_call" | custom-call | tf_op jit(solution)/shard_map/pool/pallas_call | solution.py:646
  44.8 2.7 %collective-permute-start.10 = (bf16[208,256]{1,0:T(8,128)(2,1)S(1)}, bf16[208,256]{1,0:T(8,128)(2,1)S(1)}, u32[]{:S(2)}, u32[]{:S(2)}) collective-permute-start(bf16[208,256]{1,0:T(8,128)(2,1)S(1)} %get-tuple-element.54.near_ref), channel_id=1, source_target_pairs={{0,16},{16,0},{1,17},{17,1},{2,18},{18,2},{3,19},{19,3},{4,20},{20... | collective-permute-start | bytes 319496 | tf_op jit(solution)/shard_map/ppermute | solution.py:665
  47.5 2.7 %collective-permute-done.10.far_ref = bf16[208,256]{1,0:T(8,128)(2,1)S(1)} collective-permute-done((bf16[208,256]{1,0:T(8,128)(2,1)S(1)}, bf16[208,256]{1,0:T(8,128)(2,1)S(1)}, u32[]{:S(2)}, u32[]{:S(2)}) %collective-permute-start.10) | collective-permute-done | bytes 106528 | tf_op jit(solution)/shard_map/ppermute | solution.py:665
  50.3 1.6 %collective-permute-start.12 = (f32[96,128]{1,0:T(8,128)S(1)}, f32[96,128]{1,0:T(8,128)S(1)}, u32[]{:S(2)}, u32[]{:S(2)}) collective-permute-start(f32[96,128]{1,0:T(8,128)S(1)} %get-tuple-element.55.refs_0_), channel_id=1, source_target_pairs={{0,8},{4,12},{8,0},{12,4},{1,9},{5,13},{9,1},{13,5},{2,10},{6,14},... | collective-permute-start | bytes 147464 | tf_op jit(solution)/shard_map/ppermute | solution.py:532
  52.2 2.1 %collective-permute-done.13.refs_3_ = f32[96,128]{1,0:T(8,128)S(1)} collective-permute-done((f32[96,128]{1,0:T(8,128)S(1)}, f32[96,128]{1,0:T(8,128)S(1)}, u32[]{:S(2)}, u32[]{:S(2)}) %collective-permute-start.13) | collective-permute-done | bytes 49184 | tf_op jit(solution)/shard_map/ppermute | solution.py:532
  54.3 0.9 %collective-permute-done.12.refs_2_ = f32[96,128]{1,0:T(8,128)S(1)} collective-permute-done((f32[96,128]{1,0:T(8,128)S(1)}, f32[96,128]{1,0:T(8,128)S(1)}, u32[]{:S(2)}, u32[]{:S(2)}) %collective-permute-start.12) | collective-permute-done | bytes 49184 | tf_op jit(solution)/shard_map/ppermute | solution.py:532
  55.2 1.3 %collective-permute-start.14 = (bf16[384,256]{1,0:T(8,128)(2,1)S(1)}, bf16[384,256]{1,0:T(8,128)(2,1)S(1)}, u32[]{:S(2)}, u32[]{:S(2)}) collective-permute-start(bf16[384,256]{1,0:T(8,128)(2,1)S(1)} %get-tuple-element.57.refs_4_), channel_id=1, source_target_pairs={{0,8},{4,12},{8,0},{12,4},{1,9},{5,13},{9,1},{13,5},{2,10},{6,14},... | collective-permute-start | bytes 589832 | tf_op jit(solution)/shard_map/ppermute | solution.py:683
  56.5 3.6 %collective-permute-start.17 = (f32[32,128]{1,0:T(8,128)S(1)}, f32[32,128]{1,0:T(8,128)S(1)}, u32[]{:S(2)}, u32[]{:S(2)}) collective-permute-start(f32[32,128]{1,0:T(8,128)S(1)} %fusion.6.refs_6_), channel_id=1, source_target_pairs={{0,3},{1,2},{2,1},{3,0},{4,7},{5,6},{6,5},{7,4},{8,11},{9,10},{10,... | collective-permute-start | bytes 49160 | tf_op jit(solution)/shard_map/ppermute | solution.py:532
  60.1 0.8 %collective-permute-start.15 = (f32[32,128]{1,0:T(8,128)S(1)}, f32[32,128]{1,0:T(8,128)S(1)}, u32[]{:S(2)}, u32[]{:S(2)}) collective-permute-start(f32[32,128]{1,0:T(8,128)S(1)} %fusion.6.refs_6_), channel_id=1, source_target_pairs={{0,1},{1,0},{2,3},{3,2},{4,5},{5,4},{6,7},{7,6},{8,9},{9,8},{10,11... | collective-permute-start | bytes 49160 | tf_op jit(solution)/shard_map/ppermute | solution.py:532
  62.0 2.7 %collective-permute-done.16.refs_8_ = f32[32,128]{1,0:T(8,128)S(1)} collective-permute-done((f32[32,128]{1,0:T(8,128)S(1)}, f32[32,128]{1,0:T(8,128)S(1)}, u32[]{:S(2)}, u32[]{:S(2)}) %collective-permute-start.16) | collective-permute-done | bytes 16416 | tf_op jit(solution)/shard_map/ppermute | solution.py:532
  64.7 1.0 %score.1 = (bf16[1,3,1024]{2,1,0:T(4,128)(2,1)}, f32[1,3]{1,0:T(1,128)}, f32[16,512]{1,0:T(8,128)S(1)}) custom-call(f32[96,128]{1,0:T(8,128)S(1)} %get-tuple-element.55.refs_0_, f32[96,128]{1,0:T(8,128)S(1)} %collective-permute-done.11.refs_1_, f32[96,128]{1,0:T(8,128)S(1)} %collective-permute-done.12.refs_2_, ...), custom_call_target="tpu_custom_call" | custom-call | tf_op jit(solution)/shard_map/score/pallas_call | solution.py:684
  65.7 1.2 %collective-permute-done.18 = f32[16,512]{1,0:T(8,128)S(1)} collective-permute-done((f32[16,512]{1,0:T(8,128)S(1)}, f32[16,512]{1,0:T(8,128)S(1)}, u32[]{:S(2)}, u32[]{:S(2)}) %collective-permute-start.18) | collective-permute-done | bytes 32800 | tf_op jit(solution)/shard_map/ppermute | solution.py:698
  (45 shorter events, 5.2 us)
Async XLA Ops:
  1.3 29.8 %copy-start.7 = (s32[1,12,128]{2,1,0:T(8,128)}, s32[1,12,128]{2,1,0:T(8,128)S(1)}, u32[]{:S(2)}) copy-start(s32[1,12,128]{2,1,0:T(8,128)S(1)} %copy.12) | copy-start | bytes 18436
  17.1 2.4 %collective-permute-start.5 = (bf16[1152,256]{1,0:T(8,128)(2,1)}, bf16[1152,256]{1,0:T(8,128)(2,1)}, u32[]{:S(2)}, u32[]{:S(2)}) collective-permute-start(bf16[1152,256]{1,0:T(8,128)(2,1)} %convolution_convert_fusion.6), channel_id=1, source_target_pairs={{0,4},{4,0},{8,12},{12,8},{1,5},{5,1},{9,13},{13,9},{2,6},{6,2},{1... | collective-permute-start | bytes 1769480 | tf_op jit(solution)/shard_map/ppermute | solution.py:599
  17.5 4.4 %copy-start.5 = (bf16[16,4096]{1,0:T(8,128)(2,1)S(1)}, bf16[16,4096]{1,0:T(8,128)(2,1)}, u32[]{:S(2)}) copy-start(bf16[16,4096]{1,0:T(8,128)(2,1)} %lower_ref.1) | copy-start | bytes 393220
  17.5 4.4 %copy-start.8 = (s32[3,7]{1,0:T(4,128)S(1)}, s32[3,7]{1,0:T(4,128)}, u32[]{:S(2)}) copy-start(s32[3,7]{1,0:T(4,128)} %hard_ref.1) | copy-start | bytes 256
  19.2 7.3 %copy-start.2 = (bf16[1024,1024]{1,0:T(8,128)(2,1)S(1)}, bf16[1024,1024]{1,0:T(8,128)(2,1)}, u32[]{:S(2)}) copy-start(bf16[1024,1024]{1,0:T(8,128)(2,1)} %weight_ref.1) | copy-start | bytes 6291460
  23.3 9.3 %collective-permute-start.8 = (bf16[160,256]{1,0:T(8,128)(2,1)S(1)}, bf16[160,256]{1,0:T(8,128)(2,1)}, u32[]{:S(2)}, u32[]{:S(2)}) collective-permute-start(bf16[160,256]{1,0:T(8,128)(2,1)S(1)} %statistics.3), channel_id=1, source_target_pairs={{0,4},{4,0},{8,12},{12,8},{1,5},{5,1},{9,13},{13,9},{2,6},{6,2},{1... | collective-permute-start | bytes 245768 | tf_op jit(solution)/shard_map/ppermute | solution.py:626
  23.6 18.0 %collective-permute-start.7 = (bf16[1152,256]{1,0:T(8,128)(2,1)}, bf16[1152,256]{1,0:T(8,128)(2,1)S(1)}, u32[]{:S(2)}, u32[]{:S(2)}) collective-permute-start(bf16[1152,256]{1,0:T(8,128)(2,1)} %add_convert_fusion.1), channel_id=1, source_target_pairs={{0,8},{4,12},{8,0},{12,4},{1,9},{5,13},{9,1},{13,5},{2,10},{6,14},... | collective-permute-start | bytes 1769480 | tf_op jit(solution)/shard_map/ppermute | solution.py:602
  31.1 10.6 %copy-start = (bf16[1152,256]{1,0:T(8,128)(2,1)S(1)}, bf16[1152,256]{1,0:T(8,128)(2,1)}, u32[]{:S(2)}) copy-start(bf16[1152,256]{1,0:T(8,128)(2,1)} %convolution_convert_fusion.5.own_ref) | copy-start | bytes 1769476
  31.1 10.6 %copy-start.1 = (bf16[16,1024]{1,0:T(8,128)(2,1)S(1)}, bf16[16,1024]{1,0:T(8,128)(2,1)}, u32[]{:S(2)}) copy-start(bf16[16,1024]{1,0:T(8,128)(2,1)} %raise_ref.1) | copy-start | bytes 98308
  32.6 9.1 %collective-permute-start.6 = (bf16[1152,256]{1,0:T(8,128)(2,1)}, bf16[1152,256]{1,0:T(8,128)(2,1)S(1)}, u32[]{:S(2)}, u32[]{:S(2)}) collective-permute-start(bf16[1152,256]{1,0:T(8,128)(2,1)} %convolution_convert_fusion.4), channel_id=1, source_target_pairs={{0,4},{4,0},{8,12},{12,8},{1,5},{5,1},{9,13},{13,9},{2,6},{6,2},{1... | collective-permute-start | bytes 1769480 | tf_op jit(solution)/shard_map/ppermute | solution.py:632
  33.6 8.0 %collective-permute-start.9 = (bf16[112,256]{1,0:T(8,128)(2,1)S(1)}, bf16[112,256]{1,0:T(8,128)(2,1)S(1)}, u32[]{:S(2)}, u32[]{:S(2)}) collective-permute-start(bf16[112,256]{1,0:T(8,128)(2,1)S(1)} %pad_maximum_fusion.2), channel_id=1, source_target_pairs={{0,8},{4,12},{8,0},{12,4},{1,9},{5,13},{9,1},{13,5},{2,10},{6,14},... | collective-permute-start | bytes 172040 | tf_op jit(solution)/shard_map/ppermute | solution.py:630
  44.8 5.4 %collective-permute-start.10 = (bf16[208,256]{1,0:T(8,128)(2,1)S(1)}, bf16[208,256]{1,0:T(8,128)(2,1)S(1)}, u32[]{:S(2)}, u32[]{:S(2)}) collective-permute-start(bf16[208,256]{1,0:T(8,128)(2,1)S(1)} %get-tuple-element.54.near_ref), channel_id=1, source_target_pairs={{0,16},{16,0},{1,17},{17,1},{2,18},{18,2},{3,19},{19,3},{4,20},{20... | collective-permute-start | bytes 319496 | tf_op jit(solution)/shard_map/ppermute | solution.py:665
  50.3 4.0 %collective-permute-start.13 = (f32[96,128]{1,0:T(8,128)S(1)}, f32[96,128]{1,0:T(8,128)S(1)}, u32[]{:S(2)}, u32[]{:S(2)}) collective-permute-start(f32[96,128]{1,0:T(8,128)S(1)} %get-tuple-element.55.refs_0_), channel_id=1, source_target_pairs={{0,12},{4,8},{8,4},{12,0},{1,13},{5,9},{9,5},{13,1},{2,14},{6,10},... | collective-permute-start | bytes 147464 | tf_op jit(solution)/shard_map/ppermute | solution.py:532
  50.3 4.9 %collective-permute-start.12 = (f32[96,128]{1,0:T(8,128)S(1)}, f32[96,128]{1,0:T(8,128)S(1)}, u32[]{:S(2)}, u32[]{:S(2)}) collective-permute-start(f32[96,128]{1,0:T(8,128)S(1)} %get-tuple-element.55.refs_0_), channel_id=1, source_target_pairs={{0,8},{4,12},{8,0},{12,4},{1,9},{5,13},{9,1},{13,5},{2,10},{6,14},... | collective-permute-start | bytes 147464 | tf_op jit(solution)/shard_map/ppermute | solution.py:532
  51.9 3.3 %collective-permute-start.11 = (f32[96,128]{1,0:T(8,128)S(1)}, f32[96,128]{1,0:T(8,128)S(1)}, u32[]{:S(2)}, u32[]{:S(2)}) collective-permute-start(f32[96,128]{1,0:T(8,128)S(1)} %get-tuple-element.55.refs_0_), channel_id=1, source_target_pairs={{0,4},{4,0},{8,12},{12,8},{1,5},{5,1},{9,13},{13,9},{2,6},{6,2},{1... | collective-permute-start | bytes 147464 | tf_op jit(solution)/shard_map/ppermute | solution.py:532
  55.2 9.5 %collective-permute-start.14 = (bf16[384,256]{1,0:T(8,128)(2,1)S(1)}, bf16[384,256]{1,0:T(8,128)(2,1)S(1)}, u32[]{:S(2)}, u32[]{:S(2)}) collective-permute-start(bf16[384,256]{1,0:T(8,128)(2,1)S(1)} %get-tuple-element.57.refs_4_), channel_id=1, source_target_pairs={{0,8},{4,12},{8,0},{12,4},{1,9},{5,13},{9,1},{13,5},{2,10},{6,14},... | collective-permute-start | bytes 589832 | tf_op jit(solution)/shard_map/ppermute | solution.py:683
  56.5 5.5 %collective-permute-start.17 = (f32[32,128]{1,0:T(8,128)S(1)}, f32[32,128]{1,0:T(8,128)S(1)}, u32[]{:S(2)}, u32[]{:S(2)}) collective-permute-start(f32[32,128]{1,0:T(8,128)S(1)} %fusion.6.refs_6_), channel_id=1, source_target_pairs={{0,3},{1,2},{2,1},{3,0},{4,7},{5,6},{6,5},{7,4},{8,11},{9,10},{10,... | collective-permute-start | bytes 49160 | tf_op jit(solution)/shard_map/ppermute | solution.py:532
  60.1 4.6 %collective-permute-start.16 = (f32[32,128]{1,0:T(8,128)S(1)}, f32[32,128]{1,0:T(8,128)S(1)}, u32[]{:S(2)}, u32[]{:S(2)}) collective-permute-start(f32[32,128]{1,0:T(8,128)S(1)} %fusion.6.refs_6_), channel_id=1, source_target_pairs={{0,2},{1,3},{2,0},{3,1},{4,6},{5,7},{6,4},{7,5},{8,10},{9,11},{10,... | collective-permute-start | bytes 49160 | tf_op jit(solution)/shard_map/ppermute | solution.py:532
  60.1 4.6 %collective-permute-start.15 = (f32[32,128]{1,0:T(8,128)S(1)}, f32[32,128]{1,0:T(8,128)S(1)}, u32[]{:S(2)}, u32[]{:S(2)}) collective-permute-start(f32[32,128]{1,0:T(8,128)S(1)} %fusion.6.refs_6_), channel_id=1, source_target_pairs={{0,1},{1,0},{2,3},{3,2},{4,5},{5,4},{6,7},{7,6},{8,9},{9,8},{10,11... | collective-permute-start | bytes 49160 | tf_op jit(solution)/shard_map/ppermute | solution.py:532
  65.7 1.2 %collective-permute-start.18 = (f32[16,512]{1,0:T(8,128)S(1)}, f32[16,512]{1,0:T(8,128)S(1)}, u32[]{:S(2)}, u32[]{:S(2)}) collective-permute-start(f32[16,512]{1,0:T(8,128)S(1)} %get-tuple-element.62), channel_id=1, source_target_pairs={{0,4},{4,0},{8,12},{12,8},{1,5},{5,1},{9,13},{13,9},{2,6},{6,2},{1... | collective-permute-start | bytes 98312 | tf_op jit(solution)/shard_map/ppermute | solution.py:698

commit v18 on v17

--- a/solution.py
+++ b/solution.py
@@ -173,8 +173,10 @@
     weight_ref,
     turned_any,
     member_any,
-    weight0,
-    weight1,
+    weight00,
+    weight01,
+    weight10,
+    weight11,
     turned,
     member_ref,
     held,
@@ -199,16 +201,18 @@
         return pltpu.make_async_copy(vocab_ref.at[:, columns], held.at[b], held_sems.at[b])
 
     weight_copies = []
-    for i, weight in enumerate((weight0, weight1)):
+    for q, weight in enumerate((weight00, weight01, weight10, weight11)):
         width = weight.shape[1]
-        columns = pl.ds(pl.multiple_of(split_quarter(i, 1) * width, LANES), width)
-        copy = pltpu.make_async_copy(weight_ref.at[:, columns], weight, weight_sems.at[i])
+        start = pl.multiple_of(split_quarter(q // 2, q % 2) * width, LANES)
+        copy = pltpu.make_async_copy(
+            weight_ref.at[:, pl.ds(start, width)], weight, weight_sems.at[q]
+        )
         weight_copies.append(copy)
     vocab_copy(0).start()
+    for b in range(1, blocks):
+        vocab_copy(b).start()
     for copy in weight_copies:
         copy.start()
-    for b in range(1, blocks):
-        vocab_copy(b).start()
 
     ids = ids_ref[...]
     valid = ids != 0
@@ -556,23 +560,18 @@
     other_core = [(d, d ^ 1) for d in range(shards)]
     other_y = [(d, d ^ 2) for d in range(shards)]
 
-    def columns(i, j):
-        start = split_quarter(i, j) * width
-        return lax.dynamic_slice(layer_weight_matrix, (0, start), (features, width))
-
     def project(base, span):
         stripes = pl.cdiv(span, STRIPE)
         extra_rows = (stripes + 1 + shards) * ROWS
-        turned, member, weight0, weight1 = pl.pallas_call(
+        turned, member, *weights = pl.pallas_call(
             functools.partial(gather_kernel, base=base),
             out_shape=[
                 jax.ShapeDtypeStruct((features, span), jnp.bfloat16),
                 jax.ShapeDtypeStruct((span, LANES), jnp.bfloat16),
-                jax.ShapeDtypeStruct((features, width), jnp.bfloat16),
-                jax.ShapeDtypeStruct((features, width), jnp.bfloat16),
+                *[jax.ShapeDtypeStruct((features, width), jnp.bfloat16)] * 4,
             ],
             in_specs=[vmem_spec()] + [any_spec()] * 2,
-            out_specs=[any_spec()] * 4,
+            out_specs=[any_spec()] * 6,
             scratch_shapes=[
                 pltpu.VMEM((features, span), jnp.bfloat16),
                 pltpu.VMEM((span, LANES), jnp.bfloat16),
@@ -584,7 +583,7 @@
                 pltpu.SemaphoreType.DMA((blocks,)),
                 pltpu.SemaphoreType.DMA,
                 pltpu.SemaphoreType.DMA((2,)),
-                pltpu.SemaphoreType.DMA((2,)),
+                pltpu.SemaphoreType.DMA((4,)),
             ],
             compiler_params=params,
             name="gather",
@@ -596,9 +595,8 @@
         def narrow(x):
             return x.astype(jnp.bfloat16)
 
-        core1 = lax.ppermute(narrow(product(turned, weight1)), "dp", other_core)
-        own1 = lax.optimization_barrier(narrow(product(turned, weight0)))
-        chip1 = narrow(own1.astype(jnp.float32) + core1.astype(jnp.float32))
+        core1 = lax.ppermute(narrow(product(turned, weights[3])), "dp", other_core)
+        chip1 = narrow(product(turned, weights[1]) + core1.astype(jnp.float32))
         far = lax.ppermute(chip1, "dp", other_y)
         turned, _ = lax.optimization_barrier((turned, chip1))
         extra = pl.pallas_call(
@@ -629,8 +627,8 @@
         sent = narrow(jnp.concatenate([chip, inputs[ROWS:]]))
         sent = lax.ppermute(sent, "dp", other_y).astype(jnp.float32)
         extra = jnp.concatenate([chip, inputs[0:ROWS]]) + sent
-        core0 = lax.ppermute(narrow(product(turned, columns(1, 0))), "dp", other_core)
-        own0 = narrow(product(turned, columns(0, 0)))
+        core0 = lax.ppermute(narrow(product(turned, weights[2])), "dp", other_core)
+        own0 = narrow(product(turned, weights[0]))
         return own0, core0, far, extra, member
 
     first = project(0, FIRST)

time: 68.1 us -> 65 us (0.954)
  waiting for transfers between devices: 18.1 us -> 22.3 us
  matrix products: 6.67 us -> 3.3 us
  other arithmetic: 4.61 us -> 1.35 us
  starting transfers between devices: 14.2 us -> 13.3 us
    dot_general x4, matrix products: 6.67 us -> 3.3 us  [mm(): return lax.dot_general(a, b, dims, preferred_element_type=jnp.float32)]
    convert_element_type x1 -> x0, other arithmetic: 2.38 us -> none  [narrow(): return x.astype(jnp.bfloat16)]
    ppermute x6, waiting for transfers between devices: 6.23 us -> 8.28 us  [exchange(): return [x] + [lax.ppermute(x, axis, step) for step in steps][::-1]]
    ppermute x2, waiting for transfers between devices: 0.3 us -> 1.63 us  [the longest x1 1.63 us: project(): core1 = lax.ppermute(narrow(product(turned, weights[3])), 'dp', other_core)]
    ppermute x1, starting transfers between devices: 2.7 us -> 1.78 us  [split_body(): far_side = lax.ppermute(sent, 'group', [(0, 1), (1, 0)])]
    convert_element_type x1, other arithmetic: 0.9 us -> 0.01 us  [project(): across = lax.ppermute(extra, 'dp', other_core).astype(jnp.float32)]
  transfers between devices with their start and end apart: 14 -> 14, of which waited for: 8 -> 8; matrix products, arithmetic and copies ran while one was open for 12% -> 6% of each run, Pallas kernels for 0% -> 2%
where the time goes in v18:
time: 65 us; the launch traced here: 64.9 us
  waiting for transfers between devices  22.3 us (34%)
  Pallas kernels  20.3 us (31%)
  starting transfers between devices  13.3 us (20%)
  matrix products  3.3 us (5%)
  local copies, waits for them, and re-layouts  2.13 us (3%)
  between operations  2.1 us (3%)
  other arithmetic  1.35 us (2%)
    pallas_call x1, Pallas kernels, project(): pl.pallas_call(functools.partial(gather_kernel, base=base), out_shape=[ja...  14.7 us
    ppermute x6, waiting for transfers between devices, exchange(): return [x] + [lax.ppermute(x, axis, step) for step in steps][::-1]  8.28 us
    ppermute x1, waiting for transfers between devices, project(): sent = lax.ppermute(sent, 'dp', other_y).astype(jnp.float32)  8.19 us
    ppermute x6, starting transfers between devices, exchange(): return [x] + [lax.ppermute(x, axis, step) for step in steps][::-1]  6.28 us
    dot_general x4, matrix products, mm(): return lax.dot_general(a, b, dims, preferred_element_type=jnp.float32)  3.3 us
    pallas_call x1, Pallas kernels, split_body(): pl.pallas_call(functools.partial(pool_kernel, model_width=float(features...  3.1 us
    ppermute x1, waiting for transfers between devices, split_body(): far_side = lax.ppermute(sent, 'group', [(0, 1), (1, 0)])  2.99 us
    ppermute x1, starting transfers between devices, project(): far = lax.ppermute(chip1, 'dp', other_y)  2.96 us
  transfers between devices with their start and end apart: 14, of which 8 were waited for; matrix products, arithmetic and copies ran while one was open for 6% of the time, Pallas kernels for 2%

profile of v18, /device:TPU:0, one launch (start us, length us, event | category | flops | bytes accessed | tf_op | source)
XLA Modules:
  0.0 64.9 jit_solution(13596954868012086920)
XLA Ops:
  0.6 0.7 %copy.12 = s32[1,12,128]{2,1,0:T(8,128)S(1)} copy(s32[1,12,128]{2,0,1:T(1,128)} %param.9) | data formatting | bytes 12288
  1.3 14.7 %gather.3 = (bf16[1024,1152]{1,0:T(8,128)(2,1)S(1)}, bf16[1152,128]{1,0:T(8,128)(2,1)S(1)}, bf16[1024,256]{1,0:T(8,128)(2,1)S(1)}, bf16[1024,256]{1,0:T(8,128)(2...) custom-call(s32[12,128]{1,0:T(8,128)S(1)} %bitcast.19, bf16[1024,16384]{1,0:T(8,128)(2,1)} %vocab_ref.1, ...), custom_call_target="tpu_custom_call" | custom-call | tf_op jit(solution)/shard_map/gather/pallas_call | solution.py:566
  16.0 0.8 %convolution_convert_fusion.5 = bf16[1152,256]{1,0:T(8,128)(2,1)S(1)} fusion(bf16[1024,1152]{1,0:T(8,128)(2,1)S(1)} %get-tuple-element.50.turned_any, bf16[1024,256]{1,0:T(8,128)(2,1)S(1)} %get-tuple-element.49), kind=kOutput, calls=%fused_computation.11 | convolution fusion | flops 604274688 | bytes 3473408 | tf_op jit(solution)/shard_map/dot_general | solution.py:128
  17.4 1.6 %collective-permute-done.5 = bf16[1152,256]{1,0:T(8,128)(2,1)S(1)} collective-permute-done((bf16[1152,256]{1,0:T(8,128)(2,1)S(1)}, bf16[1152,256]{1,0:T(8,128)(2,1)S(1)}, u32[]{:S(2)}, u32[]{:S(2)}) %collective-permute-start.5) | collective-permute-done | bytes 589856 | tf_op jit(solution)/shard_map/ppermute | solution.py:598
  19.0 0.8 %add_convert_fusion.1 = bf16[1152,256]{1,0:T(8,128)(2,1)S(1)} fusion(bf16[1152,256]{1,0:T(8,128)(2,1)S(1)} %collective-permute-done.5, bf16[1024,1152]{1,0:T(8,128)(2,1)S(1)} %get-tuple-element.50.turned_any, bf16[1024,256]{1,0:T(8,128)(2,1)S(1)} %get-tuple-element.48), kind=kOutput, calls=%fused_computation.12 | convolution fusion | flops 604864512 | bytes 4063232 | tf_op jit(solution)/shard_map/dot_general | solution.py:128
  19.8 3.0 %collective-permute-start.7 = (bf16[1152,256]{1,0:T(8,128)(2,1)S(1)}, bf16[1152,256]{1,0:T(8,128)(2,1)S(1)}, u32[]{:S(2)}, u32[]{:S(2)}) collective-permute-start(bf16[1152,256]{1,0:T(8,128)(2,1)S(1)} %add_convert_fusion.1), channel_id=1, source_target_pairs={{0,8},{4,12},{8,0},{12,4},{1,9},{5,13},{9,1},{13,5},{2,10},{6,14},... | collective-permute-start | bytes 1769480 | tf_op jit(solution)/shard_map/ppermute | solution.py:600
  22.8 1.4 %statistics.3 = bf16[160,256]{1,0:T(8,128)(2,1)S(1)} custom-call(bf16[1024,1152]{1,0:T(8,128)(2,1)S(1)} %get-tuple-element.50.turned_any, bf16[1152,128]{1,0:T(8,128)(2,1)S(1)} %get-tuple-element.53.member_any.member_ref, s32[3,7]{1,0:T(4,128)S(1)} %copy-done.4, bf16[16,4096]{1,0:T(8,128)(2,1)S(1)} %copy-done.3), custom_call_target="tpu_custom_call" | custom-call | flops 339738624 | bytes 2359296 | tf_op jit(solution)/shard_map/statistics/pallas_call | solution.py:602
  24.3 0.8 %convolution_convert_fusion.4.own_ref = bf16[1152,256]{1,0:T(8,128)(2,1)S(1)} fusion(bf16[1024,1152]{1,0:T(8,128)(2,1)S(1)} %get-tuple-element.50.turned_any, bf16[1024,256]{1,0:T(8,128)(2,1)S(1)} %get-tuple-element.51), kind=kOutput, calls=%fused_computation.10 | convolution fusion | flops 604274688 | bytes 3473408 | tf_op jit(solution)/shard_map/dot_general | solution.py:128
  25.1 0.8 %convolution_convert_fusion.3 = bf16[1152,256]{1,0:T(8,128)(2,1)S(1)} fusion(bf16[1024,1152]{1,0:T(8,128)(2,1)S(1)} %get-tuple-element.50.turned_any, bf16[1024,256]{1,0:T(8,128)(2,1)S(1)} %get-tuple-element.52), kind=kOutput, calls=%fused_computation.9 | convolution fusion | flops 604274688 | bytes 3473408 | tf_op jit(solution)/shard_map/dot_general | solution.py:128
  27.3 1.4 %conditional.1 = (bf16[384,256]{1,0:T(8,128)(2,1)S(1)}, bf16[384,256]{1,0:T(8,128)(2,1)}, bf16[384,256]{1,0:T(8,128)(2,1)}, f32[64,256]{1,0:T(8,128)S(1)}, bf16[384,128]{1,0:T(8,128)(2,1)S(1)}) conditional(s32[]{:T(128)} %convert_element_type.65, () %tuple.22, (s32[12,128]{1,0:T(8,128)S(1)}, bf16[1024,16384]{1,0:T(8,128)(2,1)}, ...), branch_computations={%region_1.0_spmd, %region_2.0_spmd} | conditional | flops 919347200 | bytes 11411752 | solution.py:639
  29.5 8.2 %collective-permute-done.9 = bf16[112,256]{1,0:T(8,128)(2,1)S(1)} collective-permute-done((bf16[112,256]{1,0:T(8,128)(2,1)S(1)}, bf16[112,256]{1,0:T(8,128)(2,1)S(1)}, u32[]{:S(2)}, u32[]{:S(2)}) %collective-permute-start.9) | collective-permute-done | bytes 57376 | tf_op jit(solution)/shard_map/ppermute | solution.py:628
  37.7 3.1 %pool.1 = (bf16[208,256]{1,0:T(8,128)(2,1)S(1)}, f32[16,256]{1,0:T(8,128)S(1)}) custom-call(s32[12,128]{1,0:T(8,128)S(1)} %bitcast.22, bf16[1152,256]{1,0:T(8,128)(2,1)S(1)} %convolution_convert_fusion.4.own_ref, bf16[1152,256]{1,0:T(8,128)(2,1)S(1)} %collective-permute-done.6.core_any, bf16[1152,256]{1,0:T(8,128)(2,1)S(1)} %collective-permute-done.7.far_any, ...), custom_call_target="tpu_custom_call" | custom-call | tf_op jit(solution)/shard_map/pool/pallas_call | solution.py:644
  40.8 1.8 %collective-permute-start.10 = (bf16[208,256]{1,0:T(8,128)(2,1)S(1)}, bf16[208,256]{1,0:T(8,128)(2,1)S(1)}, u32[]{:S(2)}, u32[]{:S(2)}) collective-permute-start(bf16[208,256]{1,0:T(8,128)(2,1)S(1)} %get-tuple-element.60.near_ref), channel_id=1, source_target_pairs={{0,16},{16,0},{1,17},{17,1},{2,18},{18,2},{3,19},{19,3},{4,20},{20... | collective-permute-start | bytes 319496 | tf_op jit(solution)/shard_map/ppermute | solution.py:663
  42.6 3.0 %collective-permute-done.10.far_ref = bf16[208,256]{1,0:T(8,128)(2,1)S(1)} collective-permute-done((bf16[208,256]{1,0:T(8,128)(2,1)S(1)}, bf16[208,256]{1,0:T(8,128)(2,1)S(1)}, u32[]{:S(2)}, u32[]{:S(2)}) %collective-permute-start.10) | collective-permute-done | bytes 106528 | tf_op jit(solution)/shard_map/ppermute | solution.py:663
  45.7 1.8 %collective-permute-start.12 = (f32[96,128]{1,0:T(8,128)S(1)}, f32[96,128]{1,0:T(8,128)S(1)}, u32[]{:S(2)}, u32[]{:S(2)}) collective-permute-start(f32[96,128]{1,0:T(8,128)S(1)} %get-tuple-element.61.refs_0_), channel_id=1, source_target_pairs={{0,8},{4,12},{8,0},{12,4},{1,9},{5,13},{9,1},{13,5},{2,10},{6,14},... | collective-permute-start | bytes 147464 | tf_op jit(solution)/shard_map/ppermute | solution.py:536
  47.6 2.3 %collective-permute-done.12.refs_2_ = f32[96,128]{1,0:T(8,128)S(1)} collective-permute-done((f32[96,128]{1,0:T(8,128)S(1)}, f32[96,128]{1,0:T(8,128)S(1)}, u32[]{:S(2)}, u32[]{:S(2)}) %collective-permute-start.12) | collective-permute-done | bytes 49184 | tf_op jit(solution)/shard_map/ppermute | solution.py:536
  49.9 1.4 %collective-permute-done.13.refs_3_ = f32[96,128]{1,0:T(8,128)S(1)} collective-permute-done((f32[96,128]{1,0:T(8,128)S(1)}, f32[96,128]{1,0:T(8,128)S(1)}, u32[]{:S(2)}, u32[]{:S(2)}) %collective-permute-start.13) | collective-permute-done | bytes 49184 | tf_op jit(solution)/shard_map/ppermute | solution.py:536
  51.3 1.1 %collective-permute-start.14 = (bf16[384,256]{1,0:T(8,128)(2,1)S(1)}, bf16[384,256]{1,0:T(8,128)(2,1)S(1)}, u32[]{:S(2)}, u32[]{:S(2)}) collective-permute-start(bf16[384,256]{1,0:T(8,128)(2,1)S(1)} %get-tuple-element.63.refs_4_), channel_id=1, source_target_pairs={{0,8},{4,12},{8,0},{12,4},{1,9},{5,13},{9,1},{13,5},{2,10},{6,14},... | collective-permute-start | bytes 589832 | tf_op jit(solution)/shard_map/ppermute | solution.py:681
  52.3 1.6 %collective-permute-start.15 = (f32[32,128]{1,0:T(8,128)S(1)}, f32[32,128]{1,0:T(8,128)S(1)}, u32[]{:S(2)}, u32[]{:S(2)}) collective-permute-start(f32[32,128]{1,0:T(8,128)S(1)} %fusion.refs_6_), channel_id=1, source_target_pairs={{0,1},{1,0},{2,3},{3,2},{4,5},{5,4},{6,7},{7,6},{8,9},{9,8},{10,11... | collective-permute-start | bytes 49160 | tf_op jit(solution)/shard_map/ppermute | solution.py:536
  53.9 2.6 %collective-permute-start.16 = (f32[32,128]{1,0:T(8,128)S(1)}, f32[32,128]{1,0:T(8,128)S(1)}, u32[]{:S(2)}, u32[]{:S(2)}) collective-permute-start(f32[32,128]{1,0:T(8,128)S(1)} %fusion.refs_6_), channel_id=1, source_target_pairs={{0,2},{1,3},{2,0},{3,1},{4,6},{5,7},{6,4},{7,5},{8,10},{9,11},{10,... | collective-permute-start | bytes 49160 | tf_op jit(solution)/shard_map/ppermute | solution.py:536
  57.4 1.4 %collective-permute-done.16.refs_8_ = f32[32,128]{1,0:T(8,128)S(1)} collective-permute-done((f32[32,128]{1,0:T(8,128)S(1)}, f32[32,128]{1,0:T(8,128)S(1)}, u32[]{:S(2)}, u32[]{:S(2)}) %collective-permute-start.16) | collective-permute-done | bytes 16416 | tf_op jit(solution)/shard_map/ppermute | solution.py:536
  58.8 3.3 %collective-permute-done.17.refs_9_ = f32[32,128]{1,0:T(8,128)S(1)} collective-permute-done((f32[32,128]{1,0:T(8,128)S(1)}, f32[32,128]{1,0:T(8,128)S(1)}, u32[]{:S(2)}, u32[]{:S(2)}) %collective-permute-start.17) | collective-permute-done | bytes 16416 | tf_op jit(solution)/shard_map/ppermute | solution.py:536
  62.0 1.0 %score.1 = (bf16[1,3,1024]{2,1,0:T(4,128)(2,1)}, f32[1,3]{1,0:T(1,128)}, f32[16,512]{1,0:T(8,128)S(1)}) custom-call(f32[96,128]{1,0:T(8,128)S(1)} %get-tuple-element.61.refs_0_, f32[96,128]{1,0:T(8,128)S(1)} %collective-permute-done.11.refs_1_, f32[96,128]{1,0:T(8,128)S(1)} %collective-permute-done.12.refs_2_, ...), custom_call_target="tpu_custom_call" | custom-call | tf_op jit(solution)/shard_map/score/pallas_call | solution.py:682
  63.0 1.2 %collective-permute-done.18 = f32[16,512]{1,0:T(8,128)S(1)} collective-permute-done((f32[16,512]{1,0:T(8,128)S(1)}, f32[16,512]{1,0:T(8,128)S(1)}, u32[]{:S(2)}, u32[]{:S(2)}) %collective-permute-start.18) | collective-permute-done | bytes 32800 | tf_op jit(solution)/shard_map/ppermute | solution.py:696
  (38 shorter events, 4.5 us)
Async XLA Ops:
  16.9 2.1 %collective-permute-start.5 = (bf16[1152,256]{1,0:T(8,128)(2,1)S(1)}, bf16[1152,256]{1,0:T(8,128)(2,1)S(1)}, u32[]{:S(2)}, u32[]{:S(2)}) collective-permute-start(bf16[1152,256]{1,0:T(8,128)(2,1)S(1)} %convolution_convert_fusion.5), channel_id=1, source_target_pairs={{0,4},{4,0},{8,12},{12,8},{1,5},{5,1},{9,13},{13,9},{2,6},{6,2},{1... | collective-permute-start | bytes 1769480 | tf_op jit(solution)/shard_map/ppermute | solution.py:598
  19.0 3.8 %copy-start.3 = (bf16[16,4096]{1,0:T(8,128)(2,1)S(1)}, bf16[16,4096]{1,0:T(8,128)(2,1)}, u32[]{:S(2)}) copy-start(bf16[16,4096]{1,0:T(8,128)(2,1)} %lower_ref.1) | copy-start | bytes 393220
  19.0 3.8 %copy-start.4 = (s32[3,7]{1,0:T(4,128)S(1)}, s32[3,7]{1,0:T(4,128)}, u32[]{:S(2)}) copy-start(s32[3,7]{1,0:T(4,128)} %hard_ref.1) | copy-start | bytes 256
  19.8 17.8 %collective-permute-start.7 = (bf16[1152,256]{1,0:T(8,128)(2,1)S(1)}, bf16[1152,256]{1,0:T(8,128)(2,1)S(1)}, u32[]{:S(2)}, u32[]{:S(2)}) collective-permute-start(bf16[1152,256]{1,0:T(8,128)(2,1)S(1)} %add_convert_fusion.1), channel_id=1, source_target_pairs={{0,8},{4,12},{8,0},{12,4},{1,9},{5,13},{9,1},{13,5},{2,10},{6,14},... | collective-permute-start | bytes 1769480 | tf_op jit(solution)/shard_map/ppermute | solution.py:600
  24.2 5.1 %collective-permute-start.8 = (bf16[160,256]{1,0:T(8,128)(2,1)S(1)}, bf16[160,256]{1,0:T(8,128)(2,1)S(1)}, u32[]{:S(2)}, u32[]{:S(2)}) collective-permute-start(bf16[160,256]{1,0:T(8,128)(2,1)S(1)} %statistics.3), channel_id=1, source_target_pairs={{0,4},{4,0},{8,12},{12,8},{1,5},{5,1},{9,13},{13,9},{2,6},{6,2},{1... | collective-permute-start | bytes 245768 | tf_op jit(solution)/shard_map/ppermute | solution.py:624
  27.3 10.4 %copy-start = (bf16[16,1024]{1,0:T(8,128)(2,1)S(1)}, bf16[16,1024]{1,0:T(8,128)(2,1)}, u32[]{:S(2)}) copy-start(bf16[16,1024]{1,0:T(8,128)(2,1)} %raise_ref.1) | copy-start | bytes 98308
  28.7 9.0 %collective-permute-start.6 = (bf16[1152,256]{1,0:T(8,128)(2,1)S(1)}, bf16[1152,256]{1,0:T(8,128)(2,1)S(1)}, u32[]{:S(2)}, u32[]{:S(2)}) collective-permute-start(bf16[1152,256]{1,0:T(8,128)(2,1)S(1)} %convolution_convert_fusion.3), channel_id=1, source_target_pairs={{0,4},{4,0},{8,12},{12,8},{1,5},{5,1},{9,13},{13,9},{2,6},{6,2},{1... | collective-permute-start | bytes 1769480 | tf_op jit(solution)/shard_map/ppermute | solution.py:630
  29.4 8.3 %collective-permute-start.9 = (bf16[112,256]{1,0:T(8,128)(2,1)S(1)}, bf16[112,256]{1,0:T(8,128)(2,1)S(1)}, u32[]{:S(2)}, u32[]{:S(2)}) collective-permute-start(bf16[112,256]{1,0:T(8,128)(2,1)S(1)} %pad_maximum_fusion.2), channel_id=1, source_target_pairs={{0,8},{4,12},{8,0},{12,4},{1,9},{5,13},{9,1},{13,5},{2,10},{6,14},... | collective-permute-start | bytes 172040 | tf_op jit(solution)/shard_map/ppermute | solution.py:628
  40.8 4.8 %collective-permute-start.10 = (bf16[208,256]{1,0:T(8,128)(2,1)S(1)}, bf16[208,256]{1,0:T(8,128)(2,1)S(1)}, u32[]{:S(2)}, u32[]{:S(2)}) collective-permute-start(bf16[208,256]{1,0:T(8,128)(2,1)S(1)} %get-tuple-element.60.near_ref), channel_id=1, source_target_pairs={{0,16},{16,0},{1,17},{17,1},{2,18},{18,2},{3,19},{19,3},{4,20},{20... | collective-permute-start | bytes 319496 | tf_op jit(solution)/shard_map/ppermute | solution.py:663
  45.7 1.9 %collective-permute-start.11 = (f32[96,128]{1,0:T(8,128)S(1)}, f32[96,128]{1,0:T(8,128)S(1)}, u32[]{:S(2)}, u32[]{:S(2)}) collective-permute-start(f32[96,128]{1,0:T(8,128)S(1)} %get-tuple-element.61.refs_0_), channel_id=1, source_target_pairs={{0,4},{4,0},{8,12},{12,8},{1,5},{5,1},{9,13},{13,9},{2,6},{6,2},{1... | collective-permute-start | bytes 147464 | tf_op jit(solution)/shard_map/ppermute | solution.py:536
  45.7 4.2 %collective-permute-start.12 = (f32[96,128]{1,0:T(8,128)S(1)}, f32[96,128]{1,0:T(8,128)S(1)}, u32[]{:S(2)}, u32[]{:S(2)}) collective-permute-start(f32[96,128]{1,0:T(8,128)S(1)} %get-tuple-element.61.refs_0_), channel_id=1, source_target_pairs={{0,8},{4,12},{8,0},{12,4},{1,9},{5,13},{9,1},{13,5},{2,10},{6,14},... | collective-permute-start | bytes 147464 | tf_op jit(solution)/shard_map/ppermute | solution.py:536
  47.5 3.7 %collective-permute-start.13 = (f32[96,128]{1,0:T(8,128)S(1)}, f32[96,128]{1,0:T(8,128)S(1)}, u32[]{:S(2)}, u32[]{:S(2)}) collective-permute-start(f32[96,128]{1,0:T(8,128)S(1)} %get-tuple-element.61.refs_0_), channel_id=1, source_target_pairs={{0,12},{4,8},{8,4},{12,0},{1,13},{5,9},{9,5},{13,1},{2,14},{6,10},... | collective-permute-start | bytes 147464 | tf_op jit(solution)/shard_map/ppermute | solution.py:536
  51.3 10.8 %collective-permute-start.14 = (bf16[384,256]{1,0:T(8,128)(2,1)S(1)}, bf16[384,256]{1,0:T(8,128)(2,1)S(1)}, u32[]{:S(2)}, u32[]{:S(2)}) collective-permute-start(bf16[384,256]{1,0:T(8,128)(2,1)S(1)} %get-tuple-element.63.refs_4_), channel_id=1, source_target_pairs={{0,8},{4,12},{8,0},{12,4},{1,9},{5,13},{9,1},{13,5},{2,10},{6,14},... | collective-permute-start | bytes 589832 | tf_op jit(solution)/shard_map/ppermute | solution.py:681
  52.3 5.0 %collective-permute-start.15 = (f32[32,128]{1,0:T(8,128)S(1)}, f32[32,128]{1,0:T(8,128)S(1)}, u32[]{:S(2)}, u32[]{:S(2)}) collective-permute-start(f32[32,128]{1,0:T(8,128)S(1)} %fusion.refs_6_), channel_id=1, source_target_pairs={{0,1},{1,0},{2,3},{3,2},{4,5},{5,4},{6,7},{7,6},{8,9},{9,8},{10,11... | collective-permute-start | bytes 49160 | tf_op jit(solution)/shard_map/ppermute | solution.py:536
  53.9 4.9 %collective-permute-start.16 = (f32[32,128]{1,0:T(8,128)S(1)}, f32[32,128]{1,0:T(8,128)S(1)}, u32[]{:S(2)}, u32[]{:S(2)}) collective-permute-start(f32[32,128]{1,0:T(8,128)S(1)} %fusion.refs_6_), channel_id=1, source_target_pairs={{0,2},{1,3},{2,0},{3,1},{4,6},{5,7},{6,4},{7,5},{8,10},{9,11},{10,... | collective-permute-start | bytes 49160 | tf_op jit(solution)/shard_map/ppermute | solution.py:536
  56.5 5.5 %collective-permute-start.17 = (f32[32,128]{1,0:T(8,128)S(1)}, f32[32,128]{1,0:T(8,128)S(1)}, u32[]{:S(2)}, u32[]{:S(2)}) collective-permute-start(f32[32,128]{1,0:T(8,128)S(1)} %fusion.refs_6_), channel_id=1, source_target_pairs={{0,3},{1,2},{2,1},{3,0},{4,7},{5,6},{6,5},{7,4},{8,11},{9,10},{10,... | collective-permute-start | bytes 49160 | tf_op jit(solution)/shard_map/ppermute | solution.py:536
  63.0 1.2 %collective-permute-start.18 = (f32[16,512]{1,0:T(8,128)S(1)}, f32[16,512]{1,0:T(8,128)S(1)}, u32[]{:S(2)}, u32[]{:S(2)}) collective-permute-start(f32[16,512]{1,0:T(8,128)S(1)} %get-tuple-element.68), channel_id=1, source_target_pairs={{0,4},{4,0},{8,12},{12,8},{1,5},{5,1},{9,13},{13,9},{2,6},{6,2},{1... | collective-permute-start | bytes 98312 | tf_op jit(solution)/shard_map/ppermute | solution.py:696

commit v19 on v18

--- a/solution.py
+++ b/solution.py
@@ -159,6 +159,10 @@
     return lax.gather(x, lanes[..., None], numbers, slice_sizes=(1, 1), mode=mode)
 
 
+def load_ids(ref):
+    return jnp.concatenate([ref[text] for text in range(ref.shape[0])], axis=0)
+
+
 def fetch(pairs, sems):
     copies = [pltpu.make_async_copy(a, b, sems.at[n]) for n, (a, b) in enumerate(pairs)]
     for copy in copies:
@@ -181,6 +185,7 @@
     member_ref,
     held,
     token_ref,
+    plain_ids,
     ranks,
     counted,
     bounds,
@@ -190,7 +195,7 @@
     weight_sems,
     base,
 ):
-    texts, length = ids_ref.shape
+    texts, _, length = ids_ref.shape
     features, vocab = vocab_ref.shape
     blocks = vocab // IDS_PER_BLOCK
     groups = vocab // IDS_PER_GROUP
@@ -214,7 +219,9 @@
     for copy in weight_copies:
         copy.start()
 
-    ids = ids_ref[...]
+    for text in range(texts):
+        plain_ids[pl.ds(text, 1), :] = ids_ref[text]
+    ids = plain_ids[...]
     valid = ids != 0
     group_of = jnp.where(valid, lax.shift_right_logical(ids, GROUP_BITS), groups)
     group_rows = counted.shape[0]
@@ -368,7 +375,7 @@
     sems,
     model_width,
 ):
-    texts, length = ids_ref.shape
+    texts = ids_ref.shape[0]
     width = own_ref.shape[1]
     quarter = quarter_of(lax.axis_index("dp"))
     fetch([(core_any, core_ref), (far_any, far_ref)], sems)
@@ -409,7 +416,7 @@
         total[...] += extra_ref[(stripes + 1) * ROWS : (stripes + 2) * ROWS, :]
 
     add((own_ref, core_ref, far_ref), extra_ref, member_ref, 0)
-    real = (ids_ref[...] != 0).astype(jnp.float32)
+    real = (load_ids(ids_ref) != 0).astype(jnp.float32)
 
     @pl.when(jnp.sum(real) > member_ref.shape[0])
     def _():
@@ -532,8 +539,8 @@
 
 
 def exchange(x, axis, size):
-    steps = [[(i, i ^ o) for i in range(size)] for o in reversed(range(1, size))]
-    return [x] + [lax.ppermute(x, axis, step) for step in steps][::-1]
+    steps = [[(i, i ^ o) for i in range(size)] for o in range(1, size)]
+    return [x] + [lax.ppermute(x, axis, step) for step in steps]
 
 
 def split_body(
@@ -546,8 +553,8 @@
     logit_sharpness,
 ):
     shards, parts = lax.axis_size("dp"), lax.axis_size("mp")
-    ids = query_passage_words[0]
-    texts, length = ids.shape
+    texts, length = query_passage_words.shape[1:]
+    ids = query_passage_words.reshape(texts, 1, length)
     tokens = texts * length
     features, vocab = vocabulary_vectors.shape
     blocks = vocab // IDS_PER_BLOCK
@@ -577,6 +584,7 @@
                 pltpu.VMEM((span, LANES), jnp.bfloat16),
                 pltpu.VMEM((blocks, features, IDS_PER_BLOCK), jnp.bfloat16),
                 pltpu.VMEM((8 * pl.cdiv(span // LANES, 8), LANES), jnp.int32),
+                pltpu.VMEM((texts, length), jnp.int32),
                 pltpu.VMEM((texts, length), jnp.float32),
                 pltpu.VMEM((group_rows, length), jnp.int32),
                 pltpu.SMEM((group_rows, length), jnp.int32),

time: 65 us -> 65.3 us (level)
  Pallas kernels: 20.3 us -> 21 us
  local copies, waits for them, and re-layouts: 2.13 us -> 1.45 us
    pallas_call x1, Pallas kernels: 14.7 us -> 15.4 us  [project(): pl.pallas_call(functools.partial(gather_kernel, base=base), out_shape=[ja...]
    unnamed x7 -> x8, local copies, waits for them, and re-layouts: 0.71 us -> 0.02 us
where the time goes in v19:
time: 65.3 us; the launch traced here: 65 us
  waiting for transfers between devices  21.8 us (33%)
  Pallas kernels  21 us (32%)
  starting transfers between devices  13.9 us (21%)
  matrix products  3.3 us (5%)
  between operations  2.12 us (3%)
  local copies, waits for them, and re-layouts  1.45 us (2%)
  other arithmetic  1.36 us (2%)
    pallas_call x1, Pallas kernels, project(): pl.pallas_call(functools.partial(gather_kernel, base=base), out_shape=[ja...  15.4 us
    ppermute x1, waiting for transfers between devices, project(): sent = lax.ppermute(sent, 'dp', other_y).astype(jnp.float32)  8.15 us
    ppermute x6, waiting for transfers between devices, exchange(): return [x] + [lax.ppermute(x, axis, step) for step in steps]  8.09 us
    ppermute x6, starting transfers between devices, exchange(): return [x] + [lax.ppermute(x, axis, step) for step in steps]  6.25 us
    dot_general x4, matrix products, mm(): return lax.dot_general(a, b, dims, preferred_element_type=jnp.float32)  3.3 us
    pallas_call x1, Pallas kernels, split_body(): pl.pallas_call(functools.partial(pool_kernel, model_width=float(features...  3.1 us
    ppermute x1, starting transfers between devices, project(): far = lax.ppermute(chip1, 'dp', other_y)  2.96 us
    ppermute x1, waiting for transfers between devices, split_body(): far_side = lax.ppermute(sent, 'group', [(0, 1), (1, 0)])  2.68 us
  transfers between devices with their start and end apart: 14, of which 8 were waited for; matrix products, arithmetic and copies ran while one was open for 6% of the time, Pallas kernels for 2%

profile of v19, /device:TPU:0, one launch (start us, length us, event | category | flops | bytes accessed | tf_op | source)
XLA Modules:
  0.0 65.0 jit_solution(5117482272605649220)
XLA Ops:
  0.6 15.4 %gather.3 = (bf16[1024,1152]{1,0:T(8,128)(2,1)S(1)}, bf16[1152,128]{1,0:T(8,128)(2,1)S(1)}, bf16[1024,256]{1,0:T(8,128)(2,1)S(1)}, bf16[1024,256]{1,0:T(8,128)(2...) custom-call(s32[12,1,128]{2,1,0:T(1,128)} %bitcast.17, bf16[1024,16384]{1,0:T(8,128)(2,1)} %vocab_ref.1, ...), custom_call_target="tpu_custom_call" | custom-call | tf_op jit(solution)/shard_map/gather/pallas_call | solution.py:573
  16.0 0.8 %convolution_convert_fusion.5 = bf16[1152,256]{1,0:T(8,128)(2,1)S(1)} fusion(bf16[1024,1152]{1,0:T(8,128)(2,1)S(1)} %get-tuple-element.50.turned_any, bf16[1024,256]{1,0:T(8,128)(2,1)S(1)} %get-tuple-element.49), kind=kOutput, calls=%fused_computation.11 | convolution fusion | flops 604274688 | bytes 3473408 | tf_op jit(solution)/shard_map/dot_general | solution.py:128
  17.4 1.6 %collective-permute-done.5 = bf16[1152,256]{1,0:T(8,128)(2,1)S(1)} collective-permute-done((bf16[1152,256]{1,0:T(8,128)(2,1)S(1)}, bf16[1152,256]{1,0:T(8,128)(2,1)S(1)}, u32[]{:S(2)}, u32[]{:S(2)}) %collective-permute-start.5) | collective-permute-done | bytes 589856 | tf_op jit(solution)/shard_map/ppermute | solution.py:606
  19.0 0.8 %add_convert_fusion.1 = bf16[1152,256]{1,0:T(8,128)(2,1)S(1)} fusion(bf16[1152,256]{1,0:T(8,128)(2,1)S(1)} %collective-permute-done.5, bf16[1024,1152]{1,0:T(8,128)(2,1)S(1)} %get-tuple-element.50.turned_any, bf16[1024,256]{1,0:T(8,128)(2,1)S(1)} %get-tuple-element.48), kind=kOutput, calls=%fused_computation.12 | convolution fusion | flops 604864512 | bytes 4063232 | tf_op jit(solution)/shard_map/dot_general | solution.py:128
  19.9 3.0 %collective-permute-start.7 = (bf16[1152,256]{1,0:T(8,128)(2,1)S(1)}, bf16[1152,256]{1,0:T(8,128)(2,1)S(1)}, u32[]{:S(2)}, u32[]{:S(2)}) collective-permute-start(bf16[1152,256]{1,0:T(8,128)(2,1)S(1)} %add_convert_fusion.1), channel_id=1, source_target_pairs={{0,8},{4,12},{8,0},{12,4},{1,9},{5,13},{9,1},{13,5},{2,10},{6,14},... | collective-permute-start | bytes 1769480 | tf_op jit(solution)/shard_map/ppermute | solution.py:608
  22.8 1.4 %statistics.3 = bf16[160,256]{1,0:T(8,128)(2,1)S(1)} custom-call(bf16[1024,1152]{1,0:T(8,128)(2,1)S(1)} %get-tuple-element.50.turned_any, bf16[1152,128]{1,0:T(8,128)(2,1)S(1)} %get-tuple-element.53.member_any.member_ref, s32[3,7]{1,0:T(4,128)S(1)} %copy-done.5, bf16[16,4096]{1,0:T(8,128)(2,1)S(1)} %copy-done.3), custom_call_target="tpu_custom_call" | custom-call | flops 339738624 | bytes 2359296 | tf_op jit(solution)/shard_map/statistics/pallas_call | solution.py:610
  24.3 0.8 %convolution_convert_fusion.4.own_ref = bf16[1152,256]{1,0:T(8,128)(2,1)S(1)} fusion(bf16[1024,1152]{1,0:T(8,128)(2,1)S(1)} %get-tuple-element.50.turned_any, bf16[1024,256]{1,0:T(8,128)(2,1)S(1)} %get-tuple-element.51), kind=kOutput, calls=%fused_computation.10 | convolution fusion | flops 604274688 | bytes 3473408 | tf_op jit(solution)/shard_map/dot_general | solution.py:128
  25.2 0.8 %convolution_convert_fusion.3 = bf16[1152,256]{1,0:T(8,128)(2,1)S(1)} fusion(bf16[1024,1152]{1,0:T(8,128)(2,1)S(1)} %get-tuple-element.50.turned_any, bf16[1024,256]{1,0:T(8,128)(2,1)S(1)} %get-tuple-element.52), kind=kOutput, calls=%fused_computation.9 | convolution fusion | flops 604274688 | bytes 3473408 | tf_op jit(solution)/shard_map/dot_general | solution.py:128
  27.3 1.4 %conditional.1 = (bf16[384,256]{1,0:T(8,128)(2,1)S(1)}, bf16[384,256]{1,0:T(8,128)(2,1)}, bf16[384,256]{1,0:T(8,128)(2,1)}, f32[64,256]{1,0:T(8,128)S(1)}, bf16[384,128]{1,0:T(8,128)(2,1)S(1)}) conditional(s32[]{:T(128)} %convert_element_type.65, () %tuple.22, (s32[12,1,128]{2,1,0:T(1,128)S(1)}, bf16[1024,16384]{1,0:T(8,128)(2,1)}, ...), branch_computations={%region_1.0_spmd, %region_2.0_spmd} | conditional | flops 919347200 | bytes 11411752 | solution.py:647
  28.1 0.7 %broadcast.7.clone.1 = bf16[384,256]{1,0:T(8,128)(2,1)} broadcast(bf16[]{:T(256)} %constant.4.clone), dimensions={} | broadcast | bytes 196610 | tf_op jit(solution)/shard_map/broadcast.5
  29.5 8.1 %collective-permute-done.9 = bf16[112,256]{1,0:T(8,128)(2,1)S(1)} collective-permute-done((bf16[112,256]{1,0:T(8,128)(2,1)S(1)}, bf16[112,256]{1,0:T(8,128)(2,1)S(1)}, u32[]{:S(2)}, u32[]{:S(2)}) %collective-permute-start.9) | collective-permute-done | bytes 57376 | tf_op jit(solution)/shard_map/ppermute | solution.py:636
  37.7 3.1 %pool.1 = (bf16[208,256]{1,0:T(8,128)(2,1)S(1)}, f32[16,256]{1,0:T(8,128)S(1)}) custom-call(s32[12,1,128]{2,1,0:T(1,128)S(1)} %bitcast.20, bf16[1152,256]{1,0:T(8,128)(2,1)S(1)} %convolution_convert_fusion.4.own_ref, bf16[1152,256]{1,0:T(8,128)(2,1)S(1)} %collective-permute-done.6.core_any, bf16[1152,256]{1,0:T(8,128)(2,1)S(1)} %collective-permute-done.7.far_any, ...), custom_call_target="tpu_custom_call" | custom-call | tf_op jit(solution)/shard_map/pool/pallas_call | solution.py:652
  40.8 2.4 %collective-permute-start.10 = (bf16[208,256]{1,0:T(8,128)(2,1)S(1)}, bf16[208,256]{1,0:T(8,128)(2,1)S(1)}, u32[]{:S(2)}, u32[]{:S(2)}) collective-permute-start(bf16[208,256]{1,0:T(8,128)(2,1)S(1)} %get-tuple-element.60.near_ref), channel_id=1, source_target_pairs={{0,16},{16,0},{1,17},{17,1},{2,18},{18,2},{3,19},{19,3},{4,20},{20... | collective-permute-start | bytes 319496 | tf_op jit(solution)/shard_map/ppermute | solution.py:671
  43.2 2.7 %collective-permute-done.10.far_ref = bf16[208,256]{1,0:T(8,128)(2,1)S(1)} collective-permute-done((bf16[208,256]{1,0:T(8,128)(2,1)S(1)}, bf16[208,256]{1,0:T(8,128)(2,1)S(1)}, u32[]{:S(2)}, u32[]{:S(2)}) %collective-permute-start.10) | collective-permute-done | bytes 106528 | tf_op jit(solution)/shard_map/ppermute | solution.py:671
  46.0 1.6 %collective-permute-start.12 = (f32[96,128]{1,0:T(8,128)S(1)}, f32[96,128]{1,0:T(8,128)S(1)}, u32[]{:S(2)}, u32[]{:S(2)}) collective-permute-start(f32[96,128]{1,0:T(8,128)S(1)} %get-tuple-element.61.refs_0_), channel_id=1, source_target_pairs={{0,8},{4,12},{8,0},{12,4},{1,9},{5,13},{9,1},{13,5},{2,10},{6,14},... | collective-permute-start | bytes 147464 | tf_op jit(solution)/shard_map/ppermute | solution.py:543
  47.9 2.3 %collective-permute-done.12.refs_2_ = f32[96,128]{1,0:T(8,128)S(1)} collective-permute-done((f32[96,128]{1,0:T(8,128)S(1)}, f32[96,128]{1,0:T(8,128)S(1)}, u32[]{:S(2)}, u32[]{:S(2)}) %collective-permute-start.12) | collective-permute-done | bytes 49184 | tf_op jit(solution)/shard_map/ppermute | solution.py:543
  50.2 1.1 %collective-permute-done.13.refs_3_ = f32[96,128]{1,0:T(8,128)S(1)} collective-permute-done((f32[96,128]{1,0:T(8,128)S(1)}, f32[96,128]{1,0:T(8,128)S(1)}, u32[]{:S(2)}, u32[]{:S(2)}) %collective-permute-start.13) | collective-permute-done | bytes 49184 | tf_op jit(solution)/shard_map/ppermute | solution.py:543
  51.3 1.1 %collective-permute-start.14 = (bf16[384,256]{1,0:T(8,128)(2,1)S(1)}, bf16[384,256]{1,0:T(8,128)(2,1)S(1)}, u32[]{:S(2)}, u32[]{:S(2)}) collective-permute-start(bf16[384,256]{1,0:T(8,128)(2,1)S(1)} %get-tuple-element.63.refs_4_), channel_id=1, source_target_pairs={{0,8},{4,12},{8,0},{12,4},{1,9},{5,13},{9,1},{13,5},{2,10},{6,14},... | collective-permute-start | bytes 589832 | tf_op jit(solution)/shard_map/ppermute | solution.py:689
  52.4 1.6 %collective-permute-start.15 = (f32[32,128]{1,0:T(8,128)S(1)}, f32[32,128]{1,0:T(8,128)S(1)}, u32[]{:S(2)}, u32[]{:S(2)}) collective-permute-start(f32[32,128]{1,0:T(8,128)S(1)} %fusion.refs_6_), channel_id=1, source_target_pairs={{0,1},{1,0},{2,3},{3,2},{4,5},{5,4},{6,7},{7,6},{8,9},{9,8},{10,11... | collective-permute-start | bytes 49160 | tf_op jit(solution)/shard_map/ppermute | solution.py:543
  54.0 2.6 %collective-permute-start.16 = (f32[32,128]{1,0:T(8,128)S(1)}, f32[32,128]{1,0:T(8,128)S(1)}, u32[]{:S(2)}, u32[]{:S(2)}) collective-permute-start(f32[32,128]{1,0:T(8,128)S(1)} %fusion.refs_6_), channel_id=1, source_target_pairs={{0,2},{1,3},{2,0},{3,1},{4,6},{5,7},{6,4},{7,5},{8,10},{9,11},{10,... | collective-permute-start | bytes 49160 | tf_op jit(solution)/shard_map/ppermute | solution.py:543
  57.5 1.4 %collective-permute-done.16.refs_8_ = f32[32,128]{1,0:T(8,128)S(1)} collective-permute-done((f32[32,128]{1,0:T(8,128)S(1)}, f32[32,128]{1,0:T(8,128)S(1)}, u32[]{:S(2)}, u32[]{:S(2)}) %collective-permute-start.16) | collective-permute-done | bytes 16416 | tf_op jit(solution)/shard_map/ppermute | solution.py:543
  58.9 3.3 %collective-permute-done.17.refs_9_ = f32[32,128]{1,0:T(8,128)S(1)} collective-permute-done((f32[32,128]{1,0:T(8,128)S(1)}, f32[32,128]{1,0:T(8,128)S(1)}, u32[]{:S(2)}, u32[]{:S(2)}) %collective-permute-start.17) | collective-permute-done | bytes 16416 | tf_op jit(solution)/shard_map/ppermute | solution.py:543
  62.1 1.0 %score.1 = (bf16[1,3,1024]{2,1,0:T(4,128)(2,1)}, f32[1,3]{1,0:T(1,128)}, f32[16,512]{1,0:T(8,128)S(1)}) custom-call(f32[96,128]{1,0:T(8,128)S(1)} %get-tuple-element.61.refs_0_, f32[96,128]{1,0:T(8,128)S(1)} %collective-permute-done.11.refs_1_, f32[96,128]{1,0:T(8,128)S(1)} %collective-permute-done.12.refs_2_, ...), custom_call_target="tpu_custom_call" | custom-call | tf_op jit(solution)/shard_map/score/pallas_call | solution.py:690
  63.1 1.2 %collective-permute-done.18 = f32[16,512]{1,0:T(8,128)S(1)} collective-permute-done((f32[16,512]{1,0:T(8,128)S(1)}, f32[16,512]{1,0:T(8,128)S(1)}, u32[]{:S(2)}, u32[]{:S(2)}) %collective-permute-start.18) | collective-permute-done | bytes 32800 | tf_op jit(solution)/shard_map/ppermute | solution.py:704
  (39 shorter events, 4.0 us)
Async XLA Ops:
  16.9 2.1 %collective-permute-start.5 = (bf16[1152,256]{1,0:T(8,128)(2,1)S(1)}, bf16[1152,256]{1,0:T(8,128)(2,1)S(1)}, u32[]{:S(2)}, u32[]{:S(2)}) collective-permute-start(bf16[1152,256]{1,0:T(8,128)(2,1)S(1)} %convolution_convert_fusion.5), channel_id=1, source_target_pairs={{0,4},{4,0},{8,12},{12,8},{1,5},{5,1},{9,13},{13,9},{2,6},{6,2},{1... | collective-permute-start | bytes 1769480 | tf_op jit(solution)/shard_map/ppermute | solution.py:606
  19.0 3.8 %copy-start.3 = (bf16[16,4096]{1,0:T(8,128)(2,1)S(1)}, bf16[16,4096]{1,0:T(8,128)(2,1)}, u32[]{:S(2)}) copy-start(bf16[16,4096]{1,0:T(8,128)(2,1)} %lower_ref.1) | copy-start | bytes 393220
  19.0 3.8 %copy-start.5 = (s32[3,7]{1,0:T(4,128)S(1)}, s32[3,7]{1,0:T(4,128)}, u32[]{:S(2)}) copy-start(s32[3,7]{1,0:T(4,128)} %hard_ref.1) | copy-start | bytes 256
  19.9 17.8 %collective-permute-start.7 = (bf16[1152,256]{1,0:T(8,128)(2,1)S(1)}, bf16[1152,256]{1,0:T(8,128)(2,1)S(1)}, u32[]{:S(2)}, u32[]{:S(2)}) collective-permute-start(bf16[1152,256]{1,0:T(8,128)(2,1)S(1)} %add_convert_fusion.1), channel_id=1, source_target_pairs={{0,8},{4,12},{8,0},{12,4},{1,9},{5,13},{9,1},{13,5},{2,10},{6,14},... | collective-permute-start | bytes 1769480 | tf_op jit(solution)/shard_map/ppermute | solution.py:608
  24.2 5.1 %collective-permute-start.8 = (bf16[160,256]{1,0:T(8,128)(2,1)S(1)}, bf16[160,256]{1,0:T(8,128)(2,1)S(1)}, u32[]{:S(2)}, u32[]{:S(2)}) collective-permute-start(bf16[160,256]{1,0:T(8,128)(2,1)S(1)} %statistics.3), channel_id=1, source_target_pairs={{0,4},{4,0},{8,12},{12,8},{1,5},{5,1},{9,13},{13,9},{2,6},{6,2},{1... | collective-permute-start | bytes 245768 | tf_op jit(solution)/shard_map/ppermute | solution.py:632
  25.2 0.8 %copy-start.4 = (s32[1,12,128]{2,0,1:T(1,128)S(1)}, s32[1,12,128]{2,0,1:T(1,128)}, u32[]{:S(2)}) copy-start(s32[1,12,128]{2,0,1:T(1,128)} %param.9) | copy-start | bytes 18436
  27.3 10.4 %copy-start = (bf16[16,1024]{1,0:T(8,128)(2,1)S(1)}, bf16[16,1024]{1,0:T(8,128)(2,1)}, u32[]{:S(2)}) copy-start(bf16[16,1024]{1,0:T(8,128)(2,1)} %raise_ref.1) | copy-start | bytes 98308
  28.8 8.9 %collective-permute-start.6 = (bf16[1152,256]{1,0:T(8,128)(2,1)S(1)}, bf16[1152,256]{1,0:T(8,128)(2,1)S(1)}, u32[]{:S(2)}, u32[]{:S(2)}) collective-permute-start(bf16[1152,256]{1,0:T(8,128)(2,1)S(1)} %convolution_convert_fusion.3), channel_id=1, source_target_pairs={{0,4},{4,0},{8,12},{12,8},{1,5},{5,1},{9,13},{13,9},{2,6},{6,2},{1... | collective-permute-start | bytes 1769480 | tf_op jit(solution)/shard_map/ppermute | solution.py:638
  29.4 8.2 %collective-permute-start.9 = (bf16[112,256]{1,0:T(8,128)(2,1)S(1)}, bf16[112,256]{1,0:T(8,128)(2,1)S(1)}, u32[]{:S(2)}, u32[]{:S(2)}) collective-permute-start(bf16[112,256]{1,0:T(8,128)(2,1)S(1)} %pad_maximum_fusion.2), channel_id=1, source_target_pairs={{0,8},{4,12},{8,0},{12,4},{1,9},{5,13},{9,1},{13,5},{2,10},{6,14},... | collective-permute-start | bytes 172040 | tf_op jit(solution)/shard_map/ppermute | solution.py:636
  40.8 5.1 %collective-permute-start.10 = (bf16[208,256]{1,0:T(8,128)(2,1)S(1)}, bf16[208,256]{1,0:T(8,128)(2,1)S(1)}, u32[]{:S(2)}, u32[]{:S(2)}) collective-permute-start(bf16[208,256]{1,0:T(8,128)(2,1)S(1)} %get-tuple-element.60.near_ref), channel_id=1, source_target_pairs={{0,16},{16,0},{1,17},{17,1},{2,18},{18,2},{3,19},{19,3},{4,20},{20... | collective-permute-start | bytes 319496 | tf_op jit(solution)/shard_map/ppermute | solution.py:671
  46.0 1.9 %collective-permute-start.11 = (f32[96,128]{1,0:T(8,128)S(1)}, f32[96,128]{1,0:T(8,128)S(1)}, u32[]{:S(2)}, u32[]{:S(2)}) collective-permute-start(f32[96,128]{1,0:T(8,128)S(1)} %get-tuple-element.61.refs_0_), channel_id=1, source_target_pairs={{0,4},{4,0},{8,12},{12,8},{1,5},{5,1},{9,13},{13,9},{2,6},{6,2},{1... | collective-permute-start | bytes 147464 | tf_op jit(solution)/shard_map/ppermute | solution.py:543
  46.0 4.2 %collective-permute-start.12 = (f32[96,128]{1,0:T(8,128)S(1)}, f32[96,128]{1,0:T(8,128)S(1)}, u32[]{:S(2)}, u32[]{:S(2)}) collective-permute-start(f32[96,128]{1,0:T(8,128)S(1)} %get-tuple-element.61.refs_0_), channel_id=1, source_target_pairs={{0,8},{4,12},{8,0},{12,4},{1,9},{5,13},{9,1},{13,5},{2,10},{6,14},... | collective-permute-start | bytes 147464 | tf_op jit(solution)/shard_map/ppermute | solution.py:543
  47.6 3.7 %collective-permute-start.13 = (f32[96,128]{1,0:T(8,128)S(1)}, f32[96,128]{1,0:T(8,128)S(1)}, u32[]{:S(2)}, u32[]{:S(2)}) collective-permute-start(f32[96,128]{1,0:T(8,128)S(1)} %get-tuple-element.61.refs_0_), channel_id=1, source_target_pairs={{0,12},{4,8},{8,4},{12,0},{1,13},{5,9},{9,5},{13,1},{2,14},{6,10},... | collective-permute-start | bytes 147464 | tf_op jit(solution)/shard_map/ppermute | solution.py:543
  51.3 10.8 %collective-permute-start.14 = (bf16[384,256]{1,0:T(8,128)(2,1)S(1)}, bf16[384,256]{1,0:T(8,128)(2,1)S(1)}, u32[]{:S(2)}, u32[]{:S(2)}) collective-permute-start(bf16[384,256]{1,0:T(8,128)(2,1)S(1)} %get-tuple-element.63.refs_4_), channel_id=1, source_target_pairs={{0,8},{4,12},{8,0},{12,4},{1,9},{5,13},{9,1},{13,5},{2,10},{6,14},... | collective-permute-start | bytes 589832 | tf_op jit(solution)/shard_map/ppermute | solution.py:689
  52.4 5.0 %collective-permute-start.15 = (f32[32,128]{1,0:T(8,128)S(1)}, f32[32,128]{1,0:T(8,128)S(1)}, u32[]{:S(2)}, u32[]{:S(2)}) collective-permute-start(f32[32,128]{1,0:T(8,128)S(1)} %fusion.refs_6_), channel_id=1, source_target_pairs={{0,1},{1,0},{2,3},{3,2},{4,5},{5,4},{6,7},{7,6},{8,9},{9,8},{10,11... | collective-permute-start | bytes 49160 | tf_op jit(solution)/shard_map/ppermute | solution.py:543
  54.0 4.9 %collective-permute-start.16 = (f32[32,128]{1,0:T(8,128)S(1)}, f32[32,128]{1,0:T(8,128)S(1)}, u32[]{:S(2)}, u32[]{:S(2)}) collective-permute-start(f32[32,128]{1,0:T(8,128)S(1)} %fusion.refs_6_), channel_id=1, source_target_pairs={{0,2},{1,3},{2,0},{3,1},{4,6},{5,7},{6,4},{7,5},{8,10},{9,11},{10,... | collective-permute-start | bytes 49160 | tf_op jit(solution)/shard_map/ppermute | solution.py:543
  56.6 5.5 %collective-permute-start.17 = (f32[32,128]{1,0:T(8,128)S(1)}, f32[32,128]{1,0:T(8,128)S(1)}, u32[]{:S(2)}, u32[]{:S(2)}) collective-permute-start(f32[32,128]{1,0:T(8,128)S(1)} %fusion.refs_6_), channel_id=1, source_target_pairs={{0,3},{1,2},{2,1},{3,0},{4,7},{5,6},{6,5},{7,4},{8,11},{9,10},{10,... | collective-permute-start | bytes 49160 | tf_op jit(solution)/shard_map/ppermute | solution.py:543
  63.1 1.2 %collective-permute-start.18 = (f32[16,512]{1,0:T(8,128)S(1)}, f32[16,512]{1,0:T(8,128)S(1)}, u32[]{:S(2)}, u32[]{:S(2)}) collective-permute-start(f32[16,512]{1,0:T(8,128)S(1)} %get-tuple-element.68), channel_id=1, source_target_pairs={{0,4},{4,0},{8,12},{12,8},{1,5},{5,1},{9,13},{13,9},{2,6},{6,2},{1... | collective-permute-start | bytes 98312 | tf_op jit(solution)/shard_map/ppermute | solution.py:704

commit v20 on v19

--- a/solution.py
+++ b/solution.py
@@ -451,12 +451,12 @@
 
 def score_kernel(*refs, texts, stripes, negatives):
     packed0, packed1, packed2, packed3, slopes0, slopes2 = refs[0:6]
-    dots0, dots1, dots2, dots3, misc_ref, sharp_ref = refs[6:12]
-    embed_ref, loss_ref, up_ref = refs[12:15]
+    dots0, dots1, misc_ref, sharp_ref = refs[6:10]
+    embed_ref, loss_ref, up_ref = refs[10:13]
     rows = 2 * ROWS
     per_shard = loss_ref.shape[1]
     group, shard = lax.axis_index("group"), lax.axis_index("dp")
-    dots = ((dots0[...] + dots1[...]) + (dots2[...] + dots3[...]))[:, 0:rows]
+    dots = (dots0[...] + dots1[...])[:, 0:rows]
     down, across = iota((rows, rows), 0), iota((rows, rows), 1)
     same = down == across
     real = (lax.rem(down, ROWS) < texts) & (lax.rem(across, ROWS) < texts)
@@ -685,7 +685,8 @@
     dots = [x[0:rows] for x in packed]
     dots = (dots[0] + dots[1]) + (dots[2] + dots[3])
     slopes, dots = lax.optimization_barrier((slopes, dots))
-    dots = exchange(dots, "mp", parts)
+    dots = dots + lax.ppermute(dots, "mp", [(i, i ^ 1) for i in range(parts)])
+    dots = [dots, lax.ppermute(dots, "mp", [(i, i ^ 2) for i in range(parts)])]
     slopes = [slopes, lax.ppermute(slopes, "dp", other_y)]
     embeddings, losses, update = pl.pallas_call(
         functools.partial(
@@ -696,7 +697,7 @@
             jax.ShapeDtypeStruct((1, per_shard), jnp.float32),
             jax.ShapeDtypeStruct((ROWS, part_width // 2), jnp.float32),
         ],
-        in_specs=[vmem_spec()] * 11 + [smem_spec()],
+        in_specs=[vmem_spec()] * 9 + [smem_spec()],
         out_specs=[vmem_spec()] * 3,
         compiler_params=modest,
         name="score",

time: 65.3 us -> 64.1 us (0.982)
  starting transfers between devices: 13.9 us -> 12.8 us
    ppermute x6 -> x3, waiting for transfers between devices: 8.09 us -> 3.63 us  [exchange(): return [x] + [lax.ppermute(x, axis, step) for step in steps]]
    ppermute x6 -> x3, starting transfers between devices: 6.25 us -> 1.9 us  [exchange(): return [x] + [lax.ppermute(x, axis, step) for step in steps]]
    ppermute x0 -> x2, starting transfers between devices: none -> 4.16 us  [the longest x1 2.58 us: split_body(): dots = [dots, lax.ppermute(dots, 'mp', [(i, i ^ 2) for i in range(parts)])]]
    ppermute x0 -> x2, waiting for transfers between devices: none -> 3.56 us  [the longest x1 2.16 us: split_body(): dots = dots + lax.ppermute(dots, 'mp', [(i, i ^ 1) for i in range(parts)])]
    ppermute x1, starting transfers between devices: 2.39 us -> 1.47 us  [split_body(): far_side = lax.ppermute(sent, 'group', [(0, 1), (1, 0)])]
  transfers between devices with their start and end apart: 14 -> 13, of which waited for: 8 -> 8; matrix products, arithmetic and copies ran while one was open for 6% -> 6% of each run, Pallas kernels for 2% -> 2%
where the time goes in v20:
time: 64.1 us; the launch traced here: 63.9 us
  waiting for transfers between devices  21.5 us (34%)
  Pallas kernels  21.3 us (33%)
  starting transfers between devices  12.8 us (20%)
  matrix products  3.3 us (5%)
  between operations  2.11 us (3%)
  local copies, waits for them, and re-layouts  1.44 us (2%)
  other arithmetic  1.37 us (2%)
    pallas_call x1, Pallas kernels, project(): pl.pallas_call(functools.partial(gather_kernel, base=base), out_shape=[ja...  15.7 us
    ppermute x1, waiting for transfers between devices, project(): sent = lax.ppermute(sent, 'dp', other_y).astype(jnp.float32)  8.16 us
    ppermute x3, waiting for transfers between devices, exchange(): return [x] + [lax.ppermute(x, axis, step) for step in steps]  3.63 us
    ppermute x1, waiting for transfers between devices, split_body(): far_side = lax.ppermute(sent, 'group', [(0, 1), (1, 0)])  3.3 us
    dot_general x4, matrix products, mm(): return lax.dot_general(a, b, dims, preferred_element_type=jnp.float32)  3.3 us
    pallas_call x1, Pallas kernels, split_body(): pl.pallas_call(functools.partial(pool_kernel, model_width=float(features...  3.1 us
    ppermute x1, starting transfers between devices, project(): far = lax.ppermute(chip1, 'dp', other_y)  2.96 us
    ppermute x1, starting transfers between devices, split_body(): dots = [dots, lax.ppermute(dots, 'mp', [(i, i ^ 2) for i in range(parts)])]  2.58 us
  transfers between devices with their start and end apart: 13, of which 8 were waited for; matrix products, arithmetic and copies ran while one was open for 6% of the time, Pallas kernels for 2%

profile of v20, /device:TPU:0, one launch (start us, length us, event | category | flops | bytes accessed | tf_op | source)
XLA Modules:
  0.0 63.9 jit_solution(6879379950812523487)
XLA Ops:
  0.6 15.7 %gather.3 = (bf16[1024,1152]{1,0:T(8,128)(2,1)S(1)}, bf16[1152,128]{1,0:T(8,128)(2,1)S(1)}, bf16[1024,256]{1,0:T(8,128)(2,1)S(1)}, bf16[1024,256]{1,0:T(8,128)(2...) custom-call(s32[12,1,128]{2,1,0:T(1,128)} %bitcast.17, bf16[1024,16384]{1,0:T(8,128)(2,1)} %vocab_ref.1, ...), custom_call_target="tpu_custom_call" | custom-call | tf_op jit(solution)/shard_map/gather/pallas_call | solution.py:573
  16.4 0.8 %convolution_convert_fusion.5 = bf16[1152,256]{1,0:T(8,128)(2,1)S(1)} fusion(bf16[1024,1152]{1,0:T(8,128)(2,1)S(1)} %get-tuple-element.50.turned_any, bf16[1024,256]{1,0:T(8,128)(2,1)S(1)} %get-tuple-element.49), kind=kOutput, calls=%fused_computation.11 | convolution fusion | flops 604274688 | bytes 3473408 | tf_op jit(solution)/shard_map/dot_general | solution.py:128
  17.7 1.6 %collective-permute-done.5 = bf16[1152,256]{1,0:T(8,128)(2,1)S(1)} collective-permute-done((bf16[1152,256]{1,0:T(8,128)(2,1)S(1)}, bf16[1152,256]{1,0:T(8,128)(2,1)S(1)}, u32[]{:S(2)}, u32[]{:S(2)}) %collective-permute-start.5) | collective-permute-done | bytes 589856 | tf_op jit(solution)/shard_map/ppermute | solution.py:606
  19.3 0.8 %add_convert_fusion.1 = bf16[1152,256]{1,0:T(8,128)(2,1)S(1)} fusion(bf16[1152,256]{1,0:T(8,128)(2,1)S(1)} %collective-permute-done.5, bf16[1024,1152]{1,0:T(8,128)(2,1)S(1)} %get-tuple-element.50.turned_any, bf16[1024,256]{1,0:T(8,128)(2,1)S(1)} %get-tuple-element.48), kind=kOutput, calls=%fused_computation.12 | convolution fusion | flops 604864512 | bytes 4063232 | tf_op jit(solution)/shard_map/dot_general | solution.py:128
  20.2 3.0 %collective-permute-start.7 = (bf16[1152,256]{1,0:T(8,128)(2,1)S(1)}, bf16[1152,256]{1,0:T(8,128)(2,1)S(1)}, u32[]{:S(2)}, u32[]{:S(2)}) collective-permute-start(bf16[1152,256]{1,0:T(8,128)(2,1)S(1)} %add_convert_fusion.1), channel_id=1, source_target_pairs={{0,8},{4,12},{8,0},{12,4},{1,9},{5,13},{9,1},{13,5},{2,10},{6,14},... | collective-permute-start | bytes 1769480 | tf_op jit(solution)/shard_map/ppermute | solution.py:608
  23.1 1.4 %statistics.3 = bf16[160,256]{1,0:T(8,128)(2,1)S(1)} custom-call(bf16[1024,1152]{1,0:T(8,128)(2,1)S(1)} %get-tuple-element.50.turned_any, bf16[1152,128]{1,0:T(8,128)(2,1)S(1)} %get-tuple-element.53.member_any.member_ref, s32[3,7]{1,0:T(4,128)S(1)} %copy-done.5, bf16[16,4096]{1,0:T(8,128)(2,1)S(1)} %copy-done.3), custom_call_target="tpu_custom_call" | custom-call | flops 339738624 | bytes 2359296 | tf_op jit(solution)/shard_map/statistics/pallas_call | solution.py:610
  24.6 0.8 %convolution_convert_fusion.4.own_ref = bf16[1152,256]{1,0:T(8,128)(2,1)S(1)} fusion(bf16[1024,1152]{1,0:T(8,128)(2,1)S(1)} %get-tuple-element.50.turned_any, bf16[1024,256]{1,0:T(8,128)(2,1)S(1)} %get-tuple-element.51), kind=kOutput, calls=%fused_computation.10 | convolution fusion | flops 604274688 | bytes 3473408 | tf_op jit(solution)/shard_map/dot_general | solution.py:128
  25.5 0.8 %convolution_convert_fusion.3 = bf16[1152,256]{1,0:T(8,128)(2,1)S(1)} fusion(bf16[1024,1152]{1,0:T(8,128)(2,1)S(1)} %get-tuple-element.50.turned_any, bf16[1024,256]{1,0:T(8,128)(2,1)S(1)} %get-tuple-element.52), kind=kOutput, calls=%fused_computation.9 | convolution fusion | flops 604274688 | bytes 3473408 | tf_op jit(solution)/shard_map/dot_general | solution.py:128
  27.6 1.4 %conditional.1 = (bf16[384,256]{1,0:T(8,128)(2,1)S(1)}, bf16[384,256]{1,0:T(8,128)(2,1)}, bf16[384,256]{1,0:T(8,128)(2,1)}, f32[64,256]{1,0:T(8,128)S(1)}, bf16[384,128]{1,0:T(8,128)(2,1)S(1)}) conditional(s32[]{:T(128)} %convert_element_type.65, () %tuple.22, (s32[12,1,128]{2,1,0:T(1,128)S(1)}, bf16[1024,16384]{1,0:T(8,128)(2,1)}, ...), branch_computations={%region_1.0_spmd, %region_2.0_spmd} | conditional | flops 919347200 | bytes 11411752 | solution.py:647
  27.7 0.7 %broadcast.7.clone = bf16[384,256]{1,0:T(8,128)(2,1)} broadcast(bf16[]{:T(256)} %constant.4.clone), dimensions={} | broadcast | bytes 196610 | tf_op jit(solution)/shard_map/broadcast.5
  29.8 8.2 %collective-permute-done.9 = bf16[112,256]{1,0:T(8,128)(2,1)S(1)} collective-permute-done((bf16[112,256]{1,0:T(8,128)(2,1)S(1)}, bf16[112,256]{1,0:T(8,128)(2,1)S(1)}, u32[]{:S(2)}, u32[]{:S(2)}) %collective-permute-start.9) | collective-permute-done | bytes 57376 | tf_op jit(solution)/shard_map/ppermute | solution.py:636
  38.0 3.1 %pool.1 = (bf16[208,256]{1,0:T(8,128)(2,1)S(1)}, f32[16,256]{1,0:T(8,128)S(1)}) custom-call(s32[12,1,128]{2,1,0:T(1,128)S(1)} %bitcast.20, bf16[1152,256]{1,0:T(8,128)(2,1)S(1)} %convolution_convert_fusion.4.own_ref, bf16[1152,256]{1,0:T(8,128)(2,1)S(1)} %collective-permute-done.6.core_any, bf16[1152,256]{1,0:T(8,128)(2,1)S(1)} %collective-permute-done.7.far_any, ...), custom_call_target="tpu_custom_call" | custom-call | tf_op jit(solution)/shard_map/pool/pallas_call | solution.py:652
  41.1 1.5 %collective-permute-start.10 = (bf16[208,256]{1,0:T(8,128)(2,1)S(1)}, bf16[208,256]{1,0:T(8,128)(2,1)S(1)}, u32[]{:S(2)}, u32[]{:S(2)}) collective-permute-start(bf16[208,256]{1,0:T(8,128)(2,1)S(1)} %get-tuple-element.60.near_ref), channel_id=1, source_target_pairs={{0,16},{16,0},{1,17},{17,1},{2,18},{18,2},{3,19},{19,3},{4,20},{20... | collective-permute-start | bytes 319496 | tf_op jit(solution)/shard_map/ppermute | solution.py:671
  42.6 3.3 %collective-permute-done.10.far_ref = bf16[208,256]{1,0:T(8,128)(2,1)S(1)} collective-permute-done((bf16[208,256]{1,0:T(8,128)(2,1)S(1)}, bf16[208,256]{1,0:T(8,128)(2,1)S(1)}, u32[]{:S(2)}, u32[]{:S(2)}) %collective-permute-start.10) | collective-permute-done | bytes 106528 | tf_op jit(solution)/shard_map/ppermute | solution.py:671
  46.0 1.8 %collective-permute-start.12 = (f32[96,128]{1,0:T(8,128)S(1)}, f32[96,128]{1,0:T(8,128)S(1)}, u32[]{:S(2)}, u32[]{:S(2)}) collective-permute-start(f32[96,128]{1,0:T(8,128)S(1)} %get-tuple-element.61.refs_0_), channel_id=1, source_target_pairs={{0,8},{4,12},{8,0},{12,4},{1,9},{5,13},{9,1},{13,5},{2,10},{6,14},... | collective-permute-start | bytes 147464 | tf_op jit(solution)/shard_map/ppermute | solution.py:543
  47.9 2.3 %collective-permute-done.12.refs_2_ = f32[96,128]{1,0:T(8,128)S(1)} collective-permute-done((f32[96,128]{1,0:T(8,128)S(1)}, f32[96,128]{1,0:T(8,128)S(1)}, u32[]{:S(2)}, u32[]{:S(2)}) %collective-permute-start.12) | collective-permute-done | bytes 49184 | tf_op jit(solution)/shard_map/ppermute | solution.py:543
  50.2 1.4 %collective-permute-done.13.refs_3_ = f32[96,128]{1,0:T(8,128)S(1)} collective-permute-done((f32[96,128]{1,0:T(8,128)S(1)}, f32[96,128]{1,0:T(8,128)S(1)}, u32[]{:S(2)}, u32[]{:S(2)}) %collective-permute-start.13) | collective-permute-done | bytes 49184 | tf_op jit(solution)/shard_map/ppermute | solution.py:543
  51.6 1.1 %collective-permute-start.14 = (bf16[384,256]{1,0:T(8,128)(2,1)S(1)}, bf16[384,256]{1,0:T(8,128)(2,1)S(1)}, u32[]{:S(2)}, u32[]{:S(2)}) collective-permute-start(bf16[384,256]{1,0:T(8,128)(2,1)S(1)} %get-tuple-element.63.refs_4_), channel_id=1, source_target_pairs={{0,8},{4,12},{8,0},{12,4},{1,9},{5,13},{9,1},{13,5},{2,10},{6,14},... | collective-permute-start | bytes 589832 | tf_op jit(solution)/shard_map/ppermute | solution.py:690
  52.6 1.6 %collective-permute-start.15 = (f32[32,128]{1,0:T(8,128)S(1)}, f32[32,128]{1,0:T(8,128)S(1)}, u32[]{:S(2)}, u32[]{:S(2)}) collective-permute-start(f32[32,128]{1,0:T(8,128)S(1)} %fusion), channel_id=1, source_target_pairs={{0,1},{1,0},{2,3},{3,2},{4,5},{5,4},{6,7},{7,6},{8,9},{9,8},{10,11... | collective-permute-start | bytes 49160 | tf_op jit(solution)/shard_map/ppermute | solution.py:688
  54.2 2.2 %collective-permute-done.15 = f32[32,128]{1,0:T(8,128)S(1)} collective-permute-done((f32[32,128]{1,0:T(8,128)S(1)}, f32[32,128]{1,0:T(8,128)S(1)}, u32[]{:S(2)}, u32[]{:S(2)}) %collective-permute-start.15) | collective-permute-done | bytes 16416 | tf_op jit(solution)/shard_map/ppermute | solution.py:688
  56.4 2.6 %collective-permute-start.16 = (f32[32,128]{1,0:T(8,128)S(1)}, f32[32,128]{1,0:T(8,128)S(1)}, u32[]{:S(2)}, u32[]{:S(2)}) collective-permute-start(f32[32,128]{1,0:T(8,128)S(1)} %add.43.refs_6_), channel_id=1, source_target_pairs={{0,2},{1,3},{2,0},{3,1},{4,6},{5,7},{6,4},{7,5},{8,10},{9,11},{10,... | collective-permute-start | bytes 49160 | tf_op jit(solution)/shard_map/ppermute | solution.py:689
  59.6 1.4 %collective-permute-done.16.refs_7_ = f32[32,128]{1,0:T(8,128)S(1)} collective-permute-done((f32[32,128]{1,0:T(8,128)S(1)}, f32[32,128]{1,0:T(8,128)S(1)}, u32[]{:S(2)}, u32[]{:S(2)}) %collective-permute-start.16) | collective-permute-done | bytes 16416 | tf_op jit(solution)/shard_map/ppermute | solution.py:689
  61.0 1.0 %score.1 = (bf16[1,3,1024]{2,1,0:T(4,128)(2,1)}, f32[1,3]{1,0:T(1,128)}, f32[16,512]{1,0:T(8,128)S(1)}) custom-call(f32[96,128]{1,0:T(8,128)S(1)} %get-tuple-element.61.refs_0_, f32[96,128]{1,0:T(8,128)S(1)} %collective-permute-done.11.refs_1_, f32[96,128]{1,0:T(8,128)S(1)} %collective-permute-done.12.refs_2_, ...), custom_call_target="tpu_custom_call" | custom-call | tf_op jit(solution)/shard_map/score/pallas_call | solution.py:691
  62.0 1.2 %collective-permute-done.17 = f32[16,512]{1,0:T(8,128)S(1)} collective-permute-done((f32[16,512]{1,0:T(8,128)S(1)}, f32[16,512]{1,0:T(8,128)S(1)}, u32[]{:S(2)}, u32[]{:S(2)}) %collective-permute-start.17) | collective-permute-done | bytes 32800 | tf_op jit(solution)/shard_map/ppermute | solution.py:705
  (38 shorter events, 3.6 us)
Async XLA Ops:
  17.2 2.1 %collective-permute-start.5 = (bf16[1152,256]{1,0:T(8,128)(2,1)S(1)}, bf16[1152,256]{1,0:T(8,128)(2,1)S(1)}, u32[]{:S(2)}, u32[]{:S(2)}) collective-permute-start(bf16[1152,256]{1,0:T(8,128)(2,1)S(1)} %convolution_convert_fusion.5), channel_id=1, source_target_pairs={{0,4},{4,0},{8,12},{12,8},{1,5},{5,1},{9,13},{13,9},{2,6},{6,2},{1... | collective-permute-start | bytes 1769480 | tf_op jit(solution)/shard_map/ppermute | solution.py:606
  19.3 3.8 %copy-start.3 = (bf16[16,4096]{1,0:T(8,128)(2,1)S(1)}, bf16[16,4096]{1,0:T(8,128)(2,1)}, u32[]{:S(2)}) copy-start(bf16[16,4096]{1,0:T(8,128)(2,1)} %lower_ref.1) | copy-start | bytes 393220
  19.3 3.8 %copy-start.5 = (s32[3,7]{1,0:T(4,128)S(1)}, s32[3,7]{1,0:T(4,128)}, u32[]{:S(2)}) copy-start(s32[3,7]{1,0:T(4,128)} %hard_ref.1) | copy-start | bytes 256
  20.2 17.8 %collective-permute-start.7 = (bf16[1152,256]{1,0:T(8,128)(2,1)S(1)}, bf16[1152,256]{1,0:T(8,128)(2,1)S(1)}, u32[]{:S(2)}, u32[]{:S(2)}) collective-permute-start(bf16[1152,256]{1,0:T(8,128)(2,1)S(1)} %add_convert_fusion.1), channel_id=1, source_target_pairs={{0,8},{4,12},{8,0},{12,4},{1,9},{5,13},{9,1},{13,5},{2,10},{6,14},... | collective-permute-start | bytes 1769480 | tf_op jit(solution)/shard_map/ppermute | solution.py:608
  24.5 5.1 %collective-permute-start.8 = (bf16[160,256]{1,0:T(8,128)(2,1)S(1)}, bf16[160,256]{1,0:T(8,128)(2,1)S(1)}, u32[]{:S(2)}, u32[]{:S(2)}) collective-permute-start(bf16[160,256]{1,0:T(8,128)(2,1)S(1)} %statistics.3), channel_id=1, source_target_pairs={{0,4},{4,0},{8,12},{12,8},{1,5},{5,1},{9,13},{13,9},{2,6},{6,2},{1... | collective-permute-start | bytes 245768 | tf_op jit(solution)/shard_map/ppermute | solution.py:632
  25.5 0.8 %copy-start.4 = (s32[1,12,128]{2,0,1:T(1,128)S(1)}, s32[1,12,128]{2,0,1:T(1,128)}, u32[]{:S(2)}) copy-start(s32[1,12,128]{2,0,1:T(1,128)} %param.9) | copy-start | bytes 18436
  27.6 10.4 %copy-start = (bf16[16,1024]{1,0:T(8,128)(2,1)S(1)}, bf16[16,1024]{1,0:T(8,128)(2,1)}, u32[]{:S(2)}) copy-start(bf16[16,1024]{1,0:T(8,128)(2,1)} %raise_ref.1) | copy-start | bytes 98308
  29.1 8.9 %collective-permute-start.6 = (bf16[1152,256]{1,0:T(8,128)(2,1)S(1)}, bf16[1152,256]{1,0:T(8,128)(2,1)S(1)}, u32[]{:S(2)}, u32[]{:S(2)}) collective-permute-start(bf16[1152,256]{1,0:T(8,128)(2,1)S(1)} %convolution_convert_fusion.3), channel_id=1, source_target_pairs={{0,4},{4,0},{8,12},{12,8},{1,5},{5,1},{9,13},{13,9},{2,6},{6,2},{1... | collective-permute-start | bytes 1769480 | tf_op jit(solution)/shard_map/ppermute | solution.py:638
  29.7 8.3 %collective-permute-start.9 = (bf16[112,256]{1,0:T(8,128)(2,1)S(1)}, bf16[112,256]{1,0:T(8,128)(2,1)S(1)}, u32[]{:S(2)}, u32[]{:S(2)}) collective-permute-start(bf16[112,256]{1,0:T(8,128)(2,1)S(1)} %pad_maximum_fusion.2), channel_id=1, source_target_pairs={{0,8},{4,12},{8,0},{12,4},{1,9},{5,13},{9,1},{13,5},{2,10},{6,14},... | collective-permute-start | bytes 172040 | tf_op jit(solution)/shard_map/ppermute | solution.py:636
  41.1 4.8 %collective-permute-start.10 = (bf16[208,256]{1,0:T(8,128)(2,1)S(1)}, bf16[208,256]{1,0:T(8,128)(2,1)S(1)}, u32[]{:S(2)}, u32[]{:S(2)}) collective-permute-start(bf16[208,256]{1,0:T(8,128)(2,1)S(1)} %get-tuple-element.60.near_ref), channel_id=1, source_target_pairs={{0,16},{16,0},{1,17},{17,1},{2,18},{18,2},{3,19},{19,3},{4,20},{20... | collective-permute-start | bytes 319496 | tf_op jit(solution)/shard_map/ppermute | solution.py:671
  46.0 1.9 %collective-permute-start.11 = (f32[96,128]{1,0:T(8,128)S(1)}, f32[96,128]{1,0:T(8,128)S(1)}, u32[]{:S(2)}, u32[]{:S(2)}) collective-permute-start(f32[96,128]{1,0:T(8,128)S(1)} %get-tuple-element.61.refs_0_), channel_id=1, source_target_pairs={{0,4},{4,0},{8,12},{12,8},{1,5},{5,1},{9,13},{13,9},{2,6},{6,2},{1... | collective-permute-start | bytes 147464 | tf_op jit(solution)/shard_map/ppermute | solution.py:543
  46.0 4.2 %collective-permute-start.12 = (f32[96,128]{1,0:T(8,128)S(1)}, f32[96,128]{1,0:T(8,128)S(1)}, u32[]{:S(2)}, u32[]{:S(2)}) collective-permute-start(f32[96,128]{1,0:T(8,128)S(1)} %get-tuple-element.61.refs_0_), channel_id=1, source_target_pairs={{0,8},{4,12},{8,0},{12,4},{1,9},{5,13},{9,1},{13,5},{2,10},{6,14},... | collective-permute-start | bytes 147464 | tf_op jit(solution)/shard_map/ppermute | solution.py:543
  47.8 3.7 %collective-permute-start.13 = (f32[96,128]{1,0:T(8,128)S(1)}, f32[96,128]{1,0:T(8,128)S(1)}, u32[]{:S(2)}, u32[]{:S(2)}) collective-permute-start(f32[96,128]{1,0:T(8,128)S(1)} %get-tuple-element.61.refs_0_), channel_id=1, source_target_pairs={{0,12},{4,8},{8,4},{12,0},{1,13},{5,9},{9,5},{13,1},{2,14},{6,10},... | collective-permute-start | bytes 147464 | tf_op jit(solution)/shard_map/ppermute | solution.py:543
  51.6 9.5 %collective-permute-start.14 = (bf16[384,256]{1,0:T(8,128)(2,1)S(1)}, bf16[384,256]{1,0:T(8,128)(2,1)S(1)}, u32[]{:S(2)}, u32[]{:S(2)}) collective-permute-start(bf16[384,256]{1,0:T(8,128)(2,1)S(1)} %get-tuple-element.63.refs_4_), channel_id=1, source_target_pairs={{0,8},{4,12},{8,0},{12,4},{1,9},{5,13},{9,1},{13,5},{2,10},{6,14},... | collective-permute-start | bytes 589832 | tf_op jit(solution)/shard_map/ppermute | solution.py:690
  52.6 3.7 %collective-permute-start.15 = (f32[32,128]{1,0:T(8,128)S(1)}, f32[32,128]{1,0:T(8,128)S(1)}, u32[]{:S(2)}, u32[]{:S(2)}) collective-permute-start(f32[32,128]{1,0:T(8,128)S(1)} %fusion), channel_id=1, source_target_pairs={{0,1},{1,0},{2,3},{3,2},{4,5},{5,4},{6,7},{7,6},{8,9},{9,8},{10,11... | collective-permute-start | bytes 49160 | tf_op jit(solution)/shard_map/ppermute | solution.py:688
  56.4 4.6 %collective-permute-start.16 = (f32[32,128]{1,0:T(8,128)S(1)}, f32[32,128]{1,0:T(8,128)S(1)}, u32[]{:S(2)}, u32[]{:S(2)}) collective-permute-start(f32[32,128]{1,0:T(8,128)S(1)} %add.43.refs_6_), channel_id=1, source_target_pairs={{0,2},{1,3},{2,0},{3,1},{4,6},{5,7},{6,4},{7,5},{8,10},{9,11},{10,... | collective-permute-start | bytes 49160 | tf_op jit(solution)/shard_map/ppermute | solution.py:689
  62.0 1.2 %collective-permute-start.17 = (f32[16,512]{1,0:T(8,128)S(1)}, f32[16,512]{1,0:T(8,128)S(1)}, u32[]{:S(2)}, u32[]{:S(2)}) collective-permute-start(f32[16,512]{1,0:T(8,128)S(1)} %get-tuple-element.68), channel_id=1, source_target_pairs={{0,4},{4,0},{8,12},{12,8},{1,5},{5,1},{9,13},{13,9},{2,6},{6,2},{1... | collective-permute-start | bytes 98312 | tf_op jit(solution)/shard_map/ppermute | solution.py:705

commit v21 on v20

--- a/solution.py
+++ b/solution.py
@@ -110,7 +110,7 @@
     return (embeddings, losses[None], adapter_up_gradient)
 
 
-BLOCK_BITS, GROUP_BITS, LANE_BITS, ROW_BITS = 10, 9, 7, 4
+BLOCK_BITS, GROUP_BITS, LANE_BITS, ROW_BITS = 10, 8, 7, 4
 IDS_PER_BLOCK = 1 << BLOCK_BITS
 IDS_PER_GROUP = 1 << GROUP_BITS
 CHUNK = 384

time: 64.1 us -> 67 us (1.045)
  Pallas kernels: 21.3 us -> 24 us
  starting transfers between devices: 12.8 us -> 13.5 us
  waiting for transfers between devices: 21.5 us -> 20.8 us
    pallas_call x1, Pallas kernels: 15.7 us -> 18.4 us  [project(): pl.pallas_call(functools.partial(gather_kernel, base=base), out_shape=[ja...]
    ppermute x1, starting transfers between devices: 1.47 us -> 2.2 us  [split_body(): far_side = lax.ppermute(sent, 'group', [(0, 1), (1, 0)])]
where the time goes in v21:
time: 67 us; the launch traced here: 66.5 us
  Pallas kernels  24 us (36%)
  waiting for transfers between devices  20.8 us (31%)
  starting transfers between devices  13.5 us (20%)
  matrix products  3.3 us (5%)
  between operations  2.11 us (3%)
  local copies, waits for them, and re-layouts  1.44 us (2%)
  other arithmetic  1.37 us (2%)
    pallas_call x1, Pallas kernels, project(): pl.pallas_call(functools.partial(gather_kernel, base=base), out_shape=[ja...  18.4 us
    ppermute x1, waiting for transfers between devices, project(): sent = lax.ppermute(sent, 'dp', other_y).astype(jnp.float32)  8.16 us
    ppermute x3, waiting for transfers between devices, exchange(): return [x] + [lax.ppermute(x, axis, step) for step in steps]  3.54 us
    dot_general x4, matrix products, mm(): return lax.dot_general(a, b, dims, preferred_element_type=jnp.float32)  3.3 us
    pallas_call x1, Pallas kernels, split_body(): pl.pallas_call(functools.partial(pool_kernel, model_width=float(features...  3.1 us
    ppermute x1, starting transfers between devices, project(): far = lax.ppermute(chip1, 'dp', other_y)  2.97 us
    ppermute x1, waiting for transfers between devices, split_body(): far_side = lax.ppermute(sent, 'group', [(0, 1), (1, 0)])  2.68 us
    ppermute x1, starting transfers between devices, split_body(): dots = [dots, lax.ppermute(dots, 'mp', [(i, i ^ 2) for i in range(parts)])]  2.58 us
  transfers between devices with their start and end apart: 13, of which 8 were waited for; matrix products, arithmetic and copies ran while one was open for 6% of the time, Pallas kernels for 2%

profile of v21, /device:TPU:0, one launch (start us, length us, event | category | flops | bytes accessed | tf_op | source)
XLA Modules:
  0.0 66.5 jit_solution(16396002823108504171)
XLA Ops:
  0.6 18.4 %gather.3 = (bf16[1024,1152]{1,0:T(8,128)(2,1)S(1)}, bf16[1152,128]{1,0:T(8,128)(2,1)S(1)}, bf16[1024,256]{1,0:T(8,128)(2,1)S(1)}, bf16[1024,256]{1,0:T(8,128)(2...) custom-call(s32[12,1,128]{2,1,0:T(1,128)} %bitcast.17, bf16[1024,16384]{1,0:T(8,128)(2,1)} %vocab_ref.1, ...), custom_call_target="tpu_custom_call" | custom-call | tf_op jit(solution)/shard_map/gather/pallas_call | solution.py:573
  19.0 0.8 %convolution_convert_fusion.5 = bf16[1152,256]{1,0:T(8,128)(2,1)S(1)} fusion(bf16[1024,1152]{1,0:T(8,128)(2,1)S(1)} %get-tuple-element.50.turned_any, bf16[1024,256]{1,0:T(8,128)(2,1)S(1)} %get-tuple-element.49), kind=kOutput, calls=%fused_computation.11 | convolution fusion | flops 604274688 | bytes 3473408 | tf_op jit(solution)/shard_map/dot_general | solution.py:128
  20.4 1.6 %collective-permute-done.5 = bf16[1152,256]{1,0:T(8,128)(2,1)S(1)} collective-permute-done((bf16[1152,256]{1,0:T(8,128)(2,1)S(1)}, bf16[1152,256]{1,0:T(8,128)(2,1)S(1)}, u32[]{:S(2)}, u32[]{:S(2)}) %collective-permute-start.5) | collective-permute-done | bytes 589856 | tf_op jit(solution)/shard_map/ppermute | solution.py:606
  22.0 0.8 %add_convert_fusion.1 = bf16[1152,256]{1,0:T(8,128)(2,1)S(1)} fusion(bf16[1152,256]{1,0:T(8,128)(2,1)S(1)} %collective-permute-done.5, bf16[1024,1152]{1,0:T(8,128)(2,1)S(1)} %get-tuple-element.50.turned_any, bf16[1024,256]{1,0:T(8,128)(2,1)S(1)} %get-tuple-element.48), kind=kOutput, calls=%fused_computation.12 | convolution fusion | flops 604864512 | bytes 4063232 | tf_op jit(solution)/shard_map/dot_general | solution.py:128
  22.8 3.0 %collective-permute-start.7 = (bf16[1152,256]{1,0:T(8,128)(2,1)S(1)}, bf16[1152,256]{1,0:T(8,128)(2,1)S(1)}, u32[]{:S(2)}, u32[]{:S(2)}) collective-permute-start(bf16[1152,256]{1,0:T(8,128)(2,1)S(1)} %add_convert_fusion.1), channel_id=1, source_target_pairs={{0,8},{4,12},{8,0},{12,4},{1,9},{5,13},{9,1},{13,5},{2,10},{6,14},... | collective-permute-start | bytes 1769480 | tf_op jit(solution)/shard_map/ppermute | solution.py:608
  25.8 1.4 %statistics.3 = bf16[160,256]{1,0:T(8,128)(2,1)S(1)} custom-call(bf16[1024,1152]{1,0:T(8,128)(2,1)S(1)} %get-tuple-element.50.turned_any, bf16[1152,128]{1,0:T(8,128)(2,1)S(1)} %get-tuple-element.53.member_any.member_ref, s32[3,7]{1,0:T(4,128)S(1)} %copy-done.5, bf16[16,4096]{1,0:T(8,128)(2,1)S(1)} %copy-done.3), custom_call_target="tpu_custom_call" | custom-call | flops 339738624 | bytes 2359296 | tf_op jit(solution)/shard_map/statistics/pallas_call | solution.py:610
  27.3 0.8 %convolution_convert_fusion.4.own_ref = bf16[1152,256]{1,0:T(8,128)(2,1)S(1)} fusion(bf16[1024,1152]{1,0:T(8,128)(2,1)S(1)} %get-tuple-element.50.turned_any, bf16[1024,256]{1,0:T(8,128)(2,1)S(1)} %get-tuple-element.51), kind=kOutput, calls=%fused_computation.10 | convolution fusion | flops 604274688 | bytes 3473408 | tf_op jit(solution)/shard_map/dot_general | solution.py:128
  28.2 0.8 %convolution_convert_fusion.3 = bf16[1152,256]{1,0:T(8,128)(2,1)S(1)} fusion(bf16[1024,1152]{1,0:T(8,128)(2,1)S(1)} %get-tuple-element.50.turned_any, bf16[1024,256]{1,0:T(8,128)(2,1)S(1)} %get-tuple-element.52), kind=kOutput, calls=%fused_computation.9 | convolution fusion | flops 604274688 | bytes 3473408 | tf_op jit(solution)/shard_map/dot_general | solution.py:128
  30.3 1.4 %conditional.1 = (bf16[384,256]{1,0:T(8,128)(2,1)S(1)}, bf16[384,256]{1,0:T(8,128)(2,1)}, bf16[384,256]{1,0:T(8,128)(2,1)}, f32[64,256]{1,0:T(8,128)S(1)}, bf16[384,128]{1,0:T(8,128)(2,1)S(1)}) conditional(s32[]{:T(128)} %convert_element_type.65, () %tuple.22, (s32[12,1,128]{2,1,0:T(1,128)S(1)}, bf16[1024,16384]{1,0:T(8,128)(2,1)}, ...), branch_computations={%region_1.0_spmd, %region_2.0_spmd} | conditional | flops 919347200 | bytes 11411752 | solution.py:647
  30.3 0.7 %broadcast.7.clone = bf16[384,256]{1,0:T(8,128)(2,1)} broadcast(bf16[]{:T(256)} %constant.4.clone), dimensions={} | broadcast | bytes 196610 | tf_op jit(solution)/shard_map/broadcast.5
  32.5 8.2 %collective-permute-done.9 = bf16[112,256]{1,0:T(8,128)(2,1)S(1)} collective-permute-done((bf16[112,256]{1,0:T(8,128)(2,1)S(1)}, bf16[112,256]{1,0:T(8,128)(2,1)S(1)}, u32[]{:S(2)}, u32[]{:S(2)}) %collective-permute-start.9) | collective-permute-done | bytes 57376 | tf_op jit(solution)/shard_map/ppermute | solution.py:636
  40.7 3.1 %pool.1 = (bf16[208,256]{1,0:T(8,128)(2,1)S(1)}, f32[16,256]{1,0:T(8,128)S(1)}) custom-call(s32[12,1,128]{2,1,0:T(1,128)S(1)} %bitcast.20, bf16[1152,256]{1,0:T(8,128)(2,1)S(1)} %convolution_convert_fusion.4.own_ref, bf16[1152,256]{1,0:T(8,128)(2,1)S(1)} %collective-permute-done.6.core_any, bf16[1152,256]{1,0:T(8,128)(2,1)S(1)} %collective-permute-done.7.far_any, ...), custom_call_target="tpu_custom_call" | custom-call | tf_op jit(solution)/shard_map/pool/pallas_call | solution.py:652
  43.8 2.2 %collective-permute-start.10 = (bf16[208,256]{1,0:T(8,128)(2,1)S(1)}, bf16[208,256]{1,0:T(8,128)(2,1)S(1)}, u32[]{:S(2)}, u32[]{:S(2)}) collective-permute-start(bf16[208,256]{1,0:T(8,128)(2,1)S(1)} %get-tuple-element.60.near_ref), channel_id=1, source_target_pairs={{0,16},{16,0},{1,17},{17,1},{2,18},{18,2},{3,19},{19,3},{4,20},{20... | collective-permute-start | bytes 319496 | tf_op jit(solution)/shard_map/ppermute | solution.py:671
  46.0 2.7 %collective-permute-done.10.far_ref = bf16[208,256]{1,0:T(8,128)(2,1)S(1)} collective-permute-done((bf16[208,256]{1,0:T(8,128)(2,1)S(1)}, bf16[208,256]{1,0:T(8,128)(2,1)S(1)}, u32[]{:S(2)}, u32[]{:S(2)}) %collective-permute-start.10) | collective-permute-done | bytes 106528 | tf_op jit(solution)/shard_map/ppermute | solution.py:671
  48.8 1.7 %collective-permute-start.12 = (f32[96,128]{1,0:T(8,128)S(1)}, f32[96,128]{1,0:T(8,128)S(1)}, u32[]{:S(2)}, u32[]{:S(2)}) collective-permute-start(f32[96,128]{1,0:T(8,128)S(1)} %get-tuple-element.61.refs_0_), channel_id=1, source_target_pairs={{0,8},{4,12},{8,0},{12,4},{1,9},{5,13},{9,1},{13,5},{2,10},{6,14},... | collective-permute-start | bytes 147464 | tf_op jit(solution)/shard_map/ppermute | solution.py:543
  50.7 2.3 %collective-permute-done.12.refs_2_ = f32[96,128]{1,0:T(8,128)S(1)} collective-permute-done((f32[96,128]{1,0:T(8,128)S(1)}, f32[96,128]{1,0:T(8,128)S(1)}, u32[]{:S(2)}, u32[]{:S(2)}) %collective-permute-start.12) | collective-permute-done | bytes 49184 | tf_op jit(solution)/shard_map/ppermute | solution.py:543
  53.0 1.2 %collective-permute-done.13.refs_3_ = f32[96,128]{1,0:T(8,128)S(1)} collective-permute-done((f32[96,128]{1,0:T(8,128)S(1)}, f32[96,128]{1,0:T(8,128)S(1)}, u32[]{:S(2)}, u32[]{:S(2)}) %collective-permute-start.13) | collective-permute-done | bytes 49184 | tf_op jit(solution)/shard_map/ppermute | solution.py:543
  54.2 1.1 %collective-permute-start.14 = (bf16[384,256]{1,0:T(8,128)(2,1)S(1)}, bf16[384,256]{1,0:T(8,128)(2,1)S(1)}, u32[]{:S(2)}, u32[]{:S(2)}) collective-permute-start(bf16[384,256]{1,0:T(8,128)(2,1)S(1)} %get-tuple-element.63.refs_4_), channel_id=1, source_target_pairs={{0,8},{4,12},{8,0},{12,4},{1,9},{5,13},{9,1},{13,5},{2,10},{6,14},... | collective-permute-start | bytes 589832 | tf_op jit(solution)/shard_map/ppermute | solution.py:690
  55.3 1.6 %collective-permute-start.15 = (f32[32,128]{1,0:T(8,128)S(1)}, f32[32,128]{1,0:T(8,128)S(1)}, u32[]{:S(2)}, u32[]{:S(2)}) collective-permute-start(f32[32,128]{1,0:T(8,128)S(1)} %fusion), channel_id=1, source_target_pairs={{0,1},{1,0},{2,3},{3,2},{4,5},{5,4},{6,7},{7,6},{8,9},{9,8},{10,11... | collective-permute-start | bytes 49160 | tf_op jit(solution)/shard_map/ppermute | solution.py:688
  56.9 2.2 %collective-permute-done.15 = f32[32,128]{1,0:T(8,128)S(1)} collective-permute-done((f32[32,128]{1,0:T(8,128)S(1)}, f32[32,128]{1,0:T(8,128)S(1)}, u32[]{:S(2)}, u32[]{:S(2)}) %collective-permute-start.15) | collective-permute-done | bytes 16416 | tf_op jit(solution)/shard_map/ppermute | solution.py:688
  59.1 2.6 %collective-permute-start.16 = (f32[32,128]{1,0:T(8,128)S(1)}, f32[32,128]{1,0:T(8,128)S(1)}, u32[]{:S(2)}, u32[]{:S(2)}) collective-permute-start(f32[32,128]{1,0:T(8,128)S(1)} %add.43.refs_6_), channel_id=1, source_target_pairs={{0,2},{1,3},{2,0},{3,1},{4,6},{5,7},{6,4},{7,5},{8,10},{9,11},{10,... | collective-permute-start | bytes 49160 | tf_op jit(solution)/shard_map/ppermute | solution.py:689
  62.3 1.4 %collective-permute-done.16.refs_7_ = f32[32,128]{1,0:T(8,128)S(1)} collective-permute-done((f32[32,128]{1,0:T(8,128)S(1)}, f32[32,128]{1,0:T(8,128)S(1)}, u32[]{:S(2)}, u32[]{:S(2)}) %collective-permute-start.16) | collective-permute-done | bytes 16416 | tf_op jit(solution)/shard_map/ppermute | solution.py:689
  63.7 1.0 %score.1 = (bf16[1,3,1024]{2,1,0:T(4,128)(2,1)}, f32[1,3]{1,0:T(1,128)}, f32[16,512]{1,0:T(8,128)S(1)}) custom-call(f32[96,128]{1,0:T(8,128)S(1)} %get-tuple-element.61.refs_0_, f32[96,128]{1,0:T(8,128)S(1)} %collective-permute-done.11.refs_1_, f32[96,128]{1,0:T(8,128)S(1)} %collective-permute-done.12.refs_2_, ...), custom_call_target="tpu_custom_call" | custom-call | tf_op jit(solution)/shard_map/score/pallas_call | solution.py:691
  64.7 1.2 %collective-permute-done.17 = f32[16,512]{1,0:T(8,128)S(1)} collective-permute-done((f32[16,512]{1,0:T(8,128)S(1)}, f32[16,512]{1,0:T(8,128)S(1)}, u32[]{:S(2)}, u32[]{:S(2)}) %collective-permute-start.17) | collective-permute-done | bytes 32800 | tf_op jit(solution)/shard_map/ppermute | solution.py:705
  (38 shorter events, 3.7 us)
Async XLA Ops:
  19.9 2.1 %collective-permute-start.5 = (bf16[1152,256]{1,0:T(8,128)(2,1)S(1)}, bf16[1152,256]{1,0:T(8,128)(2,1)S(1)}, u32[]{:S(2)}, u32[]{:S(2)}) collective-permute-start(bf16[1152,256]{1,0:T(8,128)(2,1)S(1)} %convolution_convert_fusion.5), channel_id=1, source_target_pairs={{0,4},{4,0},{8,12},{12,8},{1,5},{5,1},{9,13},{13,9},{2,6},{6,2},{1... | collective-permute-start | bytes 1769480 | tf_op jit(solution)/shard_map/ppermute | solution.py:606
  22.0 3.8 %copy-start.3 = (bf16[16,4096]{1,0:T(8,128)(2,1)S(1)}, bf16[16,4096]{1,0:T(8,128)(2,1)}, u32[]{:S(2)}) copy-start(bf16[16,4096]{1,0:T(8,128)(2,1)} %lower_ref.1) | copy-start | bytes 393220
  22.0 3.8 %copy-start.5 = (s32[3,7]{1,0:T(4,128)S(1)}, s32[3,7]{1,0:T(4,128)}, u32[]{:S(2)}) copy-start(s32[3,7]{1,0:T(4,128)} %hard_ref.1) | copy-start | bytes 256
  22.8 17.9 %collective-permute-start.7 = (bf16[1152,256]{1,0:T(8,128)(2,1)S(1)}, bf16[1152,256]{1,0:T(8,128)(2,1)S(1)}, u32[]{:S(2)}, u32[]{:S(2)}) collective-permute-start(bf16[1152,256]{1,0:T(8,128)(2,1)S(1)} %add_convert_fusion.1), channel_id=1, source_target_pairs={{0,8},{4,12},{8,0},{12,4},{1,9},{5,13},{9,1},{13,5},{2,10},{6,14},... | collective-permute-start | bytes 1769480 | tf_op jit(solution)/shard_map/ppermute | solution.py:608
  27.2 5.1 %collective-permute-start.8 = (bf16[160,256]{1,0:T(8,128)(2,1)S(1)}, bf16[160,256]{1,0:T(8,128)(2,1)S(1)}, u32[]{:S(2)}, u32[]{:S(2)}) collective-permute-start(bf16[160,256]{1,0:T(8,128)(2,1)S(1)} %statistics.3), channel_id=1, source_target_pairs={{0,4},{4,0},{8,12},{12,8},{1,5},{5,1},{9,13},{13,9},{2,6},{6,2},{1... | collective-permute-start | bytes 245768 | tf_op jit(solution)/shard_map/ppermute | solution.py:632
  28.1 0.8 %copy-start.4 = (s32[1,12,128]{2,0,1:T(1,128)S(1)}, s32[1,12,128]{2,0,1:T(1,128)}, u32[]{:S(2)}) copy-start(s32[1,12,128]{2,0,1:T(1,128)} %param.9) | copy-start | bytes 18436
  30.3 10.4 %copy-start = (bf16[16,1024]{1,0:T(8,128)(2,1)S(1)}, bf16[16,1024]{1,0:T(8,128)(2,1)}, u32[]{:S(2)}) copy-start(bf16[16,1024]{1,0:T(8,128)(2,1)} %raise_ref.1) | copy-start | bytes 98308
  31.7 8.9 %collective-permute-start.6 = (bf16[1152,256]{1,0:T(8,128)(2,1)S(1)}, bf16[1152,256]{1,0:T(8,128)(2,1)S(1)}, u32[]{:S(2)}, u32[]{:S(2)}) collective-permute-start(bf16[1152,256]{1,0:T(8,128)(2,1)S(1)} %convolution_convert_fusion.3), channel_id=1, source_target_pairs={{0,4},{4,0},{8,12},{12,8},{1,5},{5,1},{9,13},{13,9},{2,6},{6,2},{1... | collective-permute-start | bytes 1769480 | tf_op jit(solution)/shard_map/ppermute | solution.py:638
  32.4 8.3 %collective-permute-start.9 = (bf16[112,256]{1,0:T(8,128)(2,1)S(1)}, bf16[112,256]{1,0:T(8,128)(2,1)S(1)}, u32[]{:S(2)}, u32[]{:S(2)}) collective-permute-start(bf16[112,256]{1,0:T(8,128)(2,1)S(1)} %pad_maximum_fusion.2), channel_id=1, source_target_pairs={{0,8},{4,12},{8,0},{12,4},{1,9},{5,13},{9,1},{13,5},{2,10},{6,14},... | collective-permute-start | bytes 172040 | tf_op jit(solution)/shard_map/ppermute | solution.py:636
  43.8 4.9 %collective-permute-start.10 = (bf16[208,256]{1,0:T(8,128)(2,1)S(1)}, bf16[208,256]{1,0:T(8,128)(2,1)S(1)}, u32[]{:S(2)}, u32[]{:S(2)}) collective-permute-start(bf16[208,256]{1,0:T(8,128)(2,1)S(1)} %get-tuple-element.60.near_ref), channel_id=1, source_target_pairs={{0,16},{16,0},{1,17},{17,1},{2,18},{18,2},{3,19},{19,3},{4,20},{20... | collective-permute-start | bytes 319496 | tf_op jit(solution)/shard_map/ppermute | solution.py:671
  48.8 1.9 %collective-permute-start.11 = (f32[96,128]{1,0:T(8,128)S(1)}, f32[96,128]{1,0:T(8,128)S(1)}, u32[]{:S(2)}, u32[]{:S(2)}) collective-permute-start(f32[96,128]{1,0:T(8,128)S(1)} %get-tuple-element.61.refs_0_), channel_id=1, source_target_pairs={{0,4},{4,0},{8,12},{12,8},{1,5},{5,1},{9,13},{13,9},{2,6},{6,2},{1... | collective-permute-start | bytes 147464 | tf_op jit(solution)/shard_map/ppermute | solution.py:543
  48.8 4.2 %collective-permute-start.12 = (f32[96,128]{1,0:T(8,128)S(1)}, f32[96,128]{1,0:T(8,128)S(1)}, u32[]{:S(2)}, u32[]{:S(2)}) collective-permute-start(f32[96,128]{1,0:T(8,128)S(1)} %get-tuple-element.61.refs_0_), channel_id=1, source_target_pairs={{0,8},{4,12},{8,0},{12,4},{1,9},{5,13},{9,1},{13,5},{2,10},{6,14},... | collective-permute-start | bytes 147464 | tf_op jit(solution)/shard_map/ppermute | solution.py:543
  50.5 3.7 %collective-permute-start.13 = (f32[96,128]{1,0:T(8,128)S(1)}, f32[96,128]{1,0:T(8,128)S(1)}, u32[]{:S(2)}, u32[]{:S(2)}) collective-permute-start(f32[96,128]{1,0:T(8,128)S(1)} %get-tuple-element.61.refs_0_), channel_id=1, source_target_pairs={{0,12},{4,8},{8,4},{12,0},{1,13},{5,9},{9,5},{13,1},{2,14},{6,10},... | collective-permute-start | bytes 147464 | tf_op jit(solution)/shard_map/ppermute | solution.py:543
  54.2 9.5 %collective-permute-start.14 = (bf16[384,256]{1,0:T(8,128)(2,1)S(1)}, bf16[384,256]{1,0:T(8,128)(2,1)S(1)}, u32[]{:S(2)}, u32[]{:S(2)}) collective-permute-start(bf16[384,256]{1,0:T(8,128)(2,1)S(1)} %get-tuple-element.63.refs_4_), channel_id=1, source_target_pairs={{0,8},{4,12},{8,0},{12,4},{1,9},{5,13},{9,1},{13,5},{2,10},{6,14},... | collective-permute-start | bytes 589832 | tf_op jit(solution)/shard_map/ppermute | solution.py:690
  55.3 3.7 %collective-permute-start.15 = (f32[32,128]{1,0:T(8,128)S(1)}, f32[32,128]{1,0:T(8,128)S(1)}, u32[]{:S(2)}, u32[]{:S(2)}) collective-permute-start(f32[32,128]{1,0:T(8,128)S(1)} %fusion), channel_id=1, source_target_pairs={{0,1},{1,0},{2,3},{3,2},{4,5},{5,4},{6,7},{7,6},{8,9},{9,8},{10,11... | collective-permute-start | bytes 49160 | tf_op jit(solution)/shard_map/ppermute | solution.py:688
  59.1 4.6 %collective-permute-start.16 = (f32[32,128]{1,0:T(8,128)S(1)}, f32[32,128]{1,0:T(8,128)S(1)}, u32[]{:S(2)}, u32[]{:S(2)}) collective-permute-start(f32[32,128]{1,0:T(8,128)S(1)} %add.43.refs_6_), channel_id=1, source_target_pairs={{0,2},{1,3},{2,0},{3,1},{4,6},{5,7},{6,4},{7,5},{8,10},{9,11},{10,... | collective-permute-start | bytes 49160 | tf_op jit(solution)/shard_map/ppermute | solution.py:689
  64.7 1.2 %collective-permute-start.17 = (f32[16,512]{1,0:T(8,128)S(1)}, f32[16,512]{1,0:T(8,128)S(1)}, u32[]{:S(2)}, u32[]{:S(2)}) collective-permute-start(f32[16,512]{1,0:T(8,128)S(1)} %get-tuple-element.68), channel_id=1, source_target_pairs={{0,4},{4,0},{8,12},{12,8},{1,5},{5,1},{9,13},{13,9},{2,6},{6,2},{1... | collective-permute-start | bytes 98312 | tf_op jit(solution)/shard_map/ppermute | solution.py:705
